TPU v7x, 32 devices: a whole 2x2x4 slice. The times are simulated.
32 devices in a mesh: grp: 2 (over x), ep: 16 (over z, y, core), dp: 1.
Axes of the slice: x: 2, y: 2, z: 4, core: 2. Of those that a mesh axis runs over, the one named last changes fastest.
Arguments:
- rows_in: bfloat16 [2, 256, 4096], P('grp', ('ep', 'dp')), may hold values from -6 to 6
- cotangent: bfloat16 [256, 4096], P(('ep', 'dp')), may hold values from -6 to 6
- lengths: int32 [4], replicated, may hold values from 1 to 128, 256 in all
- train_experts: int32 [256, 8], P(('ep', 'dp')), may hold values from 0 to 15, all different within a row; in each aligned block of 16 rows (0 to 15, 16 to 31, ...) at most 10 rows name the same one
- train_gates: float32 [256, 8], P(('ep', 'dp')), may hold values from 0.02 to 0.3
- decode_experts: int32 [2, 256, 8], P(None, ('ep', 'dp')), may hold values from 0 to 15, all different within a row; in each aligned block of 16 rows (0 to 15, 16 to 31, ..., all dimensions but the last counted through in order) at most 10 rows name the same one
- decode_gates: float32 [2, 256, 8], P(None, ('ep', 'dp')), may hold values from 0.02 to 0.3
- gate_up: bfloat16 [2, 16, 4096, 2, 768], P('grp', 'ep', None, None, 'dp'), may hold values from -0.09375 to 0.09375
- down: bfloat16 [2, 16, 768, 4096], P('grp', 'ep', 'dp'), may hold values from -0.21875 to 0.21875
Outputs:
- result: bfloat16 [2, 256, 4096], P('grp', ('ep', 'dp'))
Inputs may be any that keep to these rules, and one draw needn't show every extreme that they name: `train_experts`: in every aligned block of 16 rows (the rows of one device), the 8 ids of a row differ and no id is named by more than 10 rows of the block; some block reaches 10. `decode_experts`: for each step, in every aligned block of 16 rows (the rows of one device), the 8 ids of a row differ and no id is named by more than 10 rows of the block; some block reaches 10. The lengths sum to 256 and the longest is exactly 128.
All inputs are finite; a program needn't handle non-finite values.
Results may differ from a plain program's by a relative error of at most 0.008.
Values may be sent and summed in bfloat16 or wider, within the bound.
No kernel may reach another device: no remote copies, remote signals or barrier semaphores. Data moves between devices by JAX's collectives and lax.ppermute only.
A program may use at most 192 MiB of HBM per device.

v0:
```python
import functools

import jax
import jax.numpy as jnp
from jax import lax
from jax.experimental import pallas as pl
from jax.experimental.pallas import tpu as pltpu
from jax.sharding import PartitionSpec as P

EPSILON = 1e-06
AXES = ("ep", "dp")


def across(block, source, target):
    return lax.ppermute(block, "grp", [(source, target)])


def radices(device_count):
    sizes = []
    rest = device_count
    for size in (2, 2):
        if rest % size == 0 and rest > 1:
            sizes.append(size)
            rest //= size
    while rest > 1:
        size = 4 if rest % 4 == 0 else 2
        sizes.append(size)
        rest //= size
    return sizes[::-1]


def stages(device_count):
    strides = []
    stride = device_count
    for size in radices(device_count):
        stride //= size
        strides.append((stride, size))
    return strides


def swap(block, device_count, flip, roles):
    pairs = [
        (role * device_count + i, role * device_count + (i ^ flip))
        for role in roles
        for i in range(device_count)
    ]
    return lax.ppermute(block, ("grp",) + AXES, pairs)


def gather(block, device_count, roles):
    for stride, size in stages(device_count):
        got = [swap(block, device_count, turn * stride, roles) for turn in range(1, size)]
        block = jnp.concatenate([block] + got, axis=0)
    return block


def scatter_sum(part, device_count, roles):
    for stride, size in stages(device_count)[::-1]:
        cuts = jnp.split(part, size, axis=0)
        total = cuts[0].astype(jnp.float32)
        for turn in range(1, size):
            total = total + swap(cuts[turn], device_count, turn * stride, roles).astype(jnp.float32)
        part = total.astype(jnp.bfloat16)
    return total


def two_part(table):
    upper = lax.reduce_precision(table, 8, 7)
    return [upper.astype(jnp.bfloat16), (table - upper).astype(jnp.bfloat16)]


def gate_table(expert_ids, gate_values, expert_count):
    named = expert_ids[:, :, None] == jnp.arange(expert_count, dtype=jnp.int32)[None, None, :]
    return jnp.sum(jnp.where(named, gate_values[:, :, None], 0.0), axis=1)


def renew(weights, grads, axis_number, rate):
    scale = jnp.sqrt(jnp.mean(grads * grads, axis=axis_number, keepdims=True) + EPSILON)
    return (weights.astype(jnp.float32) - rate * grads / scale).astype(jnp.bfloat16)


def wide(a, b, contract):
    return lax.dot_general(a, b, (contract, ((), ())), preferred_element_type=jnp.float32)


def nn(a, b):
    return wide(a, b, ((1,), (0,)))


def nt(a, b):
    return wide(a, b, ((1,), (1,)))


def pick_gates(table, column, step):
    places = lax.broadcasted_iota(jnp.int32, table.shape, 1)
    taken = (places == column) | (places == column + step)
    return jnp.sum(jnp.where(taken, table.astype(jnp.float32), 0.0), axis=1, keepdims=True)


def ffn_kernel(place, rows_ref, table_ref, gu_ref, dn_ref, out_ref, total, *, experts):
    step = pl.program_id(0)
    rows = rows_ref[...]
    active = nn(rows, gu_ref[0])
    upward = nn(rows, gu_ref[1])
    hidden = (active * jax.nn.sigmoid(active) * upward).astype(jnp.bfloat16)
    width = dn_ref.shape[1]
    tile = min(width, 1024)
    last = pl.num_programs(0) - 1
    gates = pick_gates(table_ref[...], place[0], experts)
    for lower in range(0, width, tile):
        cut = pl.ds(lower, tile)
        fresh = nn(hidden, dn_ref[:, cut])

        @pl.when(step == 0)
        def _():
            total[:, cut] = fresh

        @pl.when((step > 0) & (step < last))
        def _():
            total[:, cut] += fresh

        @pl.when((step > 0) & (step == last))
        def _():
            out_ref[:, cut] = (gates * (total[:, cut] + fresh)).astype(jnp.bfloat16)

    if pl.num_programs(0) == 1:
        out_ref[...] = (gates * total[...]).astype(jnp.bfloat16)


def hidden_block(hidden_count):
    return 256 if hidden_count % 256 == 0 else 128


def ffn_call(place, rows, table, planes, weights_dn, experts):
    row_count = rows.shape[0]
    hidden_count, width = weights_dn.shape
    spare = table.shape[1] - width
    size = hidden_block(hidden_count)
    steps = hidden_count // size
    return pl.pallas_call(
        functools.partial(ffn_kernel, experts=experts),
        grid_spec=pltpu.PrefetchScalarGridSpec(
            num_scalar_prefetch=1,
            grid=(steps,),
            in_specs=[
                pl.BlockSpec((row_count, width), lambda j, p: (0, 0)),
                pl.BlockSpec((row_count, spare), lambda j, p: (0, width // spare)),
                pl.BlockSpec((2, width, size), lambda j, p: (0, 0, j)),
                pl.BlockSpec((size, width), lambda j, p: (j, 0)),
            ],
            out_specs=pl.BlockSpec((row_count, width), lambda j, p: (0, 0)),
            scratch_shapes=[pltpu.VMEM((row_count, width), jnp.float32)],
        ),
        out_shape=jax.ShapeDtypeStruct((row_count, width), jnp.bfloat16),
        compiler_params=pltpu.CompilerParams(vmem_limit_bytes=40 << 20),
        cost_estimate=pl.CostEstimate(
            flops=6 * row_count * hidden_count * width,
            bytes_accessed=6 * hidden_count * width,
            transcendentals=row_count * hidden_count,
        ),
        name="ffn",
    )(place, rows, table, planes, weights_dn)


def learn_kernel(
    place, rows_ref, table_ref, cot_ref, gu_ref, dn_ref, dx_ref, new_gu_ref, new_dn_ref,
    turned, pulls, total, grads, grads_dn, *, experts, rates,
):
    step = pl.program_id(0)
    width = rows_ref.shape[1]
    tile = min(width, 512)
    tiles = width // tile

    @pl.when(step == 0)
    def _():
        gates = pick_gates(table_ref[...], place[0], experts)
        total[...] = jnp.zeros_like(total)

        @pl.loop(0, tiles)
        def _(i):
            cut = pl.ds(pl.multiple_of(i * tile, tile), tile)
            pulls[:, cut] = (gates * cot_ref[:, cut].astype(jnp.float32)).astype(jnp.bfloat16)
            turned[cut, :] = rows_ref[:, cut].T

    active = nn(rows_ref[...], gu_ref[0])
    upward = nn(rows_ref[...], gu_ref[1])
    back = nt(pulls[...], dn_ref[...])
    sigma = jax.nn.sigmoid(active)
    swish = active * sigma
    hidden = (swish * upward).astype(jnp.bfloat16)
    d_active = (back * upward * sigma * (1.0 + active * (1.0 - sigma))).astype(jnp.bfloat16)
    d_upward = (back * swish).astype(jnp.bfloat16)
    hidden_turned = hidden.T

    @pl.loop(0, tiles)
    def _(i):
        cut = pl.ds(pl.multiple_of(i * tile, tile), tile)
        total[:, cut] += nt(d_active, gu_ref[0, cut, :]) + nt(d_upward, gu_ref[1, cut, :])

    for half, sent in ((0, d_active), (1, d_upward)):
        def square(i, so_far):
            cut = pl.ds(pl.multiple_of(i * tile, tile), tile)
            fresh = nn(turned[cut, :], sent)
            grads[cut, :] = fresh
            return so_far + jnp.sum(fresh * fresh, axis=0, keepdims=True)

        squares = lax.fori_loop(0, tiles, square, jnp.zeros((1, sent.shape[1]), jnp.float32))
        scale = rates[0] / jnp.sqrt(squares / width + EPSILON)

        @pl.loop(0, tiles)
        def _(i):
            cut = pl.ds(pl.multiple_of(i * tile, tile), tile)
            old = gu_ref[half, cut, :].astype(jnp.float32)
            new_gu_ref[half, cut, :] = (old - grads[cut, :] * scale).astype(jnp.bfloat16)

    def square_dn(i, so_far):
        cut = pl.ds(pl.multiple_of(i * tile, tile), tile)
        fresh = nn(hidden_turned, pulls[:, cut])
        grads_dn[:, cut] = fresh
        return so_far + jnp.sum(fresh * fresh, axis=1, keepdims=True)

    squares = lax.fori_loop(0, tiles, square_dn, jnp.zeros((dn_ref.shape[0], 1), jnp.float32))
    scale = rates[1] / jnp.sqrt(squares / width + EPSILON)

    @pl.loop(0, tiles)
    def _(i):
        cut = pl.ds(pl.multiple_of(i * tile, tile), tile)
        old = dn_ref[:, cut].astype(jnp.float32)
        new_dn_ref[:, cut] = (old - grads_dn[:, cut] * scale).astype(jnp.bfloat16)

    @pl.when(step == pl.num_programs(0) - 1)
    def _():
        @pl.loop(0, tiles)
        def _(i):
            cut = pl.ds(pl.multiple_of(i * tile, tile), tile)
            dx_ref[:, cut] = total[:, cut].astype(jnp.bfloat16)


def learn_call(place, rows, table, cots, planes, weights_dn, experts, rates):
    row_count = rows.shape[0]
    hidden_count, width = weights_dn.shape
    spare = table.shape[1] - width
    size = hidden_block(hidden_count)
    once = pl.Buffered(1)
    return pl.pallas_call(
        functools.partial(learn_kernel, experts=experts, rates=rates),
        grid_spec=pltpu.PrefetchScalarGridSpec(
            num_scalar_prefetch=1,
            grid=(hidden_count // size,),
            in_specs=[
                pl.BlockSpec((row_count, width), lambda j, p: (0, 0), pipeline_mode=once),
                pl.BlockSpec((row_count, spare), lambda j, p: (0, width // spare)),
                pl.BlockSpec((row_count, width), lambda j, p: (0, 0), pipeline_mode=once),
                pl.BlockSpec((2, width, size), lambda j, p: (0, 0, j)),
                pl.BlockSpec((size, width), lambda j, p: (j, 0)),
            ],
            out_specs=[
                pl.BlockSpec((row_count, width), lambda j, p: (0, 0)),
                pl.BlockSpec((2, width, size), lambda j, p: (0, 0, j)),
                pl.BlockSpec((size, width), lambda j, p: (j, 0)),
            ],
            scratch_shapes=[
                pltpu.VMEM((width, row_count), jnp.bfloat16),
                pltpu.VMEM((row_count, width), jnp.bfloat16),
                pltpu.VMEM((row_count, width), jnp.float32),
                pltpu.VMEM((width, size), jnp.float32),
                pltpu.VMEM((size, width), jnp.float32),
            ],
        ),
        out_shape=[
            jax.ShapeDtypeStruct((row_count, width), jnp.bfloat16),
            jax.ShapeDtypeStruct(planes.shape, jnp.bfloat16),
            jax.ShapeDtypeStruct(weights_dn.shape, jnp.bfloat16),
        ],
        compiler_params=pltpu.CompilerParams(vmem_limit_bytes=58 << 20),
        cost_estimate=pl.CostEstimate(
            flops=16 * row_count * hidden_count * width,
            bytes_accessed=12 * hidden_count * width,
            transcendentals=row_count * hidden_count,
        ),
        name="learn",
    )(place, rows, table, cots, planes, weights_dn)


def unset(like):
    return pl.pallas_call(
        lambda out_ref: None,
        out_shape=jax.ShapeDtypeStruct(like.shape, like.dtype),
        out_specs=pl.BlockSpec(memory_space=pl.ANY),
        name="unset",
    )()


def ffn_plain(place, rows, table, planes, weights_dn, experts):
    width = weights_dn.shape[1]
    rows = rows[:, :width]
    gates = pick_gates(table[:, width:], place[0], experts)
    active = nn(rows, planes[0])
    upward = nn(rows, planes[1])
    hidden = (active * jax.nn.sigmoid(active) * upward).astype(jnp.bfloat16)
    return (gates * nn(hidden, weights_dn)).astype(jnp.bfloat16)


def learn_plain(place, rows, table, cots, planes, weights_dn, experts, rates):
    width = weights_dn.shape[1]
    rows = rows[:, :width]
    gates = pick_gates(table[:, width:], place[0], experts)
    pulls = (gates * cots.astype(jnp.float32)).astype(jnp.bfloat16)
    active = nn(rows, planes[0])
    upward = nn(rows, planes[1])
    back = nt(pulls, weights_dn)
    sigma = jax.nn.sigmoid(active)
    swish = active * sigma
    hidden = (swish * upward).astype(jnp.bfloat16)
    d_active = (back * upward * sigma * (1.0 + active * (1.0 - sigma))).astype(jnp.bfloat16)
    d_upward = (back * swish).astype(jnp.bfloat16)
    dx_part = (nt(d_active, planes[0]) + nt(d_upward, planes[1])).astype(jnp.bfloat16)
    new_planes = jnp.stack(
        [
            renew(planes[0], wide(rows, d_active, ((0,), (0,))), 0, rates[0]),
            renew(planes[1], wide(rows, d_upward, ((0,), (0,))), 0, rates[0]),
        ],
        axis=0,
    )
    new_dn = renew(weights_dn, wide(hidden, pulls, ((0,), (0,))), 1, rates[1])
    return (dx_part, new_planes, new_dn)


def per_device(
    rows_in,
    cotangent,
    lengths,
    train_experts,
    train_gates,
    decode_experts,
    decode_gates,
    gate_up,
    down,
):
    ep_count = lax.axis_size("ep")
    dp_count = lax.axis_size("dp")
    row_count, model_width = cotangent.shape
    is_learner = lax.axis_index("grp") == 0
    hidden_all = gate_up.shape[4] * dp_count
    own_dn = down[0, 0]
    planes = lax.optimization_barrier(jnp.transpose(gate_up[0, 0], (1, 0, 2)))

    own_rows = rows_in[0]
    total_rows = row_count * ep_count * dp_count
    longest = 2 * total_rows // lengths.shape[0]
    first_row = (lax.axis_index("ep") * dp_count + lax.axis_index("dp")) * row_count
    places = first_row + jnp.arange(row_count, dtype=jnp.int32)
    ends = jnp.cumsum(lengths)
    starts = ends - lengths
    inside = (places[:, None] >= starts[None, :]) & (places[:, None] < ends[None, :])
    seq_len = jnp.sum(jnp.where(inside, lengths[None, :], 0), axis=1).astype(jnp.float32)
    weight = 2.0 * longest / (seq_len + longest)
    cot_wide = weight[:, None] * cotangent.astype(jnp.float32)

    train_table = weight[:, None] * gate_table(train_experts, train_gates, ep_count)
    stale_table = gate_table(decode_experts[0], decode_gates[0], ep_count)
    fresh_table = gate_table(decode_experts[1], decode_gates[1], ep_count)
    device_count = ep_count * dp_count
    table = two_part(jnp.where(is_learner, train_table, stale_table)) + two_part(fresh_table)
    spare = -4 * ep_count % 128
    table.append(jnp.zeros((row_count, spare), jnp.bfloat16))
    every = gather(jnp.concatenate([own_rows] + table, axis=1), device_count, (0, 1))
    mine = lax.axis_index("ep").astype(jnp.int32)
    first_place = mine.reshape(1)
    fresh_place = first_place + 2 * ep_count
    rates = (0.5 / model_width**0.5, 0.5 / hidden_all**0.5)
    run_ffn, run_learn = (
        (ffn_call, learn_call) if total_rows <= 256 else (ffn_plain, learn_plain)
    )
    cots = gather(cotangent, device_count, (0,))

    def learn(every, cots, planes, own_dn):
        dx_part, new_planes, new_dn = run_learn(
            first_place, every, every, cots, planes, own_dn, ep_count, rates
        )
        return (unset(dx_part), dx_part, new_planes, new_dn)

    def decode(every, cots, planes, own_dn):
        part = run_ffn(first_place, every, every, planes, own_dn, ep_count)
        return (part, unset(part), unset(planes), unset(own_dn))

    part, dx_part, new_planes, new_dn = lax.cond(
        is_learner, learn, decode, every, cots, planes, own_dn
    )
    stale_sum = scatter_sum(part, device_count, (1,))
    current = (own_rows.astype(jnp.float32) + stale_sum).astype(jnp.bfloat16)
    dx_sum = scatter_sum(dx_part, device_count, (0,))
    arrived = gather(across(current, 1, 0), device_count, (0,))
    fresh_part = lax.cond(
        is_learner,
        lambda r, e, g, d: run_ffn(fresh_place, r, e, g, d, ep_count),
        lambda r, e, g, d: unset(r),
        arrived,
        every,
        new_planes,
        new_dn,
    )
    fresh_sum = scatter_sum(fresh_part, device_count, (0,))
    moved = across(fresh_sum.astype(jnp.bfloat16), 0, 1).astype(jnp.float32)
    final_rows = jnp.where(is_learner, cot_wide + dx_sum, current.astype(jnp.float32) + moved)
    return final_rows.astype(jnp.bfloat16)[None]


def solution(mesh):
    placed = (
        P("grp", ("ep", "dp"), None),
        P(("ep", "dp"), None),
        P(),
        P(("ep", "dp"), None),
        P(("ep", "dp"), None),
        P(None, ("ep", "dp"), None),
        P(None, ("ep", "dp"), None),
        P("grp", "ep", None, None, "dp"),
        P("grp", "ep", "dp", None),
    )
    return jax.shard_map(
        per_device,
        mesh=mesh,
        in_specs=placed,
        out_specs=P("grp", ("ep", "dp"), None),
        check_vma=False,
    )
```

profile of v0, /device:TPU:0, one launch (start us, length us, event | category | flops | bytes accessed | tf_op | source)
XLA Modules:
  0.0 242.6 jit_solution(16440839873116163593)
XLA Ops:
  0.0 6.9 %collective-permute-start.7 = (bf16[16,4096]{1,0:T(8,128)(2,1)}, bf16[16,4096]{1,0:T(8,128)(2,1)S(1)}, u32[]{:S(2)}, u32[]{:S(2)}) collective-permute-start(bf16[16,4096]{1,0:T(8,128)(2,1)} %param.14), channel_id=1, source_target_pairs={{0,12},{1,13},{2,14},{3,15},{4,8},{5,9},{6,10},{7,11},{8,4},{9,5},... | collective-permute-start | bytes 393224 | tf_op jit(solution)/shard_map/ppermute | solution.py:47
  7.0 1.9 collective-permute-start.6
  8.9 2.5 %collective-permute-start.5 = (bf16[16,4096]{1,0:T(8,128)(2,1)}, bf16[16,4096]{1,0:T(8,128)(2,1)S(1)}, u32[]{:S(2)}, u32[]{:S(2)}) collective-permute-start(bf16[16,4096]{1,0:T(8,128)(2,1)} %param.14), channel_id=1, source_target_pairs={{0,4},{1,5},{2,6},{3,7},{4,0},{5,1},{6,2},{7,3},{8,12},{9,13},{10,... | collective-permute-start | bytes 393224 | tf_op jit(solution)/shard_map/ppermute | solution.py:47
  18.2 3.8 %collective-permute-start.2 = (bf16[16,4224]{1,0:T(8,128)(2,1)S(1)}, bf16[16,4224]{1,0:T(8,128)(2,1)S(1)}, u32[]{:S(2)}, u32[]{:S(2)}) collective-permute-start(bf16[16,4224]{1,0:T(8,128)(2,1)S(1)} %concatenate.36), channel_id=1, source_target_pairs={{0,12},{1,13},{2,14},{3,15},{4,8},{5,9},{6,10},{7,11},{8,4},{9,5},... | collective-permute-start | bytes 405512 | tf_op jit(solution)/shard_map/ppermute | solution.py:47
  25.9 3.6 %collective-permute-start.8 = (bf16[64,4096]{1,0:T(8,128)(2,1)S(1)}, bf16[64,4096]{1,0:T(8,128)(2,1)S(1)}, u32[]{:S(2)}, u32[]{:S(2)}) collective-permute-start(bf16[64,4096]{1,0:T(8,128)(2,1)S(1)} %pad_maximum_fusion.1), channel_id=1, source_target_pairs={{0,2},{1,3},{2,0},{3,1},{4,6},{5,7},{6,4},{7,5},{8,10},{9,11},{10,... | collective-permute-start | bytes 1572872 | tf_op jit(solution)/shard_map/ppermute | solution.py:47
  36.2 6.5 %collective-permute-done.8 = bf16[64,4096]{1,0:T(8,128)(2,1)S(1)} collective-permute-done((bf16[64,4096]{1,0:T(8,128)(2,1)S(1)}, bf16[64,4096]{1,0:T(8,128)(2,1)S(1)}, u32[]{:S(2)}, u32[]{:S(2)}) %collective-permute-start.8) | collective-permute-done | bytes 524320 | tf_op jit(solution)/shard_map/ppermute | solution.py:47
  45.8 5.9 %collective-permute-done.3 = bf16[64,4224]{1,0:T(8,128)(2,1)S(1)} collective-permute-done((bf16[64,4224]{1,0:T(8,128)(2,1)S(1)}, bf16[64,4224]{1,0:T(8,128)(2,1)S(1)}, u32[]{:S(2)}, u32[]{:S(2)}) %collective-permute-start.3) | collective-permute-done | bytes 540704 | tf_op jit(solution)/shard_map/ppermute | solution.py:47
  52.6 11.9 %copy.25 = bf16[1,1,4096,2,768]{4,2,3,1,0:T(8,128)(2,1)} copy(bf16[1,1,4096,2,768]{4,3,2,1,0:T(2,128)(2,1)} %param.20) | data formatting | bytes 25165824 | tf_op args[7]
  64.4 2.3 constant_dynamic-update-slice_fusion.16
  66.9 48.6 %conditional.2 = (bf16[256,4096]{1,0:T(8,128)(2,1)}, bf16[256,4096]{1,0:T(8,128)(2,1)}, bf16[2,4096,768]{2,1,0:T(8,128)(2,1)}, bf16[768,4096]{1,0:T(8,128)(2,1)}) conditional(s32[]{:T(128)} %convert_element_type.136, (s32[1]{0:T(128)}, bf16[256,4224]{1,0:T(8,128)(2,1)S(1)}, bf16[2,4096,768]{2,1,0:T(8,128)(2,1)}, ...), branch_computations={%region_5.6_spmd, %region_6.7_spmd} | conditional | flops 12884901888 | bytes 37748768 | solution.py:387
  66.9 48.6 %learn.1 = (bf16[256,4096]{1,0:T(8,128)(2,1)}, bf16[2,4096,768]{2,1,0:T(8,128)(2,1)}, bf16[768,4096]{1,0:T(8,128)(2,1)}) custom-call(s32[1]{0:T(128)} %get-tuple-element.48.place, bf16[256,4224]{1,0:T(8,128)(2,1)S(1)} %get-tuple-element.49.rows_ref.table_ref, bf16[256,4224]{1,0:T(8,128)(2,1)S(1)} %get-tuple-element.49.rows_ref.table_ref, ...), custom_call_target="tpu_custom_call" | custom-call | flops 12884901888 | bytes 37748736 | tf_op jit(solution)/shard_map/cond/branch_1_fun/learn/pallas_call | solution.py:245
  122.5 6.5 %collective-permute-done.20 = bf16[16,4096]{1,0:T(8,128)(2,1)S(1)} collective-permute-done((bf16[16,4096]{1,0:T(8,128)(2,1)S(1)}, bf16[16,4096]{1,0:T(8,128)(2,1)S(1)}, u32[]{:S(2)}, u32[]{:S(2)}) %collective-permute-start.20) | collective-permute-done | bytes 131104 | tf_op jit(solution)/shard_map/ppermute | solution.py:15
  129.0 5.4 %collective-permute-start.23 = (bf16[16,4096]{1,0:T(8,128)(2,1)S(1)}, bf16[16,4096]{1,0:T(8,128)(2,1)S(1)}, u32[]{:S(2)}, u32[]{:S(2)}) collective-permute-start(bf16[16,4096]{1,0:T(8,128)(2,1)S(1)} %collective-permute-done.20), channel_id=1, source_target_pairs={{0,12},{1,13},{2,14},{3,15},{4,8},{5,9},{6,10},{7,11},{8,4},{9,5},... | collective-permute-start | bytes 393224 | tf_op jit(solution)/shard_map/ppermute | solution.py:47
  136.3 2.8 %collective-permute-start.21 = (bf16[16,4096]{1,0:T(8,128)(2,1)S(1)}, bf16[16,4096]{1,0:T(8,128)(2,1)S(1)}, u32[]{:S(2)}, u32[]{:S(2)}) collective-permute-start(bf16[16,4096]{1,0:T(8,128)(2,1)S(1)} %collective-permute-done.20), channel_id=1, source_target_pairs={{0,4},{1,5},{2,6},{3,7},{4,0},{5,1},{6,2},{7,3},{8,12},{9,13},{10,... | collective-permute-start | bytes 393224 | tf_op jit(solution)/shard_map/ppermute | solution.py:47
  139.8 5.6 %collective-permute-done.22 = bf16[16,4096]{1,0:T(8,128)(2,1)S(1)} collective-permute-done((bf16[16,4096]{1,0:T(8,128)(2,1)S(1)}, bf16[16,4096]{1,0:T(8,128)(2,1)S(1)}, u32[]{:S(2)}, u32[]{:S(2)}) %collective-permute-start.22) | collective-permute-done | bytes 131104 | tf_op jit(solution)/shard_map/ppermute | solution.py:47
  145.9 3.4 %collective-permute-start.24 = (bf16[64,4096]{1,0:T(8,128)(2,1)S(1)}, bf16[64,4096]{1,0:T(8,128)(2,1)S(1)}, u32[]{:S(2)}, u32[]{:S(2)}) collective-permute-start(bf16[64,4096]{1,0:T(8,128)(2,1)S(1)} %pad_maximum_fusion.2), channel_id=1, source_target_pairs={{0,2},{1,3},{2,0},{3,1},{4,6},{5,7},{6,4},{7,5},{8,10},{9,11},{10,... | collective-permute-start | bytes 1572872 | tf_op jit(solution)/shard_map/ppermute | solution.py:47
  151.3 8.7 %collective-permute-done.24 = bf16[64,4096]{1,0:T(8,128)(2,1)S(1)} collective-permute-done((bf16[64,4096]{1,0:T(8,128)(2,1)S(1)}, bf16[64,4096]{1,0:T(8,128)(2,1)S(1)}, u32[]{:S(2)}, u32[]{:S(2)}) %collective-permute-start.24) | collective-permute-done | bytes 524320 | tf_op jit(solution)/shard_map/ppermute | solution.py:47
  163.9 2.4 collective-permute-start.10
  167.3 13.0 %conditional.3 = (bf16[256,4096]{1,0:T(8,128)(2,1)}) conditional(s32[]{:T(128)} %convert_element_type.136, () %tuple.24, (s32[1]{0:T(128)}, bf16[256,4096]{1,0:T(8,128)(2,1)}, bf16[256,4224]{1,0:T(8,128)(2,1)S(1)}, bf16[2,4096,768]{2,1,0:T(8,128)(2,1)}, bf16[768,4096]{1,0:T(8,128)(2,1)}) %tuple.25), branch_computations={%region_7.8_spmd, %region_8.9_spmd} | conditional | flops 4831838208 | bytes 18874388 | solution.py:394
  167.3 13.0 %ffn.4 = bf16[256,4096]{1,0:T(8,128)(2,1)} custom-call(s32[1]{0:T(128)S(6)} %add.55.place, bf16[256,4096]{1,0:T(8,128)(2,1)} %get-tuple-element.57.rows_ref, bf16[256,4224]{1,0:T(8,128)(2,1)S(1)} %get-tuple-element.58.table_ref, bf16[2,4096,768]{2,1,0:T(8,128)(2,1)} %get-tuple-element.59.gu_ref, bf16[768,4096]{1,0:T(8,128)(2,1)} %get-tuple-element.60.dn_ref), custom_call_target="tpu_custom_call" | custom-call | flops 4831838208 | bytes 18874368 | tf_op jit(solution)/shard_map/cond/branch_1_fun/ffn/pallas_call | solution.py:140
  181.8 1.9 collective-permute-start.26
  184.1 3.4 %collective-permute-start.11 = (bf16[64,4096]{1,0:T(8,128)(2,1)S(1)}, bf16[64,4096]{1,0:T(8,128)(2,1)S(1)}, u32[]{:S(2)}, u32[]{:S(2)}) collective-permute-start(bf16[64,4096]{1,0:T(8,128)(2,1)S(1)} %split.97), channel_id=1, source_target_pairs={{0,2},{1,3},{2,0},{3,1},{4,6},{5,7},{6,4},{7,5},{8,10},{9,11},{10,... | collective-permute-start | bytes 1572872 | tf_op jit(solution)/shard_map/ppermute | solution.py:47
  189.0 2.4 collective-permute-start.27
  191.5 9.2 %collective-permute-done.11 = bf16[64,4096]{1,0:T(8,128)(2,1)S(1)} collective-permute-done((bf16[64,4096]{1,0:T(8,128)(2,1)S(1)}, bf16[64,4096]{1,0:T(8,128)(2,1)S(1)}, u32[]{:S(2)}, u32[]{:S(2)}) %collective-permute-start.11) | collective-permute-done | bytes 524320 | tf_op jit(solution)/shard_map/ppermute | solution.py:47
  200.8 10.7 %collective-permute-done.27 = bf16[64,4096]{1,0:T(8,128)(2,1)S(1)} collective-permute-done((bf16[64,4096]{1,0:T(8,128)(2,1)S(1)}, bf16[64,4096]{1,0:T(8,128)(2,1)S(1)}, u32[]{:S(2)}, u32[]{:S(2)}) %collective-permute-start.27) | collective-permute-done | bytes 524320 | tf_op jit(solution)/shard_map/ppermute | solution.py:47
  211.7 2.1 collective-permute-start.28
  213.8 4.7 %collective-permute-start.30 = (bf16[16,4096]{1,0:T(8,128)(2,1)S(1)}, bf16[16,4096]{1,0:T(8,128)(2,1)S(1)}, u32[]{:S(2)}, u32[]{:S(2)}) collective-permute-start(bf16[16,4096]{1,0:T(8,128)(2,1)S(1)} %get-tuple-element.75), channel_id=1, source_target_pairs={{0,12},{1,13},{2,14},{3,15},{4,8},{5,9},{6,10},{7,11},{8,4},{9,5},... | collective-permute-start | bytes 393224 | tf_op jit(solution)/shard_map/ppermute | solution.py:47
  218.5 2.5 %collective-permute-start.29 = (bf16[16,4096]{1,0:T(8,128)(2,1)S(1)}, bf16[16,4096]{1,0:T(8,128)(2,1)S(1)}, u32[]{:S(2)}, u32[]{:S(2)}) collective-permute-start(bf16[16,4096]{1,0:T(8,128)(2,1)S(1)} %get-tuple-element.76), channel_id=1, source_target_pairs={{0,8},{1,9},{2,10},{3,11},{4,12},{5,13},{6,14},{7,15},{8,0},{9,1},... | collective-permute-start | bytes 393224 | tf_op jit(solution)/shard_map/ppermute | solution.py:47
  221.0 2.9 %collective-permute-start.12 = (bf16[16,4096]{1,0:T(8,128)(2,1)S(1)}, bf16[16,4096]{1,0:T(8,128)(2,1)S(1)}, u32[]{:S(2)}, u32[]{:S(2)}) collective-permute-start(bf16[16,4096]{1,0:T(8,128)(2,1)S(1)} %get-tuple-element.71), channel_id=1, source_target_pairs={{0,4},{1,5},{2,6},{3,7},{4,0},{5,1},{6,2},{7,3},{8,12},{9,13},{10,... | collective-permute-start | bytes 393224 | tf_op jit(solution)/shard_map/ppermute | solution.py:47
  223.9 4.7 %collective-permute-start.14 = (bf16[16,4096]{1,0:T(8,128)(2,1)S(1)}, bf16[16,4096]{1,0:T(8,128)(2,1)S(1)}, u32[]{:S(2)}, u32[]{:S(2)}) collective-permute-start(bf16[16,4096]{1,0:T(8,128)(2,1)S(1)} %get-tuple-element.72), channel_id=1, source_target_pairs={{0,12},{1,13},{2,14},{3,15},{4,8},{5,9},{6,10},{7,11},{8,4},{9,5},... | collective-permute-start | bytes 393224 | tf_op jit(solution)/shard_map/ppermute | solution.py:47
  230.6 6.3 %collective-permute-done.29 = bf16[16,4096]{1,0:T(8,128)(2,1)S(1)} collective-permute-done((bf16[16,4096]{1,0:T(8,128)(2,1)S(1)}, bf16[16,4096]{1,0:T(8,128)(2,1)S(1)}, u32[]{:S(2)}, u32[]{:S(2)}) %collective-permute-start.29) | collective-permute-done | bytes 131104 | tf_op jit(solution)/shard_map/ppermute | solution.py:47
  238.3 3.5 %collective-permute-done.13 = bf16[16,4096]{1,0:T(8,128)(2,1)S(1)} collective-permute-done((bf16[16,4096]{1,0:T(8,128)(2,1)S(1)}, bf16[16,4096]{1,0:T(8,128)(2,1)S(1)}, u32[]{:S(2)}, u32[]{:S(2)}) %collective-permute-start.13) | collective-permute-done | bytes 131104 | tf_op jit(solution)/shard_map/ppermute | solution.py:47
  (106 shorter events, 46.0 us)
Async XLA Ops:
  0.0 24.4 %collective-permute-start.7 = (bf16[16,4096]{1,0:T(8,128)(2,1)}, bf16[16,4096]{1,0:T(8,128)(2,1)S(1)}, u32[]{:S(2)}, u32[]{:S(2)}) collective-permute-start(bf16[16,4096]{1,0:T(8,128)(2,1)} %param.14), channel_id=1, source_target_pairs={{0,12},{1,13},{2,14},{3,15},{4,8},{5,9},{6,10},{7,11},{8,4},{9,5},... | collective-permute-start | bytes 393224 | tf_op jit(solution)/shard_map/ppermute | solution.py:47
  7.0 18.0 %collective-permute-start.6 = (bf16[16,4096]{1,0:T(8,128)(2,1)}, bf16[16,4096]{1,0:T(8,128)(2,1)S(1)}, u32[]{:S(2)}, u32[]{:S(2)}) collective-permute-start(bf16[16,4096]{1,0:T(8,128)(2,1)} %param.14), channel_id=1, source_target_pairs={{0,8},{1,9},{2,10},{3,11},{4,12},{5,13},{6,14},{7,15},{8,0},{9,1},... | collective-permute-start | bytes 393224 | tf_op jit(solution)/shard_map/ppermute | solution.py:47
  8.9 16.1 %collective-permute-start.5 = (bf16[16,4096]{1,0:T(8,128)(2,1)}, bf16[16,4096]{1,0:T(8,128)(2,1)S(1)}, u32[]{:S(2)}, u32[]{:S(2)}) collective-permute-start(bf16[16,4096]{1,0:T(8,128)(2,1)} %param.14), channel_id=1, source_target_pairs={{0,4},{1,5},{2,6},{3,7},{4,0},{5,1},{6,2},{7,3},{8,12},{9,13},{10,... | collective-permute-start | bytes 393224 | tf_op jit(solution)/shard_map/ppermute | solution.py:47
  18.2 13.5 %collective-permute-start.2 = (bf16[16,4224]{1,0:T(8,128)(2,1)S(1)}, bf16[16,4224]{1,0:T(8,128)(2,1)S(1)}, u32[]{:S(2)}, u32[]{:S(2)}) collective-permute-start(bf16[16,4224]{1,0:T(8,128)(2,1)S(1)} %concatenate.36), channel_id=1, source_target_pairs={{0,12},{1,13},{2,14},{3,15},{4,8},{5,9},{6,10},{7,11},{8,4},{9,5},... | collective-permute-start | bytes 405512 | tf_op jit(solution)/shard_map/ppermute | solution.py:47
  22.1 10.5 %collective-permute-start.1 = (bf16[16,4224]{1,0:T(8,128)(2,1)S(1)}, bf16[16,4224]{1,0:T(8,128)(2,1)S(1)}, u32[]{:S(2)}, u32[]{:S(2)}) collective-permute-start(bf16[16,4224]{1,0:T(8,128)(2,1)S(1)} %concatenate.36), channel_id=1, source_target_pairs={{0,8},{1,9},{2,10},{3,11},{4,12},{5,13},{6,14},{7,15},{8,0},{9,1},... | collective-permute-start | bytes 405512 | tf_op jit(solution)/shard_map/ppermute | solution.py:47
  24.4 8.2 %collective-permute-start = (bf16[16,4224]{1,0:T(8,128)(2,1)S(1)}, bf16[16,4224]{1,0:T(8,128)(2,1)S(1)}, u32[]{:S(2)}, u32[]{:S(2)}) collective-permute-start(bf16[16,4224]{1,0:T(8,128)(2,1)S(1)} %concatenate.36), channel_id=1, source_target_pairs={{0,4},{1,5},{2,6},{3,7},{4,0},{5,1},{6,2},{7,3},{8,12},{9,13},{10,... | collective-permute-start | bytes 405512 | tf_op jit(solution)/shard_map/ppermute | solution.py:47
  25.9 16.8 %collective-permute-start.8 = (bf16[64,4096]{1,0:T(8,128)(2,1)S(1)}, bf16[64,4096]{1,0:T(8,128)(2,1)S(1)}, u32[]{:S(2)}, u32[]{:S(2)}) collective-permute-start(bf16[64,4096]{1,0:T(8,128)(2,1)S(1)} %pad_maximum_fusion.1), channel_id=1, source_target_pairs={{0,2},{1,3},{2,0},{3,1},{4,6},{5,7},{6,4},{7,5},{8,10},{9,11},{10,... | collective-permute-start | bytes 1572872 | tf_op jit(solution)/shard_map/ppermute | solution.py:47
  32.6 19.0 %collective-permute-start.3 = (bf16[64,4224]{1,0:T(8,128)(2,1)S(1)}, bf16[64,4224]{1,0:T(8,128)(2,1)S(1)}, u32[]{:S(2)}, u32[]{:S(2)}) collective-permute-start(bf16[64,4224]{1,0:T(8,128)(2,1)S(1)} %pad_maximum_fusion), channel_id=1, source_target_pairs={{0,2},{1,3},{2,0},{3,1},{4,6},{5,7},{6,4},{7,5},{8,10},{9,11},{10,... | collective-permute-start | bytes 1622024 | tf_op jit(solution)/shard_map/ppermute | solution.py:47
  43.9 20.6 %collective-permute-start.9 = (bf16[128,4096]{1,0:T(8,128)(2,1)}, bf16[128,4096]{1,0:T(8,128)(2,1)}, u32[]{:S(2)}, u32[]{:S(2)}) collective-permute-start(bf16[128,4096]{1,0:T(8,128)(2,1)} %get-tuple-element.82), channel_id=1, source_target_pairs={{0,1},{1,0},{2,3},{3,2},{4,5},{5,4},{6,7},{7,6},{8,9},{9,8},{10,11... | collective-permute-start | bytes 3145736 | tf_op jit(solution)/shard_map/ppermute | solution.py:47
  52.6 14.2 %collective-permute-start.4 = (bf16[128,4224]{1,0:T(8,128)(2,1)}, bf16[128,4224]{1,0:T(8,128)(2,1)S(1)}, u32[]{:S(2)}, u32[]{:S(2)}) collective-permute-start(bf16[128,4224]{1,0:T(8,128)(2,1)} %get-tuple-element.69), channel_id=1, source_target_pairs={{0,1},{1,0},{2,3},{3,2},{4,5},{5,4},{6,7},{7,6},{8,9},{9,8},{10,11... | collective-permute-start | bytes 3244040 | tf_op jit(solution)/shard_map/ppermute | solution.py:47
  116.9 0.7 collective-permute-start.15
  118.0 0.7 collective-permute-start.16
  118.9 2.0 collective-permute-start.17
  119.5 1.4 collective-permute-start.19
  120.2 0.7 collective-permute-start.18
  121.0 7.9 %collective-permute-start.20 = (bf16[16,4096]{1,0:T(8,128)(2,1)S(1)}, bf16[16,4096]{1,0:T(8,128)(2,1)S(1)}, u32[]{:S(2)}, u32[]{:S(2)}) collective-permute-start(bf16[16,4096]{1,0:T(8,128)(2,1)S(1)} %add_convert_fusion.7), channel_id=1, source_target_pairs={{16,0},{17,1},{18,2},{19,3},{20,4},{21,5},{22,6},{23,7},{24,8},{25... | collective-permute-start | bytes 393224 | tf_op jit(solution)/shard_map/ppermute | solution.py:15
  129.0 10.8 %collective-permute-start.23 = (bf16[16,4096]{1,0:T(8,128)(2,1)S(1)}, bf16[16,4096]{1,0:T(8,128)(2,1)S(1)}, u32[]{:S(2)}, u32[]{:S(2)}) collective-permute-start(bf16[16,4096]{1,0:T(8,128)(2,1)S(1)} %collective-permute-done.20), channel_id=1, source_target_pairs={{0,12},{1,13},{2,14},{3,15},{4,8},{5,9},{6,10},{7,11},{8,4},{9,5},... | collective-permute-start | bytes 393224 | tf_op jit(solution)/shard_map/ppermute | solution.py:47
  134.3 11.0 %collective-permute-start.22 = (bf16[16,4096]{1,0:T(8,128)(2,1)S(1)}, bf16[16,4096]{1,0:T(8,128)(2,1)S(1)}, u32[]{:S(2)}, u32[]{:S(2)}) collective-permute-start(bf16[16,4096]{1,0:T(8,128)(2,1)S(1)} %collective-permute-done.20), channel_id=1, source_target_pairs={{0,8},{1,9},{2,10},{3,11},{4,12},{5,13},{6,14},{7,15},{8,0},{9,1},... | collective-permute-start | bytes 393224 | tf_op jit(solution)/shard_map/ppermute | solution.py:47
  136.3 9.5 %collective-permute-start.21 = (bf16[16,4096]{1,0:T(8,128)(2,1)S(1)}, bf16[16,4096]{1,0:T(8,128)(2,1)S(1)}, u32[]{:S(2)}, u32[]{:S(2)}) collective-permute-start(bf16[16,4096]{1,0:T(8,128)(2,1)S(1)} %collective-permute-done.20), channel_id=1, source_target_pairs={{0,4},{1,5},{2,6},{3,7},{4,0},{5,1},{6,2},{7,3},{8,12},{9,13},{10,... | collective-permute-start | bytes 393224 | tf_op jit(solution)/shard_map/ppermute | solution.py:47
  145.9 14.1 %collective-permute-start.24 = (bf16[64,4096]{1,0:T(8,128)(2,1)S(1)}, bf16[64,4096]{1,0:T(8,128)(2,1)S(1)}, u32[]{:S(2)}, u32[]{:S(2)}) collective-permute-start(bf16[64,4096]{1,0:T(8,128)(2,1)S(1)} %pad_maximum_fusion.2), channel_id=1, source_target_pairs={{0,2},{1,3},{2,0},{3,1},{4,6},{5,7},{6,4},{7,5},{8,10},{9,11},{10,... | collective-permute-start | bytes 1572872 | tf_op jit(solution)/shard_map/ppermute | solution.py:47
  160.9 5.4 %collective-permute-start.25 = (bf16[128,4096]{1,0:T(8,128)(2,1)S(1)}, bf16[128,4096]{1,0:T(8,128)(2,1)S(1)}, u32[]{:S(2)}, u32[]{:S(2)}) collective-permute-start(bf16[128,4096]{1,0:T(8,128)(2,1)S(1)} %get-tuple-element.77), channel_id=1, source_target_pairs={{0,1},{1,0},{2,3},{3,2},{4,5},{5,4},{6,7},{7,6},{8,9},{9,8},{10,11... | collective-permute-start | bytes 3145736 | tf_op jit(solution)/shard_map/ppermute | solution.py:47
  163.9 19.9 %collective-permute-start.10 = (bf16[128,4096]{1,0:T(8,128)(2,1)}, bf16[128,4096]{1,0:T(8,128)(2,1)S(1)}, u32[]{:S(2)}, u32[]{:S(2)}) collective-permute-start(bf16[128,4096]{1,0:T(8,128)(2,1)} %split.73), channel_id=1, source_target_pairs={{0,1},{1,0},{2,3},{3,2},{4,5},{5,4},{6,7},{7,6},{8,9},{9,8},{10,11... | collective-permute-start | bytes 3145736 | tf_op jit(solution)/shard_map/ppermute | solution.py:47
  181.8 5.7 %collective-permute-start.26 = (bf16[128,4096]{1,0:T(8,128)(2,1)S(1)}, bf16[128,4096]{1,0:T(8,128)(2,1)S(1)}, u32[]{:S(2)}, u32[]{:S(2)}) collective-permute-start(bf16[128,4096]{1,0:T(8,128)(2,1)S(1)} %split.109), channel_id=1, source_target_pairs={{0,1},{1,0},{2,3},{3,2},{4,5},{5,4},{6,7},{7,6},{8,9},{9,8},{10,11... | collective-permute-start | bytes 3145736 | tf_op jit(solution)/shard_map/ppermute | solution.py:47
  184.1 16.6 %collective-permute-start.11 = (bf16[64,4096]{1,0:T(8,128)(2,1)S(1)}, bf16[64,4096]{1,0:T(8,128)(2,1)S(1)}, u32[]{:S(2)}, u32[]{:S(2)}) collective-permute-start(bf16[64,4096]{1,0:T(8,128)(2,1)S(1)} %split.97), channel_id=1, source_target_pairs={{0,2},{1,3},{2,0},{3,1},{4,6},{5,7},{6,4},{7,5},{8,10},{9,11},{10,... | collective-permute-start | bytes 1572872 | tf_op jit(solution)/shard_map/ppermute | solution.py:47
  189.0 22.5 %collective-permute-start.27 = (bf16[64,4096]{1,0:T(8,128)(2,1)S(1)}, bf16[64,4096]{1,0:T(8,128)(2,1)S(1)}, u32[]{:S(2)}, u32[]{:S(2)}) collective-permute-start(bf16[64,4096]{1,0:T(8,128)(2,1)S(1)} %split.111), channel_id=1, source_target_pairs={{0,2},{1,3},{2,0},{3,1},{4,6},{5,7},{6,4},{7,5},{8,10},{9,11},{10,... | collective-permute-start | bytes 1572872 | tf_op jit(solution)/shard_map/ppermute | solution.py:47
  211.7 17.0 %collective-permute-start.28 = (bf16[16,4096]{1,0:T(8,128)(2,1)S(1)}, bf16[16,4096]{1,0:T(8,128)(2,1)S(1)}, u32[]{:S(2)}, u32[]{:S(2)}) collective-permute-start(bf16[16,4096]{1,0:T(8,128)(2,1)S(1)} %get-tuple-element.74), channel_id=1, source_target_pairs={{0,4},{1,5},{2,6},{3,7},{4,0},{5,1},{6,2},{7,3},{8,12},{9,13},{10,... | collective-permute-start | bytes 393224 | tf_op jit(solution)/shard_map/ppermute | solution.py:47
  213.8 16.9 %collective-permute-start.30 = (bf16[16,4096]{1,0:T(8,128)(2,1)S(1)}, bf16[16,4096]{1,0:T(8,128)(2,1)S(1)}, u32[]{:S(2)}, u32[]{:S(2)}) collective-permute-start(bf16[16,4096]{1,0:T(8,128)(2,1)S(1)} %get-tuple-element.75), channel_id=1, source_target_pairs={{0,12},{1,13},{2,14},{3,15},{4,8},{5,9},{6,10},{7,11},{8,4},{9,5},... | collective-permute-start | bytes 393224 | tf_op jit(solution)/shard_map/ppermute | solution.py:47
  218.5 18.5 %collective-permute-start.29 = (bf16[16,4096]{1,0:T(8,128)(2,1)S(1)}, bf16[16,4096]{1,0:T(8,128)(2,1)S(1)}, u32[]{:S(2)}, u32[]{:S(2)}) collective-permute-start(bf16[16,4096]{1,0:T(8,128)(2,1)S(1)} %get-tuple-element.76), channel_id=1, source_target_pairs={{0,8},{1,9},{2,10},{3,11},{4,12},{5,13},{6,14},{7,15},{8,0},{9,1},... | collective-permute-start | bytes 393224 | tf_op jit(solution)/shard_map/ppermute | solution.py:47
  221.0 17.3 %collective-permute-start.12 = (bf16[16,4096]{1,0:T(8,128)(2,1)S(1)}, bf16[16,4096]{1,0:T(8,128)(2,1)S(1)}, u32[]{:S(2)}, u32[]{:S(2)}) collective-permute-start(bf16[16,4096]{1,0:T(8,128)(2,1)S(1)} %get-tuple-element.71), channel_id=1, source_target_pairs={{0,4},{1,5},{2,6},{3,7},{4,0},{5,1},{6,2},{7,3},{8,12},{9,13},{10,... | collective-permute-start | bytes 393224 | tf_op jit(solution)/shard_map/ppermute | solution.py:47
  223.9 14.4 %collective-permute-start.14 = (bf16[16,4096]{1,0:T(8,128)(2,1)S(1)}, bf16[16,4096]{1,0:T(8,128)(2,1)S(1)}, u32[]{:S(2)}, u32[]{:S(2)}) collective-permute-start(bf16[16,4096]{1,0:T(8,128)(2,1)S(1)} %get-tuple-element.72), channel_id=1, source_target_pairs={{0,12},{1,13},{2,14},{3,15},{4,8},{5,9},{6,10},{7,11},{8,4},{9,5},... | collective-permute-start | bytes 393224 | tf_op jit(solution)/shard_map/ppermute | solution.py:47
  228.7 13.2 %collective-permute-start.13 = (bf16[16,4096]{1,0:T(8,128)(2,1)S(1)}, bf16[16,4096]{1,0:T(8,128)(2,1)S(1)}, u32[]{:S(2)}, u32[]{:S(2)}) collective-permute-start(bf16[16,4096]{1,0:T(8,128)(2,1)S(1)} %get-tuple-element.73), channel_id=1, source_target_pairs={{0,8},{1,9},{2,10},{3,11},{4,12},{5,13},{6,14},{7,15},{8,0},{9,1},... | collective-permute-start | bytes 393224 | tf_op jit(solution)/shard_map/ppermute | solution.py:47
  237.0 4.8 %collective-permute-start.31 = (bf16[16,4096]{1,0:T(8,128)(2,1)S(1)}, bf16[16,4096]{1,0:T(8,128)(2,1)S(1)}, u32[]{:S(2)}, u32[]{:S(2)}) collective-permute-start(bf16[16,4096]{1,0:T(8,128)(2,1)S(1)} %add_convert_fusion.6), channel_id=1, source_target_pairs={{0,16},{1,17},{2,18},{3,19},{4,20},{5,21},{6,22},{7,23},{8,24},{9,... | collective-permute-start | bytes 393224 | tf_op jit(solution)/shard_map/ppermute | solution.py:15
  (5 other events, 91.4 us)
where the time goes:
time: 244 us; the launch traced here: 243 us
  starting transfers between devices  73.5 us (30%)
  waiting for transfers between devices  64.3 us (26%)
  Pallas kernels  61.6 us (25%)
  local copies, waits for them, and re-layouts  35.8 us (15%)
  other arithmetic  6.9 us (3%)
    ppermute x30, starting transfers between devices, swap(): return lax.ppermute(block, ('grp',) + AXES, pairs)  70.8 us
    ppermute x30, waiting for transfers between devices, swap(): return lax.ppermute(block, ('grp',) + AXES, pairs)  57.8 us
    pallas_call x1, Pallas kernels, learn_call(): pl.pallas_call(functools.partial(learn_kernel, experts=experts, rates=rat...  48.6 us
    unnamed x25, local copies, waits for them, and re-layouts  22.5 us
    pallas_call x1, Pallas kernels, ffn_call(): pl.pallas_call(functools.partial(ffn_kernel, experts=experts), grid_spec=...  13 us
    ppermute x2, waiting for transfers between devices, across(): return lax.ppermute(block, 'grp', [(source, target)])  6.51 us
    concatenate x6, local copies, waits for them, and re-layouts, gather(): block = jnp.concatenate([block] + got, axis=0)  6.45 us
  transfers between devices with their start and end apart: 32, of which 11 were waited for; matrix products, arithmetic and copies ran while one was open for 16% of the time, Pallas kernels for 5%

commit v1 on v0

v1 whole, which is shorter than its diff:
```python
import functools

import jax
import jax.numpy as jnp
from jax import lax
from jax.experimental import pallas as pl
from jax.experimental.pallas import tpu as pltpu
from jax.sharding import PartitionSpec as P

EPSILON = 1e-06
AXES = ("ep", "dp")


def across(block, source, target):
    return lax.ppermute(block, "grp", [(source, target)])


def stages(device_count):
    sizes = []
    rest = device_count
    while rest > 1:
        size = 2 if len(sizes) < 2 or rest % 4 else 4
        sizes.append(size)
        rest //= size
    strides = []
    stride = device_count
    for size in sizes[::-1]:
        stride //= size
        strides.append((stride, size))
    return strides


def swap(block, device_count, flip, role):
    pairs = [
        (part * device_count + i, part * device_count + (i ^ flip))
        for part in role
        for i in range(device_count)
    ]
    return lax.ppermute(block, ("grp",) + AXES, pairs)


def tied(*values):
    return lax.optimization_barrier(values)


def gather(block, device_count, role, beside=None):
    if device_count != 16:
        for stride, size in stages(device_count):
            got = [swap(block, device_count, turn * stride, role) for turn in range(1, size)]
            block = jnp.concatenate([block] + got, axis=0)
        return [block], beside
    far = [swap(block, 16, turn * 4, role) for turn in (1, 2, 3)]
    near = jnp.concatenate([block, far[0]], axis=0)
    if beside is not None:
        near, beside = tied(near, beside)
    away = jnp.concatenate(far[1:], axis=0)
    near = jnp.concatenate([near, swap(near, 16, 2, role)], axis=0)
    away = jnp.concatenate([away, swap(away, 16, 2, role)], axis=0)
    return [near, swap(near, 16, 1, role), away, swap(away, 16, 1, role)], beside


def plus(kept, *sent):
    total = kept.astype(jnp.float32)
    for one in sent:
        total = total + one.astype(jnp.float32)
    return total


def halves(array):
    return jnp.split(array, 2, axis=0)


def scatter_sum_wide(part, device_count, role):
    for stride, size in stages(device_count)[::-1]:
        cuts = jnp.split(part, size, axis=0)
        got = [swap(cuts[turn], device_count, turn * stride, role) for turn in range(1, size)]
        total = plus(cuts[0], *got)
        part = total.astype(jnp.bfloat16)
    return total


def sum_core(pieces, role):
    away = plus(pieces[2], swap(pieces[3], 16, 1, role)).astype(jnp.bfloat16)
    near = plus(pieces[0], swap(pieces[1], 16, 1, role)).astype(jnp.bfloat16)
    return near, away


def sum_y(near, away, role):
    kept, sent = halves(away)
    away = plus(kept, swap(sent, 16, 2, role)).astype(jnp.bfloat16)
    kept, sent = halves(near)
    near = plus(kept, swap(sent, 16, 2, role)).astype(jnp.bfloat16)
    return near, away


def sum_z(near, away, role):
    second, third = [swap(h, 16, f, role) for h, f in zip(halves(away), (8, 12))]
    kept, sent = halves(near)
    return plus(kept, swap(sent, 16, 4, role), second, third)


def scatter_sum(pieces, device_count, role):
    if device_count != 16:
        return scatter_sum_wide(pieces[0], device_count, role)
    near, away = sum_core(pieces, role)
    near, away = sum_y(near, away, role)
    return sum_z(near, away, role)


def renew(weights, grads, axis_number, rate):
    scale = jnp.sqrt(jnp.mean(grads * grads, axis=axis_number, keepdims=True) + EPSILON)
    return (weights.astype(jnp.float32) - rate * grads / scale).astype(jnp.bfloat16)


def wide(a, b, contract):
    return lax.dot_general(a, b, (contract, ((), ())), preferred_element_type=jnp.float32)


def nn(a, b):
    return wide(a, b, ((1,), (0,)))


def nt(a, b):
    return wide(a, b, ((1,), (1,)))


def prep_kernel(
    place, lengths, rows_ref, cot_ref, ids_ref, gates_ref, dec_ids_ref, dec_gates_ref,
    out_ref, base_ref, *, experts, longest,
):
    width = rows_ref.shape[1]
    row_count = rows_ref.shape[0]
    learner = place[1] == 0
    places = place[0] * row_count + lax.broadcasted_iota(jnp.int32, (1, row_count), 1)
    start = jnp.int32(0)
    seq_len = jnp.zeros((1, row_count), jnp.int32)
    for i in range(lengths.shape[0]):
        end = start + lengths[i]
        seq_len = jnp.where((places >= start) & (places < end), lengths[i], seq_len)
        start = end
    weight = 2.0 * longest / (seq_len.astype(jnp.float32) + longest)
    names = lax.broadcasted_iota(jnp.int32, (experts, row_count), 0)

    def table(ids, gates):
        total = jnp.zeros((experts, row_count), jnp.float32)
        for k in range(ids.shape[0]):
            total = total + jnp.where(names == ids[k : k + 1], gates[k : k + 1], 0.0)
        return total

    train = table(ids_ref[...], gates_ref[...]) * weight
    stale = table(dec_ids_ref[0], dec_gates_ref[0])
    first = jnp.where(learner, train, stale)
    fresh = table(dec_ids_ref[1], dec_gates_ref[1])
    parts = []
    for one in (first, fresh):
        upper = one.astype(jnp.bfloat16).astype(jnp.float32)
        parts += [upper, one - upper]
    spare = out_ref.shape[1] - width
    if spare > 4 * experts:
        parts.append(jnp.zeros((spare - 4 * experts, row_count), jnp.float32))
    stacked = jnp.concatenate(parts, axis=0)
    weights = jnp.broadcast_to(weight, (128, row_count))
    square = jnp.concatenate([stacked, weights], axis=0)
    square = jnp.concatenate(
        [square, jnp.zeros((square.shape[0], 128 - row_count), jnp.float32)], axis=1
    )
    for i in range(spare // 128):
        turned = square[128 * i : 128 * (i + 1)].T
        out_ref[:, width + 128 * i : width + 128 * (i + 1)] = turned[:row_count].astype(
            jnp.bfloat16
        )
    column = square[spare:].T[:row_count, 0:1]
    out_ref[:, :width] = rows_ref[...]
    base_ref[...] = jnp.where(
        learner, column * cot_ref[...].astype(jnp.float32), rows_ref[...].astype(jnp.float32)
    )


def prep_call(place, lengths, rows, cot, ids, gates, dec_ids, dec_gates, experts, longest):
    row_count, width = rows.shape
    spare = -(-4 * experts // 128) * 128
    scalars = pl.BlockSpec(memory_space=pltpu.SMEM)
    whole = pl.BlockSpec(memory_space=pltpu.VMEM)
    return pl.pallas_call(
        functools.partial(prep_kernel, experts=experts, longest=longest),
        in_specs=[scalars, scalars] + [whole] * 6,
        out_specs=[whole, whole],
        out_shape=[
            jax.ShapeDtypeStruct((row_count, width + spare), jnp.bfloat16),
            jax.ShapeDtypeStruct((row_count, width), jnp.float32),
        ],
        name="prep",
    )(place, lengths, rows, cot, ids.T, gates.T, jnp.swapaxes(dec_ids, 1, 2), jnp.swapaxes(dec_gates, 1, 2))


def pick_gates(table, column, step):
    places = lax.broadcasted_iota(jnp.int32, table.shape, 1)
    taken = (places == column) | (places == column + step)
    return jnp.sum(jnp.where(taken, table.astype(jnp.float32), 0.0), axis=1, keepdims=True)


def hidden_block(hidden_count):
    return 256 if hidden_count % 256 == 0 else 128


def ffn_kernel(place, *refs, count, experts, steps, size):
    rows_refs, table_refs = refs[:count], refs[count : 2 * count]
    gu_ref, dn_ref = refs[2 * count : 2 * count + 2]
    out_refs = refs[2 * count + 2 : 3 * count + 2]
    rows, hidden = refs[3 * count + 2 :]
    step = pl.program_id(0)
    part = rows_refs[0].shape[0]

    @pl.when(step == 0)
    def _():
        for i in range(count):
            rows[part * i : part * (i + 1), :] = rows_refs[i][...]

    for j in range(steps):

        @pl.when(step == j)
        def _():
            active = nn(rows[...], gu_ref[0])
            upward = nn(rows[...], gu_ref[1])
            hidden[:, size * j : size * (j + 1)] = (
                active * jax.nn.sigmoid(active) * upward
            ).astype(jnp.bfloat16)

    @pl.when(step >= steps)
    def _():
        out = nn(hidden[...], dn_ref[...])
        for i in range(count):
            gates = pick_gates(table_refs[i][...], place[0], experts)
            out_refs[i][...] = (gates * out[part * i : part * (i + 1)]).astype(jnp.bfloat16)


def ffn_call(place, pieces, tables, planes, weights_dn, experts):
    count = len(pieces)
    part = pieces[0].shape[0]
    hidden_count, width = weights_dn.shape
    spare = tables[0].shape[1] - width
    size = hidden_block(hidden_count)
    steps = hidden_count // size
    tile = 1024
    row_count = part * count
    table_at = width // spare
    return pl.pallas_call(
        functools.partial(ffn_kernel, count=count, experts=experts, steps=steps, size=size),
        grid_spec=pltpu.PrefetchScalarGridSpec(
            num_scalar_prefetch=1,
            grid=(steps + width // tile,),
            in_specs=[pl.BlockSpec((part, width), lambda j, p: (0, 0))] * count
            + [pl.BlockSpec((part, spare), lambda j, p: (0, table_at))] * count
            + [
                pl.BlockSpec((2, width, size), lambda j, p: (0, 0, jnp.minimum(j, steps - 1))),
                pl.BlockSpec((hidden_count, tile), lambda j, p: (0, jnp.maximum(j - steps, 0))),
            ],
            out_specs=[pl.BlockSpec((part, tile), lambda j, p: (0, jnp.maximum(j - steps, 0)))]
            * count,
            scratch_shapes=[
                pltpu.VMEM((row_count, width), jnp.bfloat16),
                pltpu.VMEM((row_count, hidden_count), jnp.bfloat16),
            ],
        ),
        out_shape=[jax.ShapeDtypeStruct((part, width), jnp.bfloat16)] * count,
        compiler_params=pltpu.CompilerParams(vmem_limit_bytes=40 << 20),
        cost_estimate=pl.CostEstimate(
            flops=6 * row_count * hidden_count * width,
            bytes_accessed=6 * hidden_count * width,
            transcendentals=row_count * hidden_count,
        ),
        name="ffn",
    )(place, *pieces, *tables, planes, weights_dn)


def learn_kernel(place, *refs, count, experts, rates):
    rows_refs, table_refs, cot_refs = refs[:count], refs[count : 2 * count], refs[2 * count : 3 * count]
    gu_ref, dn_ref = refs[3 * count : 3 * count + 2]
    dx_refs = refs[3 * count + 2 : 4 * count + 2]
    new_gu_ref, new_dn_ref = refs[4 * count + 2 : 4 * count + 4]
    rows, turned, pulls, pulls_turned, total, grads, grads_dn = refs[4 * count + 4 :]
    step = pl.program_id(0)
    part, width = rows_refs[0].shape
    tile = 1024
    cuts = [slice(lower, lower + tile) for lower in range(0, width, tile)]

    @pl.when(step == 0)
    def _():
        for i in range(count):
            here = slice(part * i, part * (i + 1))
            gates = pick_gates(table_refs[i][...], place[0], experts)
            rows[here, :] = rows_refs[i][...]
            pulls[here, :] = (gates * cot_refs[i][...].astype(jnp.float32)).astype(jnp.bfloat16)
        for cut in cuts:
            turned[cut, :] = rows[:, cut].T
            pulls_turned[cut, :] = pulls[:, cut].T
        total[...] = jnp.zeros_like(total)

    active = nn(rows[...], gu_ref[0])
    upward = nn(rows[...], gu_ref[1])
    back = nn(dn_ref[...], pulls_turned[...]).T
    sigma = jax.nn.sigmoid(active)
    swish = active * sigma
    hidden = (swish * upward).astype(jnp.bfloat16)
    d_active = (back * upward * sigma * (1.0 + active * (1.0 - sigma))).astype(jnp.bfloat16)
    d_upward = (back * swish).astype(jnp.bfloat16)
    hidden_turned = hidden.T
    d_active_turned = d_active.T
    d_upward_turned = d_upward.T

    for cut in cuts:
        total[cut, :] += nn(gu_ref[0, cut, :], d_active_turned) + nn(
            gu_ref[1, cut, :], d_upward_turned
        )

    for half, sent in ((0, d_active), (1, d_upward)):
        squares = jnp.zeros((8, sent.shape[1]), jnp.float32)
        for cut in cuts:
            fresh = nn(turned[cut, :], sent)
            grads[cut, :] = fresh
            squares = squares + jnp.sum((fresh * fresh).reshape(-1, 8, sent.shape[1]), axis=0)
        squares = jnp.sum(squares, axis=0, keepdims=True)
        scale = rates[0] / jnp.sqrt(squares / width + EPSILON)
        for cut in cuts:
            old = gu_ref[half, cut, :].astype(jnp.float32)
            new_gu_ref[half, cut, :] = (old - grads[cut, :] * scale).astype(jnp.bfloat16)

    squares = jnp.zeros((dn_ref.shape[0], 1), jnp.float32)
    for cut in cuts:
        fresh = nn(hidden_turned, pulls[:, cut])
        grads_dn[:, cut] = fresh
        squares = squares + jnp.sum(fresh * fresh, axis=1, keepdims=True)
    scale = rates[1] / jnp.sqrt(squares / width + EPSILON)
    for cut in cuts:
        old = dn_ref[:, cut].astype(jnp.float32)
        new_dn_ref[:, cut] = (old - grads_dn[:, cut] * scale).astype(jnp.bfloat16)

    @pl.when(step == pl.num_programs(0) - 1)
    def _():
        for cut in cuts:
            done = total[cut, :].T.astype(jnp.bfloat16)
            for i in range(count):
                dx_refs[i][:, cut] = done[part * i : part * (i + 1)]


def learn_call(place, pieces, tables, cots, planes, weights_dn, experts, rates):
    count = len(pieces)
    part = pieces[0].shape[0]
    hidden_count, width = weights_dn.shape
    spare = tables[0].shape[1] - width
    size = hidden_block(hidden_count)
    row_count = part * count
    table_at = width // spare
    once = pl.Buffered(1)
    piece = pl.BlockSpec((part, width), lambda j, p: (0, 0), pipeline_mode=once)
    return pl.pallas_call(
        functools.partial(learn_kernel, count=count, experts=experts, rates=rates),
        grid_spec=pltpu.PrefetchScalarGridSpec(
            num_scalar_prefetch=1,
            grid=(hidden_count // size,),
            in_specs=[piece] * count
            + [pl.BlockSpec((part, spare), lambda j, p: (0, table_at))] * count
            + [piece] * count
            + [
                pl.BlockSpec((2, width, size), lambda j, p: (0, 0, j)),
                pl.BlockSpec((size, width), lambda j, p: (j, 0)),
            ],
            out_specs=[pl.BlockSpec((part, width), lambda j, p: (0, 0))] * count
            + [
                pl.BlockSpec((2, width, size), lambda j, p: (0, 0, j)),
                pl.BlockSpec((size, width), lambda j, p: (j, 0)),
            ],
            scratch_shapes=[
                pltpu.VMEM((row_count, width), jnp.bfloat16),
                pltpu.VMEM((width, row_count), jnp.bfloat16),
                pltpu.VMEM((row_count, width), jnp.bfloat16),
                pltpu.VMEM((width, row_count), jnp.bfloat16),
                pltpu.VMEM((width, row_count), jnp.float32),
                pltpu.VMEM((width, size), jnp.float32),
                pltpu.VMEM((size, width), jnp.float32),
            ],
        ),
        out_shape=[jax.ShapeDtypeStruct((part, width), jnp.bfloat16)] * count
        + [
            jax.ShapeDtypeStruct(planes.shape, jnp.bfloat16),
            jax.ShapeDtypeStruct(weights_dn.shape, jnp.bfloat16),
        ],
        compiler_params=pltpu.CompilerParams(vmem_limit_bytes=60 << 20),
        cost_estimate=pl.CostEstimate(
            flops=16 * row_count * hidden_count * width,
            bytes_accessed=12 * hidden_count * width,
            transcendentals=row_count * hidden_count,
        ),
        name="learn",
    )(place, *pieces, *tables, *cots, planes, weights_dn)


def unset(like):
    return pl.pallas_call(
        lambda out_ref: None,
        out_shape=jax.ShapeDtypeStruct(like.shape, like.dtype),
        out_specs=pl.BlockSpec(memory_space=pl.ANY),
        name="unset",
    )()


def ffn_plain(place, pieces, tables, planes, weights_dn, experts):
    width = weights_dn.shape[1]
    rows = pieces[0][:, :width]
    gates = pick_gates(tables[0][:, width:], place[0], experts)
    active = nn(rows, planes[0])
    upward = nn(rows, planes[1])
    hidden = (active * jax.nn.sigmoid(active) * upward).astype(jnp.bfloat16)
    return [(gates * nn(hidden, weights_dn)).astype(jnp.bfloat16)]


def learn_plain(place, pieces, tables, cots, planes, weights_dn, experts, rates):
    width = weights_dn.shape[1]
    rows = pieces[0][:, :width]
    gates = pick_gates(tables[0][:, width:], place[0], experts)
    pulls = (gates * cots[0].astype(jnp.float32)).astype(jnp.bfloat16)
    active = nn(rows, planes[0])
    upward = nn(rows, planes[1])
    back = nt(pulls, weights_dn)
    sigma = jax.nn.sigmoid(active)
    swish = active * sigma
    hidden = (swish * upward).astype(jnp.bfloat16)
    d_active = (back * upward * sigma * (1.0 + active * (1.0 - sigma))).astype(jnp.bfloat16)
    d_upward = (back * swish).astype(jnp.bfloat16)
    dx_part = (nt(d_active, planes[0]) + nt(d_upward, planes[1])).astype(jnp.bfloat16)
    new_planes = jnp.stack(
        [
            renew(planes[0], wide(rows, d_active, ((0,), (0,))), 0, rates[0]),
            renew(planes[1], wide(rows, d_upward, ((0,), (0,))), 0, rates[0]),
        ],
        axis=0,
    )
    new_dn = renew(weights_dn, wide(hidden, pulls, ((0,), (0,))), 1, rates[1])
    return [dx_part, new_planes, new_dn]


def per_device(
    rows_in,
    cotangent,
    lengths,
    train_experts,
    train_gates,
    decode_experts,
    decode_gates,
    gate_up,
    down,
):
    ep_count = lax.axis_size("ep")
    dp_count = lax.axis_size("dp")
    device_count = ep_count * dp_count
    row_count, model_width = cotangent.shape
    role = lax.axis_index("grp").astype(jnp.int32)
    is_learner = role == 0
    mine = lax.axis_index("ep").astype(jnp.int32)
    own_dn = down[0, 0]
    planes = jnp.transpose(gate_up[0, 0], (1, 0, 2))
    total_rows = row_count * device_count
    longest = 2 * total_rows // lengths.shape[0]
    rates = (0.5 / model_width**0.5, 0.5 / (own_dn.shape[0] * dp_count) ** 0.5)
    small = device_count == 16
    run_ffn, run_learn = (ffn_call, learn_call) if small else (ffn_plain, learn_plain)
    first_place = mine.reshape(1)
    fresh_place = first_place + 2 * ep_count

    where = jnp.stack([mine * dp_count + lax.axis_index("dp").astype(jnp.int32), role])
    block, base = prep_call(
        where, lengths, rows_in[0], cotangent, train_experts, train_gates, decode_experts,
        decode_gates, ep_count, longest,
    )
    every, planes = gather(block, device_count, (0, 1), planes)
    count = len(every)
    cotangent, every[0] = tied(cotangent, every[0])
    cots, _ = gather(cotangent, device_count, (0,))

    def learn(every, cots, planes, own_dn):
        out = list(run_learn(first_place, every, every, cots, planes, own_dn, ep_count, rates))
        return ([unset(o) for o in out[:count]], out[:count], out[count], out[count + 1])

    def decode(every, cots, planes, own_dn):
        out = list(run_ffn(first_place, every, every, planes, own_dn, ep_count))
        return (out, [unset(o) for o in out], unset(planes), unset(own_dn))

    part, dx_part, new_planes, new_dn = lax.cond(
        is_learner, learn, decode, every, cots, planes, own_dn
    )
    stale_sum = scatter_sum(part, device_count, (1,))
    current = (base + stale_sum).astype(jnp.bfloat16)
    hopped = across(current, 1, 0)
    if small:
        dx_near, dx_away = sum_core(dx_part, (0,))
    arrived, _ = gather(hopped, device_count, (0,))
    if small:
        arrived[0], dx_near, dx_away = tied(arrived[0], dx_near, dx_away)
        dx_near, dx_away = sum_y(dx_near, dx_away, (0,))

    fresh_part = lax.cond(
        is_learner,
        lambda r, e, g, d: list(run_ffn(fresh_place, r, e, g, d, ep_count)),
        lambda r, e, g, d: [unset(o) for o in r],
        arrived,
        every,
        new_planes,
        new_dn,
    )
    if small:
        near, away = sum_core(fresh_part, (0,))
        near, away, dx_near, dx_away = tied(near, away, dx_near, dx_away)
        dx_sum = sum_z(dx_near, dx_away, (0,))
        near, away = sum_y(near, away, (0,))
        fresh_sum = sum_z(near, away, (0,))
    else:
        dx_sum = scatter_sum(dx_part, device_count, (0,))
        fresh_sum = scatter_sum(fresh_part, device_count, (0,))
    moved = across(fresh_sum.astype(jnp.bfloat16), 0, 1).astype(jnp.float32)
    final_rows = jnp.where(is_learner, base + dx_sum, current.astype(jnp.float32) + moved)
    return final_rows.astype(jnp.bfloat16)[None]


def solution(mesh):
    placed = (
        P("grp", ("ep", "dp"), None),
        P(("ep", "dp"), None),
        P(),
        P(("ep", "dp"), None),
        P(("ep", "dp"), None),
        P(None, ("ep", "dp"), None),
        P(None, ("ep", "dp"), None),
        P("grp", "ep", None, None, "dp"),
        P("grp", "ep", "dp", None),
    )
    return jax.shard_map(
        per_device,
        mesh=mesh,
        in_specs=placed,
        out_specs=P("grp", ("ep", "dp"), None),
        check_vma=False,
    )
```

time: 244 us -> 227 us (0.930)
  starting transfers between devices: 73.5 us -> 95.7 us
  local copies, waits for them, and re-layouts: 35.8 us -> 15.2 us
  Pallas kernels: 61.6 us -> 51.5 us
  waiting for transfers between devices: 64.3 us -> 54.5 us
    ppermute x30 -> x42, starting transfers between devices: 70.8 us -> 92.9 us  [swap(): return lax.ppermute(block, ('grp',) + AXES, pairs)]
    pallas_call x2 -> x3, Pallas kernels: 61.6 us -> 51.5 us  [the longest x1 36.2 us: learn_call(): pl.pallas_call(functools.partial(learn_kernel, count=count, experts=exper...]
    ppermute x30 -> x42, waiting for transfers between devices: 57.8 us -> 48.5 us  [swap(): return lax.ppermute(block, ('grp',) + AXES, pairs)]
    unnamed x25 -> x32, local copies, waits for them, and re-layouts: 22.5 us -> 14.2 us
    concatenate x7 -> x6, local copies, waits for them, and re-layouts: 7.45 us -> 0.13 us  [the longest x3 0.07 us: gather(): away = jnp.concatenate([away, swap(away, 16, 2, role)], axis=0)]
    split x9 -> x12, local copies, waits for them, and re-layouts: 4.1 us -> 0.91 us  [halves(): return jnp.split(array, 2, axis=0)]
    convert_element_type x9 -> x13, other arithmetic: 2.53 us -> 5.28 us  [the longest x3 2.45 us: sum_core(): near = plus(pieces[0], swap(pieces[1], 16, 1, role)).astype(jnp.bfloat16)]
  transfers between devices with their start and end apart: 32 -> 44, of which waited for: 11 -> 11; matrix products, arithmetic and copies ran while one was open for 16% -> 8% of each run, Pallas kernels for 5% -> 6%
where the time goes in v1:
time: 227 us; the launch traced here: 226 us
  starting transfers between devices  95.7 us (42%)
  waiting for transfers between devices  54.5 us (24%)
  Pallas kernels  51.5 us (23%)
  local copies, waits for them, and re-layouts  15.2 us (7%)
  other arithmetic  7.88 us (3%)
    ppermute x42, starting transfers between devices, swap(): return lax.ppermute(block, ('grp',) + AXES, pairs)  92.9 us
    ppermute x42, waiting for transfers between devices, swap(): return lax.ppermute(block, ('grp',) + AXES, pairs)  48.5 us
    pallas_call x1, Pallas kernels, learn_call(): pl.pallas_call(functools.partial(learn_kernel, count=count, experts=exper...  36.2 us
    unnamed x32, local copies, waits for them, and re-layouts  14.2 us
    pallas_call x1, Pallas kernels, ffn_call(): pl.pallas_call(functools.partial(ffn_kernel, count=count, experts=experts...  13.3 us
    ppermute x2, waiting for transfers between devices, across(): return lax.ppermute(block, 'grp', [(source, target)])  6 us
  transfers between devices with their start and end apart: 44, of which 11 were waited for; matrix products, arithmetic and copies ran while one was open for 8% of the time, Pallas kernels for 6%

profile of v1, /device:TPU:0, one launch (start us, length us, event | category | flops | bytes accessed | tf_op | source)
XLA Modules:
  0.0 225.8 jit_solution(5576029730876048165)
XLA Ops:
  2.6 3.1 %collective-permute-start = (bf16[16,4224]{1,0:T(8,128)(2,1)}, bf16[16,4224]{1,0:T(8,128)(2,1)S(1)}, u32[]{:S(2)}, u32[]{:S(2)}) collective-permute-start(bf16[16,4224]{1,0:T(8,128)(2,1)} %get-tuple-element.200), channel_id=1, source_target_pairs={{0,4},{1,5},{2,6},{3,7},{4,0},{5,1},{6,2},{7,3},{8,12},{9,13},{10,... | collective-permute-start | bytes 405512 | tf_op jit(solution)/shard_map/ppermute | solution.py:39
  5.7 2.5 %collective-permute-start.4 = (bf16[16,4224]{1,0:T(8,128)(2,1)}, bf16[16,4224]{1,0:T(8,128)(2,1)S(1)}, u32[]{:S(2)}, u32[]{:S(2)}) collective-permute-start(bf16[16,4224]{1,0:T(8,128)(2,1)} %get-tuple-element.200), channel_id=1, source_target_pairs={{0,12},{1,13},{2,14},{3,15},{4,8},{5,9},{6,10},{7,11},{8,4},{9,5},... | collective-permute-start | bytes 405512 | tf_op jit(solution)/shard_map/ppermute | solution.py:39
  8.3 11.8 %copy.12 = bf16[1,1,4096,2,768]{4,2,3,1,0:T(8,128)(2,1)} copy(bf16[1,1,4096,2,768]{4,3,2,1,0:T(2,128)(2,1)} %param.20) | data formatting | bytes 25165824 | tf_op args[7]
  22.3 7.2 %collective-permute-done.1 = bf16[32,4224]{1,0:T(8,128)(2,1)S(1)} collective-permute-done((bf16[32,4224]{1,0:T(8,128)(2,1)S(1)}, bf16[32,4224]{1,0:T(8,128)(2,1)S(1)}, u32[]{:S(2)}, u32[]{:S(2)}) %collective-permute-start.1) | collective-permute-done | bytes 270368 | tf_op jit(solution)/shard_map/ppermute | solution.py:39
  29.6 4.8 %collective-permute-start.11 = (bf16[16,4096]{1,0:T(8,128)(2,1)S(1)}, bf16[16,4096]{1,0:T(8,128)(2,1)S(1)}, u32[]{:S(2)}, u32[]{:S(2)}) collective-permute-start(bf16[16,4096]{1,0:T(8,128)(2,1)S(1)} %copy-done), channel_id=1, source_target_pairs={{0,12},{1,13},{2,14},{3,15},{4,8},{5,9},{6,10},{7,11},{8,4},{9,5},... | collective-permute-start | bytes 393224 | tf_op jit(solution)/shard_map/ppermute | solution.py:39
  36.7 3.0 %collective-permute-start.7 = (bf16[16,4096]{1,0:T(8,128)(2,1)S(1)}, bf16[16,4096]{1,0:T(8,128)(2,1)S(1)}, u32[]{:S(2)}, u32[]{:S(2)}) collective-permute-start(bf16[16,4096]{1,0:T(8,128)(2,1)S(1)} %copy-done), channel_id=1, source_target_pairs={{0,4},{1,5},{2,6},{3,7},{4,0},{5,1},{6,2},{7,3},{8,12},{9,13},{10,... | collective-permute-start | bytes 393224 | tf_op jit(solution)/shard_map/ppermute | solution.py:39
  40.4 3.6 %collective-permute-done.10 = bf16[16,4096]{1,0:T(8,128)(2,1)S(1)} collective-permute-done((bf16[16,4096]{1,0:T(8,128)(2,1)S(1)}, bf16[16,4096]{1,0:T(8,128)(2,1)S(1)}, u32[]{:S(2)}, u32[]{:S(2)}) %collective-permute-start.10) | collective-permute-done | bytes 131104 | tf_op jit(solution)/shard_map/ppermute | solution.py:39
  44.0 3.4 %collective-permute-start.12 = (bf16[32,4096]{1,0:T(8,128)(2,1)S(1)}, bf16[32,4096]{1,0:T(8,128)(2,1)S(1)}, u32[]{:S(2)}, u32[]{:S(2)}) collective-permute-start(bf16[32,4096]{1,0:T(8,128)(2,1)S(1)} %pad_maximum_fusion.3), channel_id=1, source_target_pairs={{0,2},{1,3},{2,0},{3,1},{4,6},{5,7},{6,4},{7,5},{8,10},{9,11},{10,... | collective-permute-start | bytes 786440 | tf_op jit(solution)/shard_map/ppermute | solution.py:39
  47.5 2.4 %collective-permute-start.8 = (bf16[32,4096]{1,0:T(8,128)(2,1)S(1)}, bf16[32,4096]{1,0:T(8,128)(2,1)S(1)}, u32[]{:S(2)}, u32[]{:S(2)}) collective-permute-start(bf16[32,4096]{1,0:T(8,128)(2,1)S(1)} %pad_maximum_fusion.2), channel_id=1, source_target_pairs={{0,2},{1,3},{2,0},{3,1},{4,6},{5,7},{6,4},{7,5},{8,10},{9,11},{10,... | collective-permute-start | bytes 786440 | tf_op jit(solution)/shard_map/ppermute | solution.py:39
  50.0 8.0 %collective-permute-done.8 = bf16[32,4096]{1,0:T(8,128)(2,1)S(1)} collective-permute-done((bf16[32,4096]{1,0:T(8,128)(2,1)S(1)}, bf16[32,4096]{1,0:T(8,128)(2,1)S(1)}, u32[]{:S(2)}, u32[]{:S(2)}) %collective-permute-start.8) | collective-permute-done | bytes 262176 | tf_op jit(solution)/shard_map/ppermute | solution.py:39
  60.0 2.4 %collective-permute-start.13 = (bf16[64,4096]{1,0:T(8,128)(2,1)S(1)}, bf16[64,4096]{1,0:T(8,128)(2,1)}, u32[]{:S(2)}, u32[]{:S(2)}) collective-permute-start(bf16[64,4096]{1,0:T(8,128)(2,1)S(1)} %constant_dynamic-update-slice_fusion.8), channel_id=1, source_target_pairs={{0,1},{1,0},{2,3},{3,2},{4,5},{5,4},{6,7},{7,6},{8,9},{9,8},{10,11... | collective-permute-start | bytes 1572872 | tf_op jit(solution)/shard_map/ppermute | solution.py:39
  64.0 37.2 %conditional.8 = (bf16[64,4096]{1,0:T(8,128)(2,1)}, bf16[64,4096]{1,0:T(8,128)(2,1)}, bf16[64,4096]{1,0:T(8,128)(2,1)}, bf16[64,4096]{1,0:T(8,128)(2,1)}, bf16[6...) conditional(s32[]{:T(128)} %convert_element_type.189, ...), branch_computations={%region_0.0_spmd, %region_1.0_spmd} | conditional | flops 12884901888 | bytes 41943176
  65.0 36.2 %learn.1 = (bf16[64,4096]{1,0:T(8,128)(2,1)S(1)}, bf16[64,4096]{1,0:T(8,128)(2,1)}, bf16[64,4096]{1,0:T(8,128)(2,1)S(1)}, bf16[64,4096]{1,0:T(8,128)(2,1)}, bf16...) custom-call(s32[1]{0:T(128)} %get-tuple-element.140.place, bf16[64,4224]{1,0:T(8,128)(2,1)S(1)} %get-tuple-element.141.refs_0_.refs_4_, ...), custom_call_target="tpu_custom_call" | custom-call | flops 12884901888 | bytes 37748736 | tf_op jit(solution)/shard_map/cond/branch_1_fun/learn/pallas_call | solution.py:356
  115.0 6.0 %collective-permute-done.21 = bf16[16,4096]{1,0:T(8,128)(2,1)S(1)} collective-permute-done((bf16[16,4096]{1,0:T(8,128)(2,1)S(1)}, bf16[16,4096]{1,0:T(8,128)(2,1)S(1)}, u32[]{:S(2)}, u32[]{:S(2)}) %collective-permute-start.21) | collective-permute-done | bytes 131104 | tf_op jit(solution)/shard_map/ppermute | solution.py:15
  121.0 3.1 %collective-permute-start.28 = (bf16[16,4096]{1,0:T(8,128)(2,1)S(1)}, bf16[16,4096]{1,0:T(8,128)(2,1)S(1)}, u32[]{:S(2)}, u32[]{:S(2)}) collective-permute-start(bf16[16,4096]{1,0:T(8,128)(2,1)S(1)} %collective-permute-done.21), channel_id=1, source_target_pairs={{0,12},{1,13},{2,14},{3,15},{4,8},{5,9},{6,10},{7,11},{8,4},{9,5},... | collective-permute-start | bytes 393224 | tf_op jit(solution)/shard_map/ppermute | solution.py:39
  126.0 5.1 %collective-permute-start.22 = (bf16[16,4096]{1,0:T(8,128)(2,1)S(1)}, bf16[16,4096]{1,0:T(8,128)(2,1)S(1)}, u32[]{:S(2)}, u32[]{:S(2)}) collective-permute-start(bf16[16,4096]{1,0:T(8,128)(2,1)S(1)} %collective-permute-done.21), channel_id=1, source_target_pairs={{0,4},{1,5},{2,6},{3,7},{4,0},{5,1},{6,2},{7,3},{8,12},{9,13},{10,... | collective-permute-start | bytes 393224 | tf_op jit(solution)/shard_map/ppermute | solution.py:39
  131.1 4.2 %collective-permute-done.27 = bf16[16,4096]{1,0:T(8,128)(2,1)S(1)} collective-permute-done((bf16[16,4096]{1,0:T(8,128)(2,1)S(1)}, bf16[16,4096]{1,0:T(8,128)(2,1)S(1)}, u32[]{:S(2)}, u32[]{:S(2)}) %collective-permute-start.27) | collective-permute-done | bytes 131104 | tf_op jit(solution)/shard_map/ppermute | solution.py:39
  135.4 3.5 %collective-permute-start.29 = (bf16[32,4096]{1,0:T(8,128)(2,1)S(1)}, bf16[32,4096]{1,0:T(8,128)(2,1)S(1)}, u32[]{:S(2)}, u32[]{:S(2)}) collective-permute-start(bf16[32,4096]{1,0:T(8,128)(2,1)S(1)} %pad_maximum_fusion.5), channel_id=1, source_target_pairs={{0,2},{1,3},{2,0},{3,1},{4,6},{5,7},{6,4},{7,5},{8,10},{9,11},{10,... | collective-permute-start | bytes 786440 | tf_op jit(solution)/shard_map/ppermute | solution.py:39
  141.3 9.7 %collective-permute-done.23 = bf16[32,4096]{1,0:T(8,128)(2,1)S(1)} collective-permute-done((bf16[32,4096]{1,0:T(8,128)(2,1)S(1)}, bf16[32,4096]{1,0:T(8,128)(2,1)S(1)}, u32[]{:S(2)}, u32[]{:S(2)}) %collective-permute-start.23) | collective-permute-done | bytes 262176 | tf_op jit(solution)/shard_map/ppermute | solution.py:39
  153.7 3.5 %collective-permute-start.34 = (bf16[32,4096]{1,0:T(8,128)(2,1)S(1)}, bf16[32,4096]{1,0:T(8,128)(2,1)S(1)}, u32[]{:S(2)}, u32[]{:S(2)}) collective-permute-start(bf16[32,4096]{1,0:T(8,128)(2,1)S(1)} %split.83), channel_id=1, source_target_pairs={{0,2},{1,3},{2,0},{3,1},{4,6},{5,7},{6,4},{7,5},{8,10},{9,11},{10,... | collective-permute-start | bytes 786440 | tf_op jit(solution)/shard_map/ppermute | solution.py:39
  157.2 2.4 %collective-permute-start.33 = (bf16[32,4096]{1,0:T(8,128)(2,1)}, bf16[32,4096]{1,0:T(8,128)(2,1)}, u32[]{:S(2)}, u32[]{:S(2)}) collective-permute-start(bf16[32,4096]{1,0:T(8,128)(2,1)} %split.81), channel_id=1, source_target_pairs={{0,2},{1,3},{2,0},{3,1},{4,6},{5,7},{6,4},{7,5},{8,10},{9,11},{10,... | collective-permute-start | bytes 786440 | tf_op jit(solution)/shard_map/ppermute | solution.py:39
  161.6 3.2 %collective-permute-done.34 = bf16[32,4096]{1,0:T(8,128)(2,1)S(1)} collective-permute-done((bf16[32,4096]{1,0:T(8,128)(2,1)S(1)}, bf16[32,4096]{1,0:T(8,128)(2,1)S(1)}, u32[]{:S(2)}, u32[]{:S(2)}) %collective-permute-start.34) | collective-permute-done | bytes 262176 | tf_op jit(solution)/shard_map/ppermute | solution.py:39
  164.8 14.6 %conditional.9 = (bf16[64,4096]{1,0:T(8,128)(2,1)}, bf16[64,4096]{1,0:T(8,128)(2,1)}, bf16[64,4096]{1,0:T(8,128)(2,1)}, bf16[64,4096]{1,0:T(8,128)(2,1)S(1)}) conditional(s32[]{:T(128)} %convert_element_type.189, () %tuple.56, (s32[1]{0:T(128)}, bf16[64,4096]{1,0:T(8,128)(2,1)S(1)}, bf16[64,4096]{1,0:T(8,128)(2,1)S(1)}, ...), branch_computations={%region_2.0_spmd, %region_3.0_spmd} | conditional | flops 4831838208 | bytes 27263132
  166.2 13.3 %ffn.4 = (bf16[64,4096]{1,0:T(8,128)(2,1)}, bf16[64,4096]{1,0:T(8,128)(2,1)}, bf16[64,4096]{1,0:T(8,128)(2,1)S(1)}, bf16[64,4096]{1,0:T(8,128)(2,1)}) custom-call(s32[1]{0:T(128)S(6)} %add.53.place, bf16[64,4096]{1,0:T(8,128)(2,1)} %copy-done.2, bf16[64,4096]{1,0:T(8,128)(2,1)} %copy-done.4, bf16[64,4096]{1,0:T(8,128)(2,1)} %copy-done.3, ...), custom_call_target="tpu_custom_call" | custom-call | flops 4831838208 | bytes 18874368 | tf_op jit(solution)/shard_map/cond/branch_1_fun/ffn/pallas_call | solution.py:247
  182.4 2.4 %collective-permute-start.31 = (bf16[64,4096]{1,0:T(8,128)(2,1)}, bf16[64,4096]{1,0:T(8,128)(2,1)S(1)}, u32[]{:S(2)}, u32[]{:S(2)}) collective-permute-start(bf16[64,4096]{1,0:T(8,128)(2,1)} %get-tuple-element.217), channel_id=1, source_target_pairs={{0,1},{1,0},{2,3},{3,2},{4,5},{5,4},{6,7},{7,6},{8,9},{9,8},{10,11... | collective-permute-start | bytes 1572872 | tf_op jit(solution)/shard_map/ppermute | solution.py:39
  187.7 3.5 %collective-permute-start.40 = (bf16[32,4096]{1,0:T(8,128)(2,1)S(1)}, bf16[32,4096]{1,0:T(8,128)(2,1)S(1)}, u32[]{:S(2)}, u32[]{:S(2)}) collective-permute-start(bf16[32,4096]{1,0:T(8,128)(2,1)S(1)} %split.93), channel_id=1, source_target_pairs={{0,2},{1,3},{2,0},{3,1},{4,6},{5,7},{6,4},{7,5},{8,10},{9,11},{10,... | collective-permute-start | bytes 786440 | tf_op jit(solution)/shard_map/ppermute | solution.py:39
  193.6 5.1 %collective-permute-done.40 = bf16[32,4096]{1,0:T(8,128)(2,1)S(1)} collective-permute-done((bf16[32,4096]{1,0:T(8,128)(2,1)S(1)}, bf16[32,4096]{1,0:T(8,128)(2,1)S(1)}, u32[]{:S(2)}, u32[]{:S(2)}) %collective-permute-start.40) | collective-permute-done | bytes 262176 | tf_op jit(solution)/shard_map/ppermute | solution.py:39
  200.8 3.3 %collective-permute-start.42 = (bf16[16,4096]{1,0:T(8,128)(2,1)S(1)}, bf16[16,4096]{1,0:T(8,128)(2,1)S(1)}, u32[]{:S(2)}, u32[]{:S(2)}) collective-permute-start(bf16[16,4096]{1,0:T(8,128)(2,1)S(1)} %get-tuple-element.251), channel_id=1, source_target_pairs={{0,12},{1,13},{2,14},{3,15},{4,8},{5,9},{6,10},{7,11},{8,4},{9,5},... | collective-permute-start | bytes 393224 | tf_op jit(solution)/shard_map/ppermute | solution.py:39
  204.3 3.9 %collective-permute-start.39 = (bf16[16,4096]{1,0:T(8,128)(2,1)S(1)}, bf16[16,4096]{1,0:T(8,128)(2,1)S(1)}, u32[]{:S(2)}, u32[]{:S(2)}) collective-permute-start(bf16[16,4096]{1,0:T(8,128)(2,1)S(1)} %split.105), channel_id=1, source_target_pairs={{0,4},{1,5},{2,6},{3,7},{4,0},{5,1},{6,2},{7,3},{8,12},{9,13},{10,... | collective-permute-start | bytes 393224 | tf_op jit(solution)/shard_map/ppermute | solution.py:39
  210.2 3.9 %collective-permute-start.36 = (bf16[16,4096]{1,0:T(8,128)(2,1)S(1)}, bf16[16,4096]{1,0:T(8,128)(2,1)S(1)}, u32[]{:S(2)}, u32[]{:S(2)}) collective-permute-start(bf16[16,4096]{1,0:T(8,128)(2,1)S(1)} %get-tuple-element.248), channel_id=1, source_target_pairs={{0,8},{1,9},{2,10},{3,11},{4,12},{5,13},{6,14},{7,15},{8,0},{9,1},... | collective-permute-start | bytes 393224 | tf_op jit(solution)/shard_map/ppermute | solution.py:39
  214.1 4.3 %collective-permute-start.37 = (bf16[16,4096]{1,0:T(8,128)(2,1)S(1)}, bf16[16,4096]{1,0:T(8,128)(2,1)S(1)}, u32[]{:S(2)}, u32[]{:S(2)}) collective-permute-start(bf16[16,4096]{1,0:T(8,128)(2,1)S(1)} %get-tuple-element.249), channel_id=1, source_target_pairs={{0,12},{1,13},{2,14},{3,15},{4,8},{5,9},{6,10},{7,11},{8,4},{9,5},... | collective-permute-start | bytes 393224 | tf_op jit(solution)/shard_map/ppermute | solution.py:39
  219.8 4.1 %collective-permute-done.36 = bf16[16,4096]{1,0:T(8,128)(2,1)S(1)} collective-permute-done((bf16[16,4096]{1,0:T(8,128)(2,1)S(1)}, bf16[16,4096]{1,0:T(8,128)(2,1)S(1)}, u32[]{:S(2)}, u32[]{:S(2)}) %collective-permute-start.36) | collective-permute-done | bytes 131104 | tf_op jit(solution)/shard_map/ppermute | solution.py:39
  (137 shorter events, 51.8 us)
Async XLA Ops:
  2.6 17.4 %collective-permute-start = (bf16[16,4224]{1,0:T(8,128)(2,1)}, bf16[16,4224]{1,0:T(8,128)(2,1)S(1)}, u32[]{:S(2)}, u32[]{:S(2)}) collective-permute-start(bf16[16,4224]{1,0:T(8,128)(2,1)} %get-tuple-element.200), channel_id=1, source_target_pairs={{0,4},{1,5},{2,6},{3,7},{4,0},{5,1},{6,2},{7,3},{8,12},{9,13},{10,... | collective-permute-start | bytes 405512 | tf_op jit(solution)/shard_map/ppermute | solution.py:39
  5.7 16.0 %collective-permute-start.4 = (bf16[16,4224]{1,0:T(8,128)(2,1)}, bf16[16,4224]{1,0:T(8,128)(2,1)S(1)}, u32[]{:S(2)}, u32[]{:S(2)}) collective-permute-start(bf16[16,4224]{1,0:T(8,128)(2,1)} %get-tuple-element.200), channel_id=1, source_target_pairs={{0,12},{1,13},{2,14},{3,15},{4,8},{5,9},{6,10},{7,11},{8,4},{9,5},... | collective-permute-start | bytes 405512 | tf_op jit(solution)/shard_map/ppermute | solution.py:39
  8.1 13.5 %collective-permute-start.3 = (bf16[16,4224]{1,0:T(8,128)(2,1)}, bf16[16,4224]{1,0:T(8,128)(2,1)S(1)}, u32[]{:S(2)}, u32[]{:S(2)}) collective-permute-start(bf16[16,4224]{1,0:T(8,128)(2,1)} %get-tuple-element.200), channel_id=1, source_target_pairs={{0,8},{1,9},{2,10},{3,11},{4,12},{5,13},{6,14},{7,15},{8,0},{9,1},... | collective-permute-start | bytes 405512 | tf_op jit(solution)/shard_map/ppermute | solution.py:39
  20.1 9.5 %collective-permute-start.1 = (bf16[32,4224]{1,0:T(8,128)(2,1)S(1)}, bf16[32,4224]{1,0:T(8,128)(2,1)S(1)}, u32[]{:S(2)}, u32[]{:S(2)}) collective-permute-start(bf16[32,4224]{1,0:T(8,128)(2,1)S(1)} %pad_maximum_fusion), channel_id=1, source_target_pairs={{0,2},{1,3},{2,0},{3,1},{4,6},{5,7},{6,4},{7,5},{8,10},{9,11},{10,... | collective-permute-start | bytes 811016 | tf_op jit(solution)/shard_map/ppermute | solution.py:39
  21.7 18.1 %collective-permute-start.5 = (bf16[32,4224]{1,0:T(8,128)(2,1)S(1)}, bf16[32,4224]{1,0:T(8,128)(2,1)S(1)}, u32[]{:S(2)}, u32[]{:S(2)}) collective-permute-start(bf16[32,4224]{1,0:T(8,128)(2,1)S(1)} %pad_maximum_fusion.1), channel_id=1, source_target_pairs={{0,2},{1,3},{2,0},{3,1},{4,6},{5,7},{6,4},{7,5},{8,10},{9,11},{10,... | collective-permute-start | bytes 811016 | tf_op jit(solution)/shard_map/ppermute | solution.py:39
  29.6 10.8 %collective-permute-start.11 = (bf16[16,4096]{1,0:T(8,128)(2,1)S(1)}, bf16[16,4096]{1,0:T(8,128)(2,1)S(1)}, u32[]{:S(2)}, u32[]{:S(2)}) collective-permute-start(bf16[16,4096]{1,0:T(8,128)(2,1)S(1)} %copy-done), channel_id=1, source_target_pairs={{0,12},{1,13},{2,14},{3,15},{4,8},{5,9},{6,10},{7,11},{8,4},{9,5},... | collective-permute-start | bytes 393224 | tf_op jit(solution)/shard_map/ppermute | solution.py:39
  34.4 9.6 %collective-permute-start.10 = (bf16[16,4096]{1,0:T(8,128)(2,1)S(1)}, bf16[16,4096]{1,0:T(8,128)(2,1)S(1)}, u32[]{:S(2)}, u32[]{:S(2)}) collective-permute-start(bf16[16,4096]{1,0:T(8,128)(2,1)S(1)} %copy-done), channel_id=1, source_target_pairs={{0,8},{1,9},{2,10},{3,11},{4,12},{5,13},{6,14},{7,15},{8,0},{9,1},... | collective-permute-start | bytes 393224 | tf_op jit(solution)/shard_map/ppermute | solution.py:39
  36.7 10.8 %collective-permute-start.7 = (bf16[16,4096]{1,0:T(8,128)(2,1)S(1)}, bf16[16,4096]{1,0:T(8,128)(2,1)S(1)}, u32[]{:S(2)}, u32[]{:S(2)}) collective-permute-start(bf16[16,4096]{1,0:T(8,128)(2,1)S(1)} %copy-done), channel_id=1, source_target_pairs={{0,4},{1,5},{2,6},{3,7},{4,0},{5,1},{6,2},{7,3},{8,12},{9,13},{10,... | collective-permute-start | bytes 393224 | tf_op jit(solution)/shard_map/ppermute | solution.py:39
  39.7 22.7 %collective-permute-start.2 = (bf16[64,4224]{1,0:T(8,128)(2,1)S(1)}, bf16[64,4224]{1,0:T(8,128)(2,1)S(1)}, u32[]{:S(2)}, u32[]{:S(2)}) collective-permute-start(bf16[64,4224]{1,0:T(8,128)(2,1)S(1)} %constant_dynamic-update-slice_fusion), channel_id=1, source_target_pairs={{0,1},{1,0},{2,3},{3,2},{4,5},{5,4},{6,7},{7,6},{8,9},{9,8},{10,11... | collective-permute-start | bytes 1622024 | tf_op jit(solution)/shard_map/ppermute | solution.py:39
  39.9 22.5 %collective-permute-start.6 = (bf16[64,4224]{1,0:T(8,128)(2,1)S(1)}, bf16[64,4224]{1,0:T(8,128)(2,1)S(1)}, u32[]{:S(2)}, u32[]{:S(2)}) collective-permute-start(bf16[64,4224]{1,0:T(8,128)(2,1)S(1)} %constant_dynamic-update-slice_fusion.2), channel_id=1, source_target_pairs={{0,1},{1,0},{2,3},{3,2},{4,5},{5,4},{6,7},{7,6},{8,9},{9,8},{10,11... | collective-permute-start | bytes 1622024 | tf_op jit(solution)/shard_map/ppermute | solution.py:39
  44.0 15.9 %collective-permute-start.12 = (bf16[32,4096]{1,0:T(8,128)(2,1)S(1)}, bf16[32,4096]{1,0:T(8,128)(2,1)S(1)}, u32[]{:S(2)}, u32[]{:S(2)}) collective-permute-start(bf16[32,4096]{1,0:T(8,128)(2,1)S(1)} %pad_maximum_fusion.3), channel_id=1, source_target_pairs={{0,2},{1,3},{2,0},{3,1},{4,6},{5,7},{6,4},{7,5},{8,10},{9,11},{10,... | collective-permute-start | bytes 786440 | tf_op jit(solution)/shard_map/ppermute | solution.py:39
  47.5 10.5 %collective-permute-start.8 = (bf16[32,4096]{1,0:T(8,128)(2,1)S(1)}, bf16[32,4096]{1,0:T(8,128)(2,1)S(1)}, u32[]{:S(2)}, u32[]{:S(2)}) collective-permute-start(bf16[32,4096]{1,0:T(8,128)(2,1)S(1)} %pad_maximum_fusion.2), channel_id=1, source_target_pairs={{0,2},{1,3},{2,0},{3,1},{4,6},{5,7},{6,4},{7,5},{8,10},{9,11},{10,... | collective-permute-start | bytes 786440 | tf_op jit(solution)/shard_map/ppermute | solution.py:39
  101.3 5.7 %collective-permute-start.17 = (bf16[64,4096]{1,0:T(8,128)(2,1)}, bf16[64,4096]{1,0:T(8,128)(2,1)S(1)}, u32[]{:S(2)}, u32[]{:S(2)}) collective-permute-start(bf16[64,4096]{1,0:T(8,128)(2,1)} %get-tuple-element.208), channel_id=1, source_target_pairs={{16,17},{17,16},{18,19},{19,18},{20,21},{21,20},{22,23},{23,22},{2... | collective-permute-start | bytes 1572872 | tf_op jit(solution)/shard_map/ppermute | solution.py:39
  101.9 11.1 %collective-permute-start.25 = (bf16[64,4096]{1,0:T(8,128)(2,1)}, bf16[64,4096]{1,0:T(8,128)(2,1)S(1)}, u32[]{:S(2)}, u32[]{:S(2)}) collective-permute-start(bf16[64,4096]{1,0:T(8,128)(2,1)} %get-tuple-element.212), channel_id=1, source_target_pairs={{0,1},{1,0},{2,3},{3,2},{4,5},{5,4},{6,7},{7,6},{8,9},{9,8},{10,11... | collective-permute-start | bytes 1572872 | tf_op jit(solution)/shard_map/ppermute | solution.py:39
  104.2 10.6 %collective-permute-start.24 = (bf16[64,4096]{1,0:T(8,128)(2,1)}, bf16[64,4096]{1,0:T(8,128)(2,1)S(1)}, u32[]{:S(2)}, u32[]{:S(2)}) collective-permute-start(bf16[64,4096]{1,0:T(8,128)(2,1)} %get-tuple-element.210), channel_id=1, source_target_pairs={{0,1},{1,0},{2,3},{3,2},{4,5},{5,4},{6,7},{7,6},{8,9},{9,8},{10,11... | collective-permute-start | bytes 1572872 | tf_op jit(solution)/shard_map/ppermute | solution.py:39
  113.3 7.7 %collective-permute-start.21 = (bf16[16,4096]{1,0:T(8,128)(2,1)S(1)}, bf16[16,4096]{1,0:T(8,128)(2,1)S(1)}, u32[]{:S(2)}, u32[]{:S(2)}) collective-permute-start(bf16[16,4096]{1,0:T(8,128)(2,1)S(1)} %add_convert_fusion.9), channel_id=1, source_target_pairs={{16,0},{17,1},{18,2},{19,3},{20,4},{21,5},{22,6},{23,7},{24,8},{25... | collective-permute-start | bytes 393224 | tf_op jit(solution)/shard_map/ppermute | solution.py:15
  121.0 10.1 %collective-permute-start.28 = (bf16[16,4096]{1,0:T(8,128)(2,1)S(1)}, bf16[16,4096]{1,0:T(8,128)(2,1)S(1)}, u32[]{:S(2)}, u32[]{:S(2)}) collective-permute-start(bf16[16,4096]{1,0:T(8,128)(2,1)S(1)} %collective-permute-done.21), channel_id=1, source_target_pairs={{0,12},{1,13},{2,14},{3,15},{4,8},{5,9},{6,10},{7,11},{8,4},{9,5},... | collective-permute-start | bytes 393224 | tf_op jit(solution)/shard_map/ppermute | solution.py:39
  124.1 11.3 %collective-permute-start.27 = (bf16[16,4096]{1,0:T(8,128)(2,1)S(1)}, bf16[16,4096]{1,0:T(8,128)(2,1)S(1)}, u32[]{:S(2)}, u32[]{:S(2)}) collective-permute-start(bf16[16,4096]{1,0:T(8,128)(2,1)S(1)} %collective-permute-done.21), channel_id=1, source_target_pairs={{0,8},{1,9},{2,10},{3,11},{4,12},{5,13},{6,14},{7,15},{8,0},{9,1},... | collective-permute-start | bytes 393224 | tf_op jit(solution)/shard_map/ppermute | solution.py:39
  126.0 12.8 %collective-permute-start.22 = (bf16[16,4096]{1,0:T(8,128)(2,1)S(1)}, bf16[16,4096]{1,0:T(8,128)(2,1)S(1)}, u32[]{:S(2)}, u32[]{:S(2)}) collective-permute-start(bf16[16,4096]{1,0:T(8,128)(2,1)S(1)} %collective-permute-done.21), channel_id=1, source_target_pairs={{0,4},{1,5},{2,6},{3,7},{4,0},{5,1},{6,2},{7,3},{8,12},{9,13},{10,... | collective-permute-start | bytes 393224 | tf_op jit(solution)/shard_map/ppermute | solution.py:39
  135.4 24.2 %collective-permute-start.29 = (bf16[32,4096]{1,0:T(8,128)(2,1)S(1)}, bf16[32,4096]{1,0:T(8,128)(2,1)S(1)}, u32[]{:S(2)}, u32[]{:S(2)}) collective-permute-start(bf16[32,4096]{1,0:T(8,128)(2,1)S(1)} %pad_maximum_fusion.5), channel_id=1, source_target_pairs={{0,2},{1,3},{2,0},{3,1},{4,6},{5,7},{6,4},{7,5},{8,10},{9,11},{10,... | collective-permute-start | bytes 786440 | tf_op jit(solution)/shard_map/ppermute | solution.py:39
  138.9 12.2 %collective-permute-start.23 = (bf16[32,4096]{1,0:T(8,128)(2,1)S(1)}, bf16[32,4096]{1,0:T(8,128)(2,1)S(1)}, u32[]{:S(2)}, u32[]{:S(2)}) collective-permute-start(bf16[32,4096]{1,0:T(8,128)(2,1)S(1)} %pad_maximum_fusion.4), channel_id=1, source_target_pairs={{0,2},{1,3},{2,0},{3,1},{4,6},{5,7},{6,4},{7,5},{8,10},{9,11},{10,... | collective-permute-start | bytes 786440 | tf_op jit(solution)/shard_map/ppermute | solution.py:39
  151.1 13.7 %collective-permute-start.26 = (bf16[64,4096]{1,0:T(8,128)(2,1)S(1)}, bf16[64,4096]{1,0:T(8,128)(2,1)S(1)}, u32[]{:S(2)}, u32[]{:S(2)}) collective-permute-start(bf16[64,4096]{1,0:T(8,128)(2,1)S(1)} %constant_dynamic-update-slice_fusion.11), channel_id=1, source_target_pairs={{0,1},{1,0},{2,3},{3,2},{4,5},{5,4},{6,7},{7,6},{8,9},{9,8},{10,11... | collective-permute-start | bytes 1572872 | tf_op jit(solution)/shard_map/ppermute | solution.py:39
  153.7 11.0 %collective-permute-start.34 = (bf16[32,4096]{1,0:T(8,128)(2,1)S(1)}, bf16[32,4096]{1,0:T(8,128)(2,1)S(1)}, u32[]{:S(2)}, u32[]{:S(2)}) collective-permute-start(bf16[32,4096]{1,0:T(8,128)(2,1)S(1)} %split.83), channel_id=1, source_target_pairs={{0,2},{1,3},{2,0},{3,1},{4,6},{5,7},{6,4},{7,5},{8,10},{9,11},{10,... | collective-permute-start | bytes 786440 | tf_op jit(solution)/shard_map/ppermute | solution.py:39
  157.2 24.2 %collective-permute-start.33 = (bf16[32,4096]{1,0:T(8,128)(2,1)}, bf16[32,4096]{1,0:T(8,128)(2,1)}, u32[]{:S(2)}, u32[]{:S(2)}) collective-permute-start(bf16[32,4096]{1,0:T(8,128)(2,1)} %split.81), channel_id=1, source_target_pairs={{0,2},{1,3},{2,0},{3,1},{4,6},{5,7},{6,4},{7,5},{8,10},{9,11},{10,... | collective-permute-start | bytes 786440 | tf_op jit(solution)/shard_map/ppermute | solution.py:39
  187.7 11.0 %collective-permute-start.40 = (bf16[32,4096]{1,0:T(8,128)(2,1)S(1)}, bf16[32,4096]{1,0:T(8,128)(2,1)S(1)}, u32[]{:S(2)}, u32[]{:S(2)}) collective-permute-start(bf16[32,4096]{1,0:T(8,128)(2,1)S(1)} %split.93), channel_id=1, source_target_pairs={{0,2},{1,3},{2,0},{3,1},{4,6},{5,7},{6,4},{7,5},{8,10},{9,11},{10,... | collective-permute-start | bytes 786440 | tf_op jit(solution)/shard_map/ppermute | solution.py:39
  191.2 12.9 %collective-permute-start.38 = (bf16[32,4096]{1,0:T(8,128)(2,1)S(1)}, bf16[32,4096]{1,0:T(8,128)(2,1)S(1)}, u32[]{:S(2)}, u32[]{:S(2)}) collective-permute-start(bf16[32,4096]{1,0:T(8,128)(2,1)S(1)} %split.89), channel_id=1, source_target_pairs={{0,2},{1,3},{2,0},{3,1},{4,6},{5,7},{6,4},{7,5},{8,10},{9,11},{10,... | collective-permute-start | bytes 786440 | tf_op jit(solution)/shard_map/ppermute | solution.py:39
  198.9 15.2 %collective-permute-start.41 = (bf16[16,4096]{1,0:T(8,128)(2,1)S(1)}, bf16[16,4096]{1,0:T(8,128)(2,1)S(1)}, u32[]{:S(2)}, u32[]{:S(2)}) collective-permute-start(bf16[16,4096]{1,0:T(8,128)(2,1)S(1)} %get-tuple-element.250), channel_id=1, source_target_pairs={{0,8},{1,9},{2,10},{3,11},{4,12},{5,13},{6,14},{7,15},{8,0},{9,1},... | collective-permute-start | bytes 393224 | tf_op jit(solution)/shard_map/ppermute | solution.py:39
  200.8 17.6 %collective-permute-start.42 = (bf16[16,4096]{1,0:T(8,128)(2,1)S(1)}, bf16[16,4096]{1,0:T(8,128)(2,1)S(1)}, u32[]{:S(2)}, u32[]{:S(2)}) collective-permute-start(bf16[16,4096]{1,0:T(8,128)(2,1)S(1)} %get-tuple-element.251), channel_id=1, source_target_pairs={{0,12},{1,13},{2,14},{3,15},{4,8},{5,9},{6,10},{7,11},{8,4},{9,5},... | collective-permute-start | bytes 393224 | tf_op jit(solution)/shard_map/ppermute | solution.py:39
  204.3 14.2 %collective-permute-start.39 = (bf16[16,4096]{1,0:T(8,128)(2,1)S(1)}, bf16[16,4096]{1,0:T(8,128)(2,1)S(1)}, u32[]{:S(2)}, u32[]{:S(2)}) collective-permute-start(bf16[16,4096]{1,0:T(8,128)(2,1)S(1)} %split.105), channel_id=1, source_target_pairs={{0,4},{1,5},{2,6},{3,7},{4,0},{5,1},{6,2},{7,3},{8,12},{9,13},{10,... | collective-permute-start | bytes 393224 | tf_op jit(solution)/shard_map/ppermute | solution.py:39
  208.3 11.6 %collective-permute-start.35 = (bf16[16,4096]{1,0:T(8,128)(2,1)S(1)}, bf16[16,4096]{1,0:T(8,128)(2,1)S(1)}, u32[]{:S(2)}, u32[]{:S(2)}) collective-permute-start(bf16[16,4096]{1,0:T(8,128)(2,1)S(1)} %split.85), channel_id=1, source_target_pairs={{0,4},{1,5},{2,6},{3,7},{4,0},{5,1},{6,2},{7,3},{8,12},{9,13},{10,... | collective-permute-start | bytes 393224 | tf_op jit(solution)/shard_map/ppermute | solution.py:39
  210.2 13.8 %collective-permute-start.36 = (bf16[16,4096]{1,0:T(8,128)(2,1)S(1)}, bf16[16,4096]{1,0:T(8,128)(2,1)S(1)}, u32[]{:S(2)}, u32[]{:S(2)}) collective-permute-start(bf16[16,4096]{1,0:T(8,128)(2,1)S(1)} %get-tuple-element.248), channel_id=1, source_target_pairs={{0,8},{1,9},{2,10},{3,11},{4,12},{5,13},{6,14},{7,15},{8,0},{9,1},... | collective-permute-start | bytes 393224 | tf_op jit(solution)/shard_map/ppermute | solution.py:39
  214.1 9.9 %collective-permute-start.37 = (bf16[16,4096]{1,0:T(8,128)(2,1)S(1)}, bf16[16,4096]{1,0:T(8,128)(2,1)S(1)}, u32[]{:S(2)}, u32[]{:S(2)}) collective-permute-start(bf16[16,4096]{1,0:T(8,128)(2,1)S(1)} %get-tuple-element.249), channel_id=1, source_target_pairs={{0,12},{1,13},{2,14},{3,15},{4,8},{5,9},{6,10},{7,11},{8,4},{9,5},... | collective-permute-start | bytes 393224 | tf_op jit(solution)/shard_map/ppermute | solution.py:39
  (22 other events, 191.9 us)

commit v2 on v1

--- a/solution.py
+++ b/solution.py
@@ -57,6 +57,12 @@
     near = jnp.concatenate([near, swap(near, 16, 2, role)], axis=0)
     away = jnp.concatenate([away, swap(away, 16, 2, role)], axis=0)
     return [near, swap(near, 16, 1, role), away, swap(away, 16, 1, role)], beside
+
+
+def piece_places():
+    near = (0, 4, 2, 6)
+    away = (8, 12, 10, 14)
+    return [near, [i ^ 1 for i in near], away, [i ^ 1 for i in away]]
 
 
 def plus(kept, *sent):
@@ -203,28 +209,35 @@
     return 256 if hidden_count % 256 == 0 else 128
 
 
-def ffn_kernel(place, *refs, count, experts, steps, size):
+def ffn_kernel(place, *refs, count, experts, steps):
     rows_refs, table_refs = refs[:count], refs[count : 2 * count]
     gu_ref, dn_ref = refs[2 * count : 2 * count + 2]
     out_refs = refs[2 * count + 2 : 3 * count + 2]
-    rows, hidden = refs[3 * count + 2 :]
+    active, upward, hidden = refs[3 * count + 2 :]
     step = pl.program_id(0)
     part = rows_refs[0].shape[0]
 
+    def products():
+        rows = jnp.concatenate([r[...] for r in rows_refs], axis=0)
+        return nn(rows, gu_ref[0]), nn(rows, gu_ref[1])
+
     @pl.when(step == 0)
     def _():
-        for i in range(count):
-            rows[part * i : part * (i + 1), :] = rows_refs[i][...]
-
-    for j in range(steps):
-
-        @pl.when(step == j)
-        def _():
-            active = nn(rows[...], gu_ref[0])
-            upward = nn(rows[...], gu_ref[1])
-            hidden[:, size * j : size * (j + 1)] = (
-                active * jax.nn.sigmoid(active) * upward
-            ).astype(jnp.bfloat16)
+        active[...], upward[...] = products()
+
+    @pl.when((step > 0) & (step < steps - 1))
+    def _():
+        more_active, more_upward = products()
+        active[...] += more_active
+        upward[...] += more_upward
+
+    @pl.when(step == steps - 1)
+    def _():
+        more_active, more_upward = products()
+        whole = active[...] + more_active
+        hidden[...] = (whole * jax.nn.sigmoid(whole) * (upward[...] + more_upward)).astype(
+            jnp.bfloat16
+        )
 
     @pl.when(step >= steps)
     def _():
@@ -239,26 +252,29 @@
     part = pieces[0].shape[0]
     hidden_count, width = weights_dn.shape
     spare = tables[0].shape[1] - width
-    size = hidden_block(hidden_count)
-    steps = hidden_count // size
     tile = 1024
+    steps = width // tile
     row_count = part * count
     table_at = width // spare
     return pl.pallas_call(
-        functools.partial(ffn_kernel, count=count, experts=experts, steps=steps, size=size),
+        functools.partial(ffn_kernel, count=count, experts=experts, steps=steps),
         grid_spec=pltpu.PrefetchScalarGridSpec(
             num_scalar_prefetch=1,
-            grid=(steps + width // tile,),
-            in_specs=[pl.BlockSpec((part, width), lambda j, p: (0, 0))] * count
+            grid=(2 * steps,),
+            in_specs=[pl.BlockSpec((part, tile), lambda j, p: (0, jnp.minimum(j, steps - 1)))]
+            * count
             + [pl.BlockSpec((part, spare), lambda j, p: (0, table_at))] * count
             + [
-                pl.BlockSpec((2, width, size), lambda j, p: (0, 0, jnp.minimum(j, steps - 1))),
+                pl.BlockSpec(
+                    (2, tile, hidden_count), lambda j, p: (0, jnp.minimum(j, steps - 1), 0)
+                ),
                 pl.BlockSpec((hidden_count, tile), lambda j, p: (0, jnp.maximum(j - steps, 0))),
             ],
             out_specs=[pl.BlockSpec((part, tile), lambda j, p: (0, jnp.maximum(j - steps, 0)))]
             * count,
             scratch_shapes=[
-                pltpu.VMEM((row_count, width), jnp.bfloat16),
+                pltpu.VMEM((row_count, hidden_count), jnp.float32),
+                pltpu.VMEM((row_count, hidden_count), jnp.float32),
                 pltpu.VMEM((row_count, hidden_count), jnp.bfloat16),
             ],
         ),
@@ -274,13 +290,14 @@
 
 
 def learn_kernel(place, *refs, count, experts, rates):
-    rows_refs, table_refs, cot_refs = refs[:count], refs[count : 2 * count], refs[2 * count : 3 * count]
-    gu_ref, dn_ref = refs[3 * count : 3 * count + 2]
-    dx_refs = refs[3 * count + 2 : 4 * count + 2]
-    new_gu_ref, new_dn_ref = refs[4 * count + 2 : 4 * count + 4]
-    rows, turned, pulls, pulls_turned, total, grads, grads_dn = refs[4 * count + 4 :]
+    rows_refs, table_refs = refs[:count], refs[count : 2 * count]
+    cot_ref, gu_ref, dn_ref, dx_ref, new_gu_ref, new_dn_ref = refs[2 * count : 2 * count + 6]
+    rows, turned, pulls, pulls_turned, total, grads_gu, grads_dn = refs[2 * count + 6 :]
     step = pl.program_id(0)
-    part, width = rows_refs[0].shape
+    part = rows_refs[0].shape[0]
+    width = dn_ref.shape[1]
+    sources = piece_places()
+    block = part // len(sources[0])
     tile = 1024
     cuts = [slice(lower, lower + tile) for lower in range(0, width, tile)]
 
@@ -290,7 +307,12 @@
             here = slice(part * i, part * (i + 1))
             gates = pick_gates(table_refs[i][...], place[0], experts)
             rows[here, :] = rows_refs[i][...]
-            pulls[here, :] = (gates * cot_refs[i][...].astype(jnp.float32)).astype(jnp.bfloat16)
+            for j, source in enumerate(sources[i]):
+                lower = part * i + block * j
+                cots = cot_ref[pl.ds(pl.multiple_of((place[0] ^ source) * block, block), block), :]
+                pulls[lower : lower + block, :] = (
+                    gates[block * j : block * (j + 1)] * cots.astype(jnp.float32)
+                ).astype(jnp.bfloat16)
         for cut in cuts:
             turned[cut, :] = rows[:, cut].T
             pulls_turned[cut, :] = pulls[:, cut].T
@@ -314,6 +336,7 @@
         )
 
     for half, sent in ((0, d_active), (1, d_upward)):
+        grads = grads_gu.at[half]
         squares = jnp.zeros((8, sent.shape[1]), jnp.float32)
         for cut in cuts:
             fresh = nn(turned[cut, :], sent)
@@ -340,7 +363,10 @@
         for cut in cuts:
             done = total[cut, :].T.astype(jnp.bfloat16)
             for i in range(count):
-                dx_refs[i][:, cut] = done[part * i : part * (i + 1)]
+                for j, source in enumerate(sources[i]):
+                    lower = part * i + block * j
+                    goal = pl.ds(pl.multiple_of((place[0] ^ source) * block, block), block)
+                    dx_ref[goal, cut] = done[lower : lower + block]
 
 
 def learn_call(place, pieces, tables, cots, planes, weights_dn, experts, rates):
@@ -360,13 +386,13 @@
             grid=(hidden_count // size,),
             in_specs=[piece] * count
             + [pl.BlockSpec((part, spare), lambda j, p: (0, table_at))] * count
-            + [piece] * count
             + [
+                pl.BlockSpec((row_count, width), lambda j, p: (0, 0), pipeline_mode=once),
                 pl.BlockSpec((2, width, size), lambda j, p: (0, 0, j)),
                 pl.BlockSpec((size, width), lambda j, p: (j, 0)),
             ],
-            out_specs=[pl.BlockSpec((part, width), lambda j, p: (0, 0))] * count
-            + [
+            out_specs=[
+                pl.BlockSpec((row_count, width), lambda j, p: (0, 0), pipeline_mode=once),
                 pl.BlockSpec((2, width, size), lambda j, p: (0, 0, j)),
                 pl.BlockSpec((size, width), lambda j, p: (j, 0)),
             ],
@@ -376,12 +402,12 @@
                 pltpu.VMEM((row_count, width), jnp.bfloat16),
                 pltpu.VMEM((width, row_count), jnp.bfloat16),
                 pltpu.VMEM((width, row_count), jnp.float32),
-                pltpu.VMEM((width, size), jnp.float32),
+                pltpu.VMEM((2, width, size), jnp.float32),
                 pltpu.VMEM((size, width), jnp.float32),
             ],
         ),
-        out_shape=[jax.ShapeDtypeStruct((part, width), jnp.bfloat16)] * count
-        + [
+        out_shape=[
+            jax.ShapeDtypeStruct((row_count, width), jnp.bfloat16),
             jax.ShapeDtypeStruct(planes.shape, jnp.bfloat16),
             jax.ShapeDtypeStruct(weights_dn.shape, jnp.bfloat16),
         ],
@@ -392,7 +418,7 @@
             transcendentals=row_count * hidden_count,
         ),
         name="learn",
-    )(place, *pieces, *tables, *cots, planes, weights_dn)
+    )(place, *pieces, *tables, cots, planes, weights_dn)
 
 
 def unset(like):
@@ -418,7 +444,7 @@
     width = weights_dn.shape[1]
     rows = pieces[0][:, :width]
     gates = pick_gates(tables[0][:, width:], place[0], experts)
-    pulls = (gates * cots[0].astype(jnp.float32)).astype(jnp.bfloat16)
+    pulls = (gates * cots.astype(jnp.float32)).astype(jnp.bfloat16)
     active = nn(rows, planes[0])
     upward = nn(rows, planes[1])
     back = nt(pulls, weights_dn)
@@ -474,30 +500,32 @@
     )
     every, planes = gather(block, device_count, (0, 1), planes)
     count = len(every)
-    cotangent, every[0] = tied(cotangent, every[0])
-    cots, _ = gather(cotangent, device_count, (0,))
+    if small:
+        cots = lax.all_gather(cotangent, AXES, tiled=True)
+    else:
+        cots = gather(cotangent, device_count, (0,))[0][0]
 
     def learn(every, cots, planes, own_dn):
         out = list(run_learn(first_place, every, every, cots, planes, own_dn, ep_count, rates))
-        return ([unset(o) for o in out[:count]], out[:count], out[count], out[count + 1])
+        blank = jax.ShapeDtypeStruct((total_rows // count, model_width), jnp.bfloat16)
+        return ([unset(blank)] * count, out[0], out[1], out[2])
 
     def decode(every, cots, planes, own_dn):
         out = list(run_ffn(first_place, every, every, planes, own_dn, ep_count))
-        return (out, [unset(o) for o in out], unset(planes), unset(own_dn))
+        return (out, unset(cots), unset(planes), unset(own_dn))
 
     part, dx_part, new_planes, new_dn = lax.cond(
         is_learner, learn, decode, every, cots, planes, own_dn
     )
     stale_sum = scatter_sum(part, device_count, (1,))
     current = (base + stale_sum).astype(jnp.bfloat16)
-    hopped = across(current, 1, 0)
     if small:
-        dx_near, dx_away = sum_core(dx_part, (0,))
-    arrived, _ = gather(hopped, device_count, (0,))
-    if small:
-        arrived[0], dx_near, dx_away = tied(arrived[0], dx_near, dx_away)
-        dx_near, dx_away = sum_y(dx_near, dx_away, (0,))
-
+        current, dx_part = tied(current, dx_part)
+        dx_sum = lax.psum_scatter(dx_part, AXES, scatter_dimension=0, tiled=True)
+        dx_sum = dx_sum.astype(jnp.float32)
+    else:
+        dx_sum = scatter_sum([dx_part], device_count, (0,))
+    arrived, _ = gather(across(current, 1, 0), device_count, (0,))
     fresh_part = lax.cond(
         is_learner,
         lambda r, e, g, d: list(run_ffn(fresh_place, r, e, g, d, ep_count)),
@@ -507,15 +535,7 @@
         new_planes,
         new_dn,
     )
-    if small:
-        near, away = sum_core(fresh_part, (0,))
-        near, away, dx_near, dx_away = tied(near, away, dx_near, dx_away)
-        dx_sum = sum_z(dx_near, dx_away, (0,))
-        near, away = sum_y(near, away, (0,))
-        fresh_sum = sum_z(near, away, (0,))
-    else:
-        dx_sum = scatter_sum(dx_part, device_count, (0,))
-        fresh_sum = scatter_sum(fresh_part, device_count, (0,))
+    fresh_sum = scatter_sum(fresh_part, device_count, (0,))
     moved = across(fresh_sum.astype(jnp.bfloat16), 0, 1).astype(jnp.float32)
     final_rows = jnp.where(is_learner, base + dx_sum, current.astype(jnp.float32) + moved)
     return final_rows.astype(jnp.bfloat16)[None]

time: 227 us -> 236 us (1.040)
  starting transfers between devices: 95.7 us -> 55.3 us
  waiting for transfers between devices: 54.5 us -> 90.4 us
  between operations: 0.88 us -> 14 us
  local copies, waits for them, and re-layouts: 15.2 us -> 18.1 us
  other arithmetic: 7.88 us -> 5.3 us
    ppermute x42 -> x28, starting transfers between devices: 92.9 us -> 52.7 us  [swap(): return lax.ppermute(block, ('grp',) + AXES, pairs)]
    reduce_scatter x0 -> x1, waiting for transfers between devices: none -> 24.8 us  [per_device(): dx_sum = lax.psum_scatter(dx_part, AXES, scatter_dimension=0, tiled=True)]
    all_gather x0 -> x1, waiting for transfers between devices: none -> 14.1 us  [per_device(): cots = lax.all_gather(cotangent, AXES, tiled=True)]
    ppermute x42 -> x28, waiting for transfers between devices: 48.5 us -> 42.8 us  [swap(): return lax.ppermute(block, ('grp',) + AXES, pairs)]
    cond x0 -> x3, local copies, waits for them, and re-layouts: none -> 3.98 us
    ppermute x2, waiting for transfers between devices: 6 us -> 8.74 us  [across(): return lax.ppermute(block, 'grp', [(source, target)])]
    unnamed x32 -> x26, local copies, waits for them, and re-layouts: 14.2 us -> 13.9 us
  transfers between devices with their start and end apart: 44 -> 32, of which waited for: 11 -> 14; matrix products, arithmetic and copies ran while one was open for 8% -> 6% of each run, Pallas kernels for 6% -> 0%
where the time goes in v2:
time: 236 us; the launch traced here: 235 us
  waiting for transfers between devices  90.4 us (38%)
  starting transfers between devices  55.3 us (23%)
  Pallas kernels  51.7 us (22%)
  local copies, waits for them, and re-layouts  18.1 us (8%)
  between operations  14 us (6%)
  other arithmetic  5.3 us (2%)
    ppermute x28, starting transfers between devices, swap(): return lax.ppermute(block, ('grp',) + AXES, pairs)  52.7 us
    ppermute x28, waiting for transfers between devices, swap(): return lax.ppermute(block, ('grp',) + AXES, pairs)  42.8 us
    pallas_call x1, Pallas kernels, learn_call(): pl.pallas_call(functools.partial(learn_kernel, count=count, experts=exper...  36.7 us
    reduce_scatter x1, waiting for transfers between devices, per_device(): dx_sum = lax.psum_scatter(dx_part, AXES, scatter_dimension=0, tiled=True)  24.8 us
    all_gather x1, waiting for transfers between devices, per_device(): cots = lax.all_gather(cotangent, AXES, tiled=True)  14.1 us
    unnamed x26, local copies, waits for them, and re-layouts  13.9 us
    pallas_call x1, Pallas kernels, ffn_call(): pl.pallas_call(functools.partial(ffn_kernel, count=count, experts=experts...  13 us
    ppermute x2, waiting for transfers between devices, across(): return lax.ppermute(block, 'grp', [(source, target)])  8.74 us
  transfers between devices with their start and end apart: 32, of which 14 were waited for; matrix products, arithmetic and copies ran while one was open for 6% of the time, Pallas kernels for 0%

profile of v2, /device:TPU:0, one launch (start us, length us, event | category | flops | bytes accessed | tf_op | source)
XLA Modules:
  0.0 234.7 jit_solution(12729886089481573530)
XLA Ops:
  7.1 1.9 prep.1
  9.1 5.0 %collective-permute-start.4 = (bf16[16,4224]{1,0:T(8,128)(2,1)}, bf16[16,4224]{1,0:T(8,128)(2,1)S(1)}, u32[]{:S(2)}, u32[]{:S(2)}) collective-permute-start(bf16[16,4224]{1,0:T(8,128)(2,1)} %get-tuple-element.150), channel_id=1, source_target_pairs={{0,12},{1,13},{2,14},{3,15},{4,8},{5,9},{6,10},{7,11},{8,4},{9,5},... | collective-permute-start | bytes 405512 | tf_op jit(solution)/shard_map/ppermute | solution.py:39
  14.9 11.8 %copy.12 = bf16[1,1,4096,2,768]{4,2,3,1,0:T(8,128)(2,1)} copy(bf16[1,1,4096,2,768]{4,3,2,1,0:T(2,128)(2,1)} %param.20) | data formatting | bytes 25165824 | tf_op args[7]
  29.0 7.2 %collective-permute-done.5 = bf16[32,4224]{1,0:T(8,128)(2,1)S(1)} collective-permute-done((bf16[32,4224]{1,0:T(8,128)(2,1)S(1)}, bf16[32,4224]{1,0:T(8,128)(2,1)S(1)}, u32[]{:S(2)}, u32[]{:S(2)}) %collective-permute-start.5) | collective-permute-done | bytes 270368 | tf_op jit(solution)/shard_map/ppermute | solution.py:39
  36.4 3.9 %collective-permute-done.1 = bf16[32,4224]{1,0:T(8,128)(2,1)S(1)} collective-permute-done((bf16[32,4224]{1,0:T(8,128)(2,1)S(1)}, bf16[32,4224]{1,0:T(8,128)(2,1)S(1)}, u32[]{:S(2)}, u32[]{:S(2)}) %collective-permute-start.1) | collective-permute-done | bytes 270368 | tf_op jit(solution)/shard_map/ppermute | solution.py:39
  42.3 14.1 %all-gather.2.cloned.1.call-done = bf16[256,4096]{1,0:T(8,128)(2,1)} async-done(((bf16[16,4096]{1,0:T(8,128)(2,1)}), bf16[256,4096]{1,0:T(8,128)(2,1)}) %all-gather.2.cloned.1.call-update) | async-done | bytes 2097168 | tf_op jit(solution)/shard_map/all_gather | solution.py:504
  56.4 40.7 %conditional.4 = (bf16[64,4096]{1,0:T(8,128)(2,1)}, bf16[64,4096]{1,0:T(8,128)(2,1)S(1)}, bf16[64,4096]{1,0:T(8,128)(2,1)S(1)}, bf16[64,4096]{1,0:T(8,128)(2,1)}...) conditional(s32[]{:T(128)} %convert_element_type.132, (s32[1]{0:T(128)}, ...), branch_computations={%region_0.0_spmd, %region_1.0_spmd} | conditional | flops 12884901888 | bytes 40894520 | solution.py:517
  60.4 36.7 %learn.1 = (bf16[256,4096]{1,0:T(8,128)(2,1)}, bf16[2,4096,768]{2,1,0:T(8,128)(2,1)}, bf16[768,4096]{1,0:T(8,128)(2,1)}) custom-call(s32[1]{0:T(128)} %get-tuple-element.106.place, bf16[64,4224]{1,0:T(8,128)(2,1)S(1)} %get-tuple-element.107.refs_0_.refs_4_, bf16[64,4224]{1,0:T(8,128)(2,1)S(1)} %get-tuple-element.108.refs_1_.refs_5_, ...), custom_call_target="tpu_custom_call" | custom-call | flops 12884901888 | bytes 37748736 | tf_op jit(solution)/shard_map/cond/branch_1_fun/learn/pallas_call | solution.py:382
  106.9 6.2 %collective-permute-done.14 = bf16[16,4096]{1,0:T(8,128)(2,1)S(1)} collective-permute-done((bf16[16,4096]{1,0:T(8,128)(2,1)S(1)}, bf16[16,4096]{1,0:T(8,128)(2,1)S(1)}, u32[]{:S(2)}, u32[]{:S(2)}) %collective-permute-start.14) | collective-permute-done | bytes 131104 | tf_op jit(solution)/shard_map/ppermute | solution.py:15
  113.1 4.0 %collective-permute-start.19 = (bf16[16,4096]{1,0:T(8,128)(2,1)S(1)}, bf16[16,4096]{1,0:T(8,128)(2,1)S(1)}, u32[]{:S(2)}, u32[]{:S(2)}) collective-permute-start(bf16[16,4096]{1,0:T(8,128)(2,1)S(1)} %collective-permute-done.14), channel_id=1, source_target_pairs={{0,12},{1,13},{2,14},{3,15},{4,8},{5,9},{6,10},{7,11},{8,4},{9,5},... | collective-permute-start | bytes 393224 | tf_op jit(solution)/shard_map/ppermute | solution.py:39
  117.1 3.2 %collective-permute-start.18 = (bf16[16,4096]{1,0:T(8,128)(2,1)S(1)}, bf16[16,4096]{1,0:T(8,128)(2,1)S(1)}, u32[]{:S(2)}, u32[]{:S(2)}) collective-permute-start(bf16[16,4096]{1,0:T(8,128)(2,1)S(1)} %collective-permute-done.14), channel_id=1, source_target_pairs={{0,8},{1,9},{2,10},{3,11},{4,12},{5,13},{6,14},{7,15},{8,0},{9,1},... | collective-permute-start | bytes 393224 | tf_op jit(solution)/shard_map/ppermute | solution.py:39
  120.4 2.9 %collective-permute-start.15 = (bf16[16,4096]{1,0:T(8,128)(2,1)S(1)}, bf16[16,4096]{1,0:T(8,128)(2,1)S(1)}, u32[]{:S(2)}, u32[]{:S(2)}) collective-permute-start(bf16[16,4096]{1,0:T(8,128)(2,1)S(1)} %collective-permute-done.14), channel_id=1, source_target_pairs={{0,4},{1,5},{2,6},{3,7},{4,0},{5,1},{6,2},{7,3},{8,12},{9,13},{10,... | collective-permute-start | bytes 393224 | tf_op jit(solution)/shard_map/ppermute | solution.py:39
  123.3 6.5 %collective-permute-done.18 = bf16[16,4096]{1,0:T(8,128)(2,1)S(1)} collective-permute-done((bf16[16,4096]{1,0:T(8,128)(2,1)S(1)}, bf16[16,4096]{1,0:T(8,128)(2,1)S(1)}, u32[]{:S(2)}, u32[]{:S(2)}) %collective-permute-start.18) | collective-permute-done | bytes 131104 | tf_op jit(solution)/shard_map/ppermute | solution.py:39
  129.8 2.5 %collective-permute-start.20 = (bf16[32,4096]{1,0:T(8,128)(2,1)S(1)}, bf16[32,4096]{1,0:T(8,128)(2,1)S(1)}, u32[]{:S(2)}, u32[]{:S(2)}) collective-permute-start(bf16[32,4096]{1,0:T(8,128)(2,1)S(1)} %pad_maximum_fusion.3), channel_id=1, source_target_pairs={{0,2},{1,3},{2,0},{3,1},{4,6},{5,7},{6,4},{7,5},{8,10},{9,11},{10,... | collective-permute-start | bytes 786440 | tf_op jit(solution)/shard_map/ppermute | solution.py:39
  132.3 3.4 %collective-permute-start.16 = (bf16[32,4096]{1,0:T(8,128)(2,1)S(1)}, bf16[32,4096]{1,0:T(8,128)(2,1)S(1)}, u32[]{:S(2)}, u32[]{:S(2)}) collective-permute-start(bf16[32,4096]{1,0:T(8,128)(2,1)S(1)} %pad_maximum_fusion.2), channel_id=1, source_target_pairs={{0,2},{1,3},{2,0},{3,1},{4,6},{5,7},{6,4},{7,5},{8,10},{9,11},{10,... | collective-permute-start | bytes 786440 | tf_op jit(solution)/shard_map/ppermute | solution.py:39
  135.8 9.2 %collective-permute-done.16 = bf16[32,4096]{1,0:T(8,128)(2,1)S(1)} collective-permute-done((bf16[32,4096]{1,0:T(8,128)(2,1)S(1)}, bf16[32,4096]{1,0:T(8,128)(2,1)S(1)}, u32[]{:S(2)}, u32[]{:S(2)}) %collective-permute-start.16) | collective-permute-done | bytes 262176 | tf_op jit(solution)/shard_map/ppermute | solution.py:39
  145.0 1.9 collective-permute-start.17
  147.0 2.4 %collective-permute-start.21 = (bf16[64,4096]{1,0:T(8,128)(2,1)S(1)}, bf16[64,4096]{1,0:T(8,128)(2,1)}, u32[]{:S(2)}, u32[]{:S(2)}) collective-permute-start(bf16[64,4096]{1,0:T(8,128)(2,1)S(1)} %constant_dynamic-update-slice_fusion.8), channel_id=1, source_target_pairs={{0,1},{1,0},{2,3},{3,2},{4,5},{5,4},{6,7},{7,6},{8,9},{9,8},{10,11... | collective-permute-start | bytes 1572872 | tf_op jit(solution)/shard_map/ppermute | solution.py:39
  151.1 14.2 %conditional.6 = (bf16[64,4096]{1,0:T(8,128)(2,1)}, bf16[64,4096]{1,0:T(8,128)(2,1)}, bf16[64,4096]{1,0:T(8,128)(2,1)S(1)}, bf16[64,4096]{1,0:T(8,128)(2,1)S(1)}) conditional(s32[]{:T(128)} %convert_element_type.132, () %tuple.44, (s32[1]{0:T(128)}, bf16[64,4096]{1,0:T(8,128)(2,1)S(1)}, bf16[64,4096]{1,0:T(8,128)(2,1)S(1)}, ...), branch_computations={%region_3.0_spmd, %region_4.0_spmd} | conditional | flops 4831838208 | bytes 25165952
  152.2 13.0 %ffn.4 = (bf16[64,4096]{1,0:T(8,128)(2,1)S(1)}, bf16[64,4096]{1,0:T(8,128)(2,1)}, bf16[64,4096]{1,0:T(8,128)(2,1)S(1)}, bf16[64,4096]{1,0:T(8,128)(2,1)}) custom-call(s32[1]{0:T(128)S(6)} %add.41.place, bf16[64,4096]{1,0:T(8,128)(2,1)} %copy-done.1, bf16[64,4096]{1,0:T(8,128)(2,1)} %copy-done.3, bf16[64,4096]{1,0:T(8,128)(2,1)} %copy-done.2, ...), custom_call_target="tpu_custom_call" | custom-call | flops 4831838208 | bytes 18874368 | tf_op jit(solution)/shard_map/cond/branch_1_fun/ffn/pallas_call | solution.py:259
  165.3 2.4 %collective-permute-start.25 = (bf16[64,4096]{1,0:T(8,128)(2,1)}, bf16[64,4096]{1,0:T(8,128)(2,1)S(1)}, u32[]{:S(2)}, u32[]{:S(2)}) collective-permute-start(bf16[64,4096]{1,0:T(8,128)(2,1)} %get-tuple-element.165), channel_id=1, source_target_pairs={{0,1},{1,0},{2,3},{3,2},{4,5},{5,4},{6,7},{7,6},{8,9},{9,8},{10,11... | collective-permute-start | bytes 1572872 | tf_op jit(solution)/shard_map/ppermute | solution.py:39
  167.7 2.0 collective-permute-start.22
  169.9 2.5 %collective-permute-start.26 = (bf16[32,4096]{1,0:T(8,128)(2,1)S(1)}, bf16[32,4096]{1,0:T(8,128)(2,1)S(1)}, u32[]{:S(2)}, u32[]{:S(2)}) collective-permute-start(bf16[32,4096]{1,0:T(8,128)(2,1)S(1)} %split.77), channel_id=1, source_target_pairs={{0,2},{1,3},{2,0},{3,1},{4,6},{5,7},{6,4},{7,5},{8,10},{9,11},{10,... | collective-permute-start | bytes 786440 | tf_op jit(solution)/shard_map/ppermute | solution.py:39
  172.6 3.4 %collective-permute-start.23 = (bf16[32,4096]{1,0:T(8,128)(2,1)S(1)}, bf16[32,4096]{1,0:T(8,128)(2,1)S(1)}, u32[]{:S(2)}, u32[]{:S(2)}) collective-permute-start(bf16[32,4096]{1,0:T(8,128)(2,1)S(1)} %split.73), channel_id=1, source_target_pairs={{0,2},{1,3},{2,0},{3,1},{4,6},{5,7},{6,4},{7,5},{8,10},{9,11},{10,... | collective-permute-start | bytes 786440 | tf_op jit(solution)/shard_map/ppermute | solution.py:39
  176.0 5.0 %collective-permute-done.26 = bf16[32,4096]{1,0:T(8,128)(2,1)S(1)} collective-permute-done((bf16[32,4096]{1,0:T(8,128)(2,1)S(1)}, bf16[32,4096]{1,0:T(8,128)(2,1)S(1)}, u32[]{:S(2)}, u32[]{:S(2)}) %collective-permute-start.26) | collective-permute-done | bytes 262176 | tf_op jit(solution)/shard_map/ppermute | solution.py:39
  181.1 1.9 collective-permute-start.27
  183.0 3.0 %collective-permute-start.28 = (bf16[16,4096]{1,0:T(8,128)(2,1)S(1)}, bf16[16,4096]{1,0:T(8,128)(2,1)S(1)}, u32[]{:S(2)}, u32[]{:S(2)}) collective-permute-start(bf16[16,4096]{1,0:T(8,128)(2,1)S(1)} %get-tuple-element.175), channel_id=1, source_target_pairs={{0,12},{1,13},{2,14},{3,15},{4,8},{5,9},{6,10},{7,11},{8,4},{9,5},... | collective-permute-start | bytes 393224 | tf_op jit(solution)/shard_map/ppermute | solution.py:39
  186.1 4.3 %collective-permute-start.24 = (bf16[16,4096]{1,0:T(8,128)(2,1)S(1)}, bf16[16,4096]{1,0:T(8,128)(2,1)S(1)}, u32[]{:S(2)}, u32[]{:S(2)}) collective-permute-start(bf16[16,4096]{1,0:T(8,128)(2,1)S(1)} %split.75), channel_id=1, source_target_pairs={{0,4},{1,5},{2,6},{3,7},{4,0},{5,1},{6,2},{7,3},{8,12},{9,13},{10,... | collective-permute-start | bytes 393224 | tf_op jit(solution)/shard_map/ppermute | solution.py:39
  190.4 2.7 %collective-permute-done.27 = bf16[16,4096]{1,0:T(8,128)(2,1)S(1)} collective-permute-done((bf16[16,4096]{1,0:T(8,128)(2,1)S(1)}, bf16[16,4096]{1,0:T(8,128)(2,1)S(1)}, u32[]{:S(2)}, u32[]{:S(2)}) %collective-permute-start.27) | collective-permute-done | bytes 131104 | tf_op jit(solution)/shard_map/ppermute | solution.py:39
  193.1 4.5 %collective-permute-done.24 = bf16[16,4096]{1,0:T(8,128)(2,1)S(1)} collective-permute-done((bf16[16,4096]{1,0:T(8,128)(2,1)S(1)}, bf16[16,4096]{1,0:T(8,128)(2,1)S(1)}, u32[]{:S(2)}, u32[]{:S(2)}) %collective-permute-start.24) | collective-permute-done | bytes 131104 | tf_op jit(solution)/shard_map/ppermute | solution.py:39
  199.0 2.5 %collective-permute-done.29 = bf16[16,4096]{1,0:T(8,128)(2,1)S(1)} collective-permute-done((bf16[16,4096]{1,0:T(8,128)(2,1)S(1)}, bf16[16,4096]{1,0:T(8,128)(2,1)S(1)}, u32[]{:S(2)}, u32[]{:S(2)}) %collective-permute-start.29) | collective-permute-done | bytes 131104 | tf_op jit(solution)/shard_map/ppermute | solution.py:15
  201.5 24.8 %reduce-scatter.2.cloned.1.call-done = bf16[16,4096]{1,0:T(8,128)(2,1)} async-done(((bf16[256,4096]{1,0:T(8,128)(2,1)}), bf16[16,4096]{1,0:T(8,128)(2,1)}) %reduce-scatter.2.cloned.1.call-update) | async-done | bytes 131088 | tf_op jit(solution)/shard_map/reduce_scatter | solution.py:524
  (97 shorter events, 25.7 us)
Async XLA Ops:
  6.5 49.9 %all-gather.2.cloned.1.call-start = ((), (), s32[]{:S(2)}) async-start(), calls=%async_computation.1 | async-start | bytes 2228224 | tf_op jit(solution)/shard_map/all_gather | solution.py:504
  9.1 17.7 %collective-permute-start.4 = (bf16[16,4224]{1,0:T(8,128)(2,1)}, bf16[16,4224]{1,0:T(8,128)(2,1)S(1)}, u32[]{:S(2)}, u32[]{:S(2)}) collective-permute-start(bf16[16,4224]{1,0:T(8,128)(2,1)} %get-tuple-element.150), channel_id=1, source_target_pairs={{0,12},{1,13},{2,14},{3,15},{4,8},{5,9},{6,10},{7,11},{8,4},{9,5},... | collective-permute-start | bytes 405512 | tf_op jit(solution)/shard_map/ppermute | solution.py:39
  14.1 12.6 %collective-permute-start.3 = (bf16[16,4224]{1,0:T(8,128)(2,1)}, bf16[16,4224]{1,0:T(8,128)(2,1)S(1)}, u32[]{:S(2)}, u32[]{:S(2)}) collective-permute-start(bf16[16,4224]{1,0:T(8,128)(2,1)} %get-tuple-element.150), channel_id=1, source_target_pairs={{0,8},{1,9},{2,10},{3,11},{4,12},{5,13},{6,14},{7,15},{8,0},{9,1},... | collective-permute-start | bytes 405512 | tf_op jit(solution)/shard_map/ppermute | solution.py:39
  14.2 212.1 %reduce-scatter.2.cloned.1.call-start = ((), (), s32[]{:S(2)}) async-start(), calls=%async_computation.2 | async-start | bytes 2228224 | tf_op jit(solution)/shard_map/reduce_scatter | solution.py:524
  14.2 14.3 %collective-permute-start = (bf16[16,4224]{1,0:T(8,128)(2,1)}, bf16[16,4224]{1,0:T(8,128)(2,1)S(1)}, u32[]{:S(2)}, u32[]{:S(2)}) collective-permute-start(bf16[16,4224]{1,0:T(8,128)(2,1)} %get-tuple-element.150), channel_id=1, source_target_pairs={{0,4},{1,5},{2,6},{3,7},{4,0},{5,1},{6,2},{7,3},{8,12},{9,13},{10,... | collective-permute-start | bytes 405512 | tf_op jit(solution)/shard_map/ppermute | solution.py:39
  26.8 9.5 %collective-permute-start.5 = (bf16[32,4224]{1,0:T(8,128)(2,1)S(1)}, bf16[32,4224]{1,0:T(8,128)(2,1)S(1)}, u32[]{:S(2)}, u32[]{:S(2)}) collective-permute-start(bf16[32,4224]{1,0:T(8,128)(2,1)S(1)} %pad_maximum_fusion.1), channel_id=1, source_target_pairs={{0,2},{1,3},{2,0},{3,1},{4,6},{5,7},{6,4},{7,5},{8,10},{9,11},{10,... | collective-permute-start | bytes 811016 | tf_op jit(solution)/shard_map/ppermute | solution.py:39
  28.5 11.7 %collective-permute-start.1 = (bf16[32,4224]{1,0:T(8,128)(2,1)S(1)}, bf16[32,4224]{1,0:T(8,128)(2,1)S(1)}, u32[]{:S(2)}, u32[]{:S(2)}) collective-permute-start(bf16[32,4224]{1,0:T(8,128)(2,1)S(1)} %pad_maximum_fusion), channel_id=1, source_target_pairs={{0,2},{1,3},{2,0},{3,1},{4,6},{5,7},{6,4},{7,5},{8,10},{9,11},{10,... | collective-permute-start | bytes 811016 | tf_op jit(solution)/shard_map/ppermute | solution.py:39
  36.3 4.1 %collective-permute-start.6 = (bf16[64,4224]{1,0:T(8,128)(2,1)S(1)}, bf16[64,4224]{1,0:T(8,128)(2,1)S(1)}, u32[]{:S(2)}, u32[]{:S(2)}) collective-permute-start(bf16[64,4224]{1,0:T(8,128)(2,1)S(1)} %constant_dynamic-update-slice_fusion.2), channel_id=1, source_target_pairs={{0,1},{1,0},{2,3},{3,2},{4,5},{5,4},{6,7},{7,6},{8,9},{9,8},{10,11... | collective-permute-start | bytes 1622024 | tf_op jit(solution)/shard_map/ppermute | solution.py:39
  40.3 2.0 collective-permute-start.2
  97.9 1.5 collective-permute-start.7
  98.7 2.6 %collective-permute-start.10 = (bf16[64,4096]{1,0:T(8,128)(2,1)}, bf16[64,4096]{1,0:T(8,128)(2,1)S(1)}, u32[]{:S(2)}, u32[]{:S(2)}) collective-permute-start(bf16[64,4096]{1,0:T(8,128)(2,1)} %get-tuple-element.156), channel_id=1, source_target_pairs={{16,17},{17,16},{18,19},{19,18},{20,21},{21,20},{22,23},{23,22},{2... | collective-permute-start | bytes 1572872 | tf_op jit(solution)/shard_map/ppermute | solution.py:39
  100.6 2.6 %collective-permute-start.8 = (bf16[32,4096]{1,0:T(8,128)(2,1)S(1)}, bf16[32,4096]{1,0:T(8,128)(2,1)S(1)}, u32[]{:S(2)}, u32[]{:S(2)}) collective-permute-start(bf16[32,4096]{1,0:T(8,128)(2,1)S(1)} %split.65), channel_id=1, source_target_pairs={{16,18},{17,19},{18,16},{19,17},{20,22},{21,23},{22,20},{23,21},{2... | collective-permute-start | bytes 786440 | tf_op jit(solution)/shard_map/ppermute | solution.py:39
  102.5 1.5 collective-permute-start.11
  103.3 2.1 collective-permute-start.9
  104.1 1.4 collective-permute-start.12
  104.8 0.7 collective-permute-start.13
  105.6 7.5 %collective-permute-start.14 = (bf16[16,4096]{1,0:T(8,128)(2,1)S(1)}, bf16[16,4096]{1,0:T(8,128)(2,1)S(1)}, u32[]{:S(2)}, u32[]{:S(2)}) collective-permute-start(bf16[16,4096]{1,0:T(8,128)(2,1)S(1)} %add_convert_fusion.7), channel_id=1, source_target_pairs={{16,0},{17,1},{18,2},{19,3},{20,4},{21,5},{22,6},{23,7},{24,8},{25... | collective-permute-start | bytes 393224 | tf_op jit(solution)/shard_map/ppermute | solution.py:15
  113.1 10.2 %collective-permute-start.19 = (bf16[16,4096]{1,0:T(8,128)(2,1)S(1)}, bf16[16,4096]{1,0:T(8,128)(2,1)S(1)}, u32[]{:S(2)}, u32[]{:S(2)}) collective-permute-start(bf16[16,4096]{1,0:T(8,128)(2,1)S(1)} %collective-permute-done.14), channel_id=1, source_target_pairs={{0,12},{1,13},{2,14},{3,15},{4,8},{5,9},{6,10},{7,11},{8,4},{9,5},... | collective-permute-start | bytes 393224 | tf_op jit(solution)/shard_map/ppermute | solution.py:39
  117.1 12.6 %collective-permute-start.18 = (bf16[16,4096]{1,0:T(8,128)(2,1)S(1)}, bf16[16,4096]{1,0:T(8,128)(2,1)S(1)}, u32[]{:S(2)}, u32[]{:S(2)}) collective-permute-start(bf16[16,4096]{1,0:T(8,128)(2,1)S(1)} %collective-permute-done.14), channel_id=1, source_target_pairs={{0,8},{1,9},{2,10},{3,11},{4,12},{5,13},{6,14},{7,15},{8,0},{9,1},... | collective-permute-start | bytes 393224 | tf_op jit(solution)/shard_map/ppermute | solution.py:39
  120.4 11.9 %collective-permute-start.15 = (bf16[16,4096]{1,0:T(8,128)(2,1)S(1)}, bf16[16,4096]{1,0:T(8,128)(2,1)S(1)}, u32[]{:S(2)}, u32[]{:S(2)}) collective-permute-start(bf16[16,4096]{1,0:T(8,128)(2,1)S(1)} %collective-permute-done.14), channel_id=1, source_target_pairs={{0,4},{1,5},{2,6},{3,7},{4,0},{5,1},{6,2},{7,3},{8,12},{9,13},{10,... | collective-permute-start | bytes 393224 | tf_op jit(solution)/shard_map/ppermute | solution.py:39
  129.8 17.2 %collective-permute-start.20 = (bf16[32,4096]{1,0:T(8,128)(2,1)S(1)}, bf16[32,4096]{1,0:T(8,128)(2,1)S(1)}, u32[]{:S(2)}, u32[]{:S(2)}) collective-permute-start(bf16[32,4096]{1,0:T(8,128)(2,1)S(1)} %pad_maximum_fusion.3), channel_id=1, source_target_pairs={{0,2},{1,3},{2,0},{3,1},{4,6},{5,7},{6,4},{7,5},{8,10},{9,11},{10,... | collective-permute-start | bytes 786440 | tf_op jit(solution)/shard_map/ppermute | solution.py:39
  132.3 12.7 %collective-permute-start.16 = (bf16[32,4096]{1,0:T(8,128)(2,1)S(1)}, bf16[32,4096]{1,0:T(8,128)(2,1)S(1)}, u32[]{:S(2)}, u32[]{:S(2)}) collective-permute-start(bf16[32,4096]{1,0:T(8,128)(2,1)S(1)} %pad_maximum_fusion.2), channel_id=1, source_target_pairs={{0,2},{1,3},{2,0},{3,1},{4,6},{5,7},{6,4},{7,5},{8,10},{9,11},{10,... | collective-permute-start | bytes 786440 | tf_op jit(solution)/shard_map/ppermute | solution.py:39
  145.0 4.4 %collective-permute-start.17 = (bf16[64,4096]{1,0:T(8,128)(2,1)S(1)}, bf16[64,4096]{1,0:T(8,128)(2,1)S(1)}, u32[]{:S(2)}, u32[]{:S(2)}) collective-permute-start(bf16[64,4096]{1,0:T(8,128)(2,1)S(1)} %constant_dynamic-update-slice_fusion.5), channel_id=1, source_target_pairs={{0,1},{1,0},{2,3},{3,2},{4,5},{5,4},{6,7},{7,6},{8,9},{9,8},{10,11... | collective-permute-start | bytes 1572872 | tf_op jit(solution)/shard_map/ppermute | solution.py:39
  147.0 4.1 %collective-permute-start.21 = (bf16[64,4096]{1,0:T(8,128)(2,1)S(1)}, bf16[64,4096]{1,0:T(8,128)(2,1)}, u32[]{:S(2)}, u32[]{:S(2)}) collective-permute-start(bf16[64,4096]{1,0:T(8,128)(2,1)S(1)} %constant_dynamic-update-slice_fusion.8), channel_id=1, source_target_pairs={{0,1},{1,0},{2,3},{3,2},{4,5},{5,4},{6,7},{7,6},{8,9},{9,8},{10,11... | collective-permute-start | bytes 1572872 | tf_op jit(solution)/shard_map/ppermute | solution.py:39
  165.3 4.5 %collective-permute-start.25 = (bf16[64,4096]{1,0:T(8,128)(2,1)}, bf16[64,4096]{1,0:T(8,128)(2,1)S(1)}, u32[]{:S(2)}, u32[]{:S(2)}) collective-permute-start(bf16[64,4096]{1,0:T(8,128)(2,1)} %get-tuple-element.165), channel_id=1, source_target_pairs={{0,1},{1,0},{2,3},{3,2},{4,5},{5,4},{6,7},{7,6},{8,9},{9,8},{10,11... | collective-permute-start | bytes 1572872 | tf_op jit(solution)/shard_map/ppermute | solution.py:39
  167.7 4.7 %collective-permute-start.22 = (bf16[64,4096]{1,0:T(8,128)(2,1)}, bf16[64,4096]{1,0:T(8,128)(2,1)S(1)}, u32[]{:S(2)}, u32[]{:S(2)}) collective-permute-start(bf16[64,4096]{1,0:T(8,128)(2,1)} %get-tuple-element.163), channel_id=1, source_target_pairs={{0,1},{1,0},{2,3},{3,2},{4,5},{5,4},{6,7},{7,6},{8,9},{9,8},{10,11... | collective-permute-start | bytes 1572872 | tf_op jit(solution)/shard_map/ppermute | solution.py:39
  169.9 11.0 %collective-permute-start.26 = (bf16[32,4096]{1,0:T(8,128)(2,1)S(1)}, bf16[32,4096]{1,0:T(8,128)(2,1)S(1)}, u32[]{:S(2)}, u32[]{:S(2)}) collective-permute-start(bf16[32,4096]{1,0:T(8,128)(2,1)S(1)} %split.77), channel_id=1, source_target_pairs={{0,2},{1,3},{2,0},{3,1},{4,6},{5,7},{6,4},{7,5},{8,10},{9,11},{10,... | collective-permute-start | bytes 786440 | tf_op jit(solution)/shard_map/ppermute | solution.py:39
  172.6 13.4 %collective-permute-start.23 = (bf16[32,4096]{1,0:T(8,128)(2,1)S(1)}, bf16[32,4096]{1,0:T(8,128)(2,1)S(1)}, u32[]{:S(2)}, u32[]{:S(2)}) collective-permute-start(bf16[32,4096]{1,0:T(8,128)(2,1)S(1)} %split.73), channel_id=1, source_target_pairs={{0,2},{1,3},{2,0},{3,1},{4,6},{5,7},{6,4},{7,5},{8,10},{9,11},{10,... | collective-permute-start | bytes 786440 | tf_op jit(solution)/shard_map/ppermute | solution.py:39
  181.1 12.0 %collective-permute-start.27 = (bf16[16,4096]{1,0:T(8,128)(2,1)S(1)}, bf16[16,4096]{1,0:T(8,128)(2,1)S(1)}, u32[]{:S(2)}, u32[]{:S(2)}) collective-permute-start(bf16[16,4096]{1,0:T(8,128)(2,1)S(1)} %get-tuple-element.174), channel_id=1, source_target_pairs={{0,8},{1,9},{2,10},{3,11},{4,12},{5,13},{6,14},{7,15},{8,0},{9,1},... | collective-permute-start | bytes 393224 | tf_op jit(solution)/shard_map/ppermute | solution.py:39
  183.0 10.1 %collective-permute-start.28 = (bf16[16,4096]{1,0:T(8,128)(2,1)S(1)}, bf16[16,4096]{1,0:T(8,128)(2,1)S(1)}, u32[]{:S(2)}, u32[]{:S(2)}) collective-permute-start(bf16[16,4096]{1,0:T(8,128)(2,1)S(1)} %get-tuple-element.175), channel_id=1, source_target_pairs={{0,12},{1,13},{2,14},{3,15},{4,8},{5,9},{6,10},{7,11},{8,4},{9,5},... | collective-permute-start | bytes 393224 | tf_op jit(solution)/shard_map/ppermute | solution.py:39
  186.1 11.5 %collective-permute-start.24 = (bf16[16,4096]{1,0:T(8,128)(2,1)S(1)}, bf16[16,4096]{1,0:T(8,128)(2,1)S(1)}, u32[]{:S(2)}, u32[]{:S(2)}) collective-permute-start(bf16[16,4096]{1,0:T(8,128)(2,1)S(1)} %split.75), channel_id=1, source_target_pairs={{0,4},{1,5},{2,6},{3,7},{4,0},{5,1},{6,2},{7,3},{8,12},{9,13},{10,... | collective-permute-start | bytes 393224 | tf_op jit(solution)/shard_map/ppermute | solution.py:39
  197.7 3.8 %collective-permute-start.29 = (bf16[16,4096]{1,0:T(8,128)(2,1)S(1)}, bf16[16,4096]{1,0:T(8,128)(2,1)S(1)}, u32[]{:S(2)}, u32[]{:S(2)}) collective-permute-start(bf16[16,4096]{1,0:T(8,128)(2,1)S(1)} %add_convert_fusion.6), channel_id=1, source_target_pairs={{0,16},{1,17},{2,18},{3,19},{4,20},{5,21},{6,22},{7,23},{8,24},{9,... | collective-permute-start | bytes 393224 | tf_op jit(solution)/shard_map/ppermute | solution.py:15
  (9 other events, 102.3 us)
Sparse Core Ops, SparseCore 0:
  14.3 42.0 all-gather.1
  167.8 58.3 reduce-scatter.1

commit v3 on v1

v3 whole, which is shorter than its diff:
```python
import functools

import jax
import jax.numpy as jnp
from jax import lax
from jax.experimental import pallas as pl
from jax.experimental.pallas import tpu as pltpu
from jax.sharding import PartitionSpec as P

EPSILON = 1e-06
AXES = ("ep", "dp")


def across(block, source, target):
    return lax.ppermute(block, "grp", [(source, target)])


def stages(device_count):
    sizes = []
    rest = device_count
    while rest > 1:
        size = 2 if len(sizes) < 2 or rest % 4 else 4
        sizes.append(size)
        rest //= size
    strides = []
    stride = device_count
    for size in sizes[::-1]:
        stride //= size
        strides.append((stride, size))
    return strides


def swap(block, device_count, flip, role):
    pairs = [
        (part * device_count + i, part * device_count + (i ^ flip))
        for part in role
        for i in range(device_count)
    ]
    return lax.ppermute(block, ("grp",) + AXES, pairs)


def tied(*values):
    return lax.optimization_barrier(values)


def gather(block, device_count, role):
    for stride, size in stages(device_count):
        got = [swap(block, device_count, turn * stride, role) for turn in range(1, size)]
        block = jnp.concatenate([block] + got, axis=0)
    return block


def send_z(block, role):
    far = [swap(block, 16, flip, role) for flip in (4, 8, 12)]
    return jnp.concatenate([block, far[0]], axis=0), jnp.concatenate(far[1:], axis=0)


def send_y(near, away, role):
    return [jnp.concatenate([part, swap(part, 16, 2, role)], axis=0) for part in (near, away)]


def send_core(near, away, role):
    return [near, swap(near, 16, 1, role), away, swap(away, 16, 1, role)]


def plus(kept, *sent):
    total = kept.astype(jnp.float32)
    for one in sent:
        total = total + one.astype(jnp.float32)
    return total


def halves(array):
    return jnp.split(array, 2, axis=0)


def scatter_sum(part, device_count, role):
    for stride, size in stages(device_count)[::-1]:
        cuts = jnp.split(part, size, axis=0)
        got = [swap(cuts[turn], device_count, turn * stride, role) for turn in range(1, size)]
        total = plus(cuts[0], *got)
        part = total.astype(jnp.bfloat16)
    return total


def sum_core(pieces, role):
    away = plus(pieces[2], swap(pieces[3], 16, 1, role)).astype(jnp.bfloat16)
    near = plus(pieces[0], swap(pieces[1], 16, 1, role)).astype(jnp.bfloat16)
    return near, away


def sum_y(near, away, role):
    kept, sent = halves(away)
    away = plus(kept, swap(sent, 16, 2, role)).astype(jnp.bfloat16)
    kept, sent = halves(near)
    near = plus(kept, swap(sent, 16, 2, role)).astype(jnp.bfloat16)
    return near, away


def sum_z(near, away, role):
    second, third = [swap(h, 16, f, role) for h, f in zip(halves(away), (8, 12))]
    kept, sent = halves(near)
    return plus(kept, swap(sent, 16, 4, role), second, third)


def renew(weights, grads, axis_number, rate):
    scale = jnp.sqrt(jnp.mean(grads * grads, axis=axis_number, keepdims=True) + EPSILON)
    return (weights.astype(jnp.float32) - rate * grads / scale).astype(jnp.bfloat16)


def wide(a, b, contract):
    return lax.dot_general(a, b, (contract, ((), ())), preferred_element_type=jnp.float32)


def nn(a, b):
    return wide(a, b, ((1,), (0,)))


def nt(a, b):
    return wide(a, b, ((1,), (1,)))


def prep_kernel(
    place, lengths, rows_ref, cot_ref, ids_ref, gates_ref, dec_ids_ref, dec_gates_ref,
    out_ref, base_ref, *, experts, longest,
):
    width = rows_ref.shape[1]
    row_count = rows_ref.shape[0]
    learner = place[1] == 0
    places = place[0] * row_count + lax.broadcasted_iota(jnp.int32, (1, row_count), 1)
    start = jnp.int32(0)
    seq_len = jnp.zeros((1, row_count), jnp.int32)
    for i in range(lengths.shape[0]):
        end = start + lengths[i]
        seq_len = jnp.where((places >= start) & (places < end), lengths[i], seq_len)
        start = end
    weight = 2.0 * longest / (seq_len.astype(jnp.float32) + longest)
    names = lax.broadcasted_iota(jnp.int32, (experts, row_count), 0)

    def table(ids, gates):
        total = jnp.zeros((experts, row_count), jnp.float32)
        for k in range(ids.shape[0]):
            total = total + jnp.where(names == ids[k : k + 1], gates[k : k + 1], 0.0)
        return total

    train = table(ids_ref[...], gates_ref[...]) * weight
    stale = table(dec_ids_ref[0], dec_gates_ref[0])
    first = jnp.where(learner, train, stale)
    fresh = table(dec_ids_ref[1], dec_gates_ref[1])
    parts = []
    for one in (first, fresh):
        upper = one.astype(jnp.bfloat16).astype(jnp.float32)
        parts += [upper, one - upper]
    spare = out_ref.shape[1] - width
    if spare > 4 * experts:
        parts.append(jnp.zeros((spare - 4 * experts, row_count), jnp.float32))
    stacked = jnp.concatenate(parts, axis=0)
    weights = jnp.broadcast_to(weight, (128, row_count))
    square = jnp.concatenate([stacked, weights], axis=0)
    square = jnp.concatenate(
        [square, jnp.zeros((square.shape[0], 128 - row_count), jnp.float32)], axis=1
    )
    for i in range(spare // 128):
        turned = square[128 * i : 128 * (i + 1)].T
        out_ref[:, width + 128 * i : width + 128 * (i + 1)] = turned[:row_count].astype(
            jnp.bfloat16
        )
    column = square[spare:].T[:row_count, 0:1]
    out_ref[:, :width] = rows_ref[...]
    base_ref[...] = jnp.where(
        learner, column * cot_ref[...].astype(jnp.float32), rows_ref[...].astype(jnp.float32)
    )


def prep_call(place, lengths, rows, cot, ids, gates, dec_ids, dec_gates, experts, longest):
    row_count, width = rows.shape
    spare = -(-4 * experts // 128) * 128
    scalars = pl.BlockSpec(memory_space=pltpu.SMEM)
    whole = pl.BlockSpec(memory_space=pltpu.VMEM)
    return pl.pallas_call(
        functools.partial(prep_kernel, experts=experts, longest=longest),
        in_specs=[scalars, scalars] + [whole] * 6,
        out_specs=[whole, whole],
        out_shape=[
            jax.ShapeDtypeStruct((row_count, width + spare), jnp.bfloat16),
            jax.ShapeDtypeStruct((row_count, width), jnp.float32),
        ],
        name="prep",
    )(place, lengths, rows, cot, ids.T, gates.T, jnp.swapaxes(dec_ids, 1, 2), jnp.swapaxes(dec_gates, 1, 2))


def pick_gates(table, column, step):
    places = lax.broadcasted_iota(jnp.int32, table.shape, 1)
    taken = (places == column) | (places == column + step)
    return jnp.sum(jnp.where(taken, table.astype(jnp.float32), 0.0), axis=1, keepdims=True)


def parts_of(array, count):
    parts = []
    for _ in range(count):
        parts.append(array.astype(jnp.bfloat16))
        array = array - parts[-1].astype(jnp.float32)
    return parts


def fine(array, other, count):
    total = None
    for part in parts_of(array, count):
        product = nn(part, other)
        total = product if total is None else total + product
    return total


def ffn_kernel(place, *refs, count, experts, changed):
    rows_refs, table_refs = refs[:count], refs[count : 2 * count]
    gu_ref, dn_ref = refs[2 * count : 2 * count + 2]
    refs = refs[2 * count + 2 :]
    if changed:
        turned_ref, pulls_ref, sent_ref, hidden_turned_ref, rates_ref = refs[:5]
        refs = refs[5:]
    out_refs, rows = refs[:count], refs[count]
    part, width = rows_refs[0].shape
    for i in range(count):
        rows[part * i : part * (i + 1), :] = rows_refs[i][...]
    active = nn(rows[...], gu_ref[0])
    upward = nn(rows[...], gu_ref[1])
    if changed:
        alike = nn(rows[...], turned_ref[...])
        active = active - fine(alike, sent_ref[0], 2) * rates_ref[0:1]
        upward = upward - fine(alike, sent_ref[1], 2) * rates_ref[1:2]
    swish = active * jax.nn.sigmoid(active)
    hidden = (swish * upward).astype(jnp.bfloat16)
    if changed:
        scaled = hidden.astype(jnp.float32) * rates_ref[2:3]
        mixed = parts_of(fine(scaled, hidden_turned_ref[...], 2), 2)
    gates = [pick_gates(table_refs[i][...], place[0], experts) for i in range(count)]
    tile = 1024
    for lower in range(0, width, tile):
        cut = slice(lower, lower + tile)
        out = nn(hidden, dn_ref[:, cut])
        if changed:
            for one in mixed:
                out = out - nn(one, pulls_ref[:, cut])
        for i in range(count):
            here = out[part * i : part * (i + 1)]
            out_refs[i][:, cut] = (gates[i] * here).astype(jnp.bfloat16)


def ffn_call(place, pieces, tables, planes, weights_dn, experts, change=()):
    count = len(pieces)
    part = pieces[0].shape[0]
    hidden_count, width = weights_dn.shape
    row_count = part * count
    whole = pl.BlockSpec(memory_space=pltpu.VMEM)
    return pl.pallas_call(
        functools.partial(ffn_kernel, count=count, experts=experts, changed=bool(change)),
        in_specs=[pl.BlockSpec(memory_space=pltpu.SMEM)] + [whole] * (2 * count + 2 + len(change)),
        out_specs=[whole] * count,
        scratch_shapes=[pltpu.VMEM((row_count, width), jnp.bfloat16)],
        out_shape=[jax.ShapeDtypeStruct((part, width), jnp.bfloat16)] * count,
        compiler_params=pltpu.CompilerParams(vmem_limit_bytes=44 << 20),
        cost_estimate=pl.CostEstimate(
            flops=6 * row_count * hidden_count * width if change else 1,
            bytes_accessed=4 * row_count * width if change else 1,
            transcendentals=row_count * hidden_count if change else 1,
        ),
        name="ffn_changed" if change else "ffn",
    )(place, *pieces, *tables, planes, weights_dn, *change)


def learn_kernel(place, *refs, count, experts, rates):
    rows_refs, table_refs = refs[:count], refs[count : 2 * count]
    cot_refs = refs[2 * count : 3 * count]
    gu_ref, dn_ref = refs[3 * count : 3 * count + 2]
    dx_refs = refs[3 * count + 2 : 4 * count + 2]
    turned, pulls, sent, hidden_turned_ref, rates_ref = refs[4 * count + 2 : 4 * count + 7]
    rows, pulls_turned = refs[4 * count + 7 :]
    part = rows_refs[0].shape[0]
    hidden_count, width = dn_ref.shape
    tile = 1024
    cuts = [slice(lower, lower + tile) for lower in range(0, width, tile)]
    for i in range(count):
        here = slice(part * i, part * (i + 1))
        gates = pick_gates(table_refs[i][...], place[0], experts)
        rows[here, :] = rows_refs[i][...]
        pulls[here, :] = (gates * cot_refs[i][...].astype(jnp.float32)).astype(jnp.bfloat16)
    for cut in cuts:
        turned[cut, :] = rows[:, cut].T
        pulls_turned[cut, :] = pulls[:, cut].T

    active = nn(rows[...], gu_ref[0])
    upward = nn(rows[...], gu_ref[1])
    back = nn(dn_ref[...], pulls_turned[...]).T
    sigma = jax.nn.sigmoid(active)
    swish = active * sigma
    hidden = (swish * upward).astype(jnp.bfloat16)
    d_active = (back * upward * sigma * (1.0 + active * (1.0 - sigma))).astype(jnp.bfloat16)
    d_upward = (back * swish).astype(jnp.bfloat16)
    sent[0] = d_active
    sent[1] = d_upward
    hidden_turned_ref[...] = hidden.T
    d_active_turned = d_active.T
    d_upward_turned = d_upward.T

    for cut in cuts:
        done = nn(gu_ref[0, cut, :], d_active_turned) + nn(gu_ref[1, cut, :], d_upward_turned)
        done = done.T.astype(jnp.bfloat16)
        for i in range(count):
            dx_refs[i][:, cut] = done[part * i : part * (i + 1)]

    def mean_square(alike, factor):
        wide_factor = factor.astype(jnp.float32)
        squares = jnp.sum(wide_factor * fine(alike, factor, 3), axis=0, keepdims=True)
        return jnp.maximum(squares, 0.0) / width

    alike = nn(rows[...], turned[...])
    rates_ref[0:1] = rates[0] / jnp.sqrt(mean_square(alike, d_active) + EPSILON)
    rates_ref[1:2] = rates[0] / jnp.sqrt(mean_square(alike, d_upward) + EPSILON)
    alike = nn(pulls[...], pulls_turned[...])
    rates_ref[2:3] = rates[1] / jnp.sqrt(mean_square(alike, hidden) + EPSILON)


def learn_call(place, pieces, tables, cots, planes, weights_dn, experts, rates):
    count = len(pieces)
    part = pieces[0].shape[0]
    hidden_count, width = weights_dn.shape
    row_count = part * count
    whole = pl.BlockSpec(memory_space=pltpu.VMEM)
    out_shape = [jax.ShapeDtypeStruct((part, width), jnp.bfloat16)] * count + [
        jax.ShapeDtypeStruct((width, row_count), jnp.bfloat16),
        jax.ShapeDtypeStruct((row_count, width), jnp.bfloat16),
        jax.ShapeDtypeStruct((2, row_count, hidden_count), jnp.bfloat16),
        jax.ShapeDtypeStruct((hidden_count, row_count), jnp.bfloat16),
        jax.ShapeDtypeStruct((8, hidden_count), jnp.float32),
    ]
    return pl.pallas_call(
        functools.partial(learn_kernel, count=count, experts=experts, rates=rates),
        in_specs=[pl.BlockSpec(memory_space=pltpu.SMEM)] + [whole] * (3 * count + 2),
        out_specs=[whole] * len(out_shape),
        scratch_shapes=[
            pltpu.VMEM((row_count, width), jnp.bfloat16),
            pltpu.VMEM((width, row_count), jnp.bfloat16),
        ],
        out_shape=out_shape,
        compiler_params=pltpu.CompilerParams(vmem_limit_bytes=44 << 20),
        cost_estimate=pl.CostEstimate(
            flops=12 * row_count * hidden_count * width,
            bytes_accessed=8 * row_count * width,
            transcendentals=row_count * hidden_count,
        ),
        name="learn",
    )(place, *pieces, *tables, *cots, planes, weights_dn)


def unset(like):
    return pl.pallas_call(
        lambda out_ref: None,
        out_shape=jax.ShapeDtypeStruct(like.shape, like.dtype),
        out_specs=pl.BlockSpec(memory_space=pl.ANY),
        name="unset",
    )()


def ffn_plain(place, pieces, tables, planes, weights_dn, experts):
    width = weights_dn.shape[1]
    rows = pieces[0][:, :width]
    gates = pick_gates(tables[0][:, width:], place[0], experts)
    active = nn(rows, planes[0])
    upward = nn(rows, planes[1])
    hidden = (active * jax.nn.sigmoid(active) * upward).astype(jnp.bfloat16)
    return [(gates * nn(hidden, weights_dn)).astype(jnp.bfloat16)]


def learn_plain(place, pieces, tables, cots, planes, weights_dn, experts, rates):
    width = weights_dn.shape[1]
    rows = pieces[0][:, :width]
    gates = pick_gates(tables[0][:, width:], place[0], experts)
    pulls = (gates * cots.astype(jnp.float32)).astype(jnp.bfloat16)
    active = nn(rows, planes[0])
    upward = nn(rows, planes[1])
    back = nt(pulls, weights_dn)
    sigma = jax.nn.sigmoid(active)
    swish = active * sigma
    hidden = (swish * upward).astype(jnp.bfloat16)
    d_active = (back * upward * sigma * (1.0 + active * (1.0 - sigma))).astype(jnp.bfloat16)
    d_upward = (back * swish).astype(jnp.bfloat16)
    dx_part = (nt(d_active, planes[0]) + nt(d_upward, planes[1])).astype(jnp.bfloat16)
    new_planes = jnp.stack(
        [
            renew(planes[0], wide(rows, d_active, ((0,), (0,))), 0, rates[0]),
            renew(planes[1], wide(rows, d_upward, ((0,), (0,))), 0, rates[0]),
        ],
        axis=0,
    )
    new_dn = renew(weights_dn, wide(hidden, pulls, ((0,), (0,))), 1, rates[1])
    return [dx_part, new_planes, new_dn]


def per_device(
    rows_in,
    cotangent,
    lengths,
    train_experts,
    train_gates,
    decode_experts,
    decode_gates,
    gate_up,
    down,
):
    ep_count = lax.axis_size("ep")
    dp_count = lax.axis_size("dp")
    device_count = ep_count * dp_count
    row_count, model_width = cotangent.shape
    role = lax.axis_index("grp").astype(jnp.int32)
    is_learner = role == 0
    mine = lax.axis_index("ep").astype(jnp.int32)
    own_dn = down[0, 0]
    planes = jnp.transpose(gate_up[0, 0], (1, 0, 2))
    total_rows = row_count * device_count
    longest = 2 * total_rows // lengths.shape[0]
    rates = (0.5 / model_width**0.5, 0.5 / (own_dn.shape[0] * dp_count) ** 0.5)
    small = device_count == 16 and dp_count == 1
    first_place = mine.reshape(1)
    fresh_place = first_place + 2 * ep_count

    where = jnp.stack([mine * dp_count + lax.axis_index("dp").astype(jnp.int32), role])
    block, base = prep_call(
        where, lengths, rows_in[0], cotangent, train_experts, train_gates, decode_experts,
        decode_gates, ep_count, longest,
    )
    if small:
        near, away = send_z(block, (0, 1))
        near, planes, cotangent = tied(near, planes, cotangent)
        cot_near, cot_away = send_z(cotangent, (0,))
        near, away = send_y(near, away, (0, 1))
        every = send_core(near, away, (0, 1))

        def blank(*shape, of=jnp.bfloat16):
            return unset(jax.ShapeDtypeStruct(shape, of))

        rows = [piece[:, :model_width] for piece in every]
        gates = [piece[:, model_width:] for piece in every]
        part = lax.cond(
            is_learner,
            lambda r, t, g, d: [blank(*one.shape) for one in r],
            lambda r, t, g, d: list(ffn_call(first_place, r, t, g, d, ep_count)),
            rows,
            gates,
            planes,
            own_dn,
        )
        near, away = sum_core(part, (1,))
        near, away, cot_near, cot_away = tied(near, away, cot_near, cot_away)
        cot_near, cot_away = send_y(cot_near, cot_away, (0,))
        near, away = sum_y(near, away, (1,))
        near, away, cot_near, cot_away = tied(near, away, cot_near, cot_away)
        cots = send_core(cot_near, cot_away, (0,))
        current = (base + sum_z(near, away, (1,))).astype(jnp.bfloat16)
        hopped = across(current, 1, 0)
        hidden_count = own_dn.shape[0]
        learned = lax.cond(
            is_learner,
            lambda r, t, c, g, d: list(learn_call(first_place, r, t, c, g, d, ep_count, rates)),
            lambda r, t, c, g, d: [blank(*one.shape) for one in r]
            + [
                blank(model_width, total_rows),
                blank(total_rows, model_width),
                blank(2, total_rows, hidden_count),
                blank(hidden_count, total_rows),
                blank(8, hidden_count, of=jnp.float32),
            ],
            rows,
            gates,
            cots,
            planes,
            own_dn,
        )
        near, away = sum_core(learned[:4], (0,))
        near, away = sum_y(near, away, (0,))
        near, away, hopped = tied(near, away, hopped)
        dx_sum = sum_z(near, away, (0,))
        near, away = send_z(hopped, (0,))
        near, away = send_y(near, away, (0,))
        arrived = send_core(near, away, (0,))
        fresh_part = lax.cond(
            is_learner,
            lambda r, t, g, d, *c: list(ffn_call(fresh_place, r, t, g, d, ep_count, c)),
            lambda r, t, g, d, *c: [blank(*one.shape) for one in r],
            arrived,
            gates,
            planes,
            own_dn,
            *learned[4:],
        )
        near, away = sum_core(fresh_part, (0,))
        near, away, dx_sum = tied(near, away, dx_sum)
        near, away = sum_y(near, away, (0,))
        fresh_sum = sum_z(near, away, (0,))
    else:
        every = [gather(block, device_count, (0, 1))]
        cots = gather(cotangent, device_count, (0,))

        def learn(every, cots, planes, own_dn):
            out = list(learn_plain(first_place, every, every, cots, planes, own_dn, ep_count, rates))
            return ([unset(out[0])], out[0], out[1], out[2])

        def decode(every, cots, planes, own_dn):
            out = list(ffn_plain(first_place, every, every, planes, own_dn, ep_count))
            return (out, unset(cots), unset(planes), unset(own_dn))

        part, dx_part, new_planes, new_dn = lax.cond(
            is_learner, learn, decode, every, cots, planes, own_dn
        )
        stale_sum = scatter_sum(part[0], device_count, (1,))
        current = (base + stale_sum).astype(jnp.bfloat16)
        dx_sum = scatter_sum(dx_part, device_count, (0,))
        arrived = [gather(across(current, 1, 0), device_count, (0,))]
        fresh_part = lax.cond(
            is_learner,
            lambda r, e, g, d: list(ffn_plain(fresh_place, r, e, g, d, ep_count)),
            lambda r, e, g, d: [unset(o) for o in r],
            arrived,
            every,
            new_planes,
            new_dn,
        )
        fresh_sum = scatter_sum(fresh_part[0], device_count, (0,))
    moved = across(fresh_sum.astype(jnp.bfloat16), 0, 1).astype(jnp.float32)
    final_rows = jnp.where(is_learner, base + dx_sum, current.astype(jnp.float32) + moved)
    return final_rows.astype(jnp.bfloat16)[None]


def solution(mesh):
    placed = (
        P("grp", ("ep", "dp"), None),
        P(("ep", "dp"), None),
        P(),
        P(("ep", "dp"), None),
        P(("ep", "dp"), None),
        P(None, ("ep", "dp"), None),
        P(None, ("ep", "dp"), None),
        P("grp", "ep", None, None, "dp"),
        P("grp", "ep", "dp", None),
    )
    return jax.shard_map(
        per_device,
        mesh=mesh,
        in_specs=placed,
        out_specs=P("grp", ("ep", "dp"), None),
        check_vma=False,
    )
```

time: 227 us -> 237 us (1.044)
  local copies, waits for them, and re-layouts: 15.2 us -> 25.3 us
  Pallas kernels: 51.5 us -> 42.5 us
  other arithmetic: 7.88 us -> 12.1 us
  waiting for transfers between devices: 54.5 us -> 57.8 us
    pallas_call x1, Pallas kernels: 36.2 us -> 23.1 us  [learn_call(): pl.pallas_call(functools.partial(learn_kernel, count=count, experts=exper...]
    ppermute x42, waiting for transfers between devices: 48.5 us -> 54.6 us  [swap(): return lax.ppermute(block, ('grp',) + AXES, pairs)]
    slice x0 -> x8, local copies, waits for them, and re-layouts: none -> 4.34 us  [the longest x4 2.54 us: per_device(): rows = [piece[:, :model_width] for piece in every]]
    pallas_call x1, Pallas kernels: 13.3 us -> 17.4 us  [ffn_call(): pl.pallas_call(functools.partial(ffn_kernel, count=count, experts=experts...]
    unnamed x32 -> x30, local copies, waits for them, and re-layouts: 14.2 us -> 17.2 us
    ppermute x2, waiting for transfers between devices: 6 us -> 3.19 us  [across(): return lax.ppermute(block, 'grp', [(source, target)])]
  transfers between devices with their start and end apart: 44 -> 44, of which waited for: 11 -> 13; matrix products, arithmetic and copies ran while one was open for 8% -> 13% of each run, Pallas kernels for 6% -> 17%
where the time goes in v3:
time: 237 us; the launch traced here: 236 us
  starting transfers between devices  96.9 us (41%)
  waiting for transfers between devices  57.8 us (24%)
  Pallas kernels  42.5 us (18%)
  local copies, waits for them, and re-layouts  25.3 us (11%)
  other arithmetic  12.1 us (5%)
    ppermute x42, starting transfers between devices, swap(): return lax.ppermute(block, ('grp',) + AXES, pairs)  94.3 us
    ppermute x42, waiting for transfers between devices, swap(): return lax.ppermute(block, ('grp',) + AXES, pairs)  54.6 us
    pallas_call x1, Pallas kernels, learn_call(): pl.pallas_call(functools.partial(learn_kernel, count=count, experts=exper...  23.1 us
    pallas_call x1, Pallas kernels, ffn_call(): pl.pallas_call(functools.partial(ffn_kernel, count=count, experts=experts...  17.4 us
    unnamed x30, local copies, waits for them, and re-layouts  17.2 us
  transfers between devices with their start and end apart: 44, of which 13 were waited for; matrix products, arithmetic and copies ran while one was open for 13% of the time, Pallas kernels for 17%

profile of v3, /device:TPU:0, one launch (start us, length us, event | category | flops | bytes accessed | tf_op | source)
XLA Modules:
  0.0 235.9 jit_solution(13435701376477539733)
XLA Ops:
  2.6 3.0 %collective-permute-start = (bf16[16,4224]{1,0:T(8,128)(2,1)}, bf16[16,4224]{1,0:T(8,128)(2,1)S(1)}, u32[]{:S(2)}, u32[]{:S(2)}) collective-permute-start(bf16[16,4224]{1,0:T(8,128)(2,1)} %get-tuple-element.273), channel_id=1, source_target_pairs={{0,4},{1,5},{2,6},{3,7},{4,0},{5,1},{6,2},{7,3},{8,12},{9,13},{10,... | collective-permute-start | bytes 405512 | tf_op jit(solution)/shard_map/ppermute | solution.py:39
  5.6 2.5 %collective-permute-start.4 = (bf16[16,4224]{1,0:T(8,128)(2,1)}, bf16[16,4224]{1,0:T(8,128)(2,1)S(1)}, u32[]{:S(2)}, u32[]{:S(2)}) collective-permute-start(bf16[16,4224]{1,0:T(8,128)(2,1)} %get-tuple-element.273), channel_id=1, source_target_pairs={{0,12},{1,13},{2,14},{3,15},{4,8},{5,9},{6,10},{7,11},{8,4},{9,5},... | collective-permute-start | bytes 405512 | tf_op jit(solution)/shard_map/ppermute | solution.py:39
  8.2 11.8 %copy.12 = bf16[1,1,4096,2,768]{4,2,3,1,0:T(8,128)(2,1)} copy(bf16[1,1,4096,2,768]{4,3,2,1,0:T(2,128)(2,1)} %param.22) | data formatting | bytes 25165824 | tf_op args[7]
  22.3 11.3 %collective-permute-done.5 = bf16[32,4224]{1,0:T(8,128)(2,1)S(1)} collective-permute-done((bf16[32,4224]{1,0:T(8,128)(2,1)S(1)}, bf16[32,4224]{1,0:T(8,128)(2,1)S(1)}, u32[]{:S(2)}, u32[]{:S(2)}) %collective-permute-start.5) | collective-permute-done | bytes 270368 | tf_op jit(solution)/shard_map/ppermute | solution.py:39
  34.3 3.4 %collective-permute-start.9 = (bf16[16,4096]{1,0:T(8,128)(2,1)S(1)}, bf16[16,4096]{1,0:T(8,128)(2,1)}, u32[]{:S(2)}, u32[]{:S(2)}) collective-permute-start(bf16[16,4096]{1,0:T(8,128)(2,1)S(1)} %copy-done.5), channel_id=1, source_target_pairs={{0,4},{1,5},{2,6},{3,7},{4,0},{5,1},{6,2},{7,3},{8,12},{9,13},{10,... | collective-permute-start | bytes 393224 | tf_op jit(solution)/shard_map/ppermute | solution.py:39
  37.7 4.4 %collective-permute-start.11 = (bf16[16,4096]{1,0:T(8,128)(2,1)S(1)}, bf16[16,4096]{1,0:T(8,128)(2,1)}, u32[]{:S(2)}, u32[]{:S(2)}) collective-permute-start(bf16[16,4096]{1,0:T(8,128)(2,1)S(1)} %copy-done.5), channel_id=1, source_target_pairs={{0,12},{1,13},{2,14},{3,15},{4,8},{5,9},{6,10},{7,11},{8,4},{9,5},... | collective-permute-start | bytes 393224 | tf_op jit(solution)/shard_map/ppermute | solution.py:39
  50.8 2.4 %collective-permute-done.10 = bf16[16,4096]{1,0:T(8,128)(2,1)} collective-permute-done((bf16[16,4096]{1,0:T(8,128)(2,1)S(1)}, bf16[16,4096]{1,0:T(8,128)(2,1)}, u32[]{:S(2)}, u32[]{:S(2)}) %collective-permute-start.10) | collective-permute-done | bytes 131104 | tf_op jit(solution)/shard_map/ppermute | solution.py:39
  57.7 3.4 %collective-permute-start.14 = (bf16[32,4096]{1,0:T(8,128)(2,1)S(1)}, bf16[32,4096]{1,0:T(8,128)(2,1)S(1)}, u32[]{:S(2)}, u32[]{:S(2)}) collective-permute-start(bf16[32,4096]{1,0:T(8,128)(2,1)S(1)} %pad_maximum_fusion.4), channel_id=1, source_target_pairs={{0,2},{1,3},{2,0},{3,1},{4,6},{5,7},{6,4},{7,5},{8,10},{9,11},{10,... | collective-permute-start | bytes 786440 | tf_op jit(solution)/shard_map/ppermute | solution.py:39
  63.7 5.1 %collective-permute-done.14 = bf16[32,4096]{1,0:T(8,128)(2,1)S(1)} collective-permute-done((bf16[32,4096]{1,0:T(8,128)(2,1)S(1)}, bf16[32,4096]{1,0:T(8,128)(2,1)S(1)}, u32[]{:S(2)}, u32[]{:S(2)}) %collective-permute-start.14) | collective-permute-done | bytes 262176 | tf_op jit(solution)/shard_map/ppermute | solution.py:39
  68.9 3.9 %collective-permute-done.15 = bf16[32,4096]{1,0:T(8,128)(2,1)S(1)} collective-permute-done((bf16[32,4096]{1,0:T(8,128)(2,1)S(1)}, bf16[32,4096]{1,0:T(8,128)(2,1)S(1)}, u32[]{:S(2)}, u32[]{:S(2)}) %collective-permute-start.15) | collective-permute-done | bytes 262176 | tf_op jit(solution)/shard_map/ppermute | solution.py:39
  81.8 24.7 %conditional.10 = (bf16[64,4096]{1,0:T(8,128)(2,1)}, bf16[64,4096]{1,0:T(8,128)(2,1)}, bf16[4096,256]{1,0:T(8,128)(2,1)}, bf16[256,4096]{1,0:T(8,128)(2,1)S(1)},...) conditional(s32[]{:T(128)} %convert_element_type.196, () %tuple.73, ...), branch_computations={%region_2.0_spmd, %region_3.0_spmd} | conditional | flops 9663676416 | bytes 16777400
  83.3 23.1 %learn.1 = (bf16[64,4096]{1,0:T(8,128)(2,1)}, bf16[64,4096]{1,0:T(8,128)(2,1)}, bf16[64,4096]{1,0:T(8,128)(2,1)}, bf16[64,4096]{1,0:T(8,128)(2,1)}, bf16[4096,25...) custom-call(s32[1]{0:T(128)} %get-tuple-element.192.place, ...), custom_call_target="tpu_custom_call" | custom-call | flops 9663676416 | bytes 8388608 | tf_op jit(solution)/shard_map/cond/branch_1_fun/learn/pallas_call | solution.py:336
  115.2 3.4 %collective-permute-start.21 = (bf16[32,4096]{1,0:T(8,128)(2,1)S(1)}, bf16[32,4096]{1,0:T(8,128)(2,1)S(1)}, u32[]{:S(2)}, u32[]{:S(2)}) collective-permute-start(bf16[32,4096]{1,0:T(8,128)(2,1)S(1)} %split.99), channel_id=1, source_target_pairs={{0,2},{1,3},{2,0},{3,1},{4,6},{5,7},{6,4},{7,5},{8,10},{9,11},{10,... | collective-permute-start | bytes 786440 | tf_op jit(solution)/shard_map/ppermute | solution.py:39
  122.3 4.0 %collective-permute-done.21 = bf16[32,4096]{1,0:T(8,128)(2,1)S(1)} collective-permute-done((bf16[32,4096]{1,0:T(8,128)(2,1)S(1)}, bf16[32,4096]{1,0:T(8,128)(2,1)S(1)}, u32[]{:S(2)}, u32[]{:S(2)}) %collective-permute-start.21) | collective-permute-done | bytes 262176 | tf_op jit(solution)/shard_map/ppermute | solution.py:39
  126.3 4.6 %collective-permute-done.19 = bf16[32,4096]{1,0:T(8,128)(2,1)S(1)} collective-permute-done((bf16[32,4096]{1,0:T(8,128)(2,1)S(1)}, bf16[32,4096]{1,0:T(8,128)(2,1)S(1)}, u32[]{:S(2)}, u32[]{:S(2)}) %collective-permute-start.19) | collective-permute-done | bytes 262176 | tf_op jit(solution)/shard_map/ppermute | solution.py:39
  131.0 4.4 %collective-permute-start.30 = (bf16[16,4096]{1,0:T(8,128)(2,1)S(1)}, bf16[16,4096]{1,0:T(8,128)(2,1)S(1)}, u32[]{:S(2)}, u32[]{:S(2)}) collective-permute-start(bf16[16,4096]{1,0:T(8,128)(2,1)S(1)} %collective-permute-done.25), channel_id=1, source_target_pairs={{0,12},{1,13},{2,14},{3,15},{4,8},{5,9},{6,10},{7,11},{8,4},{9,5},... | collective-permute-start | bytes 393224 | tf_op jit(solution)/shard_map/ppermute | solution.py:39
  137.3 3.8 %collective-permute-start.26 = (bf16[16,4096]{1,0:T(8,128)(2,1)S(1)}, bf16[16,4096]{1,0:T(8,128)(2,1)S(1)}, u32[]{:S(2)}, u32[]{:S(2)}) collective-permute-start(bf16[16,4096]{1,0:T(8,128)(2,1)S(1)} %collective-permute-done.25), channel_id=1, source_target_pairs={{0,4},{1,5},{2,6},{3,7},{4,0},{5,1},{6,2},{7,3},{8,12},{9,13},{10,... | collective-permute-start | bytes 393224 | tf_op jit(solution)/shard_map/ppermute | solution.py:39
  141.8 3.6 %collective-permute-done.29 = bf16[16,4096]{1,0:T(8,128)(2,1)S(1)} collective-permute-done((bf16[16,4096]{1,0:T(8,128)(2,1)S(1)}, bf16[16,4096]{1,0:T(8,128)(2,1)S(1)}, u32[]{:S(2)}, u32[]{:S(2)}) %collective-permute-start.29) | collective-permute-done | bytes 131104 | tf_op jit(solution)/shard_map/ppermute | solution.py:39
  145.4 3.4 %collective-permute-start.31 = (bf16[32,4096]{1,0:T(8,128)(2,1)S(1)}, bf16[32,4096]{1,0:T(8,128)(2,1)S(1)}, u32[]{:S(2)}, u32[]{:S(2)}) collective-permute-start(bf16[32,4096]{1,0:T(8,128)(2,1)S(1)} %pad_maximum_fusion.7), channel_id=1, source_target_pairs={{0,2},{1,3},{2,0},{3,1},{4,6},{5,7},{6,4},{7,5},{8,10},{9,11},{10,... | collective-permute-start | bytes 786440 | tf_op jit(solution)/shard_map/ppermute | solution.py:39
  148.9 2.4 %collective-permute-start.27 = (bf16[32,4096]{1,0:T(8,128)(2,1)S(1)}, bf16[32,4096]{1,0:T(8,128)(2,1)S(1)}, u32[]{:S(2)}, u32[]{:S(2)}) collective-permute-start(bf16[32,4096]{1,0:T(8,128)(2,1)S(1)} %pad_maximum_fusion.6), channel_id=1, source_target_pairs={{0,2},{1,3},{2,0},{3,1},{4,6},{5,7},{6,4},{7,5},{8,10},{9,11},{10,... | collective-permute-start | bytes 786440 | tf_op jit(solution)/shard_map/ppermute | solution.py:39
  153.3 7.9 %collective-permute-done.27 = bf16[32,4096]{1,0:T(8,128)(2,1)S(1)} collective-permute-done((bf16[32,4096]{1,0:T(8,128)(2,1)S(1)}, bf16[32,4096]{1,0:T(8,128)(2,1)S(1)}, u32[]{:S(2)}, u32[]{:S(2)}) %collective-permute-start.27) | collective-permute-done | bytes 262176 | tf_op jit(solution)/shard_map/ppermute | solution.py:39
  169.6 4.9 %collective-permute-start.36 = (bf16[16,4096]{1,0:T(8,128)(2,1)}, bf16[16,4096]{1,0:T(8,128)(2,1)}, u32[]{:S(2)}, u32[]{:S(2)}) collective-permute-start(bf16[16,4096]{1,0:T(8,128)(2,1)} %get-tuple-element.331), channel_id=1, source_target_pairs={{0,8},{1,9},{2,10},{3,11},{4,12},{5,13},{6,14},{7,15},{8,0},{9,1},... | collective-permute-start | bytes 393224 | tf_op jit(solution)/shard_map/ppermute | solution.py:39
  174.6 3.3 %collective-permute-start.37 = (bf16[16,4096]{1,0:T(8,128)(2,1)}, bf16[16,4096]{1,0:T(8,128)(2,1)}, u32[]{:S(2)}, u32[]{:S(2)}) collective-permute-start(bf16[16,4096]{1,0:T(8,128)(2,1)} %get-tuple-element.332), channel_id=1, source_target_pairs={{0,12},{1,13},{2,14},{3,15},{4,8},{5,9},{6,10},{7,11},{8,4},{9,5},... | collective-permute-start | bytes 393224 | tf_op jit(solution)/shard_map/ppermute | solution.py:39
  177.9 17.7 %conditional.11 = (bf16[64,4096]{1,0:T(8,128)(2,1)}, bf16[64,4096]{1,0:T(8,128)(2,1)}, bf16[64,4096]{1,0:T(8,128)(2,1)}, bf16[64,4096]{1,0:T(8,128)(2,1)}) conditional(s32[]{:T(128)} %convert_element_type.196, () %tuple.72, (s32[1]{0:T(128)}, bf16[64,4096]{1,0:T(8,128)(2,1)}, bf16[64,4096]{1,0:T(8,128)(2,1)}, bf16[64,4096]{1,0:T(8,128)(2,1)}, ...), branch_computations={%region_4.0_spmd, %region_5.0_spmd} | conditional | flops 4831838208 | bytes 4194348
  178.1 17.4 %ffn_changed.2 = (bf16[64,4096]{1,0:T(8,128)(2,1)}, bf16[64,4096]{1,0:T(8,128)(2,1)}, bf16[64,4096]{1,0:T(8,128)(2,1)}, bf16[64,4096]{1,0:T(8,128)(2,1)}) custom-call(s32[1]{0:T(128)S(6)} %add.53.place, bf16[64,4096]{1,0:T(8,128)(2,1)} %get-tuple-element.217.refs_0_, bf16[64,4096]{1,0:T(8,128)(2,1)} %get-tuple-element.218.refs_1_, ...), custom_call_target="tpu_custom_call" | custom-call | flops 4831838208 | bytes 4194304 | tf_op jit(solution)/shard_map/cond/branch_1_fun/ffn_changed/pallas_call | solution.py:255
  203.9 3.6 %collective-permute-start.40 = (bf16[32,4096]{1,0:T(8,128)(2,1)S(1)}, bf16[32,4096]{1,0:T(8,128)(2,1)S(1)}, u32[]{:S(2)}, u32[]{:S(2)}) collective-permute-start(bf16[32,4096]{1,0:T(8,128)(2,1)S(1)} %split.93), channel_id=1, source_target_pairs={{0,2},{1,3},{2,0},{3,1},{4,6},{5,7},{6,4},{7,5},{8,10},{9,11},{10,... | collective-permute-start | bytes 786440 | tf_op jit(solution)/shard_map/ppermute | solution.py:39
  209.9 5.1 %collective-permute-done.40 = bf16[32,4096]{1,0:T(8,128)(2,1)S(1)} collective-permute-done((bf16[32,4096]{1,0:T(8,128)(2,1)S(1)}, bf16[32,4096]{1,0:T(8,128)(2,1)S(1)}, u32[]{:S(2)}, u32[]{:S(2)}) %collective-permute-start.40) | collective-permute-done | bytes 262176 | tf_op jit(solution)/shard_map/ppermute | solution.py:39
  217.2 4.3 %collective-permute-start.42 = (bf16[16,4096]{1,0:T(8,128)(2,1)S(1)}, bf16[16,4096]{1,0:T(8,128)(2,1)S(1)}, u32[]{:S(2)}, u32[]{:S(2)}) collective-permute-start(bf16[16,4096]{1,0:T(8,128)(2,1)S(1)} %get-tuple-element.330), channel_id=1, source_target_pairs={{0,12},{1,13},{2,14},{3,15},{4,8},{5,9},{6,10},{7,11},{8,4},{9,5},... | collective-permute-start | bytes 393224 | tf_op jit(solution)/shard_map/ppermute | solution.py:39
  221.6 2.9 %collective-permute-start.39 = (bf16[16,4096]{1,0:T(8,128)(2,1)S(1)}, bf16[16,4096]{1,0:T(8,128)(2,1)S(1)}, u32[]{:S(2)}, u32[]{:S(2)}) collective-permute-start(bf16[16,4096]{1,0:T(8,128)(2,1)S(1)} %split.101), channel_id=1, source_target_pairs={{0,4},{1,5},{2,6},{3,7},{4,0},{5,1},{6,2},{7,3},{8,12},{9,13},{10,... | collective-permute-start | bytes 393224 | tf_op jit(solution)/shard_map/ppermute | solution.py:39
  224.5 3.6 %collective-permute-done.41 = bf16[16,4096]{1,0:T(8,128)(2,1)S(1)} collective-permute-done((bf16[16,4096]{1,0:T(8,128)(2,1)S(1)}, bf16[16,4096]{1,0:T(8,128)(2,1)S(1)}, u32[]{:S(2)}, u32[]{:S(2)}) %collective-permute-start.41) | collective-permute-done | bytes 131104 | tf_op jit(solution)/shard_map/ppermute | solution.py:39
  228.2 2.5 %collective-permute-done.39 = bf16[16,4096]{1,0:T(8,128)(2,1)S(1)} collective-permute-done((bf16[16,4096]{1,0:T(8,128)(2,1)S(1)}, bf16[16,4096]{1,0:T(8,128)(2,1)S(1)}, u32[]{:S(2)}, u32[]{:S(2)}) %collective-permute-start.39) | collective-permute-done | bytes 131104 | tf_op jit(solution)/shard_map/ppermute | solution.py:39
  232.0 3.2 %collective-permute-done.43 = bf16[16,4096]{1,0:T(8,128)(2,1)S(1)} collective-permute-done((bf16[16,4096]{1,0:T(8,128)(2,1)S(1)}, bf16[16,4096]{1,0:T(8,128)(2,1)S(1)}, u32[]{:S(2)}, u32[]{:S(2)}) %collective-permute-start.43) | collective-permute-done | bytes 131104 | tf_op jit(solution)/shard_map/ppermute | solution.py:15
  (145 shorter events, 72.0 us)
Async XLA Ops:
  2.6 17.5 %collective-permute-start = (bf16[16,4224]{1,0:T(8,128)(2,1)}, bf16[16,4224]{1,0:T(8,128)(2,1)S(1)}, u32[]{:S(2)}, u32[]{:S(2)}) collective-permute-start(bf16[16,4224]{1,0:T(8,128)(2,1)} %get-tuple-element.273), channel_id=1, source_target_pairs={{0,4},{1,5},{2,6},{3,7},{4,0},{5,1},{6,2},{7,3},{8,12},{9,13},{10,... | collective-permute-start | bytes 405512 | tf_op jit(solution)/shard_map/ppermute | solution.py:39
  5.6 16.1 %collective-permute-start.4 = (bf16[16,4224]{1,0:T(8,128)(2,1)}, bf16[16,4224]{1,0:T(8,128)(2,1)S(1)}, u32[]{:S(2)}, u32[]{:S(2)}) collective-permute-start(bf16[16,4224]{1,0:T(8,128)(2,1)} %get-tuple-element.273), channel_id=1, source_target_pairs={{0,12},{1,13},{2,14},{3,15},{4,8},{5,9},{6,10},{7,11},{8,4},{9,5},... | collective-permute-start | bytes 405512 | tf_op jit(solution)/shard_map/ppermute | solution.py:39
  8.1 13.6 %collective-permute-start.3 = (bf16[16,4224]{1,0:T(8,128)(2,1)}, bf16[16,4224]{1,0:T(8,128)(2,1)S(1)}, u32[]{:S(2)}, u32[]{:S(2)}) collective-permute-start(bf16[16,4224]{1,0:T(8,128)(2,1)} %get-tuple-element.273), channel_id=1, source_target_pairs={{0,8},{1,9},{2,10},{3,11},{4,12},{5,13},{6,14},{7,15},{8,0},{9,1},... | collective-permute-start | bytes 405512 | tf_op jit(solution)/shard_map/ppermute | solution.py:39
  20.1 13.6 %collective-permute-start.1 = (bf16[32,4224]{1,0:T(8,128)(2,1)S(1)}, bf16[32,4224]{1,0:T(8,128)(2,1)S(1)}, u32[]{:S(2)}, u32[]{:S(2)}) collective-permute-start(bf16[32,4224]{1,0:T(8,128)(2,1)S(1)} %pad_maximum_fusion.2), channel_id=1, source_target_pairs={{0,2},{1,3},{2,0},{3,1},{4,6},{5,7},{6,4},{7,5},{8,10},{9,11},{10,... | collective-permute-start | bytes 811016 | tf_op jit(solution)/shard_map/ppermute | solution.py:39
  21.7 11.9 %collective-permute-start.5 = (bf16[32,4224]{1,0:T(8,128)(2,1)S(1)}, bf16[32,4224]{1,0:T(8,128)(2,1)S(1)}, u32[]{:S(2)}, u32[]{:S(2)}) collective-permute-start(bf16[32,4224]{1,0:T(8,128)(2,1)S(1)} %pad_maximum_fusion.3), channel_id=1, source_target_pairs={{0,2},{1,3},{2,0},{3,1},{4,6},{5,7},{6,4},{7,5},{8,10},{9,11},{10,... | collective-permute-start | bytes 811016 | tf_op jit(solution)/shard_map/ppermute | solution.py:39
  33.6 11.9 %collective-permute-start.6 = (bf16[64,4224]{1,0:T(8,128)(2,1)S(1)}, bf16[64,4224]{1,0:T(8,128)(2,1)S(1)}, u32[]{:S(2)}, u32[]{:S(2)}) collective-permute-start(bf16[64,4224]{1,0:T(8,128)(2,1)S(1)} %constant_dynamic-update-slice_fusion.2), channel_id=1, source_target_pairs={{0,1},{1,0},{2,3},{3,2},{4,5},{5,4},{6,7},{7,6},{8,9},{9,8},{10,11... | collective-permute-start | bytes 1622024 | tf_op jit(solution)/shard_map/ppermute | solution.py:39
  33.7 13.2 %collective-permute-start.2 = (bf16[64,4224]{1,0:T(8,128)(2,1)S(1)}, bf16[64,4224]{1,0:T(8,128)(2,1)S(1)}, u32[]{:S(2)}, u32[]{:S(2)}) collective-permute-start(bf16[64,4224]{1,0:T(8,128)(2,1)S(1)} %constant_dynamic-update-slice_fusion), channel_id=1, source_target_pairs={{0,1},{1,0},{2,3},{3,2},{4,5},{5,4},{6,7},{7,6},{8,9},{9,8},{10,11... | collective-permute-start | bytes 1622024 | tf_op jit(solution)/shard_map/ppermute | solution.py:39
  34.3 15.6 %collective-permute-start.9 = (bf16[16,4096]{1,0:T(8,128)(2,1)S(1)}, bf16[16,4096]{1,0:T(8,128)(2,1)}, u32[]{:S(2)}, u32[]{:S(2)}) collective-permute-start(bf16[16,4096]{1,0:T(8,128)(2,1)S(1)} %copy-done.5), channel_id=1, source_target_pairs={{0,4},{1,5},{2,6},{3,7},{4,0},{5,1},{6,2},{7,3},{8,12},{9,13},{10,... | collective-permute-start | bytes 393224 | tf_op jit(solution)/shard_map/ppermute | solution.py:39
  37.7 13.1 %collective-permute-start.11 = (bf16[16,4096]{1,0:T(8,128)(2,1)S(1)}, bf16[16,4096]{1,0:T(8,128)(2,1)}, u32[]{:S(2)}, u32[]{:S(2)}) collective-permute-start(bf16[16,4096]{1,0:T(8,128)(2,1)S(1)} %copy-done.5), channel_id=1, source_target_pairs={{0,12},{1,13},{2,14},{3,15},{4,8},{5,9},{6,10},{7,11},{8,4},{9,5},... | collective-permute-start | bytes 393224 | tf_op jit(solution)/shard_map/ppermute | solution.py:39
  42.1 11.1 %collective-permute-start.10 = (bf16[16,4096]{1,0:T(8,128)(2,1)S(1)}, bf16[16,4096]{1,0:T(8,128)(2,1)}, u32[]{:S(2)}, u32[]{:S(2)}) collective-permute-start(bf16[16,4096]{1,0:T(8,128)(2,1)S(1)} %copy-done.5), channel_id=1, source_target_pairs={{0,8},{1,9},{2,10},{3,11},{4,12},{5,13},{6,14},{7,15},{8,0},{9,1},... | collective-permute-start | bytes 393224 | tf_op jit(solution)/shard_map/ppermute | solution.py:39
  57.7 11.1 %collective-permute-start.14 = (bf16[32,4096]{1,0:T(8,128)(2,1)S(1)}, bf16[32,4096]{1,0:T(8,128)(2,1)S(1)}, u32[]{:S(2)}, u32[]{:S(2)}) collective-permute-start(bf16[32,4096]{1,0:T(8,128)(2,1)S(1)} %pad_maximum_fusion.4), channel_id=1, source_target_pairs={{0,2},{1,3},{2,0},{3,1},{4,6},{5,7},{6,4},{7,5},{8,10},{9,11},{10,... | collective-permute-start | bytes 786440 | tf_op jit(solution)/shard_map/ppermute | solution.py:39
  61.1 11.6 %collective-permute-start.15 = (bf16[32,4096]{1,0:T(8,128)(2,1)S(1)}, bf16[32,4096]{1,0:T(8,128)(2,1)S(1)}, u32[]{:S(2)}, u32[]{:S(2)}) collective-permute-start(bf16[32,4096]{1,0:T(8,128)(2,1)S(1)} %pad_maximum_fusion.5), channel_id=1, source_target_pairs={{0,2},{1,3},{2,0},{3,1},{4,6},{5,7},{6,4},{7,5},{8,10},{9,11},{10,... | collective-permute-start | bytes 786440 | tf_op jit(solution)/shard_map/ppermute | solution.py:39
  78.5 29.9 %collective-permute-start.22 = (bf16[16,4096]{1,0:T(8,128)(2,1)}, bf16[16,4096]{1,0:T(8,128)(2,1)S(1)}, u32[]{:S(2)}, u32[]{:S(2)}) collective-permute-start(bf16[16,4096]{1,0:T(8,128)(2,1)} %split.81), channel_id=1, source_target_pairs={{16,20},{17,21},{18,22},{19,23},{20,16},{21,17},{22,18},{23,19},{2... | collective-permute-start | bytes 393224 | tf_op jit(solution)/shard_map/ppermute | solution.py:39
  79.1 29.3 %collective-permute-start.23 = (bf16[16,4096]{1,0:T(8,128)(2,1)}, bf16[16,4096]{1,0:T(8,128)(2,1)}, u32[]{:S(2)}, u32[]{:S(2)}) collective-permute-start(bf16[16,4096]{1,0:T(8,128)(2,1)} %get-tuple-element.333), channel_id=1, source_target_pairs={{16,24},{17,25},{18,26},{19,27},{20,28},{21,29},{22,30},{23,31},{2... | collective-permute-start | bytes 393224 | tf_op jit(solution)/shard_map/ppermute | solution.py:39
  80.5 28.0 %collective-permute-start.24 = (bf16[16,4096]{1,0:T(8,128)(2,1)}, bf16[16,4096]{1,0:T(8,128)(2,1)}, u32[]{:S(2)}, u32[]{:S(2)}) collective-permute-start(bf16[16,4096]{1,0:T(8,128)(2,1)} %get-tuple-element.334), channel_id=1, source_target_pairs={{16,28},{17,29},{18,30},{19,31},{20,24},{21,25},{22,26},{23,27},{2... | collective-permute-start | bytes 393224 | tf_op jit(solution)/shard_map/ppermute | solution.py:39
  110.3 20.7 %collective-permute-start.25 = (bf16[16,4096]{1,0:T(8,128)(2,1)S(1)}, bf16[16,4096]{1,0:T(8,128)(2,1)S(1)}, u32[]{:S(2)}, u32[]{:S(2)}) collective-permute-start(bf16[16,4096]{1,0:T(8,128)(2,1)S(1)} %add_convert_fusion.9), channel_id=1, source_target_pairs={{16,0},{17,1},{18,2},{19,3},{20,4},{21,5},{22,6},{23,7},{24,8},{25... | collective-permute-start | bytes 393224 | tf_op jit(solution)/shard_map/ppermute | solution.py:15
  115.2 11.1 %collective-permute-start.21 = (bf16[32,4096]{1,0:T(8,128)(2,1)S(1)}, bf16[32,4096]{1,0:T(8,128)(2,1)S(1)}, u32[]{:S(2)}, u32[]{:S(2)}) collective-permute-start(bf16[32,4096]{1,0:T(8,128)(2,1)S(1)} %split.99), channel_id=1, source_target_pairs={{0,2},{1,3},{2,0},{3,1},{4,6},{5,7},{6,4},{7,5},{8,10},{9,11},{10,... | collective-permute-start | bytes 786440 | tf_op jit(solution)/shard_map/ppermute | solution.py:39
  119.9 11.1 %collective-permute-start.19 = (bf16[32,4096]{1,0:T(8,128)(2,1)S(1)}, bf16[32,4096]{1,0:T(8,128)(2,1)S(1)}, u32[]{:S(2)}, u32[]{:S(2)}) collective-permute-start(bf16[32,4096]{1,0:T(8,128)(2,1)S(1)} %split.97), channel_id=1, source_target_pairs={{0,2},{1,3},{2,0},{3,1},{4,6},{5,7},{6,4},{7,5},{8,10},{9,11},{10,... | collective-permute-start | bytes 786440 | tf_op jit(solution)/shard_map/ppermute | solution.py:39
  131.0 10.8 %collective-permute-start.30 = (bf16[16,4096]{1,0:T(8,128)(2,1)S(1)}, bf16[16,4096]{1,0:T(8,128)(2,1)S(1)}, u32[]{:S(2)}, u32[]{:S(2)}) collective-permute-start(bf16[16,4096]{1,0:T(8,128)(2,1)S(1)} %collective-permute-done.25), channel_id=1, source_target_pairs={{0,12},{1,13},{2,14},{3,15},{4,8},{5,9},{6,10},{7,11},{8,4},{9,5},... | collective-permute-start | bytes 393224 | tf_op jit(solution)/shard_map/ppermute | solution.py:39
  135.4 10.0 %collective-permute-start.29 = (bf16[16,4096]{1,0:T(8,128)(2,1)S(1)}, bf16[16,4096]{1,0:T(8,128)(2,1)S(1)}, u32[]{:S(2)}, u32[]{:S(2)}) collective-permute-start(bf16[16,4096]{1,0:T(8,128)(2,1)S(1)} %collective-permute-done.25), channel_id=1, source_target_pairs={{0,8},{1,9},{2,10},{3,11},{4,12},{5,13},{6,14},{7,15},{8,0},{9,1},... | collective-permute-start | bytes 393224 | tf_op jit(solution)/shard_map/ppermute | solution.py:39
  137.3 11.5 %collective-permute-start.26 = (bf16[16,4096]{1,0:T(8,128)(2,1)S(1)}, bf16[16,4096]{1,0:T(8,128)(2,1)S(1)}, u32[]{:S(2)}, u32[]{:S(2)}) collective-permute-start(bf16[16,4096]{1,0:T(8,128)(2,1)S(1)} %collective-permute-done.25), channel_id=1, source_target_pairs={{0,4},{1,5},{2,6},{3,7},{4,0},{5,1},{6,2},{7,3},{8,12},{9,13},{10,... | collective-permute-start | bytes 393224 | tf_op jit(solution)/shard_map/ppermute | solution.py:39
  145.4 18.4 %collective-permute-start.31 = (bf16[32,4096]{1,0:T(8,128)(2,1)S(1)}, bf16[32,4096]{1,0:T(8,128)(2,1)S(1)}, u32[]{:S(2)}, u32[]{:S(2)}) collective-permute-start(bf16[32,4096]{1,0:T(8,128)(2,1)S(1)} %pad_maximum_fusion.7), channel_id=1, source_target_pairs={{0,2},{1,3},{2,0},{3,1},{4,6},{5,7},{6,4},{7,5},{8,10},{9,11},{10,... | collective-permute-start | bytes 786440 | tf_op jit(solution)/shard_map/ppermute | solution.py:39
  148.9 12.3 %collective-permute-start.27 = (bf16[32,4096]{1,0:T(8,128)(2,1)S(1)}, bf16[32,4096]{1,0:T(8,128)(2,1)S(1)}, u32[]{:S(2)}, u32[]{:S(2)}) collective-permute-start(bf16[32,4096]{1,0:T(8,128)(2,1)S(1)} %pad_maximum_fusion.6), channel_id=1, source_target_pairs={{0,2},{1,3},{2,0},{3,1},{4,6},{5,7},{6,4},{7,5},{8,10},{9,11},{10,... | collective-permute-start | bytes 786440 | tf_op jit(solution)/shard_map/ppermute | solution.py:39
  161.9 15.9 %collective-permute-start.28 = (bf16[64,4096]{1,0:T(8,128)(2,1)}, bf16[64,4096]{1,0:T(8,128)(2,1)}, u32[]{:S(2)}, u32[]{:S(2)}) collective-permute-start(bf16[64,4096]{1,0:T(8,128)(2,1)} %constant_dynamic-update-slice_fusion.5), channel_id=1, source_target_pairs={{0,1},{1,0},{2,3},{3,2},{4,5},{5,4},{6,7},{7,6},{8,9},{9,8},{10,11... | collective-permute-start | bytes 1572872 | tf_op jit(solution)/shard_map/ppermute | solution.py:39
  164.6 13.3 %collective-permute-start.32 = (bf16[64,4096]{1,0:T(8,128)(2,1)}, bf16[64,4096]{1,0:T(8,128)(2,1)}, u32[]{:S(2)}, u32[]{:S(2)}) collective-permute-start(bf16[64,4096]{1,0:T(8,128)(2,1)} %constant_dynamic-update-slice_fusion.8), channel_id=1, source_target_pairs={{0,1},{1,0},{2,3},{3,2},{4,5},{5,4},{6,7},{7,6},{8,9},{9,8},{10,11... | collective-permute-start | bytes 1572872 | tf_op jit(solution)/shard_map/ppermute | solution.py:39
  167.7 29.7 %collective-permute-start.35 = (bf16[16,4096]{1,0:T(8,128)(2,1)S(1)}, bf16[16,4096]{1,0:T(8,128)(2,1)}, u32[]{:S(2)}, u32[]{:S(2)}) collective-permute-start(bf16[16,4096]{1,0:T(8,128)(2,1)S(1)} %split.85), channel_id=1, source_target_pairs={{0,4},{1,5},{2,6},{3,7},{4,0},{5,1},{6,2},{7,3},{8,12},{9,13},{10,... | collective-permute-start | bytes 393224 | tf_op jit(solution)/shard_map/ppermute | solution.py:39
  169.6 27.8 %collective-permute-start.36 = (bf16[16,4096]{1,0:T(8,128)(2,1)}, bf16[16,4096]{1,0:T(8,128)(2,1)}, u32[]{:S(2)}, u32[]{:S(2)}) collective-permute-start(bf16[16,4096]{1,0:T(8,128)(2,1)} %get-tuple-element.331), channel_id=1, source_target_pairs={{0,8},{1,9},{2,10},{3,11},{4,12},{5,13},{6,14},{7,15},{8,0},{9,1},... | collective-permute-start | bytes 393224 | tf_op jit(solution)/shard_map/ppermute | solution.py:39
  174.6 22.9 %collective-permute-start.37 = (bf16[16,4096]{1,0:T(8,128)(2,1)}, bf16[16,4096]{1,0:T(8,128)(2,1)}, u32[]{:S(2)}, u32[]{:S(2)}) collective-permute-start(bf16[16,4096]{1,0:T(8,128)(2,1)} %get-tuple-element.332), channel_id=1, source_target_pairs={{0,12},{1,13},{2,14},{3,15},{4,8},{5,9},{6,10},{7,11},{8,4},{9,5},... | collective-permute-start | bytes 393224 | tf_op jit(solution)/shard_map/ppermute | solution.py:39
  203.9 11.2 %collective-permute-start.40 = (bf16[32,4096]{1,0:T(8,128)(2,1)S(1)}, bf16[32,4096]{1,0:T(8,128)(2,1)S(1)}, u32[]{:S(2)}, u32[]{:S(2)}) collective-permute-start(bf16[32,4096]{1,0:T(8,128)(2,1)S(1)} %split.93), channel_id=1, source_target_pairs={{0,2},{1,3},{2,0},{3,1},{4,6},{5,7},{6,4},{7,5},{8,10},{9,11},{10,... | collective-permute-start | bytes 786440 | tf_op jit(solution)/shard_map/ppermute | solution.py:39
  207.5 14.0 %collective-permute-start.38 = (bf16[32,4096]{1,0:T(8,128)(2,1)S(1)}, bf16[32,4096]{1,0:T(8,128)(2,1)S(1)}, u32[]{:S(2)}, u32[]{:S(2)}) collective-permute-start(bf16[32,4096]{1,0:T(8,128)(2,1)S(1)} %split.89), channel_id=1, source_target_pairs={{0,2},{1,3},{2,0},{3,1},{4,6},{5,7},{6,4},{7,5},{8,10},{9,11},{10,... | collective-permute-start | bytes 786440 | tf_op jit(solution)/shard_map/ppermute | solution.py:39
  215.2 13.0 %collective-permute-start.41 = (bf16[16,4096]{1,0:T(8,128)(2,1)S(1)}, bf16[16,4096]{1,0:T(8,128)(2,1)S(1)}, u32[]{:S(2)}, u32[]{:S(2)}) collective-permute-start(bf16[16,4096]{1,0:T(8,128)(2,1)S(1)} %get-tuple-element.329), channel_id=1, source_target_pairs={{0,8},{1,9},{2,10},{3,11},{4,12},{5,13},{6,14},{7,15},{8,0},{9,1},... | collective-permute-start | bytes 393224 | tf_op jit(solution)/shard_map/ppermute | solution.py:39
  217.2 10.9 %collective-permute-start.42 = (bf16[16,4096]{1,0:T(8,128)(2,1)S(1)}, bf16[16,4096]{1,0:T(8,128)(2,1)S(1)}, u32[]{:S(2)}, u32[]{:S(2)}) collective-permute-start(bf16[16,4096]{1,0:T(8,128)(2,1)S(1)} %get-tuple-element.330), channel_id=1, source_target_pairs={{0,12},{1,13},{2,14},{3,15},{4,8},{5,9},{6,10},{7,11},{8,4},{9,5},... | collective-permute-start | bytes 393224 | tf_op jit(solution)/shard_map/ppermute | solution.py:39
  (23 other events, 166.9 us)

commit v4 on v3

--- a/solution.py
+++ b/solution.py
@@ -211,39 +211,90 @@
     return total
 
 
+TILE = 1024
+
+
+def tiles_of(width):
+    return [slice(lower, lower + TILE) for lower in range(0, width, TILE)]
+
+
+def reads(pairs, sems):
+    return [pltpu.make_async_copy(src, dst, sems.at[i]) for i, (src, dst) in enumerate(pairs)]
+
+
+def row_reads(refs, count, width, rows, table):
+    part = rows.shape[0] // count
+    spare = table.shape[1]
+    here = [pl.ds(part * i, part) for i in range(count)]
+    wide_pairs = [(refs[i].at[:, pl.ds(0, width)], rows.at[here[i]]) for i in range(count)]
+    thin_pairs = [
+        (refs[count + i].at[:, pl.ds(width, spare)], table.at[here[i]]) for i in range(count)
+    ]
+    return wide_pairs + thin_pairs
+
+
+def weight_reads(gu_ref, dn_ref, gu, dn):
+    cuts = [pl.ds(lower, TILE) for lower in range(0, dn.shape[1], TILE)]
+    return [(gu_ref.at[:, cut], gu.at[:, cut]) for cut in cuts], [
+        (dn_ref.at[:, cut], dn.at[:, cut]) for cut in cuts
+    ]
+
+
+def added(total, product):
+    return product if total is None else total + product
+
+
 def ffn_kernel(place, *refs, count, experts, changed):
-    rows_refs, table_refs = refs[:count], refs[count : 2 * count]
     gu_ref, dn_ref = refs[2 * count : 2 * count + 2]
-    refs = refs[2 * count + 2 :]
+    extra = 5 if changed else 0
+    extra_refs = refs[2 * count + 2 : 2 * count + 2 + extra]
+    refs_left = refs[2 * count + 2 + extra :]
+    out_refs = refs_left[:count]
+    rows, table, gu, dn = refs_left[count : count + 4]
+    extras = refs_left[count + 4 : count + 4 + extra]
+    sems = refs_left[count + 4 + extra]
+    width = dn.shape[1]
+    cuts = tiles_of(width)
+    first = row_reads(refs, count, width, rows, table)
+    gu_pairs, dn_pairs = weight_reads(gu_ref, dn_ref, gu, dn)
+    more = list(zip(extra_refs, extras))
+    copies = reads(first + more[:1] + gu_pairs + more[1:] + dn_pairs, sems)
+    for copy in copies:
+        copy.start()
+    done = len(first) + len(more[:1])
+    for copy in copies[:done]:
+        copy.wait()
+    active = upward = alike = None
+    for cut in cuts:
+        copies[done].wait()
+        done += 1
+        active = added(active, nn(rows[:, cut], gu[0, cut]))
+        upward = added(upward, nn(rows[:, cut], gu[1, cut]))
+        if changed:
+            alike = added(alike, nn(rows[:, cut], extras[0][cut]))
+    for copy in copies[done : done + len(more[1:])]:
+        copy.wait()
+    done += len(more[1:])
     if changed:
-        turned_ref, pulls_ref, sent_ref, hidden_turned_ref, rates_ref = refs[:5]
-        refs = refs[5:]
-    out_refs, rows = refs[:count], refs[count]
-    part, width = rows_refs[0].shape
-    for i in range(count):
-        rows[part * i : part * (i + 1), :] = rows_refs[i][...]
-    active = nn(rows[...], gu_ref[0])
-    upward = nn(rows[...], gu_ref[1])
+        turned, sent, hidden_turned, rates, pulls = extras
+        active = active - fine(alike, sent[0], 2) * rates[0:1]
+        upward = upward - fine(alike, sent[1], 2) * rates[1:2]
+    hidden = (active * jax.nn.sigmoid(active) * upward).astype(jnp.bfloat16)
     if changed:
-        alike = nn(rows[...], turned_ref[...])
-        active = active - fine(alike, sent_ref[0], 2) * rates_ref[0:1]
-        upward = upward - fine(alike, sent_ref[1], 2) * rates_ref[1:2]
-    swish = active * jax.nn.sigmoid(active)
-    hidden = (swish * upward).astype(jnp.bfloat16)
-    if changed:
-        scaled = hidden.astype(jnp.float32) * rates_ref[2:3]
-        mixed = parts_of(fine(scaled, hidden_turned_ref[...], 2), 2)
-    gates = [pick_gates(table_refs[i][...], place[0], experts) for i in range(count)]
-    tile = 1024
-    for lower in range(0, width, tile):
-        cut = slice(lower, lower + tile)
-        out = nn(hidden, dn_ref[:, cut])
+        scaled = hidden.astype(jnp.float32) * rates[2:3]
+        mixed = parts_of(fine(scaled, hidden_turned[...], 2), 2)
+    gates = pick_gates(table[...], place[0], experts)
+    part = rows.shape[0] // count
+    for cut in cuts:
+        copies[done].wait()
+        done += 1
+        out = nn(hidden, dn[:, cut])
         if changed:
             for one in mixed:
-                out = out - nn(one, pulls_ref[:, cut])
+                out = out - nn(one, pulls[:, cut])
+        out = (gates * out).astype(jnp.bfloat16)
         for i in range(count):
-            here = out[part * i : part * (i + 1)]
-            out_refs[i][:, cut] = (gates[i] * here).astype(jnp.bfloat16)
+            out_refs[i][:, cut] = out[part * i : part * (i + 1)]
 
 
 def ffn_call(place, pieces, tables, planes, weights_dn, experts, change=()):
@@ -251,46 +302,66 @@
     part = pieces[0].shape[0]
     hidden_count, width = weights_dn.shape
     row_count = part * count
+    anywhere = pl.BlockSpec(memory_space=pl.ANY)
     whole = pl.BlockSpec(memory_space=pltpu.VMEM)
     return pl.pallas_call(
         functools.partial(ffn_kernel, count=count, experts=experts, changed=bool(change)),
-        in_specs=[pl.BlockSpec(memory_space=pltpu.SMEM)] + [whole] * (2 * count + 2 + len(change)),
+        in_specs=[pl.BlockSpec(memory_space=pltpu.SMEM)]
+        + [anywhere] * (2 * count + 2 + len(change)),
         out_specs=[whole] * count,
-        scratch_shapes=[pltpu.VMEM((row_count, width), jnp.bfloat16)],
+        scratch_shapes=[
+            pltpu.VMEM((row_count, width), jnp.bfloat16),
+            pltpu.VMEM((row_count, tables[0].shape[1] - width), jnp.bfloat16),
+            pltpu.VMEM(planes.shape, jnp.bfloat16),
+            pltpu.VMEM(weights_dn.shape, jnp.bfloat16),
+        ]
+        + [pltpu.VMEM(one.shape, one.dtype) for one in change]
+        + [pltpu.SemaphoreType.DMA((2 * count + len(change) + 2 * (width // TILE),))],
         out_shape=[jax.ShapeDtypeStruct((part, width), jnp.bfloat16)] * count,
         compiler_params=pltpu.CompilerParams(vmem_limit_bytes=44 << 20),
         cost_estimate=pl.CostEstimate(
-            flops=6 * row_count * hidden_count * width if change else 1,
-            bytes_accessed=4 * row_count * width if change else 1,
-            transcendentals=row_count * hidden_count if change else 1,
+            flops=6 * row_count * hidden_count * width,
+            bytes_accessed=6 * hidden_count * width,
+            transcendentals=row_count * hidden_count,
         ),
         name="ffn_changed" if change else "ffn",
     )(place, *pieces, *tables, planes, weights_dn, *change)
 
 
 def learn_kernel(place, *refs, count, experts, rates):
-    rows_refs, table_refs = refs[:count], refs[count : 2 * count]
     cot_refs = refs[2 * count : 3 * count]
     gu_ref, dn_ref = refs[3 * count : 3 * count + 2]
-    dx_refs = refs[3 * count + 2 : 4 * count + 2]
-    turned, pulls, sent, hidden_turned_ref, rates_ref = refs[4 * count + 2 : 4 * count + 7]
-    rows, pulls_turned = refs[4 * count + 7 :]
-    part = rows_refs[0].shape[0]
-    hidden_count, width = dn_ref.shape
-    tile = 1024
-    cuts = [slice(lower, lower + tile) for lower in range(0, width, tile)]
-    for i in range(count):
-        here = slice(part * i, part * (i + 1))
-        gates = pick_gates(table_refs[i][...], place[0], experts)
-        rows[here, :] = rows_refs[i][...]
-        pulls[here, :] = (gates * cot_refs[i][...].astype(jnp.float32)).astype(jnp.bfloat16)
+    dx_ref, turned, sent, hidden_turned_ref, rates_ref, pulls = refs[3 * count + 2 : 3 * count + 8]
+    rows, table, cots, pulls_turned, gu, dn, sems = refs[3 * count + 8 :]
+    hidden_count, width = dn.shape
+    part = rows.shape[0] // count
+    cuts = tiles_of(width)
+    first = row_reads(refs, count, width, rows, table)
+    first += [(cot_refs[i], cots.at[pl.ds(part * i, part)]) for i in range(count)]
+    gu_pairs, dn_pairs = weight_reads(gu_ref, dn_ref, gu, dn)
+    both = [pair for pairs in zip(gu_pairs, dn_pairs) for pair in pairs]
+    copies = reads(first + both, sems)
+    for copy in copies:
+        copy.start()
+    done = len(first)
+    for copy in copies[:done]:
+        copy.wait()
+    gates = pick_gates(table[...], place[0], experts)
     for cut in cuts:
+        pulls[:, cut] = (gates * cots[:, cut].astype(jnp.float32)).astype(jnp.bfloat16)
         turned[cut, :] = rows[:, cut].T
         pulls_turned[cut, :] = pulls[:, cut].T
-
-    active = nn(rows[...], gu_ref[0])
-    upward = nn(rows[...], gu_ref[1])
-    back = nn(dn_ref[...], pulls_turned[...]).T
+    alike_rows = nn(rows[...], turned[...])
+    alike_pulls = nn(pulls[...], pulls_turned[...])
+    active = upward = back = None
+    for cut in cuts:
+        copies[done].wait()
+        copies[done + 1].wait()
+        done += 2
+        active = added(active, nn(rows[:, cut], gu[0, cut]))
+        upward = added(upward, nn(rows[:, cut], gu[1, cut]))
+        back = added(back, nn(dn[:, cut], pulls_turned[cut]))
+    back = back.T
     sigma = jax.nn.sigmoid(active)
     swish = active * sigma
     hidden = (swish * upward).astype(jnp.bfloat16)
@@ -303,49 +374,56 @@
     d_upward_turned = d_upward.T
 
     for cut in cuts:
-        done = nn(gu_ref[0, cut, :], d_active_turned) + nn(gu_ref[1, cut, :], d_upward_turned)
-        done = done.T.astype(jnp.bfloat16)
-        for i in range(count):
-            dx_refs[i][:, cut] = done[part * i : part * (i + 1)]
+        out = nn(gu[0, cut], d_active_turned) + nn(gu[1, cut], d_upward_turned)
+        dx_ref[:, cut] = out.T.astype(jnp.bfloat16)
 
     def mean_square(alike, factor):
         wide_factor = factor.astype(jnp.float32)
         squares = jnp.sum(wide_factor * fine(alike, factor, 3), axis=0, keepdims=True)
         return jnp.maximum(squares, 0.0) / width
 
-    alike = nn(rows[...], turned[...])
-    rates_ref[0:1] = rates[0] / jnp.sqrt(mean_square(alike, d_active) + EPSILON)
-    rates_ref[1:2] = rates[0] / jnp.sqrt(mean_square(alike, d_upward) + EPSILON)
-    alike = nn(pulls[...], pulls_turned[...])
-    rates_ref[2:3] = rates[1] / jnp.sqrt(mean_square(alike, hidden) + EPSILON)
-
-
-def learn_call(place, pieces, tables, cots, planes, weights_dn, experts, rates):
-    count = len(pieces)
-    part = pieces[0].shape[0]
-    hidden_count, width = weights_dn.shape
-    row_count = part * count
-    whole = pl.BlockSpec(memory_space=pltpu.VMEM)
-    out_shape = [jax.ShapeDtypeStruct((part, width), jnp.bfloat16)] * count + [
+    rates_ref[0:1] = rates[0] / jnp.sqrt(mean_square(alike_rows, d_active) + EPSILON)
+    rates_ref[1:2] = rates[0] / jnp.sqrt(mean_square(alike_rows, d_upward) + EPSILON)
+    rates_ref[2:3] = rates[1] / jnp.sqrt(mean_square(alike_pulls, hidden) + EPSILON)
+    rates_ref[3:8] = jnp.zeros((5, hidden_count), jnp.float32)
+
+
+def learn_shapes(row_count, hidden_count, width):
+    return [
+        jax.ShapeDtypeStruct((row_count, width), jnp.bfloat16),
         jax.ShapeDtypeStruct((width, row_count), jnp.bfloat16),
-        jax.ShapeDtypeStruct((row_count, width), jnp.bfloat16),
         jax.ShapeDtypeStruct((2, row_count, hidden_count), jnp.bfloat16),
         jax.ShapeDtypeStruct((hidden_count, row_count), jnp.bfloat16),
         jax.ShapeDtypeStruct((8, hidden_count), jnp.float32),
+        jax.ShapeDtypeStruct((row_count, width), jnp.bfloat16),
     ]
+
+
+def learn_call(place, pieces, tables, cots, planes, weights_dn, experts, rates):
+    count = len(pieces)
+    hidden_count, width = weights_dn.shape
+    row_count = pieces[0].shape[0] * count
+    anywhere = pl.BlockSpec(memory_space=pl.ANY)
+    whole = pl.BlockSpec(memory_space=pltpu.VMEM)
+    out_shape = learn_shapes(row_count, hidden_count, width)
     return pl.pallas_call(
         functools.partial(learn_kernel, count=count, experts=experts, rates=rates),
-        in_specs=[pl.BlockSpec(memory_space=pltpu.SMEM)] + [whole] * (3 * count + 2),
+        in_specs=[pl.BlockSpec(memory_space=pltpu.SMEM)] + [anywhere] * (3 * count + 2),
         out_specs=[whole] * len(out_shape),
         scratch_shapes=[
             pltpu.VMEM((row_count, width), jnp.bfloat16),
+            pltpu.VMEM((row_count, tables[0].shape[1] - width), jnp.bfloat16),
+            pltpu.VMEM((row_count, width), jnp.bfloat16),
             pltpu.VMEM((width, row_count), jnp.bfloat16),
+            pltpu.VMEM(planes.shape, jnp.bfloat16),
+            pltpu.VMEM(weights_dn.shape, jnp.bfloat16),
+            pltpu.SemaphoreType.DMA((3 * count + 2 * (width // TILE),)),
         ],
         out_shape=out_shape,
-        compiler_params=pltpu.CompilerParams(vmem_limit_bytes=44 << 20),
+        compiler_params=pltpu.CompilerParams(vmem_limit_bytes=48 << 20),
         cost_estimate=pl.CostEstimate(
             flops=12 * row_count * hidden_count * width,
-            bytes_accessed=8 * row_count * width,
+            bytes_accessed=6 * hidden_count * width,
             transcendentals=row_count * hidden_count,
         ),
         name="learn",
@@ -430,71 +508,45 @@
     )
     if small:
         near, away = send_z(block, (0, 1))
-        near, planes, cotangent = tied(near, planes, cotangent)
-        cot_near, cot_away = send_z(cotangent, (0,))
+        near, planes = tied(near, planes)
         near, away = send_y(near, away, (0, 1))
+        near, cotangent = tied(near, cotangent)
         every = send_core(near, away, (0, 1))
-
-        def blank(*shape, of=jnp.bfloat16):
-            return unset(jax.ShapeDtypeStruct(shape, of))
-
-        rows = [piece[:, :model_width] for piece in every]
-        gates = [piece[:, model_width:] for piece in every]
-        part = lax.cond(
-            is_learner,
-            lambda r, t, g, d: [blank(*one.shape) for one in r],
-            lambda r, t, g, d: list(ffn_call(first_place, r, t, g, d, ep_count)),
-            rows,
-            gates,
-            planes,
-            own_dn,
-        )
-        near, away = sum_core(part, (1,))
-        near, away, cot_near, cot_away = tied(near, away, cot_near, cot_away)
-        cot_near, cot_away = send_y(cot_near, cot_away, (0,))
-        near, away = sum_y(near, away, (1,))
-        near, away, cot_near, cot_away = tied(near, away, cot_near, cot_away)
-        cots = send_core(cot_near, cot_away, (0,))
+        cots = send_core(*send_y(*send_z(cotangent, (0,)), (0,)), (0,))
+        hidden_count = own_dn.shape[0]
+        part_shape = jax.ShapeDtypeStruct(cots[0].shape, jnp.bfloat16)
+
+        def learn(every, cots, planes, own_dn):
+            out = learn_call(first_place, every, every, cots, planes, own_dn, ep_count, rates)
+            return ([unset(part_shape)] * 4, list(out))
+
+        def decode(every, cots, planes, own_dn):
+            out = ffn_call(first_place, every, every, planes, own_dn, ep_count)
+            shapes = learn_shapes(total_rows, hidden_count, model_width)
+            return (list(out), [unset(one) for one in shapes])
+
+        part, learned = lax.cond(is_learner, learn, decode, every, cots, planes, own_dn)
+        dx_part = across(learned[0], 0, 1)
+        near, away = sum_y(*sum_core(part, (1,)), (1,))
         current = (base + sum_z(near, away, (1,))).astype(jnp.bfloat16)
         hopped = across(current, 1, 0)
-        hidden_count = own_dn.shape[0]
-        learned = lax.cond(
-            is_learner,
-            lambda r, t, c, g, d: list(learn_call(first_place, r, t, c, g, d, ep_count, rates)),
-            lambda r, t, c, g, d: [blank(*one.shape) for one in r]
-            + [
-                blank(model_width, total_rows),
-                blank(total_rows, model_width),
-                blank(2, total_rows, hidden_count),
-                blank(hidden_count, total_rows),
-                blank(8, hidden_count, of=jnp.float32),
-            ],
-            rows,
-            gates,
-            cots,
-            planes,
-            own_dn,
-        )
-        near, away = sum_core(learned[:4], (0,))
-        near, away = sum_y(near, away, (0,))
-        near, away, hopped = tied(near, away, hopped)
-        dx_sum = sum_z(near, away, (0,))
-        near, away = send_z(hopped, (0,))
-        near, away = send_y(near, away, (0,))
+        near, away = send_y(*send_z(hopped, (0,)), (0,))
         arrived = send_core(near, away, (0,))
         fresh_part = lax.cond(
             is_learner,
             lambda r, t, g, d, *c: list(ffn_call(fresh_place, r, t, g, d, ep_count, c)),
-            lambda r, t, g, d, *c: [blank(*one.shape) for one in r],
+            lambda r, t, g, d, *c: [unset(one) for one in r],
             arrived,
-            gates,
+            every,
             planes,
             own_dn,
-            *learned[4:],
+            *learned[1:],
         )
-        near, away = sum_core(fresh_part, (0,))
-        near, away, dx_sum = tied(near, away, dx_sum)
-        near, away = sum_y(near, away, (0,))
+        fresh_part[3], dx_part = tied(fresh_part[3], dx_part)
+        dx_near, dx_away = sum_y(*sum_core(jnp.split(dx_part, 4, axis=0), (1,)), (1,))
+        dx_sum = sum_z(dx_near, dx_away, (1,)).astype(jnp.bfloat16)
+        dx_sum = across(dx_sum, 1, 0).astype(jnp.float32)
+        near, away = sum_y(*sum_core(fresh_part, (0,)), (0,))
         fresh_sum = sum_z(near, away, (0,))
     else:
         every = [gather(block, device_count, (0, 1))]

time: 237 us -> 212 us (0.89)
  starting transfers between devices: 96.9 us -> 86.4 us
  Pallas kernels: 42.5 us -> 36 us
  other arithmetic: 12.1 us -> 7.25 us
  waiting for transfers between devices: 57.8 us -> 54.7 us
    ppermute x42, starting transfers between devices: 94.3 us -> 76.7 us  [swap(): return lax.ppermute(block, ('grp',) + AXES, pairs)]
    ppermute x2 -> x4, starting transfers between devices: 2.59 us -> 9.76 us  [across(): return lax.ppermute(block, 'grp', [(source, target)])]
    cond x0 -> x11, local copies, waits for them, and re-layouts: none -> 6.93 us
    ppermute x42, waiting for transfers between devices: 54.6 us -> 48.3 us  [swap(): return lax.ppermute(block, ('grp',) + AXES, pairs)]
    slice x8 -> x0, local copies, waits for them, and re-layouts: 4.34 us -> none  [the longest x4 2.54 us: per_device(): rows = [piece[:, :model_width] for piece in every]]
    pallas_call x1, Pallas kernels: 23.1 us -> 19 us  [learn_call(): pl.pallas_call(functools.partial(learn_kernel, count=count, experts=exper...]
    ppermute x2 -> x4, waiting for transfers between devices: 3.19 us -> 6.4 us  [across(): return lax.ppermute(block, 'grp', [(source, target)])]
    unnamed x30 -> x23, local copies, waits for them, and re-layouts: 17.2 us -> 15.3 us
  transfers between devices with their start and end apart: 44 -> 46, of which waited for: 13 -> 13; matrix products, arithmetic and copies ran while one was open for 13% -> 11% of each run, Pallas kernels for 17% -> 7%
where the time goes in v4:
time: 212 us; the launch traced here: 210 us
  starting transfers between devices  86.4 us (41%)
  waiting for transfers between devices  54.7 us (26%)
  Pallas kernels  36 us (17%)
  local copies, waits for them, and re-layouts  25.2 us (12%)
  other arithmetic  7.25 us (3%)
    ppermute x42, starting transfers between devices, swap(): return lax.ppermute(block, ('grp',) + AXES, pairs)  76.7 us
    ppermute x42, waiting for transfers between devices, swap(): return lax.ppermute(block, ('grp',) + AXES, pairs)  48.3 us
    pallas_call x1, Pallas kernels, learn_call(): pl.pallas_call(functools.partial(learn_kernel, count=count, experts=exper...  19 us
    unnamed x23, local copies, waits for them, and re-layouts  15.3 us
    pallas_call x1, Pallas kernels, ffn_call(): pl.pallas_call(functools.partial(ffn_kernel, count=count, experts=experts...  15.1 us
    ppermute x4, starting transfers between devices, across(): return lax.ppermute(block, 'grp', [(source, target)])  9.76 us
    cond x11, local copies, waits for them, and re-layouts  6.93 us
    ppermute x4, waiting for transfers between devices, across(): return lax.ppermute(block, 'grp', [(source, target)])  6.4 us
  transfers between devices with their start and end apart: 46, of which 13 were waited for; matrix products, arithmetic and copies ran while one was open for 11% of the time, Pallas kernels for 7%

profile of v4, /device:TPU:0, one launch (start us, length us, event | category | flops | bytes accessed | tf_op | source)
XLA Modules:
  0.0 210.5 jit_solution(7162408862111934067)
XLA Ops:
  2.6 5.0 %collective-permute-start.4 = (bf16[16,4224]{1,0:T(8,128)(2,1)}, bf16[16,4224]{1,0:T(8,128)(2,1)S(1)}, u32[]{:S(2)}, u32[]{:S(2)}) collective-permute-start(bf16[16,4224]{1,0:T(8,128)(2,1)} %get-tuple-element.187), channel_id=1, source_target_pairs={{0,12},{1,13},{2,14},{3,15},{4,8},{5,9},{6,10},{7,11},{8,4},{9,5},... | collective-permute-start | bytes 405512 | tf_op jit(solution)/shard_map/ppermute | solution.py:39
  8.3 11.9 %copy.12 = bf16[1,1,4096,2,768]{4,2,3,1,0:T(8,128)(2,1)} copy(bf16[1,1,4096,2,768]{4,3,2,1,0:T(2,128)(2,1)} %param.20) | data formatting | bytes 25165824 | tf_op args[7]
  22.5 11.3 %collective-permute-done.1 = bf16[32,4224]{1,0:T(8,128)(2,1)S(1)} collective-permute-done((bf16[32,4224]{1,0:T(8,128)(2,1)S(1)}, bf16[32,4224]{1,0:T(8,128)(2,1)S(1)}, u32[]{:S(2)}, u32[]{:S(2)}) %collective-permute-start.1) | collective-permute-done | bytes 270368 | tf_op jit(solution)/shard_map/ppermute | solution.py:39
  33.8 5.4 %collective-permute-start.11 = (bf16[16,4096]{1,0:T(8,128)(2,1)S(1)}, bf16[16,4096]{1,0:T(8,128)(2,1)S(1)}, u32[]{:S(2)}, u32[]{:S(2)}) collective-permute-start(bf16[16,4096]{1,0:T(8,128)(2,1)S(1)} %copy-done), channel_id=1, source_target_pairs={{0,12},{1,13},{2,14},{3,15},{4,8},{5,9},{6,10},{7,11},{8,4},{9,5},... | collective-permute-start | bytes 393224 | tf_op jit(solution)/shard_map/ppermute | solution.py:39
  41.1 2.8 %collective-permute-start.7 = (bf16[16,4096]{1,0:T(8,128)(2,1)S(1)}, bf16[16,4096]{1,0:T(8,128)(2,1)S(1)}, u32[]{:S(2)}, u32[]{:S(2)}) collective-permute-start(bf16[16,4096]{1,0:T(8,128)(2,1)S(1)} %copy-done), channel_id=1, source_target_pairs={{0,4},{1,5},{2,6},{3,7},{4,0},{5,1},{6,2},{7,3},{8,12},{9,13},{10,... | collective-permute-start | bytes 393224 | tf_op jit(solution)/shard_map/ppermute | solution.py:39
  44.6 4.2 %collective-permute-done.10 = bf16[16,4096]{1,0:T(8,128)(2,1)S(1)} collective-permute-done((bf16[16,4096]{1,0:T(8,128)(2,1)S(1)}, bf16[16,4096]{1,0:T(8,128)(2,1)S(1)}, u32[]{:S(2)}, u32[]{:S(2)}) %collective-permute-start.10) | collective-permute-done | bytes 131104 | tf_op jit(solution)/shard_map/ppermute | solution.py:39
  48.8 3.4 %collective-permute-start.12 = (bf16[32,4096]{1,0:T(8,128)(2,1)S(1)}, bf16[32,4096]{1,0:T(8,128)(2,1)S(1)}, u32[]{:S(2)}, u32[]{:S(2)}) collective-permute-start(bf16[32,4096]{1,0:T(8,128)(2,1)S(1)} %pad_maximum_fusion.4), channel_id=1, source_target_pairs={{0,2},{1,3},{2,0},{3,1},{4,6},{5,7},{6,4},{7,5},{8,10},{9,11},{10,... | collective-permute-start | bytes 786440 | tf_op jit(solution)/shard_map/ppermute | solution.py:39
  52.3 2.4 %collective-permute-start.8 = (bf16[32,4096]{1,0:T(8,128)(2,1)S(1)}, bf16[32,4096]{1,0:T(8,128)(2,1)S(1)}, u32[]{:S(2)}, u32[]{:S(2)}) collective-permute-start(bf16[32,4096]{1,0:T(8,128)(2,1)S(1)} %pad_maximum_fusion.3), channel_id=1, source_target_pairs={{0,2},{1,3},{2,0},{3,1},{4,6},{5,7},{6,4},{7,5},{8,10},{9,11},{10,... | collective-permute-start | bytes 786440 | tf_op jit(solution)/shard_map/ppermute | solution.py:39
  54.8 9.3 %collective-permute-done.8 = bf16[32,4096]{1,0:T(8,128)(2,1)S(1)} collective-permute-done((bf16[32,4096]{1,0:T(8,128)(2,1)S(1)}, bf16[32,4096]{1,0:T(8,128)(2,1)S(1)}, u32[]{:S(2)}, u32[]{:S(2)}) %collective-permute-start.8) | collective-permute-done | bytes 262176 | tf_op jit(solution)/shard_map/ppermute | solution.py:39
  66.1 2.4 %collective-permute-start.13 = (bf16[64,4096]{1,0:T(8,128)(2,1)S(1)}, bf16[64,4096]{1,0:T(8,128)(2,1)S(1)}, u32[]{:S(2)}, u32[]{:S(2)}) collective-permute-start(bf16[64,4096]{1,0:T(8,128)(2,1)S(1)} %constant_dynamic-update-slice_fusion.6), channel_id=1, source_target_pairs={{0,1},{1,0},{2,3},{3,2},{4,5},{5,4},{6,7},{7,6},{8,9},{9,8},{10,11... | collective-permute-start | bytes 1572872 | tf_op jit(solution)/shard_map/ppermute | solution.py:39
  70.0 26.0 %conditional.4 = (bf16[64,4096]{1,0:T(8,128)(2,1)}, bf16[64,4096]{1,0:T(8,128)(2,1)}, bf16[64,4096]{1,0:T(8,128)(2,1)}, bf16[64,4096]{1,0:T(8,128)(2,1)}, bf16[2...) conditional(s32[]{:T(128)} %convert_element_type.183, ...), branch_computations={%region_0.0_spmd, %region_1.0_spmd} | conditional | flops 9663676416 | bytes 30408896 | solution.py:528
  71.3 19.0 %learn.1 = (bf16[256,4096]{1,0:T(8,128)(2,1)}, bf16[4096,256]{1,0:T(8,128)(2,1)}, bf16[2,256,768]{2,1,0:T(8,128)(2,1)}, bf16[768,256]{1,0:T(8,128)(2,1)}, f32[8,...) custom-call(s32[1]{0:T(128)} %get-tuple-element.127.place, bf16[64,4224]{1,0:T(8,128)(2,1)S(1)} %get-tuple-element.128.refs_0_.refs_4_, ...), custom_call_target="tpu_custom_call" | custom-call | flops 9663676416 | bytes 18874368 | tf_op jit(solution)/shard_map/cond/branch_1_fun/learn/pallas_call | solution.py:409
  104.7 5.9 %collective-permute-start.29 = (bf16[256,4096]{1,0:T(8,128)(2,1)}, bf16[256,4096]{1,0:T(8,128)(2,1)}, u32[]{:S(2)}, u32[]{:S(2)}) collective-permute-start(bf16[256,4096]{1,0:T(8,128)(2,1)} %get-tuple-element.202), channel_id=1, source_target_pairs={{0,16},{1,17},{2,18},{3,19},{4,20},{5,21},{6,22},{7,23},{8,24},{9,... | collective-permute-start | bytes 6291464 | tf_op jit(solution)/shard_map/ppermute | solution.py:15
  111.0 3.7 %collective-permute-start.26 = (bf16[16,4096]{1,0:T(8,128)(2,1)S(1)}, bf16[16,4096]{1,0:T(8,128)(2,1)S(1)}, u32[]{:S(2)}, u32[]{:S(2)}) collective-permute-start(bf16[16,4096]{1,0:T(8,128)(2,1)S(1)} %collective-permute-done.21), channel_id=1, source_target_pairs={{0,12},{1,13},{2,14},{3,15},{4,8},{5,9},{6,10},{7,11},{8,4},{9,5},... | collective-permute-start | bytes 393224 | tf_op jit(solution)/shard_map/ppermute | solution.py:39
  114.8 2.1 %collective-permute-start.25 = (bf16[16,4096]{1,0:T(8,128)(2,1)S(1)}, bf16[16,4096]{1,0:T(8,128)(2,1)S(1)}, u32[]{:S(2)}, u32[]{:S(2)}) collective-permute-start(bf16[16,4096]{1,0:T(8,128)(2,1)S(1)} %collective-permute-done.21), channel_id=1, source_target_pairs={{0,8},{1,9},{2,10},{3,11},{4,12},{5,13},{6,14},{7,15},{8,0},{9,1},... | collective-permute-start | bytes 393224 | tf_op jit(solution)/shard_map/ppermute | solution.py:39
  116.9 4.4 %collective-permute-start.22 = (bf16[16,4096]{1,0:T(8,128)(2,1)S(1)}, bf16[16,4096]{1,0:T(8,128)(2,1)S(1)}, u32[]{:S(2)}, u32[]{:S(2)}) collective-permute-start(bf16[16,4096]{1,0:T(8,128)(2,1)S(1)} %collective-permute-done.21), channel_id=1, source_target_pairs={{0,4},{1,5},{2,6},{3,7},{4,0},{5,1},{6,2},{7,3},{8,12},{9,13},{10,... | collective-permute-start | bytes 393224 | tf_op jit(solution)/shard_map/ppermute | solution.py:39
  122.0 3.4 %collective-permute-done.25 = bf16[16,4096]{1,0:T(8,128)(2,1)S(1)} collective-permute-done((bf16[16,4096]{1,0:T(8,128)(2,1)S(1)}, bf16[16,4096]{1,0:T(8,128)(2,1)S(1)}, u32[]{:S(2)}, u32[]{:S(2)}) %collective-permute-start.25) | collective-permute-done | bytes 131104 | tf_op jit(solution)/shard_map/ppermute | solution.py:39
  125.4 3.4 %collective-permute-start.27 = (bf16[32,4096]{1,0:T(8,128)(2,1)S(1)}, bf16[32,4096]{1,0:T(8,128)(2,1)S(1)}, u32[]{:S(2)}, u32[]{:S(2)}) collective-permute-start(bf16[32,4096]{1,0:T(8,128)(2,1)S(1)} %pad_maximum_fusion.6), channel_id=1, source_target_pairs={{0,2},{1,3},{2,0},{3,1},{4,6},{5,7},{6,4},{7,5},{8,10},{9,11},{10,... | collective-permute-start | bytes 786440 | tf_op jit(solution)/shard_map/ppermute | solution.py:39
  128.9 2.4 %collective-permute-start.23 = (bf16[32,4096]{1,0:T(8,128)(2,1)S(1)}, bf16[32,4096]{1,0:T(8,128)(2,1)S(1)}, u32[]{:S(2)}, u32[]{:S(2)}) collective-permute-start(bf16[32,4096]{1,0:T(8,128)(2,1)S(1)} %pad_maximum_fusion.5), channel_id=1, source_target_pairs={{0,2},{1,3},{2,0},{3,1},{4,6},{5,7},{6,4},{7,5},{8,10},{9,11},{10,... | collective-permute-start | bytes 786440 | tf_op jit(solution)/shard_map/ppermute | solution.py:39
  133.3 7.8 %collective-permute-done.23 = bf16[32,4096]{1,0:T(8,128)(2,1)S(1)} collective-permute-done((bf16[32,4096]{1,0:T(8,128)(2,1)S(1)}, bf16[32,4096]{1,0:T(8,128)(2,1)S(1)}, u32[]{:S(2)}, u32[]{:S(2)}) %collective-permute-start.23) | collective-permute-done | bytes 262176 | tf_op jit(solution)/shard_map/ppermute | solution.py:39
  144.5 2.4 %collective-permute-start.28 = (bf16[64,4096]{1,0:T(8,128)(2,1)}, bf16[64,4096]{1,0:T(8,128)(2,1)}, u32[]{:S(2)}, u32[]{:S(2)}) collective-permute-start(bf16[64,4096]{1,0:T(8,128)(2,1)} %constant_dynamic-update-slice_fusion.12), channel_id=1, source_target_pairs={{0,1},{1,0},{2,3},{3,2},{4,5},{5,4},{6,7},{7,6},{8,9},{9,8},{10,11... | collective-permute-start | bytes 1572872 | tf_op jit(solution)/shard_map/ppermute | solution.py:39
  148.7 15.1 %conditional.6 = (bf16[64,4096]{1,0:T(8,128)(2,1)}, bf16[64,4096]{1,0:T(8,128)(2,1)}, bf16[64,4096]{1,0:T(8,128)(2,1)}, bf16[64,4096]{1,0:T(8,128)(2,1)}) conditional(s32[]{:T(128)} %convert_element_type.183, () %tuple.41, (s32[1]{0:T(128)}, bf16[64,4096]{1,0:T(8,128)(2,1)}, bf16[64,4096]{1,0:T(8,128)(2,1)}, bf16[64,4096]{1,0:T(8,128)(2,1)}, ...), branch_computations={%region_2.0_spmd, %region_3.0_spmd} | conditional | flops 4831838208 | bytes 18874412
  148.7 15.1 %ffn_changed.2 = (bf16[64,4096]{1,0:T(8,128)(2,1)}, bf16[64,4096]{1,0:T(8,128)(2,1)}, bf16[64,4096]{1,0:T(8,128)(2,1)}, bf16[64,4096]{1,0:T(8,128)(2,1)}) custom-call(s32[1]{0:T(128)S(6)} %add.53.place, bf16[64,4096]{1,0:T(8,128)(2,1)} %get-tuple-element.145.refs_0_, bf16[64,4096]{1,0:T(8,128)(2,1)} %get-tuple-element.146.refs_1_, ...), custom_call_target="tpu_custom_call" | custom-call | flops 4831838208 | bytes 18874368 | tf_op jit(solution)/shard_map/cond/branch_1_fun/ffn_changed/pallas_call | solution.py:307
  163.8 2.3 %collective-permute-start.38 = (bf16[64,4096]{1,0:T(8,128)(2,1)}, bf16[64,4096]{1,0:T(8,128)(2,1)S(1)}, u32[]{:S(2)}, u32[]{:S(2)}) collective-permute-start(bf16[64,4096]{1,0:T(8,128)(2,1)} %get-tuple-element.205), channel_id=1, source_target_pairs={{0,1},{1,0},{2,3},{3,2},{4,5},{5,4},{6,7},{7,6},{8,9},{9,8},{10,11... | collective-permute-start | bytes 1572872 | tf_op jit(solution)/shard_map/ppermute | solution.py:39
  166.1 2.0 collective-permute-start.41
  172.0 3.4 %collective-permute-start.39 = (bf16[32,4096]{1,0:T(8,128)(2,1)S(1)}, bf16[32,4096]{1,0:T(8,128)(2,1)S(1)}, u32[]{:S(2)}, u32[]{:S(2)}) collective-permute-start(bf16[32,4096]{1,0:T(8,128)(2,1)S(1)} %split.129), channel_id=1, source_target_pairs={{0,2},{1,3},{2,0},{3,1},{4,6},{5,7},{6,4},{7,5},{8,10},{9,11},{10,... | collective-permute-start | bytes 786440 | tf_op jit(solution)/shard_map/ppermute | solution.py:39
  176.7 2.4 %collective-permute-start.42 = (bf16[32,4096]{1,0:T(8,128)(2,1)S(1)}, bf16[32,4096]{1,0:T(8,128)(2,1)S(1)}, u32[]{:S(2)}, u32[]{:S(2)}) collective-permute-start(bf16[32,4096]{1,0:T(8,128)(2,1)S(1)} %split.133), channel_id=1, source_target_pairs={{0,2},{1,3},{2,0},{3,1},{4,6},{5,7},{6,4},{7,5},{8,10},{9,11},{10,... | collective-permute-start | bytes 786440 | tf_op jit(solution)/shard_map/ppermute | solution.py:39
  185.1 3.0 %collective-permute-done.42 = bf16[32,4096]{1,0:T(8,128)(2,1)S(1)} collective-permute-done((bf16[32,4096]{1,0:T(8,128)(2,1)S(1)}, bf16[32,4096]{1,0:T(8,128)(2,1)S(1)}, u32[]{:S(2)}, u32[]{:S(2)}) %collective-permute-start.42) | collective-permute-done | bytes 262176 | tf_op jit(solution)/shard_map/ppermute | solution.py:39
  188.3 2.1 collective-permute-start.43
  190.3 3.7 %collective-permute-start.44 = (bf16[16,4096]{1,0:T(8,128)(2,1)S(1)}, bf16[16,4096]{1,0:T(8,128)(2,1)S(1)}, u32[]{:S(2)}, u32[]{:S(2)}) collective-permute-start(bf16[16,4096]{1,0:T(8,128)(2,1)S(1)} %get-tuple-element.223), channel_id=1, source_target_pairs={{0,12},{1,13},{2,14},{3,15},{4,8},{5,9},{6,10},{7,11},{8,4},{9,5},... | collective-permute-start | bytes 393224 | tf_op jit(solution)/shard_map/ppermute | solution.py:39
  196.3 4.7 %collective-permute-done.43 = bf16[16,4096]{1,0:T(8,128)(2,1)S(1)} collective-permute-done((bf16[16,4096]{1,0:T(8,128)(2,1)S(1)}, bf16[16,4096]{1,0:T(8,128)(2,1)S(1)}, u32[]{:S(2)}, u32[]{:S(2)}) %collective-permute-start.43) | collective-permute-done | bytes 131104 | tf_op jit(solution)/shard_map/ppermute | solution.py:39
  205.5 4.2 %collective-permute-done.37 = bf16[16,4096]{1,0:T(8,128)(2,1)S(1)} collective-permute-done((bf16[16,4096]{1,0:T(8,128)(2,1)S(1)}, bf16[16,4096]{1,0:T(8,128)(2,1)S(1)}, u32[]{:S(2)}, u32[]{:S(2)}) %collective-permute-start.37) | collective-permute-done | bytes 131104 | tf_op jit(solution)/shard_map/ppermute | solution.py:15
  (141 shorter events, 53.6 us)
Async XLA Ops:
  2.6 17.6 %collective-permute-start.4 = (bf16[16,4224]{1,0:T(8,128)(2,1)}, bf16[16,4224]{1,0:T(8,128)(2,1)S(1)}, u32[]{:S(2)}, u32[]{:S(2)}) collective-permute-start(bf16[16,4224]{1,0:T(8,128)(2,1)} %get-tuple-element.187), channel_id=1, source_target_pairs={{0,12},{1,13},{2,14},{3,15},{4,8},{5,9},{6,10},{7,11},{8,4},{9,5},... | collective-permute-start | bytes 405512 | tf_op jit(solution)/shard_map/ppermute | solution.py:39
  7.7 12.5 %collective-permute-start.3 = (bf16[16,4224]{1,0:T(8,128)(2,1)}, bf16[16,4224]{1,0:T(8,128)(2,1)S(1)}, u32[]{:S(2)}, u32[]{:S(2)}) collective-permute-start(bf16[16,4224]{1,0:T(8,128)(2,1)} %get-tuple-element.187), channel_id=1, source_target_pairs={{0,8},{1,9},{2,10},{3,11},{4,12},{5,13},{6,14},{7,15},{8,0},{9,1},... | collective-permute-start | bytes 405512 | tf_op jit(solution)/shard_map/ppermute | solution.py:39
  7.7 14.3 %collective-permute-start = (bf16[16,4224]{1,0:T(8,128)(2,1)}, bf16[16,4224]{1,0:T(8,128)(2,1)S(1)}, u32[]{:S(2)}, u32[]{:S(2)}) collective-permute-start(bf16[16,4224]{1,0:T(8,128)(2,1)} %get-tuple-element.187), channel_id=1, source_target_pairs={{0,4},{1,5},{2,6},{3,7},{4,0},{5,1},{6,2},{7,3},{8,12},{9,13},{10,... | collective-permute-start | bytes 405512 | tf_op jit(solution)/shard_map/ppermute | solution.py:39
  20.2 23.7 %collective-permute-start.5 = (bf16[32,4224]{1,0:T(8,128)(2,1)S(1)}, bf16[32,4224]{1,0:T(8,128)(2,1)S(1)}, u32[]{:S(2)}, u32[]{:S(2)}) collective-permute-start(bf16[32,4224]{1,0:T(8,128)(2,1)S(1)} %pad_maximum_fusion.2), channel_id=1, source_target_pairs={{0,2},{1,3},{2,0},{3,1},{4,6},{5,7},{6,4},{7,5},{8,10},{9,11},{10,... | collective-permute-start | bytes 811016 | tf_op jit(solution)/shard_map/ppermute | solution.py:39
  22.0 11.8 %collective-permute-start.1 = (bf16[32,4224]{1,0:T(8,128)(2,1)S(1)}, bf16[32,4224]{1,0:T(8,128)(2,1)S(1)}, u32[]{:S(2)}, u32[]{:S(2)}) collective-permute-start(bf16[32,4224]{1,0:T(8,128)(2,1)S(1)} %pad_maximum_fusion.1), channel_id=1, source_target_pairs={{0,2},{1,3},{2,0},{3,1},{4,6},{5,7},{6,4},{7,5},{8,10},{9,11},{10,... | collective-permute-start | bytes 811016 | tf_op jit(solution)/shard_map/ppermute | solution.py:39
  33.8 10.8 %collective-permute-start.11 = (bf16[16,4096]{1,0:T(8,128)(2,1)S(1)}, bf16[16,4096]{1,0:T(8,128)(2,1)S(1)}, u32[]{:S(2)}, u32[]{:S(2)}) collective-permute-start(bf16[16,4096]{1,0:T(8,128)(2,1)S(1)} %copy-done), channel_id=1, source_target_pairs={{0,12},{1,13},{2,14},{3,15},{4,8},{5,9},{6,10},{7,11},{8,4},{9,5},... | collective-permute-start | bytes 393224 | tf_op jit(solution)/shard_map/ppermute | solution.py:39
  39.2 9.6 %collective-permute-start.10 = (bf16[16,4096]{1,0:T(8,128)(2,1)S(1)}, bf16[16,4096]{1,0:T(8,128)(2,1)S(1)}, u32[]{:S(2)}, u32[]{:S(2)}) collective-permute-start(bf16[16,4096]{1,0:T(8,128)(2,1)S(1)} %copy-done), channel_id=1, source_target_pairs={{0,8},{1,9},{2,10},{3,11},{4,12},{5,13},{6,14},{7,15},{8,0},{9,1},... | collective-permute-start | bytes 393224 | tf_op jit(solution)/shard_map/ppermute | solution.py:39
  41.1 11.1 %collective-permute-start.7 = (bf16[16,4096]{1,0:T(8,128)(2,1)S(1)}, bf16[16,4096]{1,0:T(8,128)(2,1)S(1)}, u32[]{:S(2)}, u32[]{:S(2)}) collective-permute-start(bf16[16,4096]{1,0:T(8,128)(2,1)S(1)} %copy-done), channel_id=1, source_target_pairs={{0,4},{1,5},{2,6},{3,7},{4,0},{5,1},{6,2},{7,3},{8,12},{9,13},{10,... | collective-permute-start | bytes 393224 | tf_op jit(solution)/shard_map/ppermute | solution.py:39
  44.0 24.5 %collective-permute-start.6 = (bf16[64,4224]{1,0:T(8,128)(2,1)S(1)}, bf16[64,4224]{1,0:T(8,128)(2,1)}, u32[]{:S(2)}, u32[]{:S(2)}) collective-permute-start(bf16[64,4224]{1,0:T(8,128)(2,1)S(1)} %constant_dynamic-update-slice_fusion), channel_id=1, source_target_pairs={{0,1},{1,0},{2,3},{3,2},{4,5},{5,4},{6,7},{7,6},{8,9},{9,8},{10,11... | collective-permute-start | bytes 1622024 | tf_op jit(solution)/shard_map/ppermute | solution.py:39
  44.1 24.5 %collective-permute-start.2 = (bf16[64,4224]{1,0:T(8,128)(2,1)S(1)}, bf16[64,4224]{1,0:T(8,128)(2,1)}, u32[]{:S(2)}, u32[]{:S(2)}) collective-permute-start(bf16[64,4224]{1,0:T(8,128)(2,1)S(1)} %pad_maximum_fusion), channel_id=1, source_target_pairs={{0,1},{1,0},{2,3},{3,2},{4,5},{5,4},{6,7},{7,6},{8,9},{9,8},{10,11... | collective-permute-start | bytes 1622024 | tf_op jit(solution)/shard_map/ppermute | solution.py:39
  48.8 17.2 %collective-permute-start.12 = (bf16[32,4096]{1,0:T(8,128)(2,1)S(1)}, bf16[32,4096]{1,0:T(8,128)(2,1)S(1)}, u32[]{:S(2)}, u32[]{:S(2)}) collective-permute-start(bf16[32,4096]{1,0:T(8,128)(2,1)S(1)} %pad_maximum_fusion.4), channel_id=1, source_target_pairs={{0,2},{1,3},{2,0},{3,1},{4,6},{5,7},{6,4},{7,5},{8,10},{9,11},{10,... | collective-permute-start | bytes 786440 | tf_op jit(solution)/shard_map/ppermute | solution.py:39
  52.3 11.8 %collective-permute-start.8 = (bf16[32,4096]{1,0:T(8,128)(2,1)S(1)}, bf16[32,4096]{1,0:T(8,128)(2,1)S(1)}, u32[]{:S(2)}, u32[]{:S(2)}) collective-permute-start(bf16[32,4096]{1,0:T(8,128)(2,1)S(1)} %pad_maximum_fusion.3), channel_id=1, source_target_pairs={{0,2},{1,3},{2,0},{3,1},{4,6},{5,7},{6,4},{7,5},{8,10},{9,11},{10,... | collective-permute-start | bytes 786440 | tf_op jit(solution)/shard_map/ppermute | solution.py:39
  103.4 7.7 %collective-permute-start.21 = (bf16[16,4096]{1,0:T(8,128)(2,1)S(1)}, bf16[16,4096]{1,0:T(8,128)(2,1)S(1)}, u32[]{:S(2)}, u32[]{:S(2)}) collective-permute-start(bf16[16,4096]{1,0:T(8,128)(2,1)S(1)} %add_convert_fusion.12), channel_id=1, source_target_pairs={{16,0},{17,1},{18,2},{19,3},{20,4},{21,5},{22,6},{23,7},{24,8},{25... | collective-permute-start | bytes 393224 | tf_op jit(solution)/shard_map/ppermute | solution.py:15
  104.7 61.5 %collective-permute-start.29 = (bf16[256,4096]{1,0:T(8,128)(2,1)}, bf16[256,4096]{1,0:T(8,128)(2,1)}, u32[]{:S(2)}, u32[]{:S(2)}) collective-permute-start(bf16[256,4096]{1,0:T(8,128)(2,1)} %get-tuple-element.202), channel_id=1, source_target_pairs={{0,16},{1,17},{2,18},{3,19},{4,20},{5,21},{6,22},{7,23},{8,24},{9,... | collective-permute-start | bytes 6291464 | tf_op jit(solution)/shard_map/ppermute | solution.py:15
  111.0 11.0 %collective-permute-start.26 = (bf16[16,4096]{1,0:T(8,128)(2,1)S(1)}, bf16[16,4096]{1,0:T(8,128)(2,1)S(1)}, u32[]{:S(2)}, u32[]{:S(2)}) collective-permute-start(bf16[16,4096]{1,0:T(8,128)(2,1)S(1)} %collective-permute-done.21), channel_id=1, source_target_pairs={{0,12},{1,13},{2,14},{3,15},{4,8},{5,9},{6,10},{7,11},{8,4},{9,5},... | collective-permute-start | bytes 393224 | tf_op jit(solution)/shard_map/ppermute | solution.py:39
  114.8 10.6 %collective-permute-start.25 = (bf16[16,4096]{1,0:T(8,128)(2,1)S(1)}, bf16[16,4096]{1,0:T(8,128)(2,1)S(1)}, u32[]{:S(2)}, u32[]{:S(2)}) collective-permute-start(bf16[16,4096]{1,0:T(8,128)(2,1)S(1)} %collective-permute-done.21), channel_id=1, source_target_pairs={{0,8},{1,9},{2,10},{3,11},{4,12},{5,13},{6,14},{7,15},{8,0},{9,1},... | collective-permute-start | bytes 393224 | tf_op jit(solution)/shard_map/ppermute | solution.py:39
  116.9 11.9 %collective-permute-start.22 = (bf16[16,4096]{1,0:T(8,128)(2,1)S(1)}, bf16[16,4096]{1,0:T(8,128)(2,1)S(1)}, u32[]{:S(2)}, u32[]{:S(2)}) collective-permute-start(bf16[16,4096]{1,0:T(8,128)(2,1)S(1)} %collective-permute-done.21), channel_id=1, source_target_pairs={{0,4},{1,5},{2,6},{3,7},{4,0},{5,1},{6,2},{7,3},{8,12},{9,13},{10,... | collective-permute-start | bytes 393224 | tf_op jit(solution)/shard_map/ppermute | solution.py:39
  125.4 18.3 %collective-permute-start.27 = (bf16[32,4096]{1,0:T(8,128)(2,1)S(1)}, bf16[32,4096]{1,0:T(8,128)(2,1)S(1)}, u32[]{:S(2)}, u32[]{:S(2)}) collective-permute-start(bf16[32,4096]{1,0:T(8,128)(2,1)S(1)} %pad_maximum_fusion.6), channel_id=1, source_target_pairs={{0,2},{1,3},{2,0},{3,1},{4,6},{5,7},{6,4},{7,5},{8,10},{9,11},{10,... | collective-permute-start | bytes 786440 | tf_op jit(solution)/shard_map/ppermute | solution.py:39
  128.9 12.2 %collective-permute-start.23 = (bf16[32,4096]{1,0:T(8,128)(2,1)S(1)}, bf16[32,4096]{1,0:T(8,128)(2,1)S(1)}, u32[]{:S(2)}, u32[]{:S(2)}) collective-permute-start(bf16[32,4096]{1,0:T(8,128)(2,1)S(1)} %pad_maximum_fusion.5), channel_id=1, source_target_pairs={{0,2},{1,3},{2,0},{3,1},{4,6},{5,7},{6,4},{7,5},{8,10},{9,11},{10,... | collective-permute-start | bytes 786440 | tf_op jit(solution)/shard_map/ppermute | solution.py:39
  166.1 9.4 %collective-permute-start.41 = (bf16[64,4096]{1,0:T(8,128)(2,1)}, bf16[64,4096]{1,0:T(8,128)(2,1)S(1)}, u32[]{:S(2)}, u32[]{:S(2)}) collective-permute-start(bf16[64,4096]{1,0:T(8,128)(2,1)} %get-tuple-element.207), channel_id=1, source_target_pairs={{0,1},{1,0},{2,3},{3,2},{4,5},{5,4},{6,7},{7,6},{8,9},{9,8},{10,11... | collective-permute-start | bytes 1572872 | tf_op jit(solution)/shard_map/ppermute | solution.py:39
  169.4 9.7 %collective-permute-start.30 = (bf16[64,4096]{1,0:T(8,128)(2,1)S(1)}, bf16[64,4096]{1,0:T(8,128)(2,1)S(1)}, u32[]{:S(2)}, u32[]{:S(2)}) collective-permute-start(bf16[64,4096]{1,0:T(8,128)(2,1)S(1)} %get-tuple-element.218), channel_id=1, source_target_pairs={{16,17},{17,16},{18,19},{19,18},{20,21},{21,20},{22,23},{23,22},{2... | collective-permute-start | bytes 1572872 | tf_op jit(solution)/shard_map/ppermute | solution.py:39
  170.1 9.0 %collective-permute-start.33 = (bf16[64,4096]{1,0:T(8,128)(2,1)S(1)}, bf16[64,4096]{1,0:T(8,128)(2,1)S(1)}, u32[]{:S(2)}, u32[]{:S(2)}) collective-permute-start(bf16[64,4096]{1,0:T(8,128)(2,1)S(1)} %get-tuple-element.219), channel_id=1, source_target_pairs={{16,17},{17,16},{18,19},{19,18},{20,21},{21,20},{22,23},{23,22},{2... | collective-permute-start | bytes 1572872 | tf_op jit(solution)/shard_map/ppermute | solution.py:39
  172.0 11.0 %collective-permute-start.39 = (bf16[32,4096]{1,0:T(8,128)(2,1)S(1)}, bf16[32,4096]{1,0:T(8,128)(2,1)S(1)}, u32[]{:S(2)}, u32[]{:S(2)}) collective-permute-start(bf16[32,4096]{1,0:T(8,128)(2,1)S(1)} %split.129), channel_id=1, source_target_pairs={{0,2},{1,3},{2,0},{3,1},{4,6},{5,7},{6,4},{7,5},{8,10},{9,11},{10,... | collective-permute-start | bytes 786440 | tf_op jit(solution)/shard_map/ppermute | solution.py:39
  176.7 11.4 %collective-permute-start.42 = (bf16[32,4096]{1,0:T(8,128)(2,1)S(1)}, bf16[32,4096]{1,0:T(8,128)(2,1)S(1)}, u32[]{:S(2)}, u32[]{:S(2)}) collective-permute-start(bf16[32,4096]{1,0:T(8,128)(2,1)S(1)} %split.133), channel_id=1, source_target_pairs={{0,2},{1,3},{2,0},{3,1},{4,6},{5,7},{6,4},{7,5},{8,10},{9,11},{10,... | collective-permute-start | bytes 786440 | tf_op jit(solution)/shard_map/ppermute | solution.py:39
  180.7 13.4 %collective-permute-start.34 = (bf16[32,4096]{1,0:T(8,128)(2,1)S(1)}, bf16[32,4096]{1,0:T(8,128)(2,1)S(1)}, u32[]{:S(2)}, u32[]{:S(2)}) collective-permute-start(bf16[32,4096]{1,0:T(8,128)(2,1)S(1)} %split.125), channel_id=1, source_target_pairs={{16,18},{17,19},{18,16},{19,17},{20,22},{21,23},{22,20},{23,21},{2... | collective-permute-start | bytes 786440 | tf_op jit(solution)/shard_map/ppermute | solution.py:39
  181.3 13.5 %collective-permute-start.31 = (bf16[32,4096]{1,0:T(8,128)(2,1)S(1)}, bf16[32,4096]{1,0:T(8,128)(2,1)S(1)}, u32[]{:S(2)}, u32[]{:S(2)}) collective-permute-start(bf16[32,4096]{1,0:T(8,128)(2,1)S(1)} %split.121), channel_id=1, source_target_pairs={{16,18},{17,19},{18,16},{19,17},{20,22},{21,23},{22,20},{23,21},{2... | collective-permute-start | bytes 786440 | tf_op jit(solution)/shard_map/ppermute | solution.py:39
  183.2 12.5 %collective-permute-start.40 = (bf16[16,4096]{1,0:T(8,128)(2,1)S(1)}, bf16[16,4096]{1,0:T(8,128)(2,1)S(1)}, u32[]{:S(2)}, u32[]{:S(2)}) collective-permute-start(bf16[16,4096]{1,0:T(8,128)(2,1)S(1)} %split.131), channel_id=1, source_target_pairs={{0,4},{1,5},{2,6},{3,7},{4,0},{5,1},{6,2},{7,3},{8,12},{9,13},{10,... | collective-permute-start | bytes 393224 | tf_op jit(solution)/shard_map/ppermute | solution.py:39
  188.3 12.8 %collective-permute-start.43 = (bf16[16,4096]{1,0:T(8,128)(2,1)S(1)}, bf16[16,4096]{1,0:T(8,128)(2,1)S(1)}, u32[]{:S(2)}, u32[]{:S(2)}) collective-permute-start(bf16[16,4096]{1,0:T(8,128)(2,1)S(1)} %get-tuple-element.222), channel_id=1, source_target_pairs={{0,8},{1,9},{2,10},{3,11},{4,12},{5,13},{6,14},{7,15},{8,0},{9,1},... | collective-permute-start | bytes 393224 | tf_op jit(solution)/shard_map/ppermute | solution.py:39
  190.3 10.7 %collective-permute-start.44 = (bf16[16,4096]{1,0:T(8,128)(2,1)S(1)}, bf16[16,4096]{1,0:T(8,128)(2,1)S(1)}, u32[]{:S(2)}, u32[]{:S(2)}) collective-permute-start(bf16[16,4096]{1,0:T(8,128)(2,1)S(1)} %get-tuple-element.223), channel_id=1, source_target_pairs={{0,12},{1,13},{2,14},{3,15},{4,8},{5,9},{6,10},{7,11},{8,4},{9,5},... | collective-permute-start | bytes 393224 | tf_op jit(solution)/shard_map/ppermute | solution.py:39
  194.2 8.3 %collective-permute-start.35 = (bf16[16,4096]{1,0:T(8,128)(2,1)S(1)}, bf16[16,4096]{1,0:T(8,128)(2,1)S(1)}, u32[]{:S(2)}, u32[]{:S(2)}) collective-permute-start(bf16[16,4096]{1,0:T(8,128)(2,1)S(1)} %get-tuple-element.220), channel_id=1, source_target_pairs={{16,24},{17,25},{18,26},{19,27},{20,28},{21,29},{22,30},{23,31},{2... | collective-permute-start | bytes 393224 | tf_op jit(solution)/shard_map/ppermute | solution.py:39
  194.9 7.6 %collective-permute-start.36 = (bf16[16,4096]{1,0:T(8,128)(2,1)S(1)}, bf16[16,4096]{1,0:T(8,128)(2,1)S(1)}, u32[]{:S(2)}, u32[]{:S(2)}) collective-permute-start(bf16[16,4096]{1,0:T(8,128)(2,1)S(1)} %get-tuple-element.221), channel_id=1, source_target_pairs={{16,28},{17,29},{18,30},{19,31},{20,24},{21,25},{22,26},{23,27},{2... | collective-permute-start | bytes 393224 | tf_op jit(solution)/shard_map/ppermute | solution.py:39
  202.5 7.2 %collective-permute-start.37 = (bf16[16,4096]{1,0:T(8,128)(2,1)S(1)}, bf16[16,4096]{1,0:T(8,128)(2,1)S(1)}, u32[]{:S(2)}, u32[]{:S(2)}) collective-permute-start(bf16[16,4096]{1,0:T(8,128)(2,1)S(1)} %add_convert_fusion.11), channel_id=1, source_target_pairs={{16,0},{17,1},{18,2},{19,3},{20,4},{21,5},{22,6},{23,7},{24,8},{25... | collective-permute-start | bytes 393224 | tf_op jit(solution)/shard_map/ppermute | solution.py:15
  (24 other events, 113.2 us)

commit v5 on v4

--- a/solution.py
+++ b/solution.py
@@ -30,9 +30,9 @@
     return strides
 
 
-def swap(block, device_count, flip, role):
+def swap(block, device_count, flip, role, onward=0):
     pairs = [
-        (part * device_count + i, part * device_count + (i ^ flip))
+        (part * device_count + i, (part + onward) * device_count + (i ^ flip))
         for part in role
         for i in range(device_count)
     ]
@@ -331,8 +331,10 @@
 def learn_kernel(place, *refs, count, experts, rates):
     cot_refs = refs[2 * count : 3 * count]
     gu_ref, dn_ref = refs[3 * count : 3 * count + 2]
-    dx_ref, turned, sent, hidden_turned_ref, rates_ref, pulls = refs[3 * count + 2 : 3 * count + 8]
-    rows, table, cots, pulls_turned, gu, dn, sems = refs[3 * count + 8 :]
+    goals = refs[3 * count + 2 : 3 * count + 8]
+    rows, table, cots, pulls_turned, gu, dn, sems, out_sems = refs[3 * count + 8 : 3 * count + 16]
+    held = refs[3 * count + 16 :]
+    dx, turned, sent, hidden_turned, factors, pulls = held
     hidden_count, width = dn.shape
     part = rows.shape[0] // count
     cuts = tiles_of(width)
@@ -351,6 +353,15 @@
         pulls[:, cut] = (gates * cots[:, cut].astype(jnp.float32)).astype(jnp.bfloat16)
         turned[cut, :] = rows[:, cut].T
         pulls_turned[cut, :] = pulls[:, cut].T
+    writes = []
+
+    def write(source, goal):
+        copy = pltpu.make_async_copy(source, goal, out_sems.at[len(writes)])
+        copy.start()
+        writes.append(copy)
+
+    write(turned, goals[1])
+    write(pulls, goals[5])
     alike_rows = nn(rows[...], turned[...])
     alike_pulls = nn(pulls[...], pulls_turned[...])
     active = upward = back = None
@@ -369,23 +380,36 @@
     d_upward = (back * swish).astype(jnp.bfloat16)
     sent[0] = d_active
     sent[1] = d_upward
-    hidden_turned_ref[...] = hidden.T
+    hidden_turned[...] = hidden.T
+    write(sent, goals[2])
+    write(hidden_turned, goals[3])
     d_active_turned = d_active.T
     d_upward_turned = d_upward.T
 
     for cut in cuts:
         out = nn(gu[0, cut], d_active_turned) + nn(gu[1, cut], d_upward_turned)
-        dx_ref[:, cut] = out.T.astype(jnp.bfloat16)
+        out = out.T.astype(jnp.bfloat16)
+        slab = part // 2
+        for i in range(count):
+            for half in range(2):
+                lower = ((i % 2) * 2 + half) * part + (i // 2) * slab
+                here = part * i + slab * half
+                dx[lower : lower + slab, cut] = out[here : here + slab]
+        columns = pl.ds(cut.start, TILE)
+        write(dx.at[:, columns], goals[0].at[:, columns])
 
     def mean_square(alike, factor):
         wide_factor = factor.astype(jnp.float32)
         squares = jnp.sum(wide_factor * fine(alike, factor, 3), axis=0, keepdims=True)
         return jnp.maximum(squares, 0.0) / width
 
-    rates_ref[0:1] = rates[0] / jnp.sqrt(mean_square(alike_rows, d_active) + EPSILON)
-    rates_ref[1:2] = rates[0] / jnp.sqrt(mean_square(alike_rows, d_upward) + EPSILON)
-    rates_ref[2:3] = rates[1] / jnp.sqrt(mean_square(alike_pulls, hidden) + EPSILON)
-    rates_ref[3:8] = jnp.zeros((5, hidden_count), jnp.float32)
+    factors[0:1] = rates[0] / jnp.sqrt(mean_square(alike_rows, d_active) + EPSILON)
+    factors[1:2] = rates[0] / jnp.sqrt(mean_square(alike_rows, d_upward) + EPSILON)
+    factors[2:3] = rates[1] / jnp.sqrt(mean_square(alike_pulls, hidden) + EPSILON)
+    factors[3:8] = jnp.zeros((5, hidden_count), jnp.float32)
+    write(factors, goals[4])
+    for copy in writes:
+        copy.wait()
 
 
 def learn_shapes(row_count, hidden_count, width):
@@ -404,12 +428,11 @@
     hidden_count, width = weights_dn.shape
     row_count = pieces[0].shape[0] * count
     anywhere = pl.BlockSpec(memory_space=pl.ANY)
-    whole = pl.BlockSpec(memory_space=pltpu.VMEM)
     out_shape = learn_shapes(row_count, hidden_count, width)
     return pl.pallas_call(
         functools.partial(learn_kernel, count=count, experts=experts, rates=rates),
         in_specs=[pl.BlockSpec(memory_space=pltpu.SMEM)] + [anywhere] * (3 * count + 2),
-        out_specs=[whole] * len(out_shape),
+        out_specs=[anywhere] * len(out_shape),
         scratch_shapes=[
             pltpu.VMEM((row_count, width), jnp.bfloat16),
             pltpu.VMEM((row_count, tables[0].shape[1] - width), jnp.bfloat16),
@@ -418,7 +441,9 @@
             pltpu.VMEM(planes.shape, jnp.bfloat16),
             pltpu.VMEM(weights_dn.shape, jnp.bfloat16),
             pltpu.SemaphoreType.DMA((3 * count + 2 * (width // TILE),)),
-        ],
+            pltpu.SemaphoreType.DMA((5 + width // TILE,)),
+        ]
+        + [pltpu.VMEM(one.shape, one.dtype) for one in out_shape],
         out_shape=out_shape,
         compiler_params=pltpu.CompilerParams(vmem_limit_bytes=48 << 20),
         cost_estimate=pl.CostEstimate(
@@ -509,10 +534,11 @@
     if small:
         near, away = send_z(block, (0, 1))
         near, planes = tied(near, planes)
+        cot_near, cot_away = send_z(tied(cotangent, near)[0], (0,))
         near, away = send_y(near, away, (0, 1))
-        near, cotangent = tied(near, cotangent)
+        near, away, cot_near, cot_away = tied(near, away, cot_near, cot_away)
         every = send_core(near, away, (0, 1))
-        cots = send_core(*send_y(*send_z(cotangent, (0,)), (0,)), (0,))
+        cots = send_core(*send_y(cot_near, cot_away, (0,)), (0,))
         hidden_count = own_dn.shape[0]
         part_shape = jax.ShapeDtypeStruct(cots[0].shape, jnp.bfloat16)
 
@@ -543,11 +569,11 @@
             *learned[1:],
         )
         fresh_part[3], dx_part = tied(fresh_part[3], dx_part)
-        dx_near, dx_away = sum_y(*sum_core(jnp.split(dx_part, 4, axis=0), (1,)), (1,))
-        dx_sum = sum_z(dx_near, dx_away, (1,)).astype(jnp.bfloat16)
+        dx_sum = scatter_sum(dx_part, 16, (1,)).astype(jnp.bfloat16)
         dx_sum = across(dx_sum, 1, 0).astype(jnp.float32)
         near, away = sum_y(*sum_core(fresh_part, (0,)), (0,))
-        fresh_sum = sum_z(near, away, (0,))
+        blocks = halves(away) + halves(near)[::-1]
+        moved = plus(*[swap(b, 16, f, (0,), 1) for b, f in zip(blocks, (8, 12, 4, 0))])
     else:
         every = [gather(block, device_count, (0, 1))]
         cots = gather(cotangent, device_count, (0,))
@@ -577,7 +603,7 @@
             new_dn,
         )
         fresh_sum = scatter_sum(fresh_part[0], device_count, (0,))
-    moved = across(fresh_sum.astype(jnp.bfloat16), 0, 1).astype(jnp.float32)
+        moved = across(fresh_sum.astype(jnp.bfloat16), 0, 1).astype(jnp.float32)
     final_rows = jnp.where(is_learner, base + dx_sum, current.astype(jnp.float32) + moved)
     return final_rows.astype(jnp.bfloat16)[None]
 

time: 212 us -> 205 us (0.967)
  waiting for transfers between devices: 54.7 us -> 42.9 us
  starting transfers between devices: 86.4 us -> 89.8 us
    ppermute x42 -> x41, waiting for transfers between devices: 48.3 us -> 37.6 us  [swap(): return lax.ppermute(block, ('grp',) + AXES, pairs)]
    ppermute x42 -> x41, starting transfers between devices: 76.7 us -> 81.3 us  [swap(): return lax.ppermute(block, ('grp',) + AXES, pairs)]
    ppermute x4 -> x3, starting transfers between devices: 9.76 us -> 8.46 us  [across(): return lax.ppermute(block, 'grp', [(source, target)])]
    ppermute x4 -> x3, waiting for transfers between devices: 6.4 us -> 5.34 us  [across(): return lax.ppermute(block, 'grp', [(source, target)])]
    unnamed x23 -> x19, local copies, waits for them, and re-layouts: 15.3 us -> 15.2 us
  transfers between devices with their start and end apart: 46 -> 44, of which waited for: 13 -> 11; matrix products, arithmetic and copies ran while one was open for 11% -> 11% of each run, Pallas kernels for 7% -> 7%
where the time goes in v5:
time: 205 us; the launch traced here: 202 us
  starting transfers between devices  89.8 us (44%)
  waiting for transfers between devices  42.9 us (21%)
  Pallas kernels  36.4 us (18%)
  local copies, waits for them, and re-layouts  25.2 us (12%)
  other arithmetic  7.22 us (4%)
    ppermute x41, starting transfers between devices, swap(): return lax.ppermute(block, ('grp',) + AXES, pairs)  81.3 us
    ppermute x41, waiting for transfers between devices, swap(): return lax.ppermute(block, ('grp',) + AXES, pairs)  37.6 us
    pallas_call x1, Pallas kernels, learn_call(): pl.pallas_call(functools.partial(learn_kernel, count=count, experts=exper...  19.4 us
    unnamed x19, local copies, waits for them, and re-layouts  15.2 us
    pallas_call x1, Pallas kernels, ffn_call(): pl.pallas_call(functools.partial(ffn_kernel, count=count, experts=experts...  15.1 us
    ppermute x3, starting transfers between devices, across(): return lax.ppermute(block, 'grp', [(source, target)])  8.46 us
    cond x11, local copies, waits for them, and re-layouts  6.94 us
    ppermute x3, waiting for transfers between devices, across(): return lax.ppermute(block, 'grp', [(source, target)])  5.34 us
  transfers between devices with their start and end apart: 44, of which 11 were waited for; matrix products, arithmetic and copies ran while one was open for 11% of the time, Pallas kernels for 7%

profile of v5, /device:TPU:0, one launch (start us, length us, event | category | flops | bytes accessed | tf_op | source)
XLA Modules:
  0.0 202.4 jit_solution(18023669199986804112)
XLA Ops:
  2.6 3.1 %collective-permute-start = (bf16[16,4224]{1,0:T(8,128)(2,1)}, bf16[16,4224]{1,0:T(8,128)(2,1)S(1)}, u32[]{:S(2)}, u32[]{:S(2)}) collective-permute-start(bf16[16,4224]{1,0:T(8,128)(2,1)} %get-tuple-element.190), channel_id=1, source_target_pairs={{0,4},{1,5},{2,6},{3,7},{4,0},{5,1},{6,2},{7,3},{8,12},{9,13},{10,... | collective-permute-start | bytes 405512 | tf_op jit(solution)/shard_map/ppermute | solution.py:39
  5.7 2.5 %collective-permute-start.3 = (bf16[16,4224]{1,0:T(8,128)(2,1)}, bf16[16,4224]{1,0:T(8,128)(2,1)S(1)}, u32[]{:S(2)}, u32[]{:S(2)}) collective-permute-start(bf16[16,4224]{1,0:T(8,128)(2,1)} %get-tuple-element.190), channel_id=1, source_target_pairs={{0,12},{1,13},{2,14},{3,15},{4,8},{5,9},{6,10},{7,11},{8,4},{9,5},... | collective-permute-start | bytes 405512 | tf_op jit(solution)/shard_map/ppermute | solution.py:39
  8.3 11.9 %copy.12 = bf16[1,1,4096,2,768]{4,2,3,1,0:T(8,128)(2,1)} copy(bf16[1,1,4096,2,768]{4,3,2,1,0:T(2,128)(2,1)} %param.20) | data formatting | bytes 25165824 | tf_op args[7]
  20.2 4.8 %collective-permute-start.7 = (bf16[16,4096]{1,0:T(8,128)(2,1)S(1)}, bf16[16,4096]{1,0:T(8,128)(2,1)S(1)}, u32[]{:S(2)}, u32[]{:S(2)}) collective-permute-start(bf16[16,4096]{1,0:T(8,128)(2,1)S(1)} %copy-done.4), channel_id=1, source_target_pairs={{0,12},{1,13},{2,14},{3,15},{4,8},{5,9},{6,10},{7,11},{8,4},{9,5},... | collective-permute-start | bytes 393224 | tf_op jit(solution)/shard_map/ppermute | solution.py:39
  25.0 2.2 %collective-permute-start.6 = (bf16[16,4096]{1,0:T(8,128)(2,1)S(1)}, bf16[16,4096]{1,0:T(8,128)(2,1)S(1)}, u32[]{:S(2)}, u32[]{:S(2)}) collective-permute-start(bf16[16,4096]{1,0:T(8,128)(2,1)S(1)} %copy-done.4), channel_id=1, source_target_pairs={{0,8},{1,9},{2,10},{3,11},{4,12},{5,13},{6,14},{7,15},{8,0},{9,1},... | collective-permute-start | bytes 393224 | tf_op jit(solution)/shard_map/ppermute | solution.py:39
  27.3 3.0 %collective-permute-start.5 = (bf16[16,4096]{1,0:T(8,128)(2,1)S(1)}, bf16[16,4096]{1,0:T(8,128)(2,1)S(1)}, u32[]{:S(2)}, u32[]{:S(2)}) collective-permute-start(bf16[16,4096]{1,0:T(8,128)(2,1)S(1)} %copy-done.4), channel_id=1, source_target_pairs={{0,4},{1,5},{2,6},{3,7},{4,0},{5,1},{6,2},{7,3},{8,12},{9,13},{10,... | collective-permute-start | bytes 393224 | tf_op jit(solution)/shard_map/ppermute | solution.py:39
  32.5 4.1 %collective-permute-done.5 = bf16[16,4096]{1,0:T(8,128)(2,1)S(1)} collective-permute-done((bf16[16,4096]{1,0:T(8,128)(2,1)S(1)}, bf16[16,4096]{1,0:T(8,128)(2,1)S(1)}, u32[]{:S(2)}, u32[]{:S(2)}) %collective-permute-start.5) | collective-permute-done | bytes 131104 | tf_op jit(solution)/shard_map/ppermute | solution.py:39
  36.7 6.3 %collective-permute-done.4 = bf16[32,4224]{1,0:T(8,128)(2,1)S(1)} collective-permute-done((bf16[32,4224]{1,0:T(8,128)(2,1)S(1)}, bf16[32,4224]{1,0:T(8,128)(2,1)S(1)}, u32[]{:S(2)}, u32[]{:S(2)}) %collective-permute-start.4) | collective-permute-done | bytes 270368 | tf_op jit(solution)/shard_map/ppermute | solution.py:39
  43.1 3.4 %collective-permute-start.10 = (bf16[32,4096]{1,0:T(8,128)(2,1)S(1)}, bf16[32,4096]{1,0:T(8,128)(2,1)S(1)}, u32[]{:S(2)}, u32[]{:S(2)}) collective-permute-start(bf16[32,4096]{1,0:T(8,128)(2,1)S(1)} %pad_maximum_fusion.4), channel_id=1, source_target_pairs={{0,2},{1,3},{2,0},{3,1},{4,6},{5,7},{6,4},{7,5},{8,10},{9,11},{10,... | collective-permute-start | bytes 786440 | tf_op jit(solution)/shard_map/ppermute | solution.py:39
  46.6 2.4 %collective-permute-start.12 = (bf16[32,4096]{1,0:T(8,128)(2,1)S(1)}, bf16[32,4096]{1,0:T(8,128)(2,1)S(1)}, u32[]{:S(2)}, u32[]{:S(2)}) collective-permute-start(bf16[32,4096]{1,0:T(8,128)(2,1)S(1)} %pad_maximum_fusion.5), channel_id=1, source_target_pairs={{0,2},{1,3},{2,0},{3,1},{4,6},{5,7},{6,4},{7,5},{8,10},{9,11},{10,... | collective-permute-start | bytes 786440 | tf_op jit(solution)/shard_map/ppermute | solution.py:39
  49.6 7.1 %collective-permute-done.12 = bf16[32,4096]{1,0:T(8,128)(2,1)S(1)} collective-permute-done((bf16[32,4096]{1,0:T(8,128)(2,1)S(1)}, bf16[32,4096]{1,0:T(8,128)(2,1)S(1)}, u32[]{:S(2)}, u32[]{:S(2)}) %collective-permute-start.12) | collective-permute-done | bytes 262176 | tf_op jit(solution)/shard_map/ppermute | solution.py:39
  58.7 2.4 %collective-permute-start.11 = (bf16[64,4096]{1,0:T(8,128)(2,1)S(1)}, bf16[64,4096]{1,0:T(8,128)(2,1)S(1)}, u32[]{:S(2)}, u32[]{:S(2)}) collective-permute-start(bf16[64,4096]{1,0:T(8,128)(2,1)S(1)} %constant_dynamic-update-slice_fusion), channel_id=1, source_target_pairs={{0,1},{1,0},{2,3},{3,2},{4,5},{5,4},{6,7},{7,6},{8,9},{9,8},{10,11... | collective-permute-start | bytes 1572872 | tf_op jit(solution)/shard_map/ppermute | solution.py:39
  62.6 26.4 %conditional.4 = (bf16[64,4096]{1,0:T(8,128)(2,1)}, bf16[64,4096]{1,0:T(8,128)(2,1)}, bf16[64,4096]{1,0:T(8,128)(2,1)}, bf16[64,4096]{1,0:T(8,128)(2,1)}, bf16[2...) conditional(s32[]{:T(128)} %convert_element_type.159, ...), branch_computations={%region_0.0_spmd, %region_1.0_spmd} | conditional | flops 9663676416 | bytes 30408896 | solution.py:554
  63.9 19.4 %learn.1 = (bf16[256,4096]{1,0:T(8,128)(2,1)}, bf16[4096,256]{1,0:T(8,128)(2,1)}, bf16[2,256,768]{2,1,0:T(8,128)(2,1)}, bf16[768,256]{1,0:T(8,128)(2,1)}, f32[8,...) custom-call(s32[1]{0:T(128)} %get-tuple-element.127.place, bf16[64,4224]{1,0:T(8,128)(2,1)S(1)} %get-tuple-element.128.refs_0_.refs_4_, ...), custom_call_target="tpu_custom_call" | custom-call | flops 9663676416 | bytes 18874368 | tf_op jit(solution)/shard_map/cond/branch_1_fun/learn/pallas_call | solution.py:432
  97.8 5.9 %collective-permute-start.29 = (bf16[256,4096]{1,0:T(8,128)(2,1)}, bf16[256,4096]{1,0:T(8,128)(2,1)}, u32[]{:S(2)}, u32[]{:S(2)}) collective-permute-start(bf16[256,4096]{1,0:T(8,128)(2,1)} %get-tuple-element.208), channel_id=1, source_target_pairs={{0,16},{1,17},{2,18},{3,19},{4,20},{5,21},{6,22},{7,23},{8,24},{9,... | collective-permute-start | bytes 6291464 | tf_op jit(solution)/shard_map/ppermute | solution.py:15
  104.2 4.3 %collective-permute-start.26 = (bf16[16,4096]{1,0:T(8,128)(2,1)S(1)}, bf16[16,4096]{1,0:T(8,128)(2,1)S(1)}, u32[]{:S(2)}, u32[]{:S(2)}) collective-permute-start(bf16[16,4096]{1,0:T(8,128)(2,1)S(1)} %collective-permute-done.21), channel_id=1, source_target_pairs={{0,12},{1,13},{2,14},{3,15},{4,8},{5,9},{6,10},{7,11},{8,4},{9,5},... | collective-permute-start | bytes 393224 | tf_op jit(solution)/shard_map/ppermute | solution.py:39
  110.4 3.9 %collective-permute-start.22 = (bf16[16,4096]{1,0:T(8,128)(2,1)S(1)}, bf16[16,4096]{1,0:T(8,128)(2,1)S(1)}, u32[]{:S(2)}, u32[]{:S(2)}) collective-permute-start(bf16[16,4096]{1,0:T(8,128)(2,1)S(1)} %collective-permute-done.21), channel_id=1, source_target_pairs={{0,4},{1,5},{2,6},{3,7},{4,0},{5,1},{6,2},{7,3},{8,12},{9,13},{10,... | collective-permute-start | bytes 393224 | tf_op jit(solution)/shard_map/ppermute | solution.py:39
  115.0 4.4 %collective-permute-done.25 = bf16[16,4096]{1,0:T(8,128)(2,1)S(1)} collective-permute-done((bf16[16,4096]{1,0:T(8,128)(2,1)S(1)}, bf16[16,4096]{1,0:T(8,128)(2,1)S(1)}, u32[]{:S(2)}, u32[]{:S(2)}) %collective-permute-start.25) | collective-permute-done | bytes 131104 | tf_op jit(solution)/shard_map/ppermute | solution.py:39
  119.4 3.0 %collective-permute-start.27 = (bf16[32,4096]{1,0:T(8,128)(2,1)S(1)}, bf16[32,4096]{1,0:T(8,128)(2,1)S(1)}, u32[]{:S(2)}, u32[]{:S(2)}) collective-permute-start(bf16[32,4096]{1,0:T(8,128)(2,1)S(1)} %pad_maximum_fusion.7), channel_id=1, source_target_pairs={{0,2},{1,3},{2,0},{3,1},{4,6},{5,7},{6,4},{7,5},{8,10},{9,11},{10,... | collective-permute-start | bytes 786440 | tf_op jit(solution)/shard_map/ppermute | solution.py:39
  122.5 2.8 %collective-permute-start.23 = (bf16[32,4096]{1,0:T(8,128)(2,1)S(1)}, bf16[32,4096]{1,0:T(8,128)(2,1)S(1)}, u32[]{:S(2)}, u32[]{:S(2)}) collective-permute-start(bf16[32,4096]{1,0:T(8,128)(2,1)S(1)} %pad_maximum_fusion.6), channel_id=1, source_target_pairs={{0,2},{1,3},{2,0},{3,1},{4,6},{5,7},{6,4},{7,5},{8,10},{9,11},{10,... | collective-permute-start | bytes 786440 | tf_op jit(solution)/shard_map/ppermute | solution.py:39
  127.3 7.2 %collective-permute-done.23 = bf16[32,4096]{1,0:T(8,128)(2,1)S(1)} collective-permute-done((bf16[32,4096]{1,0:T(8,128)(2,1)S(1)}, bf16[32,4096]{1,0:T(8,128)(2,1)S(1)}, u32[]{:S(2)}, u32[]{:S(2)}) %collective-permute-start.23) | collective-permute-done | bytes 262176 | tf_op jit(solution)/shard_map/ppermute | solution.py:39
  137.9 2.4 %collective-permute-start.28 = (bf16[64,4096]{1,0:T(8,128)(2,1)}, bf16[64,4096]{1,0:T(8,128)(2,1)}, u32[]{:S(2)}, u32[]{:S(2)}) collective-permute-start(bf16[64,4096]{1,0:T(8,128)(2,1)} %constant_dynamic-update-slice_fusion.7), channel_id=1, source_target_pairs={{0,1},{1,0},{2,3},{3,2},{4,5},{5,4},{6,7},{7,6},{8,9},{9,8},{10,11... | collective-permute-start | bytes 1572872 | tf_op jit(solution)/shard_map/ppermute | solution.py:39
  142.2 15.1 %conditional.6 = (bf16[64,4096]{1,0:T(8,128)(2,1)}, bf16[64,4096]{1,0:T(8,128)(2,1)}, bf16[64,4096]{1,0:T(8,128)(2,1)}, bf16[64,4096]{1,0:T(8,128)(2,1)}) conditional(s32[]{:T(128)} %convert_element_type.159, () %tuple.42, (s32[1]{0:T(128)}, bf16[64,4096]{1,0:T(8,128)(2,1)}, bf16[64,4096]{1,0:T(8,128)(2,1)}, bf16[64,4096]{1,0:T(8,128)(2,1)}, ...), branch_computations={%region_2.0_spmd, %region_3.0_spmd} | conditional | flops 4831838208 | bytes 18874412
  142.2 15.1 %ffn_changed.2 = (bf16[64,4096]{1,0:T(8,128)(2,1)}, bf16[64,4096]{1,0:T(8,128)(2,1)}, bf16[64,4096]{1,0:T(8,128)(2,1)}, bf16[64,4096]{1,0:T(8,128)(2,1)}) custom-call(s32[1]{0:T(128)S(6)} %add.49.place, bf16[64,4096]{1,0:T(8,128)(2,1)} %get-tuple-element.145.refs_0_, bf16[64,4096]{1,0:T(8,128)(2,1)} %get-tuple-element.146.refs_1_, ...), custom_call_target="tpu_custom_call" | custom-call | flops 4831838208 | bytes 18874368 | tf_op jit(solution)/shard_map/cond/branch_1_fun/ffn_changed/pallas_call | solution.py:307
  157.3 2.3 %collective-permute-start.40 = (bf16[64,4096]{1,0:T(8,128)(2,1)}, bf16[64,4096]{1,0:T(8,128)(2,1)S(1)}, u32[]{:S(2)}, u32[]{:S(2)}) collective-permute-start(bf16[64,4096]{1,0:T(8,128)(2,1)} %get-tuple-element.213), channel_id=1, source_target_pairs={{0,1},{1,0},{2,3},{3,2},{4,5},{5,4},{6,7},{7,6},{8,9},{9,8},{10,11... | collective-permute-start | bytes 1572872 | tf_op jit(solution)/shard_map/ppermute | solution.py:39
  159.6 2.0 %collective-permute-start.36 = (bf16[64,4096]{1,0:T(8,128)(2,1)}, bf16[64,4096]{1,0:T(8,128)(2,1)S(1)}, u32[]{:S(2)}, u32[]{:S(2)}) collective-permute-start(bf16[64,4096]{1,0:T(8,128)(2,1)} %get-tuple-element.211), channel_id=1, source_target_pairs={{0,1},{1,0},{2,3},{3,2},{4,5},{5,4},{6,7},{7,6},{8,9},{9,8},{10,11... | collective-permute-start | bytes 1572872 | tf_op jit(solution)/shard_map/ppermute | solution.py:39
  164.9 3.1 %collective-permute-start.41 = (bf16[32,4096]{1,0:T(8,128)(2,1)S(1)}, bf16[32,4096]{1,0:T(8,128)(2,1)S(1)}, u32[]{:S(2)}, u32[]{:S(2)}) collective-permute-start(bf16[32,4096]{1,0:T(8,128)(2,1)S(1)} %split.115), channel_id=1, source_target_pairs={{0,2},{1,3},{2,0},{3,1},{4,6},{5,7},{6,4},{7,5},{8,10},{9,11},{10,... | collective-permute-start | bytes 786440 | tf_op jit(solution)/shard_map/ppermute | solution.py:39
  169.1 2.8 %collective-permute-start.37 = (bf16[32,4096]{1,0:T(8,128)(2,1)S(1)}, bf16[32,4096]{1,0:T(8,128)(2,1)S(1)}, u32[]{:S(2)}, u32[]{:S(2)}) collective-permute-start(bf16[32,4096]{1,0:T(8,128)(2,1)S(1)} %split.111), channel_id=1, source_target_pairs={{0,2},{1,3},{2,0},{3,1},{4,6},{5,7},{6,4},{7,5},{8,10},{9,11},{10,... | collective-permute-start | bytes 786440 | tf_op jit(solution)/shard_map/ppermute | solution.py:39
  171.9 4.0 %collective-permute-done.41 = bf16[32,4096]{1,0:T(8,128)(2,1)S(1)} collective-permute-done((bf16[32,4096]{1,0:T(8,128)(2,1)S(1)}, bf16[32,4096]{1,0:T(8,128)(2,1)S(1)}, u32[]{:S(2)}, u32[]{:S(2)}) %collective-permute-start.41) | collective-permute-done | bytes 262176 | tf_op jit(solution)/shard_map/ppermute | solution.py:39
  183.3 8.4 %collective-permute-start.38 = (bf16[16,4096]{1,0:T(8,128)(2,1)S(1)}, bf16[16,4096]{1,0:T(8,128)(2,1)S(1)}, u32[]{:S(2)}, u32[]{:S(2)}) collective-permute-start(bf16[16,4096]{1,0:T(8,128)(2,1)S(1)} %get-tuple-element.225), channel_id=1, source_target_pairs={{0,24},{1,25},{2,26},{3,27},{4,28},{5,29},{6,30},{7,31},{8,16},{9,... | collective-permute-start | bytes 393224 | tf_op jit(solution)/shard_map/ppermute | solution.py:39
  191.7 2.6 %collective-permute-start.39 = (bf16[16,4096]{1,0:T(8,128)(2,1)S(1)}, bf16[16,4096]{1,0:T(8,128)(2,1)S(1)}, u32[]{:S(2)}, u32[]{:S(2)}) collective-permute-start(bf16[16,4096]{1,0:T(8,128)(2,1)S(1)} %get-tuple-element.226), channel_id=1, source_target_pairs={{0,28},{1,29},{2,30},{3,31},{4,24},{5,25},{6,26},{7,27},{8,20},{9,... | collective-permute-start | bytes 393224 | tf_op jit(solution)/shard_map/ppermute | solution.py:39
  196.8 4.8 %collective-permute-done.35 = bf16[16,4096]{1,0:T(8,128)(2,1)S(1)} collective-permute-done((bf16[16,4096]{1,0:T(8,128)(2,1)S(1)}, bf16[16,4096]{1,0:T(8,128)(2,1)S(1)}, u32[]{:S(2)}, u32[]{:S(2)}) %collective-permute-start.35) | collective-permute-done | bytes 131104 | tf_op jit(solution)/shard_map/ppermute | solution.py:15
  (129 shorter events, 49.9 us)
Async XLA Ops:
  2.6 17.5 %collective-permute-start = (bf16[16,4224]{1,0:T(8,128)(2,1)}, bf16[16,4224]{1,0:T(8,128)(2,1)S(1)}, u32[]{:S(2)}, u32[]{:S(2)}) collective-permute-start(bf16[16,4224]{1,0:T(8,128)(2,1)} %get-tuple-element.190), channel_id=1, source_target_pairs={{0,4},{1,5},{2,6},{3,7},{4,0},{5,1},{6,2},{7,3},{8,12},{9,13},{10,... | collective-permute-start | bytes 405512 | tf_op jit(solution)/shard_map/ppermute | solution.py:39
  5.7 24.6 %collective-permute-start.3 = (bf16[16,4224]{1,0:T(8,128)(2,1)}, bf16[16,4224]{1,0:T(8,128)(2,1)S(1)}, u32[]{:S(2)}, u32[]{:S(2)}) collective-permute-start(bf16[16,4224]{1,0:T(8,128)(2,1)} %get-tuple-element.190), channel_id=1, source_target_pairs={{0,12},{1,13},{2,14},{3,15},{4,8},{5,9},{6,10},{7,11},{8,4},{9,5},... | collective-permute-start | bytes 405512 | tf_op jit(solution)/shard_map/ppermute | solution.py:39
  8.1 23.8 %collective-permute-start.2 = (bf16[16,4224]{1,0:T(8,128)(2,1)}, bf16[16,4224]{1,0:T(8,128)(2,1)S(1)}, u32[]{:S(2)}, u32[]{:S(2)}) collective-permute-start(bf16[16,4224]{1,0:T(8,128)(2,1)} %get-tuple-element.190), channel_id=1, source_target_pairs={{0,8},{1,9},{2,10},{3,11},{4,12},{5,13},{6,14},{7,15},{8,0},{9,1},... | collective-permute-start | bytes 405512 | tf_op jit(solution)/shard_map/ppermute | solution.py:39
  20.2 16.5 %collective-permute-start.7 = (bf16[16,4096]{1,0:T(8,128)(2,1)S(1)}, bf16[16,4096]{1,0:T(8,128)(2,1)S(1)}, u32[]{:S(2)}, u32[]{:S(2)}) collective-permute-start(bf16[16,4096]{1,0:T(8,128)(2,1)S(1)} %copy-done.4), channel_id=1, source_target_pairs={{0,12},{1,13},{2,14},{3,15},{4,8},{5,9},{6,10},{7,11},{8,4},{9,5},... | collective-permute-start | bytes 393224 | tf_op jit(solution)/shard_map/ppermute | solution.py:39
  25.0 11.6 %collective-permute-start.6 = (bf16[16,4096]{1,0:T(8,128)(2,1)S(1)}, bf16[16,4096]{1,0:T(8,128)(2,1)S(1)}, u32[]{:S(2)}, u32[]{:S(2)}) collective-permute-start(bf16[16,4096]{1,0:T(8,128)(2,1)S(1)} %copy-done.4), channel_id=1, source_target_pairs={{0,8},{1,9},{2,10},{3,11},{4,12},{5,13},{6,14},{7,15},{8,0},{9,1},... | collective-permute-start | bytes 393224 | tf_op jit(solution)/shard_map/ppermute | solution.py:39
  27.3 9.4 %collective-permute-start.5 = (bf16[16,4096]{1,0:T(8,128)(2,1)S(1)}, bf16[16,4096]{1,0:T(8,128)(2,1)S(1)}, u32[]{:S(2)}, u32[]{:S(2)}) collective-permute-start(bf16[16,4096]{1,0:T(8,128)(2,1)S(1)} %copy-done.4), channel_id=1, source_target_pairs={{0,4},{1,5},{2,6},{3,7},{4,0},{5,1},{6,2},{7,3},{8,12},{9,13},{10,... | collective-permute-start | bytes 393224 | tf_op jit(solution)/shard_map/ppermute | solution.py:39
  30.3 12.7 %collective-permute-start.1 = (bf16[32,4224]{1,0:T(8,128)(2,1)S(1)}, bf16[32,4224]{1,0:T(8,128)(2,1)S(1)}, u32[]{:S(2)}, u32[]{:S(2)}) collective-permute-start(bf16[32,4224]{1,0:T(8,128)(2,1)S(1)} %pad_maximum_fusion.2), channel_id=1, source_target_pairs={{0,2},{1,3},{2,0},{3,1},{4,6},{5,7},{6,4},{7,5},{8,10},{9,11},{10,... | collective-permute-start | bytes 811016 | tf_op jit(solution)/shard_map/ppermute | solution.py:39
  31.9 11.1 %collective-permute-start.4 = (bf16[32,4224]{1,0:T(8,128)(2,1)S(1)}, bf16[32,4224]{1,0:T(8,128)(2,1)S(1)}, u32[]{:S(2)}, u32[]{:S(2)}) collective-permute-start(bf16[32,4224]{1,0:T(8,128)(2,1)S(1)} %pad_maximum_fusion.3), channel_id=1, source_target_pairs={{0,2},{1,3},{2,0},{3,1},{4,6},{5,7},{6,4},{7,5},{8,10},{9,11},{10,... | collective-permute-start | bytes 811016 | tf_op jit(solution)/shard_map/ppermute | solution.py:39
  43.1 15.6 %collective-permute-start.10 = (bf16[32,4096]{1,0:T(8,128)(2,1)S(1)}, bf16[32,4096]{1,0:T(8,128)(2,1)S(1)}, u32[]{:S(2)}, u32[]{:S(2)}) collective-permute-start(bf16[32,4096]{1,0:T(8,128)(2,1)S(1)} %pad_maximum_fusion.4), channel_id=1, source_target_pairs={{0,2},{1,3},{2,0},{3,1},{4,6},{5,7},{6,4},{7,5},{8,10},{9,11},{10,... | collective-permute-start | bytes 786440 | tf_op jit(solution)/shard_map/ppermute | solution.py:39
  46.6 10.1 %collective-permute-start.12 = (bf16[32,4096]{1,0:T(8,128)(2,1)S(1)}, bf16[32,4096]{1,0:T(8,128)(2,1)S(1)}, u32[]{:S(2)}, u32[]{:S(2)}) collective-permute-start(bf16[32,4096]{1,0:T(8,128)(2,1)S(1)} %pad_maximum_fusion.5), channel_id=1, source_target_pairs={{0,2},{1,3},{2,0},{3,1},{4,6},{5,7},{6,4},{7,5},{8,10},{9,11},{10,... | collective-permute-start | bytes 786440 | tf_op jit(solution)/shard_map/ppermute | solution.py:39
  49.0 12.1 %collective-permute-start.8 = (bf16[64,4224]{1,0:T(8,128)(2,1)S(1)}, bf16[64,4224]{1,0:T(8,128)(2,1)}, u32[]{:S(2)}, u32[]{:S(2)}) collective-permute-start(bf16[64,4224]{1,0:T(8,128)(2,1)S(1)} %pad_maximum_fusion), channel_id=1, source_target_pairs={{0,1},{1,0},{2,3},{3,2},{4,5},{5,4},{6,7},{7,6},{8,9},{9,8},{10,11... | collective-permute-start | bytes 1622024 | tf_op jit(solution)/shard_map/ppermute | solution.py:39
  49.1 12.1 %collective-permute-start.9 = (bf16[64,4224]{1,0:T(8,128)(2,1)S(1)}, bf16[64,4224]{1,0:T(8,128)(2,1)}, u32[]{:S(2)}, u32[]{:S(2)}) collective-permute-start(bf16[64,4224]{1,0:T(8,128)(2,1)S(1)} %pad_maximum_fusion.1), channel_id=1, source_target_pairs={{0,1},{1,0},{2,3},{3,2},{4,5},{5,4},{6,7},{7,6},{8,9},{9,8},{10,11... | collective-permute-start | bytes 1622024 | tf_op jit(solution)/shard_map/ppermute | solution.py:39
  96.6 7.7 %collective-permute-start.21 = (bf16[16,4096]{1,0:T(8,128)(2,1)S(1)}, bf16[16,4096]{1,0:T(8,128)(2,1)S(1)}, u32[]{:S(2)}, u32[]{:S(2)}) collective-permute-start(bf16[16,4096]{1,0:T(8,128)(2,1)S(1)} %add_convert_fusion.9), channel_id=1, source_target_pairs={{16,0},{17,1},{18,2},{19,3},{20,4},{21,5},{22,6},{23,7},{24,8},{25... | collective-permute-start | bytes 393224 | tf_op jit(solution)/shard_map/ppermute | solution.py:15
  97.8 61.7 %collective-permute-start.29 = (bf16[256,4096]{1,0:T(8,128)(2,1)}, bf16[256,4096]{1,0:T(8,128)(2,1)}, u32[]{:S(2)}, u32[]{:S(2)}) collective-permute-start(bf16[256,4096]{1,0:T(8,128)(2,1)} %get-tuple-element.208), channel_id=1, source_target_pairs={{0,16},{1,17},{2,18},{3,19},{4,20},{5,21},{6,22},{7,23},{8,24},{9,... | collective-permute-start | bytes 6291464 | tf_op jit(solution)/shard_map/ppermute | solution.py:15
  104.2 10.8 %collective-permute-start.26 = (bf16[16,4096]{1,0:T(8,128)(2,1)S(1)}, bf16[16,4096]{1,0:T(8,128)(2,1)S(1)}, u32[]{:S(2)}, u32[]{:S(2)}) collective-permute-start(bf16[16,4096]{1,0:T(8,128)(2,1)S(1)} %collective-permute-done.21), channel_id=1, source_target_pairs={{0,12},{1,13},{2,14},{3,15},{4,8},{5,9},{6,10},{7,11},{8,4},{9,5},... | collective-permute-start | bytes 393224 | tf_op jit(solution)/shard_map/ppermute | solution.py:39
  108.5 10.9 %collective-permute-start.25 = (bf16[16,4096]{1,0:T(8,128)(2,1)S(1)}, bf16[16,4096]{1,0:T(8,128)(2,1)S(1)}, u32[]{:S(2)}, u32[]{:S(2)}) collective-permute-start(bf16[16,4096]{1,0:T(8,128)(2,1)S(1)} %collective-permute-done.21), channel_id=1, source_target_pairs={{0,8},{1,9},{2,10},{3,11},{4,12},{5,13},{6,14},{7,15},{8,0},{9,1},... | collective-permute-start | bytes 393224 | tf_op jit(solution)/shard_map/ppermute | solution.py:39
  110.4 12.0 %collective-permute-start.22 = (bf16[16,4096]{1,0:T(8,128)(2,1)S(1)}, bf16[16,4096]{1,0:T(8,128)(2,1)S(1)}, u32[]{:S(2)}, u32[]{:S(2)}) collective-permute-start(bf16[16,4096]{1,0:T(8,128)(2,1)S(1)} %collective-permute-done.21), channel_id=1, source_target_pairs={{0,4},{1,5},{2,6},{3,7},{4,0},{5,1},{6,2},{7,3},{8,12},{9,13},{10,... | collective-permute-start | bytes 393224 | tf_op jit(solution)/shard_map/ppermute | solution.py:39
  119.4 17.8 %collective-permute-start.27 = (bf16[32,4096]{1,0:T(8,128)(2,1)S(1)}, bf16[32,4096]{1,0:T(8,128)(2,1)S(1)}, u32[]{:S(2)}, u32[]{:S(2)}) collective-permute-start(bf16[32,4096]{1,0:T(8,128)(2,1)S(1)} %pad_maximum_fusion.7), channel_id=1, source_target_pairs={{0,2},{1,3},{2,0},{3,1},{4,6},{5,7},{6,4},{7,5},{8,10},{9,11},{10,... | collective-permute-start | bytes 786440 | tf_op jit(solution)/shard_map/ppermute | solution.py:39
  122.5 12.0 %collective-permute-start.23 = (bf16[32,4096]{1,0:T(8,128)(2,1)S(1)}, bf16[32,4096]{1,0:T(8,128)(2,1)S(1)}, u32[]{:S(2)}, u32[]{:S(2)}) collective-permute-start(bf16[32,4096]{1,0:T(8,128)(2,1)S(1)} %pad_maximum_fusion.6), channel_id=1, source_target_pairs={{0,2},{1,3},{2,0},{3,1},{4,6},{5,7},{6,4},{7,5},{8,10},{9,11},{10,... | collective-permute-start | bytes 786440 | tf_op jit(solution)/shard_map/ppermute | solution.py:39
  135.3 5.1 %collective-permute-start.24 = (bf16[64,4096]{1,0:T(8,128)(2,1)}, bf16[64,4096]{1,0:T(8,128)(2,1)}, u32[]{:S(2)}, u32[]{:S(2)}) collective-permute-start(bf16[64,4096]{1,0:T(8,128)(2,1)} %constant_dynamic-update-slice_fusion.4), channel_id=1, source_target_pairs={{0,1},{1,0},{2,3},{3,2},{4,5},{5,4},{6,7},{7,6},{8,9},{9,8},{10,11... | collective-permute-start | bytes 1572872 | tf_op jit(solution)/shard_map/ppermute | solution.py:39
  157.3 6.4 %collective-permute-start.40 = (bf16[64,4096]{1,0:T(8,128)(2,1)}, bf16[64,4096]{1,0:T(8,128)(2,1)S(1)}, u32[]{:S(2)}, u32[]{:S(2)}) collective-permute-start(bf16[64,4096]{1,0:T(8,128)(2,1)} %get-tuple-element.213), channel_id=1, source_target_pairs={{0,1},{1,0},{2,3},{3,2},{4,5},{5,4},{6,7},{7,6},{8,9},{9,8},{10,11... | collective-permute-start | bytes 1572872 | tf_op jit(solution)/shard_map/ppermute | solution.py:39
  159.6 8.4 %collective-permute-start.36 = (bf16[64,4096]{1,0:T(8,128)(2,1)}, bf16[64,4096]{1,0:T(8,128)(2,1)S(1)}, u32[]{:S(2)}, u32[]{:S(2)}) collective-permute-start(bf16[64,4096]{1,0:T(8,128)(2,1)} %get-tuple-element.211), channel_id=1, source_target_pairs={{0,1},{1,0},{2,3},{3,2},{4,5},{5,4},{6,7},{7,6},{8,9},{9,8},{10,11... | collective-permute-start | bytes 1572872 | tf_op jit(solution)/shard_map/ppermute | solution.py:39
  162.9 15.7 %collective-permute-start.30 = (bf16[128,4096]{1,0:T(8,128)(2,1)S(1)}, bf16[128,4096]{1,0:T(8,128)(2,1)S(1)}, u32[]{:S(2)}, u32[]{:S(2)}) collective-permute-start(bf16[128,4096]{1,0:T(8,128)(2,1)S(1)} %split.81), channel_id=1, source_target_pairs={{16,17},{17,16},{18,19},{19,18},{20,21},{21,20},{22,23},{23,22},{2... | collective-permute-start | bytes 3145736 | tf_op jit(solution)/shard_map/ppermute | solution.py:39
  164.9 11.0 %collective-permute-start.41 = (bf16[32,4096]{1,0:T(8,128)(2,1)S(1)}, bf16[32,4096]{1,0:T(8,128)(2,1)S(1)}, u32[]{:S(2)}, u32[]{:S(2)}) collective-permute-start(bf16[32,4096]{1,0:T(8,128)(2,1)S(1)} %split.115), channel_id=1, source_target_pairs={{0,2},{1,3},{2,0},{3,1},{4,6},{5,7},{6,4},{7,5},{8,10},{9,11},{10,... | collective-permute-start | bytes 786440 | tf_op jit(solution)/shard_map/ppermute | solution.py:39
  169.1 11.8 %collective-permute-start.37 = (bf16[32,4096]{1,0:T(8,128)(2,1)S(1)}, bf16[32,4096]{1,0:T(8,128)(2,1)S(1)}, u32[]{:S(2)}, u32[]{:S(2)}) collective-permute-start(bf16[32,4096]{1,0:T(8,128)(2,1)S(1)} %split.111), channel_id=1, source_target_pairs={{0,2},{1,3},{2,0},{3,1},{4,6},{5,7},{6,4},{7,5},{8,10},{9,11},{10,... | collective-permute-start | bytes 786440 | tf_op jit(solution)/shard_map/ppermute | solution.py:39
  176.0 19.7 %collective-permute-start.42 = (bf16[16,4096]{1,0:T(8,128)(2,1)S(1)}, bf16[16,4096]{1,0:T(8,128)(2,1)S(1)}, u32[]{:S(2)}, u32[]{:S(2)}) collective-permute-start(bf16[16,4096]{1,0:T(8,128)(2,1)S(1)} %get-tuple-element.227), channel_id=1, source_target_pairs={{0,20},{1,21},{2,22},{3,23},{4,16},{5,17},{6,18},{7,19},{8,28},{9,... | collective-permute-start | bytes 393224 | tf_op jit(solution)/shard_map/ppermute | solution.py:39
  177.3 18.4 %collective-permute-start.43 = (bf16[16,4096]{1,0:T(8,128)(2,1)S(1)}, bf16[16,4096]{1,0:T(8,128)(2,1)S(1)}, u32[]{:S(2)}, u32[]{:S(2)}) collective-permute-start(bf16[16,4096]{1,0:T(8,128)(2,1)S(1)} %get-tuple-element.228), channel_id=1, source_target_pairs={{0,16},{1,17},{2,18},{3,19},{4,20},{5,21},{6,22},{7,23},{8,24},{9,... | collective-permute-start | bytes 393224 | tf_op jit(solution)/shard_map/ppermute | solution.py:39
  181.9 9.8 %collective-permute-start.34 = (bf16[16,4096]{1,0:T(8,128)(2,1)S(1)}, bf16[16,4096]{1,0:T(8,128)(2,1)S(1)}, u32[]{:S(2)}, u32[]{:S(2)}) collective-permute-start(bf16[16,4096]{1,0:T(8,128)(2,1)S(1)} %get-tuple-element.223), channel_id=1, source_target_pairs={{16,28},{17,29},{18,30},{19,31},{20,24},{21,25},{22,26},{23,27},{2... | collective-permute-start | bytes 393224 | tf_op jit(solution)/shard_map/ppermute | solution.py:39
  182.6 11.7 %collective-permute-start.33 = (bf16[16,4096]{1,0:T(8,128)(2,1)S(1)}, bf16[16,4096]{1,0:T(8,128)(2,1)S(1)}, u32[]{:S(2)}, u32[]{:S(2)}) collective-permute-start(bf16[16,4096]{1,0:T(8,128)(2,1)S(1)} %get-tuple-element.224), channel_id=1, source_target_pairs={{16,24},{17,25},{18,26},{19,27},{20,28},{21,29},{22,30},{23,31},{2... | collective-permute-start | bytes 393224 | tf_op jit(solution)/shard_map/ppermute | solution.py:39
  183.3 12.4 %collective-permute-start.38 = (bf16[16,4096]{1,0:T(8,128)(2,1)S(1)}, bf16[16,4096]{1,0:T(8,128)(2,1)S(1)}, u32[]{:S(2)}, u32[]{:S(2)}) collective-permute-start(bf16[16,4096]{1,0:T(8,128)(2,1)S(1)} %get-tuple-element.225), channel_id=1, source_target_pairs={{0,24},{1,25},{2,26},{3,27},{4,28},{5,29},{6,30},{7,31},{8,16},{9,... | collective-permute-start | bytes 393224 | tf_op jit(solution)/shard_map/ppermute | solution.py:39
  191.7 5.1 %collective-permute-start.39 = (bf16[16,4096]{1,0:T(8,128)(2,1)S(1)}, bf16[16,4096]{1,0:T(8,128)(2,1)S(1)}, u32[]{:S(2)}, u32[]{:S(2)}) collective-permute-start(bf16[16,4096]{1,0:T(8,128)(2,1)S(1)} %get-tuple-element.226), channel_id=1, source_target_pairs={{0,28},{1,29},{2,30},{3,31},{4,24},{5,25},{6,26},{7,27},{8,20},{9,... | collective-permute-start | bytes 393224 | tf_op jit(solution)/shard_map/ppermute | solution.py:39
  194.4 7.3 %collective-permute-start.35 = (bf16[16,4096]{1,0:T(8,128)(2,1)S(1)}, bf16[16,4096]{1,0:T(8,128)(2,1)S(1)}, u32[]{:S(2)}, u32[]{:S(2)}) collective-permute-start(bf16[16,4096]{1,0:T(8,128)(2,1)S(1)} %add_convert_fusion.8), channel_id=1, source_target_pairs={{16,0},{17,1},{18,2},{19,3},{20,4},{21,5},{22,6},{23,7},{24,8},{25... | collective-permute-start | bytes 393224 | tf_op jit(solution)/shard_map/ppermute | solution.py:15
  (22 other events, 95.7 us)

commit v6 on v5

--- a/solution.py
+++ b/solution.py
@@ -544,7 +544,7 @@
 
         def learn(every, cots, planes, own_dn):
             out = learn_call(first_place, every, every, cots, planes, own_dn, ep_count, rates)
-            return ([unset(part_shape)] * 4, list(out))
+            return ([unset(part_shape) for _ in range(4)], list(out))
 
         def decode(every, cots, planes, own_dn):
             out = ffn_call(first_place, every, every, planes, own_dn, ep_count)
@@ -572,8 +572,7 @@
         dx_sum = scatter_sum(dx_part, 16, (1,)).astype(jnp.bfloat16)
         dx_sum = across(dx_sum, 1, 0).astype(jnp.float32)
         near, away = sum_y(*sum_core(fresh_part, (0,)), (0,))
-        blocks = halves(away) + halves(near)[::-1]
-        moved = plus(*[swap(b, 16, f, (0,), 1) for b, f in zip(blocks, (8, 12, 4, 0))])
+        moved = across(sum_z(near, away, (0,)).astype(jnp.bfloat16), 0, 1).astype(jnp.float32)
     else:
         every = [gather(block, device_count, (0, 1))]
         cots = gather(cotangent, device_count, (0,))

time: 205 us -> 202 us (0.985)
  waiting for transfers between devices: 42.9 us -> 50.8 us
  local copies, waits for them, and re-layouts: 25.2 us -> 19.4 us
  starting transfers between devices: 89.8 us -> 85.6 us
    ppermute x41 -> x40, waiting for transfers between devices: 37.6 us -> 44.4 us  [swap(): return lax.ppermute(block, ('grp',) + AXES, pairs)]
    cond x11 -> x8, local copies, waits for them, and re-layouts: 6.94 us -> 1.28 us
    ppermute x41 -> x40, starting transfers between devices: 81.3 us -> 75.9 us  [swap(): return lax.ppermute(block, ('grp',) + AXES, pairs)]
    ppermute x3 -> x4, starting transfers between devices: 8.46 us -> 9.75 us  [across(): return lax.ppermute(block, 'grp', [(source, target)])]
    ppermute x3 -> x4, waiting for transfers between devices: 5.34 us -> 6.42 us  [across(): return lax.ppermute(block, 'grp', [(source, target)])]
  transfers between devices with their start and end apart: 44 -> 44, of which waited for: 11 -> 13; matrix products, arithmetic and copies ran while one was open for 11% -> 12% of each run, Pallas kernels for 7% -> 8%
where the time goes in v6:
time: 202 us; the launch traced here: 200 us
  starting transfers between devices  85.6 us (42%)
  waiting for transfers between devices  50.8 us (25%)
  Pallas kernels  36.4 us (18%)
  local copies, waits for them, and re-layouts  19.4 us (10%)
  other arithmetic  7.21 us (4%)
    ppermute x40, starting transfers between devices, swap(): return lax.ppermute(block, ('grp',) + AXES, pairs)  75.9 us
    ppermute x40, waiting for transfers between devices, swap(): return lax.ppermute(block, ('grp',) + AXES, pairs)  44.4 us
    pallas_call x1, Pallas kernels, learn_call(): pl.pallas_call(functools.partial(learn_kernel, count=count, experts=exper...  19.4 us
    unnamed x19, local copies, waits for them, and re-layouts  15.1 us
    pallas_call x1, Pallas kernels, ffn_call(): pl.pallas_call(functools.partial(ffn_kernel, count=count, experts=experts...  15.1 us
    ppermute x4, starting transfers between devices, across(): return lax.ppermute(block, 'grp', [(source, target)])  9.75 us
    ppermute x4, waiting for transfers between devices, across(): return lax.ppermute(block, 'grp', [(source, target)])  6.42 us
  transfers between devices with their start and end apart: 44, of which 13 were waited for; matrix products, arithmetic and copies ran while one was open for 12% of the time, Pallas kernels for 8%

profile of v6, /device:TPU:0, one launch (start us, length us, event | category | flops | bytes accessed | tf_op | source)
XLA Modules:
  0.0 200.3 jit_solution(15418000627373606612)
XLA Ops:
  2.5 3.1 %collective-permute-start = (bf16[16,4224]{1,0:T(8,128)(2,1)}, bf16[16,4224]{1,0:T(8,128)(2,1)S(1)}, u32[]{:S(2)}, u32[]{:S(2)}) collective-permute-start(bf16[16,4224]{1,0:T(8,128)(2,1)} %get-tuple-element.190), channel_id=1, source_target_pairs={{0,4},{1,5},{2,6},{3,7},{4,0},{5,1},{6,2},{7,3},{8,12},{9,13},{10,... | collective-permute-start | bytes 405512 | tf_op jit(solution)/shard_map/ppermute | solution.py:39
  5.6 2.5 %collective-permute-start.3 = (bf16[16,4224]{1,0:T(8,128)(2,1)}, bf16[16,4224]{1,0:T(8,128)(2,1)S(1)}, u32[]{:S(2)}, u32[]{:S(2)}) collective-permute-start(bf16[16,4224]{1,0:T(8,128)(2,1)} %get-tuple-element.190), channel_id=1, source_target_pairs={{0,12},{1,13},{2,14},{3,15},{4,8},{5,9},{6,10},{7,11},{8,4},{9,5},... | collective-permute-start | bytes 405512 | tf_op jit(solution)/shard_map/ppermute | solution.py:39
  8.2 11.8 %copy.12 = bf16[1,1,4096,2,768]{4,2,3,1,0:T(8,128)(2,1)} copy(bf16[1,1,4096,2,768]{4,3,2,1,0:T(2,128)(2,1)} %param.20) | data formatting | bytes 25165824 | tf_op args[7]
  20.0 4.8 %collective-permute-start.7 = (bf16[16,4096]{1,0:T(8,128)(2,1)S(1)}, bf16[16,4096]{1,0:T(8,128)(2,1)S(1)}, u32[]{:S(2)}, u32[]{:S(2)}) collective-permute-start(bf16[16,4096]{1,0:T(8,128)(2,1)S(1)} %copy-done.4), channel_id=1, source_target_pairs={{0,12},{1,13},{2,14},{3,15},{4,8},{5,9},{6,10},{7,11},{8,4},{9,5},... | collective-permute-start | bytes 393224 | tf_op jit(solution)/shard_map/ppermute | solution.py:39
  24.9 2.2 %collective-permute-start.6 = (bf16[16,4096]{1,0:T(8,128)(2,1)S(1)}, bf16[16,4096]{1,0:T(8,128)(2,1)S(1)}, u32[]{:S(2)}, u32[]{:S(2)}) collective-permute-start(bf16[16,4096]{1,0:T(8,128)(2,1)S(1)} %copy-done.4), channel_id=1, source_target_pairs={{0,8},{1,9},{2,10},{3,11},{4,12},{5,13},{6,14},{7,15},{8,0},{9,1},... | collective-permute-start | bytes 393224 | tf_op jit(solution)/shard_map/ppermute | solution.py:39
  27.1 3.0 %collective-permute-start.5 = (bf16[16,4096]{1,0:T(8,128)(2,1)S(1)}, bf16[16,4096]{1,0:T(8,128)(2,1)S(1)}, u32[]{:S(2)}, u32[]{:S(2)}) collective-permute-start(bf16[16,4096]{1,0:T(8,128)(2,1)S(1)} %copy-done.4), channel_id=1, source_target_pairs={{0,4},{1,5},{2,6},{3,7},{4,0},{5,1},{6,2},{7,3},{8,12},{9,13},{10,... | collective-permute-start | bytes 393224 | tf_op jit(solution)/shard_map/ppermute | solution.py:39
  32.4 4.1 %collective-permute-done.5 = bf16[16,4096]{1,0:T(8,128)(2,1)S(1)} collective-permute-done((bf16[16,4096]{1,0:T(8,128)(2,1)S(1)}, bf16[16,4096]{1,0:T(8,128)(2,1)S(1)}, u32[]{:S(2)}, u32[]{:S(2)}) %collective-permute-start.5) | collective-permute-done | bytes 131104 | tf_op jit(solution)/shard_map/ppermute | solution.py:39
  36.6 6.3 %collective-permute-done.4 = bf16[32,4224]{1,0:T(8,128)(2,1)S(1)} collective-permute-done((bf16[32,4224]{1,0:T(8,128)(2,1)S(1)}, bf16[32,4224]{1,0:T(8,128)(2,1)S(1)}, u32[]{:S(2)}, u32[]{:S(2)}) %collective-permute-start.4) | collective-permute-done | bytes 270368 | tf_op jit(solution)/shard_map/ppermute | solution.py:39
  43.0 3.4 %collective-permute-start.10 = (bf16[32,4096]{1,0:T(8,128)(2,1)S(1)}, bf16[32,4096]{1,0:T(8,128)(2,1)S(1)}, u32[]{:S(2)}, u32[]{:S(2)}) collective-permute-start(bf16[32,4096]{1,0:T(8,128)(2,1)S(1)} %pad_maximum_fusion.4), channel_id=1, source_target_pairs={{0,2},{1,3},{2,0},{3,1},{4,6},{5,7},{6,4},{7,5},{8,10},{9,11},{10,... | collective-permute-start | bytes 786440 | tf_op jit(solution)/shard_map/ppermute | solution.py:39
  46.4 2.4 %collective-permute-start.12 = (bf16[32,4096]{1,0:T(8,128)(2,1)S(1)}, bf16[32,4096]{1,0:T(8,128)(2,1)S(1)}, u32[]{:S(2)}, u32[]{:S(2)}) collective-permute-start(bf16[32,4096]{1,0:T(8,128)(2,1)S(1)} %pad_maximum_fusion.5), channel_id=1, source_target_pairs={{0,2},{1,3},{2,0},{3,1},{4,6},{5,7},{6,4},{7,5},{8,10},{9,11},{10,... | collective-permute-start | bytes 786440 | tf_op jit(solution)/shard_map/ppermute | solution.py:39
  49.4 7.1 %collective-permute-done.12 = bf16[32,4096]{1,0:T(8,128)(2,1)S(1)} collective-permute-done((bf16[32,4096]{1,0:T(8,128)(2,1)S(1)}, bf16[32,4096]{1,0:T(8,128)(2,1)S(1)}, u32[]{:S(2)}, u32[]{:S(2)}) %collective-permute-start.12) | collective-permute-done | bytes 262176 | tf_op jit(solution)/shard_map/ppermute | solution.py:39
  58.6 2.4 %collective-permute-start.11 = (bf16[64,4096]{1,0:T(8,128)(2,1)S(1)}, bf16[64,4096]{1,0:T(8,128)(2,1)S(1)}, u32[]{:S(2)}, u32[]{:S(2)}) collective-permute-start(bf16[64,4096]{1,0:T(8,128)(2,1)S(1)} %constant_dynamic-update-slice_fusion), channel_id=1, source_target_pairs={{0,1},{1,0},{2,3},{3,2},{4,5},{5,4},{6,7},{7,6},{8,9},{9,8},{10,11... | collective-permute-start | bytes 1572872 | tf_op jit(solution)/shard_map/ppermute | solution.py:39
  62.5 20.7 %conditional.4 = (bf16[64,4096]{1,0:T(8,128)(2,1)}, bf16[64,4096]{1,0:T(8,128)(2,1)}, bf16[64,4096]{1,0:T(8,128)(2,1)}, bf16[64,4096]{1,0:T(8,128)(2,1)}, bf16[2...) conditional(s32[]{:T(128)} %convert_element_type.165, ...), branch_computations={%region_0.0_spmd, %region_1.0_spmd} | conditional | flops 9663676416 | bytes 27263168 | solution.py:554
  63.8 19.4 %learn.1 = (bf16[256,4096]{1,0:T(8,128)(2,1)}, bf16[4096,256]{1,0:T(8,128)(2,1)}, bf16[2,256,768]{2,1,0:T(8,128)(2,1)}, bf16[768,256]{1,0:T(8,128)(2,1)}, f32[8,...) custom-call(s32[1]{0:T(128)} %get-tuple-element.127.place, bf16[64,4224]{1,0:T(8,128)(2,1)S(1)} %get-tuple-element.128.refs_0_.refs_4_, ...), custom_call_target="tpu_custom_call" | custom-call | flops 9663676416 | bytes 18874368 | tf_op jit(solution)/shard_map/cond/branch_1_fun/learn/pallas_call | solution.py:432
  92.1 5.9 %collective-permute-start.29 = (bf16[256,4096]{1,0:T(8,128)(2,1)}, bf16[256,4096]{1,0:T(8,128)(2,1)}, u32[]{:S(2)}, u32[]{:S(2)}) collective-permute-start(bf16[256,4096]{1,0:T(8,128)(2,1)} %get-tuple-element.208), channel_id=1, source_target_pairs={{0,16},{1,17},{2,18},{3,19},{4,20},{5,21},{6,22},{7,23},{8,24},{9,... | collective-permute-start | bytes 6291464 | tf_op jit(solution)/shard_map/ppermute | solution.py:15
  98.4 4.3 %collective-permute-start.26 = (bf16[16,4096]{1,0:T(8,128)(2,1)S(1)}, bf16[16,4096]{1,0:T(8,128)(2,1)S(1)}, u32[]{:S(2)}, u32[]{:S(2)}) collective-permute-start(bf16[16,4096]{1,0:T(8,128)(2,1)S(1)} %collective-permute-done.21), channel_id=1, source_target_pairs={{0,12},{1,13},{2,14},{3,15},{4,8},{5,9},{6,10},{7,11},{8,4},{9,5},... | collective-permute-start | bytes 393224 | tf_op jit(solution)/shard_map/ppermute | solution.py:39
  104.6 3.9 %collective-permute-start.22 = (bf16[16,4096]{1,0:T(8,128)(2,1)S(1)}, bf16[16,4096]{1,0:T(8,128)(2,1)S(1)}, u32[]{:S(2)}, u32[]{:S(2)}) collective-permute-start(bf16[16,4096]{1,0:T(8,128)(2,1)S(1)} %collective-permute-done.21), channel_id=1, source_target_pairs={{0,4},{1,5},{2,6},{3,7},{4,0},{5,1},{6,2},{7,3},{8,12},{9,13},{10,... | collective-permute-start | bytes 393224 | tf_op jit(solution)/shard_map/ppermute | solution.py:39
  109.2 4.4 %collective-permute-done.25 = bf16[16,4096]{1,0:T(8,128)(2,1)S(1)} collective-permute-done((bf16[16,4096]{1,0:T(8,128)(2,1)S(1)}, bf16[16,4096]{1,0:T(8,128)(2,1)S(1)}, u32[]{:S(2)}, u32[]{:S(2)}) %collective-permute-start.25) | collective-permute-done | bytes 131104 | tf_op jit(solution)/shard_map/ppermute | solution.py:39
  113.6 3.0 %collective-permute-start.27 = (bf16[32,4096]{1,0:T(8,128)(2,1)S(1)}, bf16[32,4096]{1,0:T(8,128)(2,1)S(1)}, u32[]{:S(2)}, u32[]{:S(2)}) collective-permute-start(bf16[32,4096]{1,0:T(8,128)(2,1)S(1)} %pad_maximum_fusion.7), channel_id=1, source_target_pairs={{0,2},{1,3},{2,0},{3,1},{4,6},{5,7},{6,4},{7,5},{8,10},{9,11},{10,... | collective-permute-start | bytes 786440 | tf_op jit(solution)/shard_map/ppermute | solution.py:39
  116.7 2.8 %collective-permute-start.23 = (bf16[32,4096]{1,0:T(8,128)(2,1)S(1)}, bf16[32,4096]{1,0:T(8,128)(2,1)S(1)}, u32[]{:S(2)}, u32[]{:S(2)}) collective-permute-start(bf16[32,4096]{1,0:T(8,128)(2,1)S(1)} %pad_maximum_fusion.6), channel_id=1, source_target_pairs={{0,2},{1,3},{2,0},{3,1},{4,6},{5,7},{6,4},{7,5},{8,10},{9,11},{10,... | collective-permute-start | bytes 786440 | tf_op jit(solution)/shard_map/ppermute | solution.py:39
  121.5 7.3 %collective-permute-done.23 = bf16[32,4096]{1,0:T(8,128)(2,1)S(1)} collective-permute-done((bf16[32,4096]{1,0:T(8,128)(2,1)S(1)}, bf16[32,4096]{1,0:T(8,128)(2,1)S(1)}, u32[]{:S(2)}, u32[]{:S(2)}) %collective-permute-start.23) | collective-permute-done | bytes 262176 | tf_op jit(solution)/shard_map/ppermute | solution.py:39
  132.2 2.4 %collective-permute-start.28 = (bf16[64,4096]{1,0:T(8,128)(2,1)}, bf16[64,4096]{1,0:T(8,128)(2,1)}, u32[]{:S(2)}, u32[]{:S(2)}) collective-permute-start(bf16[64,4096]{1,0:T(8,128)(2,1)} %constant_dynamic-update-slice_fusion.7), channel_id=1, source_target_pairs={{0,1},{1,0},{2,3},{3,2},{4,5},{5,4},{6,7},{7,6},{8,9},{9,8},{10,11... | collective-permute-start | bytes 1572872 | tf_op jit(solution)/shard_map/ppermute | solution.py:39
  136.4 15.1 %conditional.6 = (bf16[64,4096]{1,0:T(8,128)(2,1)}, bf16[64,4096]{1,0:T(8,128)(2,1)}, bf16[64,4096]{1,0:T(8,128)(2,1)}, bf16[64,4096]{1,0:T(8,128)(2,1)}) conditional(s32[]{:T(128)} %convert_element_type.165, () %tuple.42, (s32[1]{0:T(128)}, bf16[64,4096]{1,0:T(8,128)(2,1)}, bf16[64,4096]{1,0:T(8,128)(2,1)}, bf16[64,4096]{1,0:T(8,128)(2,1)}, ...), branch_computations={%region_2.0_spmd, %region_3.0_spmd} | conditional | flops 4831838208 | bytes 18874412
  136.4 15.1 %ffn_changed.2 = (bf16[64,4096]{1,0:T(8,128)(2,1)}, bf16[64,4096]{1,0:T(8,128)(2,1)}, bf16[64,4096]{1,0:T(8,128)(2,1)}, bf16[64,4096]{1,0:T(8,128)(2,1)}) custom-call(s32[1]{0:T(128)S(6)} %add.49.place, bf16[64,4096]{1,0:T(8,128)(2,1)} %get-tuple-element.145.refs_0_, bf16[64,4096]{1,0:T(8,128)(2,1)} %get-tuple-element.146.refs_1_, ...), custom_call_target="tpu_custom_call" | custom-call | flops 4831838208 | bytes 18874368 | tf_op jit(solution)/shard_map/cond/branch_1_fun/ffn_changed/pallas_call | solution.py:307
  151.5 2.3 %collective-permute-start.36 = (bf16[64,4096]{1,0:T(8,128)(2,1)}, bf16[64,4096]{1,0:T(8,128)(2,1)S(1)}, u32[]{:S(2)}, u32[]{:S(2)}) collective-permute-start(bf16[64,4096]{1,0:T(8,128)(2,1)} %get-tuple-element.211), channel_id=1, source_target_pairs={{0,1},{1,0},{2,3},{3,2},{4,5},{5,4},{6,7},{7,6},{8,9},{9,8},{10,11... | collective-permute-start | bytes 1572872 | tf_op jit(solution)/shard_map/ppermute | solution.py:39
  159.1 3.1 %collective-permute-start.37 = (bf16[32,4096]{1,0:T(8,128)(2,1)S(1)}, bf16[32,4096]{1,0:T(8,128)(2,1)S(1)}, u32[]{:S(2)}, u32[]{:S(2)}) collective-permute-start(bf16[32,4096]{1,0:T(8,128)(2,1)S(1)} %split.111), channel_id=1, source_target_pairs={{0,2},{1,3},{2,0},{3,1},{4,6},{5,7},{6,4},{7,5},{8,10},{9,11},{10,... | collective-permute-start | bytes 786440 | tf_op jit(solution)/shard_map/ppermute | solution.py:39
  163.4 2.8 %collective-permute-start.40 = (bf16[32,4096]{1,0:T(8,128)(2,1)S(1)}, bf16[32,4096]{1,0:T(8,128)(2,1)S(1)}, u32[]{:S(2)}, u32[]{:S(2)}) collective-permute-start(bf16[32,4096]{1,0:T(8,128)(2,1)S(1)} %split.115), channel_id=1, source_target_pairs={{0,2},{1,3},{2,0},{3,1},{4,6},{5,7},{6,4},{7,5},{8,10},{9,11},{10,... | collective-permute-start | bytes 786440 | tf_op jit(solution)/shard_map/ppermute | solution.py:39
  166.2 4.0 %collective-permute-done.37 = bf16[32,4096]{1,0:T(8,128)(2,1)S(1)} collective-permute-done((bf16[32,4096]{1,0:T(8,128)(2,1)S(1)}, bf16[32,4096]{1,0:T(8,128)(2,1)S(1)}, u32[]{:S(2)}, u32[]{:S(2)}) %collective-permute-start.37) | collective-permute-done | bytes 262176 | tf_op jit(solution)/shard_map/ppermute | solution.py:39
  172.2 3.0 %collective-permute-done.40 = bf16[32,4096]{1,0:T(8,128)(2,1)S(1)} collective-permute-done((bf16[32,4096]{1,0:T(8,128)(2,1)S(1)}, bf16[32,4096]{1,0:T(8,128)(2,1)S(1)}, u32[]{:S(2)}, u32[]{:S(2)}) %collective-permute-start.40) | collective-permute-done | bytes 262176 | tf_op jit(solution)/shard_map/ppermute | solution.py:39
  179.6 4.3 %collective-permute-start.42 = (bf16[16,4096]{1,0:T(8,128)(2,1)S(1)}, bf16[16,4096]{1,0:T(8,128)(2,1)S(1)}, u32[]{:S(2)}, u32[]{:S(2)}) collective-permute-start(bf16[16,4096]{1,0:T(8,128)(2,1)S(1)} %get-tuple-element.226), channel_id=1, source_target_pairs={{0,12},{1,13},{2,14},{3,15},{4,8},{5,9},{6,10},{7,11},{8,4},{9,5},... | collective-permute-start | bytes 393224 | tf_op jit(solution)/shard_map/ppermute | solution.py:39
  186.1 4.8 %collective-permute-done.41 = bf16[16,4096]{1,0:T(8,128)(2,1)S(1)} collective-permute-done((bf16[16,4096]{1,0:T(8,128)(2,1)S(1)}, bf16[16,4096]{1,0:T(8,128)(2,1)S(1)}, u32[]{:S(2)}, u32[]{:S(2)}) %collective-permute-start.41) | collective-permute-done | bytes 131104 | tf_op jit(solution)/shard_map/ppermute | solution.py:39
  195.3 4.2 %collective-permute-done.35 = bf16[16,4096]{1,0:T(8,128)(2,1)S(1)} collective-permute-done((bf16[16,4096]{1,0:T(8,128)(2,1)S(1)}, bf16[16,4096]{1,0:T(8,128)(2,1)S(1)}, u32[]{:S(2)}, u32[]{:S(2)}) %collective-permute-start.35) | collective-permute-done | bytes 131104 | tf_op jit(solution)/shard_map/ppermute | solution.py:15
  (130 shorter events, 49.4 us)
Async XLA Ops:
  2.5 17.4 %collective-permute-start = (bf16[16,4224]{1,0:T(8,128)(2,1)}, bf16[16,4224]{1,0:T(8,128)(2,1)S(1)}, u32[]{:S(2)}, u32[]{:S(2)}) collective-permute-start(bf16[16,4224]{1,0:T(8,128)(2,1)} %get-tuple-element.190), channel_id=1, source_target_pairs={{0,4},{1,5},{2,6},{3,7},{4,0},{5,1},{6,2},{7,3},{8,12},{9,13},{10,... | collective-permute-start | bytes 405512 | tf_op jit(solution)/shard_map/ppermute | solution.py:39
  5.6 24.5 %collective-permute-start.3 = (bf16[16,4224]{1,0:T(8,128)(2,1)}, bf16[16,4224]{1,0:T(8,128)(2,1)S(1)}, u32[]{:S(2)}, u32[]{:S(2)}) collective-permute-start(bf16[16,4224]{1,0:T(8,128)(2,1)} %get-tuple-element.190), channel_id=1, source_target_pairs={{0,12},{1,13},{2,14},{3,15},{4,8},{5,9},{6,10},{7,11},{8,4},{9,5},... | collective-permute-start | bytes 405512 | tf_op jit(solution)/shard_map/ppermute | solution.py:39
  8.1 23.7 %collective-permute-start.2 = (bf16[16,4224]{1,0:T(8,128)(2,1)}, bf16[16,4224]{1,0:T(8,128)(2,1)S(1)}, u32[]{:S(2)}, u32[]{:S(2)}) collective-permute-start(bf16[16,4224]{1,0:T(8,128)(2,1)} %get-tuple-element.190), channel_id=1, source_target_pairs={{0,8},{1,9},{2,10},{3,11},{4,12},{5,13},{6,14},{7,15},{8,0},{9,1},... | collective-permute-start | bytes 405512 | tf_op jit(solution)/shard_map/ppermute | solution.py:39
  20.0 16.5 %collective-permute-start.7 = (bf16[16,4096]{1,0:T(8,128)(2,1)S(1)}, bf16[16,4096]{1,0:T(8,128)(2,1)S(1)}, u32[]{:S(2)}, u32[]{:S(2)}) collective-permute-start(bf16[16,4096]{1,0:T(8,128)(2,1)S(1)} %copy-done.4), channel_id=1, source_target_pairs={{0,12},{1,13},{2,14},{3,15},{4,8},{5,9},{6,10},{7,11},{8,4},{9,5},... | collective-permute-start | bytes 393224 | tf_op jit(solution)/shard_map/ppermute | solution.py:39
  24.9 11.6 %collective-permute-start.6 = (bf16[16,4096]{1,0:T(8,128)(2,1)S(1)}, bf16[16,4096]{1,0:T(8,128)(2,1)S(1)}, u32[]{:S(2)}, u32[]{:S(2)}) collective-permute-start(bf16[16,4096]{1,0:T(8,128)(2,1)S(1)} %copy-done.4), channel_id=1, source_target_pairs={{0,8},{1,9},{2,10},{3,11},{4,12},{5,13},{6,14},{7,15},{8,0},{9,1},... | collective-permute-start | bytes 393224 | tf_op jit(solution)/shard_map/ppermute | solution.py:39
  27.1 9.4 %collective-permute-start.5 = (bf16[16,4096]{1,0:T(8,128)(2,1)S(1)}, bf16[16,4096]{1,0:T(8,128)(2,1)S(1)}, u32[]{:S(2)}, u32[]{:S(2)}) collective-permute-start(bf16[16,4096]{1,0:T(8,128)(2,1)S(1)} %copy-done.4), channel_id=1, source_target_pairs={{0,4},{1,5},{2,6},{3,7},{4,0},{5,1},{6,2},{7,3},{8,12},{9,13},{10,... | collective-permute-start | bytes 393224 | tf_op jit(solution)/shard_map/ppermute | solution.py:39
  30.2 12.7 %collective-permute-start.1 = (bf16[32,4224]{1,0:T(8,128)(2,1)S(1)}, bf16[32,4224]{1,0:T(8,128)(2,1)S(1)}, u32[]{:S(2)}, u32[]{:S(2)}) collective-permute-start(bf16[32,4224]{1,0:T(8,128)(2,1)S(1)} %pad_maximum_fusion.2), channel_id=1, source_target_pairs={{0,2},{1,3},{2,0},{3,1},{4,6},{5,7},{6,4},{7,5},{8,10},{9,11},{10,... | collective-permute-start | bytes 811016 | tf_op jit(solution)/shard_map/ppermute | solution.py:39
  31.8 11.1 %collective-permute-start.4 = (bf16[32,4224]{1,0:T(8,128)(2,1)S(1)}, bf16[32,4224]{1,0:T(8,128)(2,1)S(1)}, u32[]{:S(2)}, u32[]{:S(2)}) collective-permute-start(bf16[32,4224]{1,0:T(8,128)(2,1)S(1)} %pad_maximum_fusion.3), channel_id=1, source_target_pairs={{0,2},{1,3},{2,0},{3,1},{4,6},{5,7},{6,4},{7,5},{8,10},{9,11},{10,... | collective-permute-start | bytes 811016 | tf_op jit(solution)/shard_map/ppermute | solution.py:39
  43.0 15.6 %collective-permute-start.10 = (bf16[32,4096]{1,0:T(8,128)(2,1)S(1)}, bf16[32,4096]{1,0:T(8,128)(2,1)S(1)}, u32[]{:S(2)}, u32[]{:S(2)}) collective-permute-start(bf16[32,4096]{1,0:T(8,128)(2,1)S(1)} %pad_maximum_fusion.4), channel_id=1, source_target_pairs={{0,2},{1,3},{2,0},{3,1},{4,6},{5,7},{6,4},{7,5},{8,10},{9,11},{10,... | collective-permute-start | bytes 786440 | tf_op jit(solution)/shard_map/ppermute | solution.py:39
  46.4 10.1 %collective-permute-start.12 = (bf16[32,4096]{1,0:T(8,128)(2,1)S(1)}, bf16[32,4096]{1,0:T(8,128)(2,1)S(1)}, u32[]{:S(2)}, u32[]{:S(2)}) collective-permute-start(bf16[32,4096]{1,0:T(8,128)(2,1)S(1)} %pad_maximum_fusion.5), channel_id=1, source_target_pairs={{0,2},{1,3},{2,0},{3,1},{4,6},{5,7},{6,4},{7,5},{8,10},{9,11},{10,... | collective-permute-start | bytes 786440 | tf_op jit(solution)/shard_map/ppermute | solution.py:39
  48.8 12.1 %collective-permute-start.8 = (bf16[64,4224]{1,0:T(8,128)(2,1)S(1)}, bf16[64,4224]{1,0:T(8,128)(2,1)}, u32[]{:S(2)}, u32[]{:S(2)}) collective-permute-start(bf16[64,4224]{1,0:T(8,128)(2,1)S(1)} %pad_maximum_fusion), channel_id=1, source_target_pairs={{0,1},{1,0},{2,3},{3,2},{4,5},{5,4},{6,7},{7,6},{8,9},{9,8},{10,11... | collective-permute-start | bytes 1622024 | tf_op jit(solution)/shard_map/ppermute | solution.py:39
  48.9 12.1 %collective-permute-start.9 = (bf16[64,4224]{1,0:T(8,128)(2,1)S(1)}, bf16[64,4224]{1,0:T(8,128)(2,1)}, u32[]{:S(2)}, u32[]{:S(2)}) collective-permute-start(bf16[64,4224]{1,0:T(8,128)(2,1)S(1)} %pad_maximum_fusion.1), channel_id=1, source_target_pairs={{0,1},{1,0},{2,3},{3,2},{4,5},{5,4},{6,7},{7,6},{8,9},{9,8},{10,11... | collective-permute-start | bytes 1622024 | tf_op jit(solution)/shard_map/ppermute | solution.py:39
  90.8 7.7 %collective-permute-start.21 = (bf16[16,4096]{1,0:T(8,128)(2,1)S(1)}, bf16[16,4096]{1,0:T(8,128)(2,1)S(1)}, u32[]{:S(2)}, u32[]{:S(2)}) collective-permute-start(bf16[16,4096]{1,0:T(8,128)(2,1)S(1)} %add_convert_fusion.10), channel_id=1, source_target_pairs={{16,0},{17,1},{18,2},{19,3},{20,4},{21,5},{22,6},{23,7},{24,8},{25... | collective-permute-start | bytes 393224 | tf_op jit(solution)/shard_map/ppermute | solution.py:15
  92.1 61.7 %collective-permute-start.29 = (bf16[256,4096]{1,0:T(8,128)(2,1)}, bf16[256,4096]{1,0:T(8,128)(2,1)}, u32[]{:S(2)}, u32[]{:S(2)}) collective-permute-start(bf16[256,4096]{1,0:T(8,128)(2,1)} %get-tuple-element.208), channel_id=1, source_target_pairs={{0,16},{1,17},{2,18},{3,19},{4,20},{5,21},{6,22},{7,23},{8,24},{9,... | collective-permute-start | bytes 6291464 | tf_op jit(solution)/shard_map/ppermute | solution.py:15
  98.4 10.8 %collective-permute-start.26 = (bf16[16,4096]{1,0:T(8,128)(2,1)S(1)}, bf16[16,4096]{1,0:T(8,128)(2,1)S(1)}, u32[]{:S(2)}, u32[]{:S(2)}) collective-permute-start(bf16[16,4096]{1,0:T(8,128)(2,1)S(1)} %collective-permute-done.21), channel_id=1, source_target_pairs={{0,12},{1,13},{2,14},{3,15},{4,8},{5,9},{6,10},{7,11},{8,4},{9,5},... | collective-permute-start | bytes 393224 | tf_op jit(solution)/shard_map/ppermute | solution.py:39
  102.7 10.9 %collective-permute-start.25 = (bf16[16,4096]{1,0:T(8,128)(2,1)S(1)}, bf16[16,4096]{1,0:T(8,128)(2,1)S(1)}, u32[]{:S(2)}, u32[]{:S(2)}) collective-permute-start(bf16[16,4096]{1,0:T(8,128)(2,1)S(1)} %collective-permute-done.21), channel_id=1, source_target_pairs={{0,8},{1,9},{2,10},{3,11},{4,12},{5,13},{6,14},{7,15},{8,0},{9,1},... | collective-permute-start | bytes 393224 | tf_op jit(solution)/shard_map/ppermute | solution.py:39
  104.6 12.0 %collective-permute-start.22 = (bf16[16,4096]{1,0:T(8,128)(2,1)S(1)}, bf16[16,4096]{1,0:T(8,128)(2,1)S(1)}, u32[]{:S(2)}, u32[]{:S(2)}) collective-permute-start(bf16[16,4096]{1,0:T(8,128)(2,1)S(1)} %collective-permute-done.21), channel_id=1, source_target_pairs={{0,4},{1,5},{2,6},{3,7},{4,0},{5,1},{6,2},{7,3},{8,12},{9,13},{10,... | collective-permute-start | bytes 393224 | tf_op jit(solution)/shard_map/ppermute | solution.py:39
  113.6 17.8 %collective-permute-start.27 = (bf16[32,4096]{1,0:T(8,128)(2,1)S(1)}, bf16[32,4096]{1,0:T(8,128)(2,1)S(1)}, u32[]{:S(2)}, u32[]{:S(2)}) collective-permute-start(bf16[32,4096]{1,0:T(8,128)(2,1)S(1)} %pad_maximum_fusion.7), channel_id=1, source_target_pairs={{0,2},{1,3},{2,0},{3,1},{4,6},{5,7},{6,4},{7,5},{8,10},{9,11},{10,... | collective-permute-start | bytes 786440 | tf_op jit(solution)/shard_map/ppermute | solution.py:39
  116.7 12.1 %collective-permute-start.23 = (bf16[32,4096]{1,0:T(8,128)(2,1)S(1)}, bf16[32,4096]{1,0:T(8,128)(2,1)S(1)}, u32[]{:S(2)}, u32[]{:S(2)}) collective-permute-start(bf16[32,4096]{1,0:T(8,128)(2,1)S(1)} %pad_maximum_fusion.6), channel_id=1, source_target_pairs={{0,2},{1,3},{2,0},{3,1},{4,6},{5,7},{6,4},{7,5},{8,10},{9,11},{10,... | collective-permute-start | bytes 786440 | tf_op jit(solution)/shard_map/ppermute | solution.py:39
  151.5 6.4 %collective-permute-start.36 = (bf16[64,4096]{1,0:T(8,128)(2,1)}, bf16[64,4096]{1,0:T(8,128)(2,1)S(1)}, u32[]{:S(2)}, u32[]{:S(2)}) collective-permute-start(bf16[64,4096]{1,0:T(8,128)(2,1)} %get-tuple-element.211), channel_id=1, source_target_pairs={{0,1},{1,0},{2,3},{3,2},{4,5},{5,4},{6,7},{7,6},{8,9},{9,8},{10,11... | collective-permute-start | bytes 1572872 | tf_op jit(solution)/shard_map/ppermute | solution.py:39
  153.8 8.4 %collective-permute-start.39 = (bf16[64,4096]{1,0:T(8,128)(2,1)}, bf16[64,4096]{1,0:T(8,128)(2,1)S(1)}, u32[]{:S(2)}, u32[]{:S(2)}) collective-permute-start(bf16[64,4096]{1,0:T(8,128)(2,1)} %get-tuple-element.213), channel_id=1, source_target_pairs={{0,1},{1,0},{2,3},{3,2},{4,5},{5,4},{6,7},{7,6},{8,9},{9,8},{10,11... | collective-permute-start | bytes 1572872 | tf_op jit(solution)/shard_map/ppermute | solution.py:39
  157.2 18.1 %collective-permute-start.30 = (bf16[128,4096]{1,0:T(8,128)(2,1)S(1)}, bf16[128,4096]{1,0:T(8,128)(2,1)S(1)}, u32[]{:S(2)}, u32[]{:S(2)}) collective-permute-start(bf16[128,4096]{1,0:T(8,128)(2,1)S(1)} %split.81), channel_id=1, source_target_pairs={{16,17},{17,16},{18,19},{19,18},{20,21},{21,20},{22,23},{23,22},{2... | collective-permute-start | bytes 3145736 | tf_op jit(solution)/shard_map/ppermute | solution.py:39
  159.1 11.0 %collective-permute-start.37 = (bf16[32,4096]{1,0:T(8,128)(2,1)S(1)}, bf16[32,4096]{1,0:T(8,128)(2,1)S(1)}, u32[]{:S(2)}, u32[]{:S(2)}) collective-permute-start(bf16[32,4096]{1,0:T(8,128)(2,1)S(1)} %split.111), channel_id=1, source_target_pairs={{0,2},{1,3},{2,0},{3,1},{4,6},{5,7},{6,4},{7,5},{8,10},{9,11},{10,... | collective-permute-start | bytes 786440 | tf_op jit(solution)/shard_map/ppermute | solution.py:39
  163.4 11.8 %collective-permute-start.40 = (bf16[32,4096]{1,0:T(8,128)(2,1)S(1)}, bf16[32,4096]{1,0:T(8,128)(2,1)S(1)}, u32[]{:S(2)}, u32[]{:S(2)}) collective-permute-start(bf16[32,4096]{1,0:T(8,128)(2,1)S(1)} %split.115), channel_id=1, source_target_pairs={{0,2},{1,3},{2,0},{3,1},{4,6},{5,7},{6,4},{7,5},{8,10},{9,11},{10,... | collective-permute-start | bytes 786440 | tf_op jit(solution)/shard_map/ppermute | solution.py:39
  170.2 15.2 %collective-permute-start.38 = (bf16[16,4096]{1,0:T(8,128)(2,1)S(1)}, bf16[16,4096]{1,0:T(8,128)(2,1)S(1)}, u32[]{:S(2)}, u32[]{:S(2)}) collective-permute-start(bf16[16,4096]{1,0:T(8,128)(2,1)S(1)} %split.113), channel_id=1, source_target_pairs={{0,4},{1,5},{2,6},{3,7},{4,0},{5,1},{6,2},{7,3},{8,12},{9,13},{10,... | collective-permute-start | bytes 393224 | tf_op jit(solution)/shard_map/ppermute | solution.py:39
  176.8 7.1 %collective-permute-start.31 = (bf16[64,4096]{1,0:T(8,128)(2,1)S(1)}, bf16[64,4096]{1,0:T(8,128)(2,1)S(1)}, u32[]{:S(2)}, u32[]{:S(2)}) collective-permute-start(bf16[64,4096]{1,0:T(8,128)(2,1)S(1)} %split.105), channel_id=1, source_target_pairs={{16,18},{17,19},{18,16},{19,17},{20,22},{21,23},{22,20},{23,21},{2... | collective-permute-start | bytes 1572872 | tf_op jit(solution)/shard_map/ppermute | solution.py:39
  177.7 13.2 %collective-permute-start.41 = (bf16[16,4096]{1,0:T(8,128)(2,1)S(1)}, bf16[16,4096]{1,0:T(8,128)(2,1)S(1)}, u32[]{:S(2)}, u32[]{:S(2)}) collective-permute-start(bf16[16,4096]{1,0:T(8,128)(2,1)S(1)} %get-tuple-element.225), channel_id=1, source_target_pairs={{0,8},{1,9},{2,10},{3,11},{4,12},{5,13},{6,14},{7,15},{8,0},{9,1},... | collective-permute-start | bytes 393224 | tf_op jit(solution)/shard_map/ppermute | solution.py:39
  179.6 11.3 %collective-permute-start.42 = (bf16[16,4096]{1,0:T(8,128)(2,1)S(1)}, bf16[16,4096]{1,0:T(8,128)(2,1)S(1)}, u32[]{:S(2)}, u32[]{:S(2)}) collective-permute-start(bf16[16,4096]{1,0:T(8,128)(2,1)S(1)} %get-tuple-element.226), channel_id=1, source_target_pairs={{0,12},{1,13},{2,14},{3,15},{4,8},{5,9},{6,10},{7,11},{8,4},{9,5},... | collective-permute-start | bytes 393224 | tf_op jit(solution)/shard_map/ppermute | solution.py:39
  184.1 8.2 %collective-permute-start.32 = (bf16[16,4096]{1,0:T(8,128)(2,1)S(1)}, bf16[16,4096]{1,0:T(8,128)(2,1)S(1)}, u32[]{:S(2)}, u32[]{:S(2)}) collective-permute-start(bf16[16,4096]{1,0:T(8,128)(2,1)S(1)} %get-tuple-element.222), channel_id=1, source_target_pairs={{16,20},{17,21},{18,22},{19,23},{20,16},{21,17},{22,18},{23,19},{2... | collective-permute-start | bytes 393224 | tf_op jit(solution)/shard_map/ppermute | solution.py:39
  184.7 7.5 %collective-permute-start.34 = (bf16[16,4096]{1,0:T(8,128)(2,1)S(1)}, bf16[16,4096]{1,0:T(8,128)(2,1)S(1)}, u32[]{:S(2)}, u32[]{:S(2)}) collective-permute-start(bf16[16,4096]{1,0:T(8,128)(2,1)S(1)} %get-tuple-element.223), channel_id=1, source_target_pairs={{16,28},{17,29},{18,30},{19,31},{20,24},{21,25},{22,26},{23,27},{2... | collective-permute-start | bytes 393224 | tf_op jit(solution)/shard_map/ppermute | solution.py:39
  185.4 6.8 %collective-permute-start.33 = (bf16[16,4096]{1,0:T(8,128)(2,1)S(1)}, bf16[16,4096]{1,0:T(8,128)(2,1)S(1)}, u32[]{:S(2)}, u32[]{:S(2)}) collective-permute-start(bf16[16,4096]{1,0:T(8,128)(2,1)S(1)} %get-tuple-element.224), channel_id=1, source_target_pairs={{16,24},{17,25},{18,26},{19,27},{20,28},{21,29},{22,30},{23,31},{2... | collective-permute-start | bytes 393224 | tf_op jit(solution)/shard_map/ppermute | solution.py:39
  192.4 7.2 %collective-permute-start.35 = (bf16[16,4096]{1,0:T(8,128)(2,1)S(1)}, bf16[16,4096]{1,0:T(8,128)(2,1)S(1)}, u32[]{:S(2)}, u32[]{:S(2)}) collective-permute-start(bf16[16,4096]{1,0:T(8,128)(2,1)S(1)} %add_convert_fusion.9), channel_id=1, source_target_pairs={{16,0},{17,1},{18,2},{19,3},{20,4},{21,5},{22,6},{23,7},{24,8},{25... | collective-permute-start | bytes 393224 | tf_op jit(solution)/shard_map/ppermute | solution.py:15
  (22 other events, 103.2 us)

commit v7 on v6

--- a/solution.py
+++ b/solution.py
@@ -542,19 +542,27 @@
         hidden_count = own_dn.shape[0]
         part_shape = jax.ShapeDtypeStruct(cots[0].shape, jnp.bfloat16)
 
-        def learn(every, cots, planes, own_dn):
-            out = learn_call(first_place, every, every, cots, planes, own_dn, ep_count, rates)
-            return ([unset(part_shape) for _ in range(4)], list(out))
-
-        def decode(every, cots, planes, own_dn):
-            out = ffn_call(first_place, every, every, planes, own_dn, ep_count)
-            shapes = learn_shapes(total_rows, hidden_count, model_width)
-            return (list(out), [unset(one) for one in shapes])
-
-        part, learned = lax.cond(is_learner, learn, decode, every, cots, planes, own_dn)
-        dx_part = across(learned[0], 0, 1)
+        part = lax.cond(
+            is_learner,
+            lambda r, g, d: [unset(part_shape) for _ in r],
+            lambda r, g, d: list(ffn_call(first_place, r, r, g, d, ep_count)),
+            every,
+            planes,
+            own_dn,
+        )
         near, away = sum_y(*sum_core(part, (1,)), (1,))
         current = (base + sum_z(near, away, (1,))).astype(jnp.bfloat16)
+        current, cots[3] = tied(current, cots[3])
+        learned = lax.cond(
+            is_learner,
+            lambda r, c, g, d: list(learn_call(first_place, r, r, c, g, d, ep_count, rates)),
+            lambda r, c, g, d: [unset(one) for one in learn_shapes(total_rows, hidden_count, model_width)],
+            every,
+            cots,
+            planes,
+            own_dn,
+        )
+        dx_part = across(learned[0], 0, 1)
         hopped = across(current, 1, 0)
         near, away = send_y(*send_z(hopped, (0,)), (0,))
         arrived = send_core(near, away, (0,))

time: 202 us -> 192 us (0.950)
  waiting for transfers between devices: 50.8 us -> 31.9 us
  starting transfers between devices: 85.6 us -> 91.5 us
  other arithmetic: 7.21 us -> 9.68 us
    ppermute x40, waiting for transfers between devices: 44.4 us -> 26.4 us  [swap(): return lax.ppermute(block, ('grp',) + AXES, pairs)]
    ppermute x40, starting transfers between devices: 75.9 us -> 83.6 us  [swap(): return lax.ppermute(block, ('grp',) + AXES, pairs)]
    unnamed x19 -> x17, local copies, waits for them, and re-layouts: 15.1 us -> 16.2 us
  transfers between devices with their start and end apart: 44 -> 44, of which waited for: 13 -> 15; matrix products, arithmetic and copies ran while one was open for 12% -> 14% of each run, Pallas kernels for 8% -> 18%
where the time goes in v7:
time: 192 us; the launch traced here: 191 us
  starting transfers between devices  91.5 us (48%)
  Pallas kernels  35.5 us (18%)
  waiting for transfers between devices  31.9 us (17%)
  local copies, waits for them, and re-layouts  21.4 us (11%)
  other arithmetic  9.68 us (5%)
    ppermute x40, starting transfers between devices, swap(): return lax.ppermute(block, ('grp',) + AXES, pairs)  83.6 us
    ppermute x40, waiting for transfers between devices, swap(): return lax.ppermute(block, ('grp',) + AXES, pairs)  26.4 us
    pallas_call x1, Pallas kernels, learn_call(): pl.pallas_call(functools.partial(learn_kernel, count=count, experts=exper...  19 us
    unnamed x17, local copies, waits for them, and re-layouts  16.2 us
    pallas_call x1, Pallas kernels, ffn_call(): pl.pallas_call(functools.partial(ffn_kernel, count=count, experts=experts...  14.5 us
    ppermute x4, starting transfers between devices, across(): return lax.ppermute(block, 'grp', [(source, target)])  7.87 us
    ppermute x4, waiting for transfers between devices, across(): return lax.ppermute(block, 'grp', [(source, target)])  5.57 us
  transfers between devices with their start and end apart: 44, of which 15 were waited for; matrix products, arithmetic and copies ran while one was open for 14% of the time, Pallas kernels for 18%

profile of v7, /device:TPU:0, one launch (start us, length us, event | category | flops | bytes accessed | tf_op | source)
XLA Modules:
  0.0 191.0 jit_solution(6437805638683070032)
XLA Ops:
  2.5 3.1 %collective-permute-start = (bf16[16,4224]{1,0:T(8,128)(2,1)}, bf16[16,4224]{1,0:T(8,128)(2,1)S(1)}, u32[]{:S(2)}, u32[]{:S(2)}) collective-permute-start(bf16[16,4224]{1,0:T(8,128)(2,1)} %get-tuple-element.196), channel_id=1, source_target_pairs={{0,4},{1,5},{2,6},{3,7},{4,0},{5,1},{6,2},{7,3},{8,12},{9,13},{10,... | collective-permute-start | bytes 405512 | tf_op jit(solution)/shard_map/ppermute | solution.py:39
  5.6 2.6 %collective-permute-start.2 = (bf16[16,4224]{1,0:T(8,128)(2,1)}, bf16[16,4224]{1,0:T(8,128)(2,1)S(1)}, u32[]{:S(2)}, u32[]{:S(2)}) collective-permute-start(bf16[16,4224]{1,0:T(8,128)(2,1)} %get-tuple-element.196), channel_id=1, source_target_pairs={{0,8},{1,9},{2,10},{3,11},{4,12},{5,13},{6,14},{7,15},{8,0},{9,1},... | collective-permute-start | bytes 405512 | tf_op jit(solution)/shard_map/ppermute | solution.py:39
  8.2 11.9 %copy.12 = bf16[1,1,4096,2,768]{4,2,3,1,0:T(8,128)(2,1)} copy(bf16[1,1,4096,2,768]{4,3,2,1,0:T(2,128)(2,1)} %param.22) | data formatting | bytes 25165824 | tf_op args[7]
  20.1 3.8 %collective-permute-start.6 = (bf16[16,4096]{1,0:T(8,128)(2,1)S(1)}, bf16[16,4096]{1,0:T(8,128)(2,1)S(1)}, u32[]{:S(2)}, u32[]{:S(2)}) collective-permute-start(bf16[16,4096]{1,0:T(8,128)(2,1)S(1)} %copy-done.5), channel_id=1, source_target_pairs={{0,8},{1,9},{2,10},{3,11},{4,12},{5,13},{6,14},{7,15},{8,0},{9,1},... | collective-permute-start | bytes 393224 | tf_op jit(solution)/shard_map/ppermute | solution.py:39
  23.9 3.8 %collective-permute-start.7 = (bf16[16,4096]{1,0:T(8,128)(2,1)S(1)}, bf16[16,4096]{1,0:T(8,128)(2,1)S(1)}, u32[]{:S(2)}, u32[]{:S(2)}) collective-permute-start(bf16[16,4096]{1,0:T(8,128)(2,1)S(1)} %copy-done.5), channel_id=1, source_target_pairs={{0,12},{1,13},{2,14},{3,15},{4,8},{5,9},{6,10},{7,11},{8,4},{9,5},... | collective-permute-start | bytes 393224 | tf_op jit(solution)/shard_map/ppermute | solution.py:39
  27.8 2.5 %collective-permute-start.5 = (bf16[16,4096]{1,0:T(8,128)(2,1)S(1)}, bf16[16,4096]{1,0:T(8,128)(2,1)S(1)}, u32[]{:S(2)}, u32[]{:S(2)}) collective-permute-start(bf16[16,4096]{1,0:T(8,128)(2,1)S(1)} %copy-done.5), channel_id=1, source_target_pairs={{0,4},{1,5},{2,6},{3,7},{4,0},{5,1},{6,2},{7,3},{8,12},{9,13},{10,... | collective-permute-start | bytes 393224 | tf_op jit(solution)/shard_map/ppermute | solution.py:39
  32.5 3.7 %collective-permute-done.5 = bf16[16,4096]{1,0:T(8,128)(2,1)S(1)} collective-permute-done((bf16[16,4096]{1,0:T(8,128)(2,1)S(1)}, bf16[16,4096]{1,0:T(8,128)(2,1)S(1)}, u32[]{:S(2)}, u32[]{:S(2)}) %collective-permute-start.5) | collective-permute-done | bytes 131104 | tf_op jit(solution)/shard_map/ppermute | solution.py:39
  36.2 3.5 %collective-permute-done.1 = bf16[32,4224]{1,0:T(8,128)(2,1)S(1)} collective-permute-done((bf16[32,4224]{1,0:T(8,128)(2,1)S(1)}, bf16[32,4224]{1,0:T(8,128)(2,1)S(1)}, u32[]{:S(2)}, u32[]{:S(2)}) %collective-permute-start.1) | collective-permute-done | bytes 270368 | tf_op jit(solution)/shard_map/ppermute | solution.py:39
  39.8 3.1 %collective-permute-done.4 = bf16[32,4224]{1,0:T(8,128)(2,1)S(1)} collective-permute-done((bf16[32,4224]{1,0:T(8,128)(2,1)S(1)}, bf16[32,4224]{1,0:T(8,128)(2,1)S(1)}, u32[]{:S(2)}, u32[]{:S(2)}) %collective-permute-start.4) | collective-permute-done | bytes 270368 | tf_op jit(solution)/shard_map/ppermute | solution.py:39
  43.6 3.4 %collective-permute-start.27 = (bf16[32,4096]{1,0:T(8,128)(2,1)S(1)}, bf16[32,4096]{1,0:T(8,128)(2,1)S(1)}, u32[]{:S(2)}, u32[]{:S(2)}) collective-permute-start(bf16[32,4096]{1,0:T(8,128)(2,1)S(1)} %pad_maximum_fusion.4), channel_id=1, source_target_pairs={{0,2},{1,3},{2,0},{3,1},{4,6},{5,7},{6,4},{7,5},{8,10},{9,11},{10,... | collective-permute-start | bytes 786440 | tf_op jit(solution)/shard_map/ppermute | solution.py:39
  48.6 2.4 %collective-permute-start.17 = (bf16[32,4096]{1,0:T(8,128)(2,1)S(1)}, bf16[32,4096]{1,0:T(8,128)(2,1)S(1)}, u32[]{:S(2)}, u32[]{:S(2)}) collective-permute-start(bf16[32,4096]{1,0:T(8,128)(2,1)S(1)} %pad_maximum_fusion.5), channel_id=1, source_target_pairs={{0,2},{1,3},{2,0},{3,1},{4,6},{5,7},{6,4},{7,5},{8,10},{9,11},{10,... | collective-permute-start | bytes 786440 | tf_op jit(solution)/shard_map/ppermute | solution.py:39
  51.0 3.6 %collective-permute-done.27 = bf16[32,4096]{1,0:T(8,128)(2,1)S(1)} collective-permute-done((bf16[32,4096]{1,0:T(8,128)(2,1)S(1)}, bf16[32,4096]{1,0:T(8,128)(2,1)S(1)}, u32[]{:S(2)}, u32[]{:S(2)}) %collective-permute-start.27) | collective-permute-done | bytes 262176 | tf_op jit(solution)/shard_map/ppermute | solution.py:39
  63.1 2.4 %collective-permute-start.18 = (bf16[64,4096]{1,0:T(8,128)(2,1)S(1)}, bf16[64,4096]{1,0:T(8,128)(2,1)S(1)}, u32[]{:S(2)}, u32[]{:S(2)}) collective-permute-start(bf16[64,4096]{1,0:T(8,128)(2,1)S(1)} %constant_dynamic-update-slice_fusion), channel_id=1, source_target_pairs={{0,1},{1,0},{2,3},{3,2},{4,5},{5,4},{6,7},{7,6},{8,9},{9,8},{10,11... | collective-permute-start | bytes 1572872 | tf_op jit(solution)/shard_map/ppermute | solution.py:39
  68.4 20.7 %conditional.6 = ((bf16[256,4096]{1,0:T(8,128)(2,1)}, bf16[4096,256]{1,0:T(8,128)(2,1)S(1)}, bf16[2,256,768]{2,1,0:T(8,128)(2,1)}, bf16[768,256]{1,0:T(8,128)(2,...) conditional(s32[]{:T(128)} %convert_element_type.172, () %tuple.64, (s32[1]{0:T(128)}, ...), branch_computations={%region_2.0_spmd, %region_3.0_spmd} | conditional | flops 9663676416 | bytes 29491348 | solution.py:556
  70.1 19.0 %learn.1 = (bf16[256,4096]{1,0:T(8,128)(2,1)}, bf16[4096,256]{1,0:T(8,128)(2,1)S(1)}, bf16[2,256,768]{2,1,0:T(8,128)(2,1)}, bf16[768,256]{1,0:T(8,128)(2,1)}, f3...) custom-call(s32[1]{0:T(128)} %get-tuple-element.137.place, bf16[64,4224]{1,0:T(8,128)(2,1)S(1)} %get-tuple-element.138.refs_0_.refs_4_, ...), custom_call_target="tpu_custom_call" | custom-call | flops 9663676416 | bytes 18874368 | tf_op jit(solution)/shard_map/cond/branch_1_fun/learn/pallas_call | solution.py:432
  89.1 4.0 %collective-permute-start.29 = (bf16[256,4096]{1,0:T(8,128)(2,1)}, bf16[256,4096]{1,0:T(8,128)(2,1)}, u32[]{:S(2)}, u32[]{:S(2)}) collective-permute-start(bf16[256,4096]{1,0:T(8,128)(2,1)} %get-tuple-element.216), channel_id=1, source_target_pairs={{0,16},{1,17},{2,18},{3,19},{4,20},{5,21},{6,22},{7,23},{8,24},{9,... | collective-permute-start | bytes 6291464 | tf_op jit(solution)/shard_map/ppermute | solution.py:15
  93.1 5.3 %collective-permute-start.23 = (bf16[16,4096]{1,0:T(8,128)(2,1)}, bf16[16,4096]{1,0:T(8,128)(2,1)S(1)}, u32[]{:S(2)}, u32[]{:S(2)}) collective-permute-start(bf16[16,4096]{1,0:T(8,128)(2,1)} %collective-permute-done.19), channel_id=1, source_target_pairs={{0,8},{1,9},{2,10},{3,11},{4,12},{5,13},{6,14},{7,15},{8,0},{9,1},... | collective-permute-start | bytes 393224 | tf_op jit(solution)/shard_map/ppermute | solution.py:39
  98.4 3.2 %collective-permute-start.24 = (bf16[16,4096]{1,0:T(8,128)(2,1)}, bf16[16,4096]{1,0:T(8,128)(2,1)S(1)}, u32[]{:S(2)}, u32[]{:S(2)}) collective-permute-start(bf16[16,4096]{1,0:T(8,128)(2,1)} %collective-permute-done.19), channel_id=1, source_target_pairs={{0,12},{1,13},{2,14},{3,15},{4,8},{5,9},{6,10},{7,11},{8,4},{9,5},... | collective-permute-start | bytes 393224 | tf_op jit(solution)/shard_map/ppermute | solution.py:39
  108.4 3.4 %collective-permute-start.25 = (bf16[32,4096]{1,0:T(8,128)(2,1)S(1)}, bf16[32,4096]{1,0:T(8,128)(2,1)S(1)}, u32[]{:S(2)}, u32[]{:S(2)}) collective-permute-start(bf16[32,4096]{1,0:T(8,128)(2,1)S(1)} %pad_maximum_fusion.7), channel_id=1, source_target_pairs={{0,2},{1,3},{2,0},{3,1},{4,6},{5,7},{6,4},{7,5},{8,10},{9,11},{10,... | collective-permute-start | bytes 786440 | tf_op jit(solution)/shard_map/ppermute | solution.py:39
  112.8 2.6 %collective-permute-start.21 = (bf16[32,4096]{1,0:T(8,128)(2,1)S(1)}, bf16[32,4096]{1,0:T(8,128)(2,1)S(1)}, u32[]{:S(2)}, u32[]{:S(2)}) collective-permute-start(bf16[32,4096]{1,0:T(8,128)(2,1)S(1)} %pad_maximum_fusion.6), channel_id=1, source_target_pairs={{0,2},{1,3},{2,0},{3,1},{4,6},{5,7},{6,4},{7,5},{8,10},{9,11},{10,... | collective-permute-start | bytes 786440 | tf_op jit(solution)/shard_map/ppermute | solution.py:39
  125.0 2.2 %collective-permute-done.22 = bf16[64,4096]{1,0:T(8,128)(2,1)} collective-permute-done((bf16[64,4096]{1,0:T(8,128)(2,1)}, bf16[64,4096]{1,0:T(8,128)(2,1)}, u32[]{:S(2)}, u32[]{:S(2)}) %collective-permute-start.22) | collective-permute-done | bytes 524320 | tf_op jit(solution)/shard_map/ppermute | solution.py:39
  127.2 14.5 %conditional.15 = (bf16[64,4096]{1,0:T(8,128)(2,1)}, bf16[64,4096]{1,0:T(8,128)(2,1)}, bf16[64,4096]{1,0:T(8,128)(2,1)}, bf16[64,4096]{1,0:T(8,128)(2,1)}) conditional(s32[]{:T(128)} %convert_element_type.172, () %tuple.57, (s32[1]{0:T(128)}, bf16[64,4096]{1,0:T(8,128)(2,1)}, bf16[64,4096]{1,0:T(8,128)(2,1)}, bf16[64,4096]{1,0:T(8,128)(2,1)}, ...), branch_computations={%region_4.0_spmd, %region_5.0_spmd} | conditional | flops 4831838208 | bytes 18874412
  127.2 14.5 %ffn_changed.2 = (bf16[64,4096]{1,0:T(8,128)(2,1)}, bf16[64,4096]{1,0:T(8,128)(2,1)}, bf16[64,4096]{1,0:T(8,128)(2,1)}, bf16[64,4096]{1,0:T(8,128)(2,1)}) custom-call(s32[1]{0:T(128)S(6)} %add.49.place, bf16[64,4096]{1,0:T(8,128)(2,1)} %get-tuple-element.149.refs_0_, bf16[64,4096]{1,0:T(8,128)(2,1)} %get-tuple-element.150.refs_1_, ...), custom_call_target="tpu_custom_call" | custom-call | flops 4831838208 | bytes 18874368 | tf_op jit(solution)/shard_map/cond/branch_1_fun/ffn_changed/pallas_call | solution.py:307
  141.7 2.0 %collective-permute-start.36 = (bf16[64,4096]{1,0:T(8,128)(2,1)}, bf16[64,4096]{1,0:T(8,128)(2,1)S(1)}, u32[]{:S(2)}, u32[]{:S(2)}) collective-permute-start(bf16[64,4096]{1,0:T(8,128)(2,1)} %get-tuple-element.219), channel_id=1, source_target_pairs={{0,1},{1,0},{2,3},{3,2},{4,5},{5,4},{6,7},{7,6},{8,9},{9,8},{10,11... | collective-permute-start | bytes 1572872 | tf_op jit(solution)/shard_map/ppermute | solution.py:39
  143.8 2.3 %collective-permute-start.39 = (bf16[64,4096]{1,0:T(8,128)(2,1)}, bf16[64,4096]{1,0:T(8,128)(2,1)S(1)}, u32[]{:S(2)}, u32[]{:S(2)}) collective-permute-start(bf16[64,4096]{1,0:T(8,128)(2,1)} %get-tuple-element.221), channel_id=1, source_target_pairs={{0,1},{1,0},{2,3},{3,2},{4,5},{5,4},{6,7},{7,6},{8,9},{9,8},{10,11... | collective-permute-start | bytes 1572872 | tf_op jit(solution)/shard_map/ppermute | solution.py:39
  147.3 3.4 %collective-permute-start.37 = (bf16[32,4096]{1,0:T(8,128)(2,1)S(1)}, bf16[32,4096]{1,0:T(8,128)(2,1)S(1)}, u32[]{:S(2)}, u32[]{:S(2)}) collective-permute-start(bf16[32,4096]{1,0:T(8,128)(2,1)S(1)} %split.111), channel_id=1, source_target_pairs={{0,2},{1,3},{2,0},{3,1},{4,6},{5,7},{6,4},{7,5},{8,10},{9,11},{10,... | collective-permute-start | bytes 786440 | tf_op jit(solution)/shard_map/ppermute | solution.py:39
  153.9 2.4 %collective-permute-start.40 = (bf16[32,4096]{1,0:T(8,128)(2,1)S(1)}, bf16[32,4096]{1,0:T(8,128)(2,1)S(1)}, u32[]{:S(2)}, u32[]{:S(2)}) collective-permute-start(bf16[32,4096]{1,0:T(8,128)(2,1)S(1)} %split.115), channel_id=1, source_target_pairs={{0,2},{1,3},{2,0},{3,1},{4,6},{5,7},{6,4},{7,5},{8,10},{9,11},{10,... | collective-permute-start | bytes 786440 | tf_op jit(solution)/shard_map/ppermute | solution.py:39
  157.6 6.0 %collective-permute-start.38 = (bf16[16,4096]{1,0:T(8,128)(2,1)S(1)}, bf16[16,4096]{1,0:T(8,128)(2,1)S(1)}, u32[]{:S(2)}, u32[]{:S(2)}) collective-permute-start(bf16[16,4096]{1,0:T(8,128)(2,1)S(1)} %split.113), channel_id=1, source_target_pairs={{0,4},{1,5},{2,6},{3,7},{4,0},{5,1},{6,2},{7,3},{8,12},{9,13},{10,... | collective-permute-start | bytes 393224 | tf_op jit(solution)/shard_map/ppermute | solution.py:39
  166.2 5.7 %collective-permute-start.41 = (bf16[16,4096]{1,0:T(8,128)(2,1)S(1)}, bf16[16,4096]{1,0:T(8,128)(2,1)S(1)}, u32[]{:S(2)}, u32[]{:S(2)}) collective-permute-start(bf16[16,4096]{1,0:T(8,128)(2,1)S(1)} %get-tuple-element.233), channel_id=1, source_target_pairs={{0,8},{1,9},{2,10},{3,11},{4,12},{5,13},{6,14},{7,15},{8,0},{9,1},... | collective-permute-start | bytes 393224 | tf_op jit(solution)/shard_map/ppermute | solution.py:39
  171.9 4.6 %collective-permute-start.42 = (bf16[16,4096]{1,0:T(8,128)(2,1)S(1)}, bf16[16,4096]{1,0:T(8,128)(2,1)S(1)}, u32[]{:S(2)}, u32[]{:S(2)}) collective-permute-start(bf16[16,4096]{1,0:T(8,128)(2,1)S(1)} %get-tuple-element.234), channel_id=1, source_target_pairs={{0,12},{1,13},{2,14},{3,15},{4,8},{5,9},{6,10},{7,11},{8,4},{9,5},... | collective-permute-start | bytes 393224 | tf_op jit(solution)/shard_map/ppermute | solution.py:39
  178.7 2.4 %collective-permute-done.41 = bf16[16,4096]{1,0:T(8,128)(2,1)S(1)} collective-permute-done((bf16[16,4096]{1,0:T(8,128)(2,1)S(1)}, bf16[16,4096]{1,0:T(8,128)(2,1)S(1)}, u32[]{:S(2)}, u32[]{:S(2)}) %collective-permute-start.41) | collective-permute-done | bytes 131104 | tf_op jit(solution)/shard_map/ppermute | solution.py:39
  184.9 4.5 %collective-permute-done.35 = bf16[16,4096]{1,0:T(8,128)(2,1)S(1)} collective-permute-done((bf16[16,4096]{1,0:T(8,128)(2,1)S(1)}, bf16[16,4096]{1,0:T(8,128)(2,1)S(1)}, u32[]{:S(2)}, u32[]{:S(2)}) %collective-permute-start.35) | collective-permute-done | bytes 131104 | tf_op jit(solution)/shard_map/ppermute | solution.py:15
  (131 shorter events, 52.6 us)
Async XLA Ops:
  2.5 17.5 %collective-permute-start = (bf16[16,4224]{1,0:T(8,128)(2,1)}, bf16[16,4224]{1,0:T(8,128)(2,1)S(1)}, u32[]{:S(2)}, u32[]{:S(2)}) collective-permute-start(bf16[16,4224]{1,0:T(8,128)(2,1)} %get-tuple-element.196), channel_id=1, source_target_pairs={{0,4},{1,5},{2,6},{3,7},{4,0},{5,1},{6,2},{7,3},{8,12},{9,13},{10,... | collective-permute-start | bytes 405512 | tf_op jit(solution)/shard_map/ppermute | solution.py:39
  5.6 24.6 %collective-permute-start.2 = (bf16[16,4224]{1,0:T(8,128)(2,1)}, bf16[16,4224]{1,0:T(8,128)(2,1)S(1)}, u32[]{:S(2)}, u32[]{:S(2)}) collective-permute-start(bf16[16,4224]{1,0:T(8,128)(2,1)} %get-tuple-element.196), channel_id=1, source_target_pairs={{0,8},{1,9},{2,10},{3,11},{4,12},{5,13},{6,14},{7,15},{8,0},{9,1},... | collective-permute-start | bytes 405512 | tf_op jit(solution)/shard_map/ppermute | solution.py:39
  8.2 23.7 %collective-permute-start.3 = (bf16[16,4224]{1,0:T(8,128)(2,1)}, bf16[16,4224]{1,0:T(8,128)(2,1)S(1)}, u32[]{:S(2)}, u32[]{:S(2)}) collective-permute-start(bf16[16,4224]{1,0:T(8,128)(2,1)} %get-tuple-element.196), channel_id=1, source_target_pairs={{0,12},{1,13},{2,14},{3,15},{4,8},{5,9},{6,10},{7,11},{8,4},{9,5},... | collective-permute-start | bytes 405512 | tf_op jit(solution)/shard_map/ppermute | solution.py:39
  20.1 16.0 %collective-permute-start.6 = (bf16[16,4096]{1,0:T(8,128)(2,1)S(1)}, bf16[16,4096]{1,0:T(8,128)(2,1)S(1)}, u32[]{:S(2)}, u32[]{:S(2)}) collective-permute-start(bf16[16,4096]{1,0:T(8,128)(2,1)S(1)} %copy-done.5), channel_id=1, source_target_pairs={{0,8},{1,9},{2,10},{3,11},{4,12},{5,13},{6,14},{7,15},{8,0},{9,1},... | collective-permute-start | bytes 393224 | tf_op jit(solution)/shard_map/ppermute | solution.py:39
  23.9 12.2 %collective-permute-start.7 = (bf16[16,4096]{1,0:T(8,128)(2,1)S(1)}, bf16[16,4096]{1,0:T(8,128)(2,1)S(1)}, u32[]{:S(2)}, u32[]{:S(2)}) collective-permute-start(bf16[16,4096]{1,0:T(8,128)(2,1)S(1)} %copy-done.5), channel_id=1, source_target_pairs={{0,12},{1,13},{2,14},{3,15},{4,8},{5,9},{6,10},{7,11},{8,4},{9,5},... | collective-permute-start | bytes 393224 | tf_op jit(solution)/shard_map/ppermute | solution.py:39
  27.8 8.4 %collective-permute-start.5 = (bf16[16,4096]{1,0:T(8,128)(2,1)S(1)}, bf16[16,4096]{1,0:T(8,128)(2,1)S(1)}, u32[]{:S(2)}, u32[]{:S(2)}) collective-permute-start(bf16[16,4096]{1,0:T(8,128)(2,1)S(1)} %copy-done.5), channel_id=1, source_target_pairs={{0,4},{1,5},{2,6},{3,7},{4,0},{5,1},{6,2},{7,3},{8,12},{9,13},{10,... | collective-permute-start | bytes 393224 | tf_op jit(solution)/shard_map/ppermute | solution.py:39
  30.3 9.5 %collective-permute-start.1 = (bf16[32,4224]{1,0:T(8,128)(2,1)S(1)}, bf16[32,4224]{1,0:T(8,128)(2,1)S(1)}, u32[]{:S(2)}, u32[]{:S(2)}) collective-permute-start(bf16[32,4224]{1,0:T(8,128)(2,1)S(1)} %pad_maximum_fusion.2), channel_id=1, source_target_pairs={{0,2},{1,3},{2,0},{3,1},{4,6},{5,7},{6,4},{7,5},{8,10},{9,11},{10,... | collective-permute-start | bytes 811016 | tf_op jit(solution)/shard_map/ppermute | solution.py:39
  31.9 11.1 %collective-permute-start.4 = (bf16[32,4224]{1,0:T(8,128)(2,1)S(1)}, bf16[32,4224]{1,0:T(8,128)(2,1)S(1)}, u32[]{:S(2)}, u32[]{:S(2)}) collective-permute-start(bf16[32,4224]{1,0:T(8,128)(2,1)S(1)} %pad_maximum_fusion.3), channel_id=1, source_target_pairs={{0,2},{1,3},{2,0},{3,1},{4,6},{5,7},{6,4},{7,5},{8,10},{9,11},{10,... | collective-permute-start | bytes 811016 | tf_op jit(solution)/shard_map/ppermute | solution.py:39
  43.0 4.8 %collective-permute-start.8 = (bf16[64,4224]{1,0:T(8,128)(2,1)S(1)}, bf16[64,4224]{1,0:T(8,128)(2,1)S(1)}, u32[]{:S(2)}, u32[]{:S(2)}) collective-permute-start(bf16[64,4224]{1,0:T(8,128)(2,1)S(1)} %pad_maximum_fusion), channel_id=1, source_target_pairs={{0,1},{1,0},{2,3},{3,2},{4,5},{5,4},{6,7},{7,6},{8,9},{9,8},{10,11... | collective-permute-start | bytes 1622024 | tf_op jit(solution)/shard_map/ppermute | solution.py:39
  43.6 11.0 %collective-permute-start.27 = (bf16[32,4096]{1,0:T(8,128)(2,1)S(1)}, bf16[32,4096]{1,0:T(8,128)(2,1)S(1)}, u32[]{:S(2)}, u32[]{:S(2)}) collective-permute-start(bf16[32,4096]{1,0:T(8,128)(2,1)S(1)} %pad_maximum_fusion.4), channel_id=1, source_target_pairs={{0,2},{1,3},{2,0},{3,1},{4,6},{5,7},{6,4},{7,5},{8,10},{9,11},{10,... | collective-permute-start | bytes 786440 | tf_op jit(solution)/shard_map/ppermute | solution.py:39
  47.8 10.1 %collective-permute-start.10 = (bf16[64,4096]{1,0:T(8,128)(2,1)}, bf16[64,4096]{1,0:T(8,128)(2,1)S(1)}, u32[]{:S(2)}, u32[]{:S(2)}) collective-permute-start(bf16[64,4096]{1,0:T(8,128)(2,1)} %get-tuple-element.203), channel_id=1, source_target_pairs={{16,17},{17,16},{18,19},{19,18},{20,21},{21,20},{22,23},{23,22},{2... | collective-permute-start | bytes 1572872 | tf_op jit(solution)/shard_map/ppermute | solution.py:39
  48.6 14.5 %collective-permute-start.17 = (bf16[32,4096]{1,0:T(8,128)(2,1)S(1)}, bf16[32,4096]{1,0:T(8,128)(2,1)S(1)}, u32[]{:S(2)}, u32[]{:S(2)}) collective-permute-start(bf16[32,4096]{1,0:T(8,128)(2,1)S(1)} %pad_maximum_fusion.5), channel_id=1, source_target_pairs={{0,2},{1,3},{2,0},{3,1},{4,6},{5,7},{6,4},{7,5},{8,10},{9,11},{10,... | collective-permute-start | bytes 786440 | tf_op jit(solution)/shard_map/ppermute | solution.py:39
  55.3 13.0 %collective-permute-start.28 = (bf16[64,4096]{1,0:T(8,128)(2,1)}, bf16[64,4096]{1,0:T(8,128)(2,1)S(1)}, u32[]{:S(2)}, u32[]{:S(2)}) collective-permute-start(bf16[64,4096]{1,0:T(8,128)(2,1)} %constant_dynamic-update-slice_fusion.8), channel_id=1, source_target_pairs={{0,1},{1,0},{2,3},{3,2},{4,5},{5,4},{6,7},{7,6},{8,9},{9,8},{10,11... | collective-permute-start | bytes 1572872 | tf_op jit(solution)/shard_map/ppermute | solution.py:39
  67.1 26.1 %collective-permute-start.19 = (bf16[16,4096]{1,0:T(8,128)(2,1)}, bf16[16,4096]{1,0:T(8,128)(2,1)}, u32[]{:S(2)}, u32[]{:S(2)}) collective-permute-start(bf16[16,4096]{1,0:T(8,128)(2,1)} %add_convert_fusion.10), channel_id=1, source_target_pairs={{16,0},{17,1},{18,2},{19,3},{20,4},{21,5},{22,6},{23,7},{24,8},{25... | collective-permute-start | bytes 393224 | tf_op jit(solution)/shard_map/ppermute | solution.py:15
  89.1 54.6 %collective-permute-start.29 = (bf16[256,4096]{1,0:T(8,128)(2,1)}, bf16[256,4096]{1,0:T(8,128)(2,1)}, u32[]{:S(2)}, u32[]{:S(2)}) collective-permute-start(bf16[256,4096]{1,0:T(8,128)(2,1)} %get-tuple-element.216), channel_id=1, source_target_pairs={{0,16},{1,17},{2,18},{3,19},{4,20},{5,21},{6,22},{7,23},{8,24},{9,... | collective-permute-start | bytes 6291464 | tf_op jit(solution)/shard_map/ppermute | solution.py:15
  93.1 13.9 %collective-permute-start.23 = (bf16[16,4096]{1,0:T(8,128)(2,1)}, bf16[16,4096]{1,0:T(8,128)(2,1)S(1)}, u32[]{:S(2)}, u32[]{:S(2)}) collective-permute-start(bf16[16,4096]{1,0:T(8,128)(2,1)} %collective-permute-done.19), channel_id=1, source_target_pairs={{0,8},{1,9},{2,10},{3,11},{4,12},{5,13},{6,14},{7,15},{8,0},{9,1},... | collective-permute-start | bytes 393224 | tf_op jit(solution)/shard_map/ppermute | solution.py:39
  98.4 10.0 %collective-permute-start.24 = (bf16[16,4096]{1,0:T(8,128)(2,1)}, bf16[16,4096]{1,0:T(8,128)(2,1)S(1)}, u32[]{:S(2)}, u32[]{:S(2)}) collective-permute-start(bf16[16,4096]{1,0:T(8,128)(2,1)} %collective-permute-done.19), channel_id=1, source_target_pairs={{0,12},{1,13},{2,14},{3,15},{4,8},{5,9},{6,10},{7,11},{8,4},{9,5},... | collective-permute-start | bytes 393224 | tf_op jit(solution)/shard_map/ppermute | solution.py:39
  101.6 10.3 %collective-permute-start.20 = (bf16[16,4096]{1,0:T(8,128)(2,1)}, bf16[16,4096]{1,0:T(8,128)(2,1)S(1)}, u32[]{:S(2)}, u32[]{:S(2)}) collective-permute-start(bf16[16,4096]{1,0:T(8,128)(2,1)} %collective-permute-done.19), channel_id=1, source_target_pairs={{0,4},{1,5},{2,6},{3,7},{4,0},{5,1},{6,2},{7,3},{8,12},{9,13},{10,... | collective-permute-start | bytes 393224 | tf_op jit(solution)/shard_map/ppermute | solution.py:39
  108.4 9.4 %collective-permute-start.25 = (bf16[32,4096]{1,0:T(8,128)(2,1)S(1)}, bf16[32,4096]{1,0:T(8,128)(2,1)S(1)}, u32[]{:S(2)}, u32[]{:S(2)}) collective-permute-start(bf16[32,4096]{1,0:T(8,128)(2,1)S(1)} %pad_maximum_fusion.7), channel_id=1, source_target_pairs={{0,2},{1,3},{2,0},{3,1},{4,6},{5,7},{6,4},{7,5},{8,10},{9,11},{10,... | collective-permute-start | bytes 786440 | tf_op jit(solution)/shard_map/ppermute | solution.py:39
  112.8 9.5 %collective-permute-start.21 = (bf16[32,4096]{1,0:T(8,128)(2,1)S(1)}, bf16[32,4096]{1,0:T(8,128)(2,1)S(1)}, u32[]{:S(2)}, u32[]{:S(2)}) collective-permute-start(bf16[32,4096]{1,0:T(8,128)(2,1)S(1)} %pad_maximum_fusion.6), channel_id=1, source_target_pairs={{0,2},{1,3},{2,0},{3,1},{4,6},{5,7},{6,4},{7,5},{8,10},{9,11},{10,... | collective-permute-start | bytes 786440 | tf_op jit(solution)/shard_map/ppermute | solution.py:39
  118.6 6.4 %collective-permute-start.26 = (bf16[64,4096]{1,0:T(8,128)(2,1)}, bf16[64,4096]{1,0:T(8,128)(2,1)}, u32[]{:S(2)}, u32[]{:S(2)}) collective-permute-start(bf16[64,4096]{1,0:T(8,128)(2,1)} %constant_dynamic-update-slice_fusion.5), channel_id=1, source_target_pairs={{0,1},{1,0},{2,3},{3,2},{4,5},{5,4},{6,7},{7,6},{8,9},{9,8},{10,11... | collective-permute-start | bytes 1572872 | tf_op jit(solution)/shard_map/ppermute | solution.py:39
  143.8 9.0 %collective-permute-start.39 = (bf16[64,4096]{1,0:T(8,128)(2,1)}, bf16[64,4096]{1,0:T(8,128)(2,1)S(1)}, u32[]{:S(2)}, u32[]{:S(2)}) collective-permute-start(bf16[64,4096]{1,0:T(8,128)(2,1)} %get-tuple-element.221), channel_id=1, source_target_pairs={{0,1},{1,0},{2,3},{3,2},{4,5},{5,4},{6,7},{7,6},{8,9},{9,8},{10,11... | collective-permute-start | bytes 1572872 | tf_op jit(solution)/shard_map/ppermute | solution.py:39
  147.3 10.2 %collective-permute-start.37 = (bf16[32,4096]{1,0:T(8,128)(2,1)S(1)}, bf16[32,4096]{1,0:T(8,128)(2,1)S(1)}, u32[]{:S(2)}, u32[]{:S(2)}) collective-permute-start(bf16[32,4096]{1,0:T(8,128)(2,1)S(1)} %split.111), channel_id=1, source_target_pairs={{0,2},{1,3},{2,0},{3,1},{4,6},{5,7},{6,4},{7,5},{8,10},{9,11},{10,... | collective-permute-start | bytes 786440 | tf_op jit(solution)/shard_map/ppermute | solution.py:39
  152.0 12.0 %collective-permute-start.30 = (bf16[128,4096]{1,0:T(8,128)(2,1)S(1)}, bf16[128,4096]{1,0:T(8,128)(2,1)S(1)}, u32[]{:S(2)}, u32[]{:S(2)}) collective-permute-start(bf16[128,4096]{1,0:T(8,128)(2,1)S(1)} %split.81), channel_id=1, source_target_pairs={{16,17},{17,16},{18,19},{19,18},{20,21},{21,20},{22,23},{23,22},{2... | collective-permute-start | bytes 3145736 | tf_op jit(solution)/shard_map/ppermute | solution.py:39
  153.9 10.0 %collective-permute-start.40 = (bf16[32,4096]{1,0:T(8,128)(2,1)S(1)}, bf16[32,4096]{1,0:T(8,128)(2,1)S(1)}, u32[]{:S(2)}, u32[]{:S(2)}) collective-permute-start(bf16[32,4096]{1,0:T(8,128)(2,1)S(1)} %split.115), channel_id=1, source_target_pairs={{0,2},{1,3},{2,0},{3,1},{4,6},{5,7},{6,4},{7,5},{8,10},{9,11},{10,... | collective-permute-start | bytes 786440 | tf_op jit(solution)/shard_map/ppermute | solution.py:39
  157.6 20.4 %collective-permute-start.38 = (bf16[16,4096]{1,0:T(8,128)(2,1)S(1)}, bf16[16,4096]{1,0:T(8,128)(2,1)S(1)}, u32[]{:S(2)}, u32[]{:S(2)}) collective-permute-start(bf16[16,4096]{1,0:T(8,128)(2,1)S(1)} %split.113), channel_id=1, source_target_pairs={{0,4},{1,5},{2,6},{3,7},{4,0},{5,1},{6,2},{7,3},{8,12},{9,13},{10,... | collective-permute-start | bytes 393224 | tf_op jit(solution)/shard_map/ppermute | solution.py:39
  165.5 11.0 %collective-permute-start.31 = (bf16[64,4096]{1,0:T(8,128)(2,1)S(1)}, bf16[64,4096]{1,0:T(8,128)(2,1)S(1)}, u32[]{:S(2)}, u32[]{:S(2)}) collective-permute-start(bf16[64,4096]{1,0:T(8,128)(2,1)S(1)} %split.105), channel_id=1, source_target_pairs={{16,18},{17,19},{18,16},{19,17},{20,22},{21,23},{22,20},{23,21},{2... | collective-permute-start | bytes 1572872 | tf_op jit(solution)/shard_map/ppermute | solution.py:39
  166.2 14.8 %collective-permute-start.41 = (bf16[16,4096]{1,0:T(8,128)(2,1)S(1)}, bf16[16,4096]{1,0:T(8,128)(2,1)S(1)}, u32[]{:S(2)}, u32[]{:S(2)}) collective-permute-start(bf16[16,4096]{1,0:T(8,128)(2,1)S(1)} %get-tuple-element.233), channel_id=1, source_target_pairs={{0,8},{1,9},{2,10},{3,11},{4,12},{5,13},{6,14},{7,15},{8,0},{9,1},... | collective-permute-start | bytes 393224 | tf_op jit(solution)/shard_map/ppermute | solution.py:39
  171.9 9.1 %collective-permute-start.42 = (bf16[16,4096]{1,0:T(8,128)(2,1)S(1)}, bf16[16,4096]{1,0:T(8,128)(2,1)S(1)}, u32[]{:S(2)}, u32[]{:S(2)}) collective-permute-start(bf16[16,4096]{1,0:T(8,128)(2,1)S(1)} %get-tuple-element.234), channel_id=1, source_target_pairs={{0,12},{1,13},{2,14},{3,15},{4,8},{5,9},{6,10},{7,11},{8,4},{9,5},... | collective-permute-start | bytes 393224 | tf_op jit(solution)/shard_map/ppermute | solution.py:39
  176.7 5.8 %collective-permute-start.32 = (bf16[16,4096]{1,0:T(8,128)(2,1)S(1)}, bf16[16,4096]{1,0:T(8,128)(2,1)S(1)}, u32[]{:S(2)}, u32[]{:S(2)}) collective-permute-start(bf16[16,4096]{1,0:T(8,128)(2,1)S(1)} %get-tuple-element.230), channel_id=1, source_target_pairs={{16,20},{17,21},{18,22},{19,23},{20,16},{21,17},{22,18},{23,19},{2... | collective-permute-start | bytes 393224 | tf_op jit(solution)/shard_map/ppermute | solution.py:39
  177.3 5.1 %collective-permute-start.33 = (bf16[16,4096]{1,0:T(8,128)(2,1)S(1)}, bf16[16,4096]{1,0:T(8,128)(2,1)S(1)}, u32[]{:S(2)}, u32[]{:S(2)}) collective-permute-start(bf16[16,4096]{1,0:T(8,128)(2,1)S(1)} %get-tuple-element.232), channel_id=1, source_target_pairs={{16,24},{17,25},{18,26},{19,27},{20,28},{21,29},{22,30},{23,31},{2... | collective-permute-start | bytes 393224 | tf_op jit(solution)/shard_map/ppermute | solution.py:39
  182.6 6.9 %collective-permute-start.35 = (bf16[16,4096]{1,0:T(8,128)(2,1)S(1)}, bf16[16,4096]{1,0:T(8,128)(2,1)S(1)}, u32[]{:S(2)}, u32[]{:S(2)}) collective-permute-start(bf16[16,4096]{1,0:T(8,128)(2,1)S(1)} %add_convert_fusion.9), channel_id=1, source_target_pairs={{16,0},{17,1},{18,2},{19,3},{20,4},{21,5},{22,6},{23,7},{24,8},{25... | collective-permute-start | bytes 393224 | tf_op jit(solution)/shard_map/ppermute | solution.py:15
  (22 other events, 130.3 us)
